TPU v7x, 32 devices: a whole 2x2x4 slice. The times are simulated.
32 devices in a mesh: task: 4 (over y, core), feat: 8 (over z, x).
Axes of the slice: x: 2, y: 2, z: 4, core: 2. Of those that a mesh axis runs over, the one named last changes fastest.
Arguments:
- tokens: bfloat16 [4, 32, 512, 512], P('task', 'feat'), may hold values from -6 to 6
- cotangent: bfloat16 [4, 32, 512, 512], P('task', 'feat'), may hold values from -6 to 6
- attn_weights: bfloat16 [4096, 512], replicated
- weight_in: bfloat16 [512, 2048], replicated, may hold values from -0.25 to 0.25
- weight_out: bfloat16 [2048, 512], replicated, may hold values from -0.125 to 0.125
- norm_params: float32 [6, 512], replicated
- master_attn: float32 [4096, 512], P(('task', 'feat')), may hold values from -0.25 to 0.25
- master_in: float32 [512, 2048], P(None, ('task', 'feat')), may hold values from -0.25 to 0.25
- master_out: float32 [2048, 512], P(('task', 'feat')), may hold values from -0.125 to 0.125
- first_attn: float32 [4096, 512], P(('task', 'feat')), may hold values from -0.0008544922 to 0.0008544922
- first_in: float32 [512, 2048], P(None, ('task', 'feat')), may hold values from -0.0008544922 to 0.0008544922
- first_out: float32 [2048, 512], P(('task', 'feat')), may hold values from -0.0008544922 to 0.0008544922
- first_norms: float32 [6, 512], replicated, may hold values from -0.0034179688 to 0.0034179688
- second_attn: float32 [4096, 512], P(('task', 'feat')), may hold values from 2.384186e-10 to 9.536744e-10
- second_in: float32 [512, 2048], P(None, ('task', 'feat')), may hold values from 2.384186e-10 to 9.536744e-10
- second_out: float32 [2048, 512], P(('task', 'feat')), may hold values from 2.384186e-10 to 9.536744e-10
- second_norms: float32 [6, 512], replicated, may hold values from 3.8146974e-09 to 1.525879e-08
- sample_count: int32 [4], P('task'), may hold values from 64 to 512, as said below
- feature_count: int32 [4], P('task'), may hold values from 4 to 32, as said below
Outputs:
- block_out: bfloat16 [4, 32, 512, 512], P('task', 'feat')
- input_grad: bfloat16 [4, 32, 512, 512], P('task', 'feat')
- grad_norm: float32 [1], replicated
- new_attn: float32 [4096, 512], P(('task', 'feat'))
- new_in: float32 [512, 2048], P(None, ('task', 'feat'))
- new_out: float32 [2048, 512], P(('task', 'feat'))
- new_norms: float32 [6, 512], replicated
- moment_attn: float32 [4096, 512], P(('task', 'feat'))
- moment_in: float32 [512, 2048], P(None, ('task', 'feat'))
- moment_out: float32 [2048, 512], P(('task', 'feat'))
- moment_norms: float32 [6, 512], replicated
- square_attn: float32 [4096, 512], P(('task', 'feat'))
- square_in: float32 [512, 2048], P(None, ('task', 'feat'))
- square_out: float32 [2048, 512], P(('task', 'feat'))
- square_norms: float32 [6, 512], replicated
- copy_attn: bfloat16 [4096, 512], replicated
- copy_in: bfloat16 [512, 2048], replicated
- copy_out: bfloat16 [2048, 512], replicated
Inputs may be any that keep to these rules, and one draw needn't show every extreme that they name: `sample_count`: each task uses at least 64 samples, and some task uses all 512. `feature_count`: each task uses at least 4 features, and some task uses all 32.
All inputs are finite; a program needn't handle non-finite values.
Results may differ from a plain program's by a relative error of at most 0.015.
Values may be sent and summed in bfloat16 or wider, within the bound.
No kernel may reach another device: no remote copies, remote signals or barrier semaphores. Data moves between devices by JAX's collectives and lax.ppermute only.
A program may use at most 384 MiB of HBM per device.

v0:
```python
import jax
import jax.numpy as jnp
from jax import lax
from jax.sharding import PartitionSpec as P

HEADS = 8
STEP = 5


NEGATIVE = -1e30
LN_EPS = 1e-05
CLIP_AT = 1.0
BETA_ONE = 0.9
BETA_TWO = 0.999
RATE = 0.02
NORM_RATE = 0.25
DECAY = 0.1
ADAM_EPS = 1e-08


def layer_norm(values, gain, shift):
    center = jnp.mean(values, axis=-1, keepdims=True)
    centred = values - center
    spread = jnp.mean(centred * centred, axis=-1, keepdims=True)
    return centred * lax.rsqrt(spread + LN_EPS) * gain + shift


def matmul(left, right):
    return jnp.einsum("...d,de->...e", left, right, preferred_element_type=jnp.float32)


def times_back(left, right):
    return jnp.einsum("...e,de->...d", left, right, preferred_element_type=jnp.float32)


def outer_sum(left, right):
    return jnp.einsum("fsd,fse->de", left, right, preferred_element_type=jnp.float32)


def soft_rows(scores):
    row_max = jnp.max(scores, axis=-1, keepdims=True)
    return row_max + jnp.log(jnp.sum(jnp.exp(scores - row_max), axis=-1, keepdims=True))


def feature_scores(queries, key_rows, key_live, score_scale):
    scores = (
        jnp.einsum("qshe,kshe->shqk", queries, key_rows, preferred_element_type=jnp.float32)
        * score_scale
    )
    return jnp.where(key_live[None, None, None, :], scores, NEGATIVE)


def soft_grad(probs, d_probs):
    return (probs * (d_probs - jnp.sum(probs * d_probs, axis=-1, keepdims=True))).astype(
        jnp.bfloat16
    )


def adam_step(weight, grad, first_m, second_m, rate):
    moment = BETA_ONE * first_m + (1.0 - BETA_ONE) * grad
    square = BETA_TWO * second_m + (1.0 - BETA_TWO) * grad * grad
    fix_one = 1.0 - BETA_ONE**STEP
    fix_two = 1.0 - BETA_TWO**STEP
    fresh = weight - rate * (
        moment / fix_one / (jnp.sqrt(square / fix_two) + ADAM_EPS) + DECAY * weight
    )
    return (fresh, moment, square)


def shards(
    tokens,
    cotangent,
    attn_weights,
    weight_in,
    weight_out,
    norm_params,
    master_attn,
    master_in,
    master_out,
    first_attn,
    first_in,
    first_out,
    first_norms,
    second_attn,
    second_in,
    second_out,
    second_norms,
    sample_count,
    feature_count,
):
    feat_local = tokens.shape[1]
    samples = tokens.shape[2]
    model_width = tokens.shape[3]
    head_count = HEADS
    head_size = model_width // head_count
    score_scale = head_size ** (-0.5)
    feat_total = feat_local * lax.axis_size("feat")
    start_feat = lax.axis_index("feat") * feat_local
    sample_live = jnp.arange(samples) < sample_count[0]
    feat_all_live = jnp.arange(feat_total) < feature_count[0]
    feat_live = start_feat + jnp.arange(feat_local) < feature_count[0]
    live_mask = (feat_live[:, None] & sample_live[None, :]).astype(jnp.float32)[:, :, None]
    weights = attn_weights.reshape(8, model_width, model_width)
    inputs = tokens[0].astype(jnp.float32)

    def sample_heads(rows):
        queries = (
            matmul(rows, weights[0]).astype(jnp.bfloat16).reshape(samples, head_count, head_size)
        )
        key_rows = (
            matmul(rows, weights[1]).astype(jnp.bfloat16).reshape(samples, head_count, head_size)
        )
        values = (
            matmul(rows, weights[2]).astype(jnp.bfloat16).reshape(samples, head_count, head_size)
        )
        scores = (
            jnp.einsum("qhe,khe->hqk", queries, key_rows, preferred_element_type=jnp.float32)
            * score_scale
        )
        scores = jnp.where(sample_live[None, None, :], scores, NEGATIVE)
        return (queries, key_rows, values, scores)

    def sample_forward(rows):
        queries, key_rows, values, scores = sample_heads(rows)
        log_total = soft_rows(scores)
        attn_probs = jnp.exp(scores - log_total).astype(jnp.bfloat16)
        mixed = jnp.einsum("hqk,khe->qhe", attn_probs, values, preferred_element_type=jnp.float32)
        return (mixed.astype(jnp.bfloat16).reshape(samples, model_width), log_total)

    def sample_backward(item):
        rows, d_rows, log_total = item
        queries, key_rows, values, scores = sample_heads(rows)
        attn_probs = jnp.exp(scores - log_total)
        d_mix = d_rows.reshape(samples, head_count, head_size)
        d_probs = jnp.einsum("qhe,khe->hqk", d_mix, values, preferred_element_type=jnp.float32)
        d_scores = soft_grad(attn_probs, d_probs)
        d_query = (
            score_scale
            * jnp.einsum("hqk,khe->qhe", d_scores, key_rows, preferred_element_type=jnp.float32)
        ).astype(jnp.bfloat16)
        d_key = (
            score_scale
            * jnp.einsum("hqk,qhe->khe", d_scores, queries, preferred_element_type=jnp.float32)
        ).astype(jnp.bfloat16)
        d_value = jnp.einsum(
            "hqk,qhe->khe",
            attn_probs.astype(jnp.bfloat16),
            d_mix,
            preferred_element_type=jnp.float32,
        ).astype(jnp.bfloat16)
        return (
            d_query.reshape(samples, model_width),
            d_key.reshape(samples, model_width),
            d_value.reshape(samples, model_width),
        )

    first_f, first_pull = jax.vjp(layer_norm, inputs, norm_params[0], norm_params[1])
    first = first_f.astype(jnp.bfloat16)
    mixed_one, log_one = lax.map(sample_forward, first)
    after_one = inputs + matmul(mixed_one, weights[3])
    second_f, second_pull = jax.vjp(layer_norm, after_one, norm_params[2], norm_params[3])
    second = second_f.astype(jnp.bfloat16)
    query_two = matmul(second, weights[4]).astype(jnp.bfloat16)
    key_two = matmul(second, weights[5]).astype(jnp.bfloat16)
    value_two = matmul(second, weights[6]).astype(jnp.bfloat16)
    key_all, value_all = (
        lax.all_gather(key_two, "feat", axis=0, tiled=True),
        lax.all_gather(value_two, "feat", axis=0, tiled=True),
    )
    query_four = query_two.reshape(feat_local, samples, head_count, head_size)
    key_four = key_all.reshape(feat_total, samples, head_count, head_size)
    value_four = value_all.reshape(feat_total, samples, head_count, head_size)
    scores_two = feature_scores(query_four, key_four, feat_all_live, score_scale)
    log_two = soft_rows(scores_two)
    probs_two = jnp.exp(scores_two - log_two).astype(jnp.bfloat16)
    mixed_two = jnp.einsum(
        "shqk,kshe->qshe", probs_two, value_four, preferred_element_type=jnp.float32
    )
    mixed_two = mixed_two.astype(jnp.bfloat16).reshape(feat_local, samples, model_width)
    after_two = after_one + matmul(mixed_two, weights[7])
    third_f, third_pull = jax.vjp(layer_norm, after_two, norm_params[4], norm_params[5])
    third = third_f.astype(jnp.bfloat16)
    pre_act = matmul(third, weight_in)
    hidden_f, gelu_pull = jax.vjp(jax.nn.gelu, pre_act)
    hidden = hidden_f.astype(jnp.bfloat16)
    result = after_two + matmul(hidden, weight_out)
    block_out = result.astype(jnp.bfloat16)[None]
    d_out = cotangent[0].astype(jnp.float32) * live_mask
    d_out_low = d_out.astype(jnp.bfloat16)
    grad_out_w = outer_sum(hidden, d_out_low)
    d_hidden = times_back(d_out_low, weight_out)
    d_pre = gelu_pull(d_hidden)[0].astype(jnp.bfloat16)
    grad_in_w = outer_sum(third, d_pre)
    d_third = times_back(d_pre, weight_in)
    d_part_two, d_gain_two, d_shift_two = third_pull(d_third)
    d_after_two = d_out + d_part_two
    d_y_two = d_after_two.astype(jnp.bfloat16)
    grad_o_two = outer_sum(mixed_two, d_y_two)
    d_mixed_two = times_back(d_y_two, weights[7]).astype(jnp.bfloat16)
    d_four = d_mixed_two.reshape(feat_local, samples, head_count, head_size)
    scores_two = feature_scores(query_four, key_four, feat_all_live, score_scale)
    probs_full = jnp.exp(scores_two - log_two)
    d_probs = jnp.einsum("qshe,kshe->shqk", d_four, value_four, preferred_element_type=jnp.float32)
    d_scores = soft_grad(probs_full, d_probs)
    d_query = score_scale * jnp.einsum(
        "shqk,kshe->qshe", d_scores, key_four, preferred_element_type=jnp.float32
    )
    d_query = d_query.astype(jnp.bfloat16).reshape(feat_local, samples, model_width)
    probs_low = probs_full.astype(jnp.bfloat16)
    d_key_block = score_scale * jnp.einsum(
        "shqk,qshe->kshe", d_scores, query_four, preferred_element_type=jnp.float32
    )
    d_value_block = jnp.einsum(
        "shqk,qshe->kshe", probs_low, d_four, preferred_element_type=jnp.float32
    )
    key_grads = lax.psum_scatter(
        jnp.concatenate(
            [
                d_key_block.reshape(feat_local * lax.axis_size("feat"), samples, model_width),
                d_value_block.reshape(feat_local * lax.axis_size("feat"), samples, model_width),
            ],
            axis=2,
        ).astype(jnp.bfloat16),
        "feat",
        scatter_dimension=0,
        tiled=True,
    ).astype(jnp.float32)
    d_key = key_grads[:, :, :model_width].astype(jnp.bfloat16)
    d_value = key_grads[:, :, model_width:].astype(jnp.bfloat16)
    grad_q_two = outer_sum(second, d_query)
    grad_k_two = outer_sum(second, d_key)
    grad_v_two = outer_sum(second, d_value)
    d_second = (
        times_back(d_query, weights[4])
        + times_back(d_key, weights[5])
        + times_back(d_value, weights[6])
    )
    d_part_one, d_gain_one, d_shift_one = second_pull(d_second)
    d_after_one = d_after_two + d_part_one
    d_y_one = d_after_one.astype(jnp.bfloat16)
    grad_o_one = outer_sum(mixed_one, d_y_one)
    d_mixed_one = times_back(d_y_one, weights[3]).astype(jnp.bfloat16)
    d_query_one, d_key_one, d_value_one = lax.map(sample_backward, (first, d_mixed_one, log_one))
    grad_q_one = outer_sum(first, d_query_one)
    grad_k_one = outer_sum(first, d_key_one)
    grad_v_one = outer_sum(first, d_value_one)
    d_first = (
        times_back(d_query_one, weights[0])
        + times_back(d_key_one, weights[1])
        + times_back(d_value_one, weights[2])
    )
    d_part_zero, d_gain_zero, d_shift_zero = first_pull(d_first)
    input_grad = (d_after_one + d_part_zero).astype(jnp.bfloat16)[None]
    grad_attn = jnp.concatenate(
        [
            grad_q_one,
            grad_k_one,
            grad_v_one,
            grad_o_one,
            grad_q_two,
            grad_k_two,
            grad_v_two,
            grad_o_two,
        ],
        axis=0,
    )
    grad_norms = jnp.stack(
        [d_gain_zero, d_shift_zero, d_gain_one, d_shift_one, d_gain_two, d_shift_two]
    )
    shard_attn = master_attn.shape[0]
    shard_ff = master_in.shape[1]
    own_index = lax.axis_index(("task", "feat"))
    total_attn, total_in, total_out, total_norms = lax.psum(
        (grad_attn, grad_in_w, grad_out_w, grad_norms), ("task", "feat")
    )
    squares = (
        jnp.sum(total_attn * total_attn)
        + jnp.sum(total_in * total_in)
        + jnp.sum(total_out * total_out)
        + jnp.sum(total_norms * total_norms)
    )
    share_attn = lax.dynamic_slice_in_dim(total_attn, own_index * shard_attn, shard_attn, 0)
    share_in = lax.dynamic_slice_in_dim(total_in, own_index * shard_ff, shard_ff, 1)
    share_out = lax.dynamic_slice_in_dim(total_out, own_index * shard_ff, shard_ff, 0)
    grad_norm = jnp.sqrt(squares)
    factor = jnp.minimum(1.0, CLIP_AT / (grad_norm + 1e-06))
    new_attn, moment_attn, square_attn = adam_step(
        master_attn, factor * share_attn, first_attn, second_attn, RATE
    )
    new_in, moment_in, square_in = adam_step(
        master_in, factor * share_in, first_in, second_in, RATE
    )
    new_out, moment_out, square_out = adam_step(
        master_out, factor * share_out, first_out, second_out, RATE
    )
    new_norms, moment_norms, square_norms = adam_step(
        norm_params, factor * total_norms, first_norms, second_norms, NORM_RATE
    )
    copy_attn, copy_in, copy_out = (
        lax.all_gather(new_attn.astype(jnp.bfloat16), ("task", "feat"), axis=0, tiled=True),
        lax.all_gather(new_in.astype(jnp.bfloat16), ("task", "feat"), axis=1, tiled=True),
        lax.all_gather(new_out.astype(jnp.bfloat16), ("task", "feat"), axis=0, tiled=True),
    )
    return (
        block_out,
        input_grad,
        grad_norm.reshape(1),
        new_attn,
        new_in,
        new_out,
        new_norms,
        moment_attn,
        moment_in,
        moment_out,
        moment_norms,
        square_attn,
        square_in,
        square_out,
        square_norms,
        copy_attn,
        copy_in,
        copy_out,
    )


def solution(mesh):
    placed = (
        P("task", "feat", None, None),
        P("task", "feat", None, None),
        P(),
        P(),
        P(),
        P(),
        P(("task", "feat"), None),
        P(None, ("task", "feat")),
        P(("task", "feat"), None),
        P(("task", "feat"), None),
        P(None, ("task", "feat")),
        P(("task", "feat"), None),
        P(),
        P(("task", "feat"), None),
        P(None, ("task", "feat")),
        P(("task", "feat"), None),
        P(),
        P("task"),
        P("task"),
    )
    return jax.shard_map(
        shards,
        mesh=mesh,
        in_specs=placed,
        out_specs=(
            P("task", "feat", None, None),
            P("task", "feat", None, None),
            P(),
            P(("task", "feat"), None),
            P(None, ("task", "feat")),
            P(("task", "feat"), None),
            P(),
            P(("task", "feat"), None),
            P(None, ("task", "feat")),
            P(("task", "feat"), None),
            P(),
            P(("task", "feat"), None),
            P(None, ("task", "feat")),
            P(("task", "feat"), None),
            P(),
            P(),
            P(),
            P(),
        ),
        check_vma=False,
    )
```

profile of v0, /device:TPU:0, one launch (start us, length us, event | category | flops | bytes accessed | tf_op | source)
XLA Modules:
  0.0 2131.3 jit_solution(3899317272582790122)
XLA Ops:
  8.8 4.1 copy.243
  20.5 4.1 copy.244
  26.1 53.1 %while.28 = (s32[]{:T(128)}, bf16[4,512,512]{1,2,0:T(8,128)(2,1)}, f32[4,8,512,1]{2,1,3,0:T(8,128)}, bf16[4,512,512]{2,1,0:T(8,128)(2,1)}, bf16[8,512,512]{2,1,0:T(8,128)(2,1)}, /*index=5*/s32[]{:T(128)}, s32[]{:T(128)}) while((s32[]{:T(128)}, bf16[4,512,512]{1,2,0:T(8,128)(2,1)}, f32[4,8,512,1]{2,1,3,0:T(8,128)}, ...), condition=%wide.region_5.6_spmd.clone, body=%wide.region_2.5_spmd.clone.sunk | while | flops 1366290944 | bytes 33163372 | solution.py:159
  79.2 3.7 fusion.169
  86.7 3.6 convolution_convert_fusion.11
  90.4 4.3 convolution_convert_fusion.10
  96.1 4.2 copy.261
  100.3 4.9 convolution_convert_fusion.8
  105.2 7.6 copy.253
  112.9 207.9 %all-gather.6.cloned.1.call-done = bf16[32,512,512]{2,1,0:T(8,128)(2,1)} async-done(((bf16[4,512,512]{2,1,0:T(8,128)(2,1)}), bf16[32,512,512]{2,1,0:T(8,128)(2,1)}) %all-gather.6.cloned.1.call-update) | async-done | bytes 16777232 | tf_op jit(solution)/shard_map/all_gather | solution.py:168
  320.8 22.8 %copy.248 = bf16[32,512,512]{1,2,0:T(8,128)(2,1)} copy(bf16[32,512,512]{2,1,0:T(8,128)(2,1)} %all-gather.6.cloned.1.call-done) | data formatting | bytes 33554432 | tf_op jit(solution)/shard_map/all_gather | solution.py:168
  343.6 46.7 %copy.255 = bf16[32,512,8,64]{3,0,2,1:T(8,128)(2,1)} copy(bf16[32,512,8,64]{1,3,2,0:T(8,128)(2,1)} %bitcast.359) | data formatting | bytes 33554432 | tf_op jit(solution)/shard_map/reshape | solution.py:172
  390.4 158.4 %all-gather.8.cloned.1.call-done = bf16[32,512,512]{2,1,0:T(8,128)(2,1)} async-done(((bf16[4,512,512]{2,1,0:T(8,128)(2,1)}), bf16[32,512,512]{2,1,0:T(8,128)(2,1)}) %all-gather.8.cloned.1.call-update) | async-done | bytes 16777232 | tf_op jit(solution)/shard_map/all_gather | solution.py:167
  548.8 22.6 %copy.252 = bf16[32,512,512]{1,2,0:T(8,128)(2,1)} copy(bf16[32,512,512]{2,1,0:T(8,128)(2,1)} %all-gather.8.cloned.1.call-done) | data formatting | bytes 33554432 | tf_op jit(solution)/shard_map/all_gather | solution.py:167
  571.3 46.7 %copy.254 = bf16[32,512,8,64]{3,0,2,1:T(8,128)(2,1)} copy(bf16[32,512,8,64]{1,3,2,0:T(8,128)(2,1)} %bitcast.360) | data formatting | bytes 33554432 | tf_op jit(solution)/shard_map/reshape | solution.py:171
  618.0 24.6 %fusion.170 = (f32[512,8,4]{2,1,0:T(8,128)}, f32[512,8,4,32]{3,2,1,0:T(4,128)}) fusion(bf16[4,512,8,64]{3,0,2,1:T(4,128)(2,1)} %copy.253, bf16[32,512,8,64]{3,0,2,1:T(8,128)(2,1)} %copy.254, pred[32]{0:T(512)(128)(4,1)S(1)} %iota_compare_fusion.3), kind=kOutput, calls=%fused_computation.253 | convolution fusion | flops 68665344 | bytes 21037088 | tf_op jit(solution)/shard_map/qshe,kshe->shqk/dot_general | solution.py:47
  642.6 11.4 exponential_reduce_fusion.1
  655.6 18.3 fusion.75
  673.9 6.9 copy.256
  680.9 4.3 fusion.171
  687.3 8.5 fusion.85
  695.8 17.6 fusion.58
  713.4 10.3 fusion.172
  723.7 5.2 copy.263
  728.9 5.5 multiply_reduce_fusion.3
  738.1 4.1 convolution_convert_fusion.7
  742.1 7.7 copy.266
  749.8 25.8 %multiply_reduce_fusion.2 = (f32[512,8,4]{2,1,0:T(8,128)}, f32[512,8,4,32]{3,2,1,0:T(4,128)}) fusion(f32[512,8,4,32]{3,2,1,0:T(4,128)} %get-tuple-element.350, f32[512,8,4]{2,1,0:T(8,128)S(1)} %copy-done.15, bf16[4,512,8,64]{3,0,2,1:T(4,128)(2,1)} %copy.266, bf16[32,512,8,64]{3,0,2,1:T(8,128)(2,1)} %copy.255), kind=kOutput, calls=%fused_computation.87 | convolution fusion | flops 68665344 | bytes 23199744 | tf_op jit(solution)/shard_map/qshe,kshe->shqk/dot_general | solution.py:203
  775.7 28.1 %convert_bitcast_fusion = bf16[32,512,8,64]{3,0,2,1:T(8,128)(2,1)} fusion(bf16[4,512,8,64]{3,0,2,1:T(4,128)(2,1)} %copy.266, f32[512,8,4,32]{3,2,1,0:T(4,128)} %get-tuple-element.350, f32[512,8,4]{2,1,0:T(8,128)S(1)} %copy-done.15), kind=kOutput, calls=%fused_computation.73 | convolution fusion | flops 76546048 | bytes 21037056 | tf_op jit(solution)/shard_map/shqk,qshe->kshe/dot_general | solution.py:213
  803.8 35.4 %copy.275 = bf16[32,512,8,64]{1,3,2,0:T(8,128)(2,1)} copy(bf16[32,512,8,64]{3,0,2,1:T(8,128)(2,1)} %convert_bitcast_fusion) | data formatting | bytes 33554432 | tf_op jit(solution)/shard_map/shqk,qshe->kshe/transpose | solution.py:213
  839.1 22.6 %copy.277 = bf16[32,512,512]{2,1,0:T(8,128)(2,1)} copy(bf16[32,512,512]{1,2,0:T(8,128)(2,1)} %bitcast.361) | data formatting | bytes 33554432 | tf_op jit(solution)/shard_map/reshape | solution.py:220
  861.7 12.5 multiply_convert_fusion.4
  874.2 16.5 fusion.51
  890.6 35.4 %copy.273 = bf16[32,512,8,64]{1,3,2,0:T(8,128)(2,1)} copy(bf16[32,512,8,64]{3,0,2,1:T(8,128)(2,1)} %fusion.51) | data formatting | bytes 33554432 | tf_op jit(solution)/shard_map/mul | solution.py:210
  926.0 22.5 %copy.276 = bf16[32,512,512]{2,1,0:T(8,128)(2,1)} copy(bf16[32,512,512]{1,2,0:T(8,128)(2,1)} %bitcast.362) | data formatting | bytes 33554432 | tf_op jit(solution)/shard_map/reshape | solution.py:219
  948.5 22.7 %pad_maximum_fusion = bf16[32,512,1024]{2,1,0:T(8,128)(2,1)} fusion(bf16[32,512,512]{2,1,0:T(8,128)(2,1)} %copy.277, bf16[32,512,512]{2,1,0:T(8,128)(2,1)} %copy.276), kind=kLoop, calls=%fused_computation.72 | loop fusion | flops 67108864 | bytes 67108864 | tf_op jit(solution)/shard_map/concatenate | solution.py:217
  971.3 18.0 fusion.76
  989.2 7.0 copy.269
  996.2 11.6 convolution_bitcast_fusion.1
  1007.8 12.3 convolution_bitcast_fusion
  1020.1 492.3 %reduce-scatter.2.cloned.1.call-done = bf16[4,512,1024]{2,1,0:T(8,128)(2,1)} async-done(((bf16[32,512,1024]{2,1,0:T(8,128)(2,1)}), bf16[4,512,1024]{2,1,0:T(8,128)(2,1)}) %reduce-scatter.2.cloned.1.call-update) | async-done | bytes 4194320 | tf_op jit(solution)/shard_map/reduce_scatter | solution.py:216
  1512.4 3.1 fusion.89
  1518.6 3.6 fusion.158
  1526.9 4.2 convolution_convert_fusion.9
  1535.6 85.8 %while.29 = (s32[]{:T(128)}, bf16[4,512,512]{1,2,0:T(8,128)(2,1)}, bf16[4,512,512]{1,2,0:T(8,128)(2,1)}, bf16[4,512,512]{1,2,0:T(8,128)(2,1)}, bf16[4,512,512]{2...) while((s32[]{:T(128)}, bf16[4,512,512]{1,2,0:T(8,128)(2,1)}, ...), condition=%wide.region_20.21_spmd.clone, body=%wide.region_18.20_spmd.clone.sunk | while | flops 2181034496 | bytes 78235784 | solution.py:243
  1547.1 3.0 multiply_reduce_fusion.13
  1550.1 2.9 multiply_convert_fusion.8
  1568.4 3.0 multiply_reduce_fusion.13
  1589.6 3.0 multiply_reduce_fusion.13
  1610.9 3.0 multiply_reduce_fusion.13
  1621.3 4.7 fusion.116
  1656.9 39.9 %psum.31 = f32[6,512]{1,0:T(8,128)S(1)} all-reduce(f32[6,512]{1,0:T(8,128)S(1)} %stack.27), channel_id=1, replica_groups=mesh['task'=4,'feat'=8] {'task','feat'}, use_global_device_ids=true, to_apply=%region_35.36 | all-reduce | flops 3072 | bytes 24576 | tf_op jit(solution)/shard_map/psum | solution.py:273
  1697.4 225.2 %all-reduce.3.cloned.1.call-done = (f32[4096,512]{1,0:T(8,128)}, f32[512,2048]{0,1:T(8,128)}, f32[2048,512]{1,0:T(8,128)}) async-done(((f32[4096,512]{1,0:T(8,128)}, f32[512,2048]{0,1:T(8,128)}, f32[2048,512]{1,0:T(8,128)}), (f32[4096,512]{1,0:T(8,128)}, f32[512,2048]{0,1:T(8,128)}, f32[2048,512]{1,0:T(8,128)})) %all-reduce.3.cloned.1.call-update) | async-done | bytes 16777232 | tf_op jit(solution)/shard_map/psum | solution.py:273
  1922.6 4.0 multiply_reduce_fusion.5
  1926.6 3.9 multiply_reduce_fusion.6
  1941.8 12.5 fusion.78
  1954.3 4.1 copy.301
  1958.5 6.3 fusion.79
  1964.7 4.2 copy.302
  1969.6 24.8 %all-gather.14.cloned.1.call-done = bf16[2048,512]{1,0:T(8,128)(2,1)} async-done(((bf16[64,512]{1,0:T(8,128)(2,1)}), bf16[2048,512]{1,0:T(8,128)(2,1)}) %all-gather.14.cloned.1.call-update) | async-done | bytes 2097168 | tf_op jit(solution)/shard_map/all_gather | solution.py:302
  1994.3 58.8 %all-gather.12.cloned.1.call-done = bf16[512,2048]{0,1:T(8,128)(2,1)} async-done(((bf16[512,64]{0,1:T(8,128)(2,1)}), bf16[512,2048]{0,1:T(8,128)(2,1)}) %all-gather.12.cloned.1.call-update) | async-done | bytes 2097168 | tf_op jit(solution)/shard_map/all_gather | solution.py:301
  2053.2 3.9 copy.303
  2057.1 60.1 %all-gather.10.cloned.1.call-done = bf16[4096,512]{1,0:T(8,128)(2,1)} async-done(((bf16[128,512]{1,0:T(8,128)(2,1)}), bf16[4096,512]{1,0:T(8,128)(2,1)}) %all-gather.10.cloned.1.call-update) | async-done | bytes 4194320 | tf_op jit(solution)/shard_map/all_gather | solution.py:300
  2117.1 4.6 copy.390
  (320 shorter events, 198.5 us)
Async XLA Ops:
  7.2 680.1 %copy-start = (bf16[512,2048]{1,0:T(8,128)(2,1)S(1)}, bf16[512,2048]{1,0:T(8,128)(2,1)}, u32[]{:S(2)}) copy-start(bf16[512,2048]{1,0:T(8,128)(2,1)} %param.26) | copy-start | bytes 6291460
  7.2 313.6 %all-gather.6.cloned.1.call-start = ((), (), s32[]{:S(2)}) async-start(), calls=%async_computation.1 | async-start | bytes 18874368 | tf_op jit(solution)/shard_map/all_gather | solution.py:168
  8.8 9.0 copy-start.65
  8.8 75.8 %copy-start.67 = (f32[1,512]{1,0:T(1,128)}, f32[1,512]{1,0:T(1,128)S(1)}, u32[]{:S(2)}) copy-start(f32[1,512]{1,0:T(1,128)S(1)} %get-tuple-element.343) | copy-start | bytes 6148
  12.9 5.4 copy-start.4
  15.0 2.8 copy-start.38
  90.4 458.4 %all-gather.8.cloned.1.call-start = ((), (), s32[]{:S(2)}) async-start(), calls=%async_computation.2 | async-start | bytes 18874368 | tf_op jit(solution)/shard_map/all_gather | solution.py:167
  94.7 1417.7 %reduce-scatter.2.cloned.1.call-start = ((), (), s32[]{:S(2)}) async-start(), calls=%async_computation.3 | async-start | bytes 37748736 | tf_op jit(solution)/shard_map/reduce_scatter | solution.py:216
  112.9 623.3 %copy-start.59 = (f32[4,512]{1,0:T(4,128)}, f32[4,512]{1,0:T(4,128)S(1)}, u32[]{:S(2)}) copy-start(f32[4,512]{1,0:T(4,128)S(1)} %and_convert_fusion) | copy-start | bytes 24580
  642.6 11.4 copy-start.16
  685.3 49.2 %copy-start.53 = (f32[4,512]{1,0:T(4,128)}, f32[4,512]{1,0:T(4,128)S(1)}, u32[]{:S(2)}) copy-start(f32[4,512]{1,0:T(4,128)S(1)} %broadcast_multiply_fusion) | copy-start | bytes 24580
  685.9 48.6 %copy-start.63 = (f32[4,512]{1,0:T(4,128)}, f32[4,512]{1,0:T(4,128)S(1)}, u32[]{:S(2)}) copy-start(f32[4,512]{1,0:T(4,128)S(1)} %fusion.154) | copy-start | bytes 24580
  687.3 8.5 copy-start.17
  687.3 8.5 copy-start.80
  728.9 5.6 copy-start.7
  728.9 5.9 copy-start.9
  738.1 4.1 copy-start.36
  742.1 7.7 copy-start.15
  861.7 12.5 copy-start.8
  971.2 951.4 %all-reduce.3.cloned.1.call-start = ((), (), s32[]{:S(2)}) async-start(), calls=%async_computation.7 | async-start | bytes 33554432 | tf_op jit(solution)/shard_map/psum | solution.py:273
  989.2 7.0 copy-start.54
  989.2 7.0 copy-start.64
  989.2 7.0 copy-start.71
  989.2 7.0 copy-start.79
  996.2 11.6 copy-start.19
  996.2 11.6 copy-start.60
  1512.4 3.1 copy-start.31
  1515.5 2.6 copy-start.3
  1515.6 3.0 copy-start.25
  1515.6 3.0 copy-start.41
  1515.6 3.0 copy-start.68
  1518.6 3.6 copy-start.58
  1518.6 3.6 copy-start.52
  1526.9 5.6 copy-start.10
  1621.3 4.7 copy-start.20
  1621.3 4.7 copy-start.27
  1628.3 3.2 copy-start.23
  1642.9 351.4 %all-gather.14.cloned.1.call-start = ((), (), s32[]{:S(2)}) async-start(), calls=%async_computation.6 | async-start | bytes 2162688 | tf_op jit(solution)/shard_map/all_gather | solution.py:302
  1644.5 2.4 copy-start.21
  1646.9 2.7 copy-start.5
  1647.0 3.4 copy-start.30
  1647.0 3.4 copy-start.39
  1647.0 3.4 copy-start.66
  1650.4 2.8 copy-start.56
  1650.4 4.7 copy-start.50
  1653.1 3.7 copy-start.74
  1653.1 3.7 copy-start.75
  1653.1 3.7 copy-start.76
  1653.1 3.7 copy-start.77
  1922.6 7.9 copy-start.24
  1930.5 5.5 copy-start.45
  1930.5 5.5 copy-start.46
  1930.5 5.5 copy-start.47
  1930.5 7.3 copy-start.48
  1930.5 9.2 copy-start.42
  1930.5 9.2 copy-start.43
  1930.5 9.2 copy-start.44
  1937.8 115.4 %all-gather.12.cloned.1.call-start = ((), (), s32[]{:S(2)}) async-start(), calls=%async_computation.5 | async-start | bytes 2162688 | tf_op jit(solution)/shard_map/all_gather | solution.py:301
  1939.7 177.4 %all-gather.10.cloned.1.call-start = ((), (), s32[]{:S(2)}) async-start(), calls=%async_computation.4 | async-start | bytes 4325376 | tf_op jit(solution)/shard_map/all_gather | solution.py:300
  1964.7 4.2 copy-start.69
  1964.7 4.2 copy-start.72
  1964.7 4.2 copy-start.73
  2117.1 4.6 copy-start.33
  2117.1 6.0 copy-start.1
  (24 other events, 45.3 us)
Sparse Core Ops, SparseCore 0:
  90.5 230.2 all-gather.5
  322.9 225.7 all-gather.7
  971.3 541.0 reduce-scatter.1
  1643.0 279.5 all-reduce.2
  1937.9 56.3 all-gather.13
  1997.7 55.3 all-gather.11
  2056.1 60.9 all-gather.9
where the time goes:
time: 2150 us; the launch traced here: 2130 us
  waiting for transfers between devices  1230 us (57%)
  matrix products  362 us (17%)
  local copies, waits for them, and re-layouts  358 us (17%)
  other arithmetic  121 us (6%)
  blocking collectives  39.9 us (2%)
    reduce_scatter x1, waiting for transfers between devices, shards(): lax.psum_scatter(jnp.concatenate([d_key_block.reshape(feat_local * lax.ax...  492 us
    psum x1, waiting for transfers between devices, shards(): lax.psum((grad_attn, grad_in_w, grad_out_w, grad_norms), ('task', 'feat'))  225 us
    all_gather x1, waiting for transfers between devices, shards(): lax.all_gather(value_two, 'feat', axis=0, tiled=True)  208 us
    all_gather x1, waiting for transfers between devices, shards(): lax.all_gather(key_two, 'feat', axis=0, tiled=True)  158 us
    dot_general x31, matrix products, matmul(): jnp.einsum('...d,de->...e', left, right, preferred_element_type=jnp.float32)  82.4 us
    all_gather x1, waiting for transfers between devices, shards(): lax.all_gather(new_attn.astype(jnp.bfloat16), ('task', 'feat'), axis=0, t...  60.1 us
    all_gather x1, waiting for transfers between devices, shards(): lax.all_gather(new_in.astype(jnp.bfloat16), ('task', 'feat'), axis=1, til...  58.8 us
    dot_general x10, matrix products, times_back(): jnp.einsum('...e,de->...d', left, right, preferred_element_type=jnp.float32)  53.1 us
  transfers between devices with their start and end apart: 7, of which 7 were waited for; matrix products, arithmetic and copies ran while one was open for 9% of the time, Pallas kernels for 0%

commit v1 on v0

v1 whole, which is shorter than its diff:
```python
import functools

import jax
import jax.numpy as jnp
from jax import lax
from jax.experimental import pallas as pl
from jax.experimental.pallas import tpu as pltpu
from jax.sharding import PartitionSpec as P

HEADS = 8
STEP = 5
NEGATIVE = -1e30
LN_EPS = 1e-05
CLIP_AT = 1.0
BETA_ONE = 0.9
BETA_TWO = 0.999
RATE = 0.02
NORM_RATE = 0.25
DECAY = 0.1
ADAM_EPS = 1e-08

BLOCK = 16
UNIT = 128
ROWS = 128
QUERIES = 256
VMEM_BYTES = 60 * 1024 * 1024

BF = jnp.bfloat16
F32 = jnp.float32
NN = ((1,), (0,))
NT = ((1,), (1,))
TN = ((0,), (0,))


def dot(left, right, dims=NN):
    return lax.dot_general(left, right, (dims, ((), ())), preferred_element_type=F32)


def normalize(values):
    center = jnp.mean(values, axis=-1, keepdims=True)
    centred = values - center
    spread = jnp.mean(centred * centred, axis=-1, keepdims=True)
    scale = lax.rsqrt(spread + LN_EPS)
    return centred * scale, scale


def normalize_back(normal, scale, grad, gain):
    d_normal = grad * gain
    mean_one = jnp.mean(d_normal, axis=-1, keepdims=True)
    mean_two = jnp.mean(d_normal * normal, axis=-1, keepdims=True)
    return scale * (d_normal - mean_one - normal * mean_two)


def column_sum(values):
    return jnp.sum(values, axis=0, keepdims=True)


def row_index(shape):
    return lax.broadcasted_iota(jnp.int32, shape, 0)


def sample_forward(
    counts, tokens, weights, norms, x_out, first_out, heads_out, mixed_out, log_out, turned
):
    samples, width = tokens.shape[1:]
    head_size = width // HEADS
    score_scale = head_size ** (-0.5)
    group = x_out.shape[0] * BLOCK

    @pl.when(pl.program_id(0) == 0)
    def _():
        for which in range(3):
            turned[which] = weights[which].T

    for low in range(0, samples, ROWS):
        rows = slice(low, low + ROWS)
        normal, _ = normalize(tokens[0, rows].astype(F32))
        first_out[0, rows] = (normal * norms[0:1] + norms[1:2]).astype(BF)
    first = first_out[0]
    for which in range(3):
        heads_out[0, which] = dot(turned[which], first, NT).astype(BF)
    live = row_index((samples, 1)) < counts[0]
    for head in range(HEADS):
        lanes = slice(head * head_size, (head + 1) * head_size)
        keys = heads_out[0, 1, lanes]
        values = heads_out[0, 2, lanes]
        for low in range(0, samples, QUERIES):
            cols = slice(low, low + QUERIES)
            scores = dot(keys, heads_out[0, 0, lanes, cols], TN) * score_scale
            scores = jnp.where(live, scores, NEGATIVE)
            top = jnp.max(scores, axis=0, keepdims=True)
            powers = jnp.exp(scores - top)
            total = jnp.sum(powers, axis=0, keepdims=True)
            mixed = dot(values, powers.astype(BF)) * (1.0 / total)
            mixed_out[0, lanes, cols] = mixed.astype(BF)
            log_out[0, head : head + 1, cols] = top + jnp.log(total)
    for low in range(0, samples, group):
        rows = slice(low, low + group)
        part = tokens[0, rows].astype(F32) + dot(mixed_out[0, :, rows], weights[3], TN)
        x_out[:, low // group, 0] = part.astype(BF).reshape(group // BLOCK, BLOCK, width)


def sample_backward(
    counts,
    d_x,
    tokens,
    first,
    heads,
    mixed,
    logs,
    weights,
    norms,
    grad_out,
    weight_out,
    norm_out,
    d_rows,
    d_mix,
    d_heads,
    d_turned,
    total,
    norm_total,
):
    samples, width = tokens.shape[1:]
    head_size = width // HEADS
    score_scale = head_size ** (-0.5)
    group = d_x.shape[0] * BLOCK
    step = pl.program_id(0)

    @pl.when(step == 0)
    def _():
        total[...] = jnp.zeros_like(total)
        norm_total[...] = jnp.zeros_like(norm_total)

    feature_live = counts[2] + step < counts[1]

    @pl.when(jnp.logical_not(feature_live))
    def _():
        grad_out[...] = jnp.zeros_like(grad_out)

    @pl.when(feature_live)
    def _():
        for low in range(0, samples, group):
            d_rows[low : low + group] = d_x[:, low // group, 0].reshape(group, width)
        d_mix[...] = dot(weights[3], d_rows[...], NT).astype(BF)
        total[3] += dot(mixed[0], d_rows[...])
        live = row_index((samples, 1)) < counts[0]
        for head in range(HEADS):
            lanes = slice(head * head_size, (head + 1) * head_size)
            keys = heads[0, 1, lanes]
            values = heads[0, 2, lanes]
            d_key = jnp.zeros((head_size, samples), F32)
            d_value = jnp.zeros((head_size, samples), F32)
            for low in range(0, samples, QUERIES):
                cols = slice(low, low + QUERIES)
                queries = heads[0, 0, lanes, cols]
                grads = d_mix[lanes, cols]
                shared = column_sum(grads.astype(F32) * mixed[0, lanes, cols].astype(F32))
                scores = dot(keys, queries, TN) * score_scale
                scores = jnp.where(live, scores, NEGATIVE)
                probs = jnp.exp(scores - logs[0, head : head + 1, cols])
                d_probs = dot(values, grads, TN)
                d_scores = (probs * (d_probs - shared)).astype(BF)
                d_heads[0, lanes, cols] = (dot(keys, d_scores) * score_scale).astype(BF)
                d_key = d_key + dot(queries, d_scores, NT)
                d_value = d_value + dot(grads, probs.astype(BF), NT)
            d_heads[1, lanes] = (d_key * score_scale).astype(BF)
            d_heads[2, lanes] = d_value.astype(BF)
        for which in range(3):
            d_turned[which] = d_heads[which].T
        for which in range(3):
            total[which] += dot(first[0], d_turned[which], TN)
        for low in range(0, samples, ROWS):
            rows = slice(low, low + ROWS)
            d_first = dot(d_turned[0, rows], weights[0], NT)
            d_first = d_first + dot(d_turned[1, rows], weights[1], NT)
            d_first = d_first + dot(d_turned[2, rows], weights[2], NT)
            normal, scale = normalize(tokens[0, rows].astype(F32))
            norm_total[0:1] += column_sum(d_first * normal)
            norm_total[1:2] += column_sum(d_first)
            back = normalize_back(normal, scale, d_first, norms[0:1])
            grad_out[0, rows] = (d_rows[rows].astype(F32) + back).astype(BF)

    @pl.when(step == pl.num_programs(0) - 1)
    def _():
        weight_out[...] = total[...].astype(BF)
        norm_out[...] = norm_total[...]


def gelu_parts(pre):
    root = 0.7978845608028654
    square = pre * pre
    curve = jnp.tanh(root * pre * (1.0 + 0.044715 * square))
    half = 0.5 * (1.0 + curve)
    slope = half + (0.5 * root) * pre * (1.0 - curve * curve) * (1.0 + 3 * 0.044715 * square)
    return pre * half, slope


def middle(
    counts,
    x_in,
    cot_in,
    weights,
    weight_in,
    weight_out,
    norms,
    y_out,
    d_out,
    grad_in_out,
    grad_out_out,
    grad_attn_out,
    norm_out,
    turned,
    order,
    back_order,
    x_one,
    normal_one,
    scale_one,
    normal_two,
    scale_two,
    x_two,
    low_rows,
    heads,
    d_heads,
    d_turned,
    mixed,
    d_mix,
    probs,
    live_grad,
    third,
    grad_rows,
    total_attn,
    total_in,
    total_out,
    norm_total,
):
    devices, _, local, _, width = x_in.shape
    features = devices * local
    cells = features * BLOCK
    head_size = width // HEADS
    score_scale = head_size ** (-0.5)
    hidden_width = weight_in.shape[1]
    step = pl.program_id(0)
    first_sample = (step * devices + counts[3]) * BLOCK

    @pl.when(step == 0)
    def _():
        for which in range(3):
            turned[which] = weights[which].T
        here = row_index((cells, cells))
        there = lax.broadcasted_iota(jnp.int32, (cells, cells), 1)
        source = (here % features) * BLOCK + here // features
        order[...] = jnp.where(source == there, 1.0, 0.0).astype(BF)
        source = (here % BLOCK) * features + here // BLOCK
        back_order[...] = jnp.where(source == there, 1.0, 0.0).astype(BF)
        total_attn[...] = jnp.zeros_like(total_attn)
        total_in[...] = jnp.zeros_like(total_in)
        total_out[...] = jnp.zeros_like(total_out)
        norm_total[...] = jnp.zeros_like(norm_total)

    x_one[...] = dot(order[...], x_in[:, 0].reshape(cells, width))
    for low in range(0, cells, ROWS):
        rows = slice(low, low + ROWS)
        normal, scale = normalize(x_one[rows])
        normal_one[rows] = normal
        scale_one[rows] = scale
        low_rows[rows] = (normal * norms[2:3] + norms[3:4]).astype(BF)
    for which in range(3):
        heads[which] = dot(turned[which], low_rows[...], NT).astype(BF)

    unit = (UNIT, UNIT)
    key_row = row_index(unit)
    query_row = lax.broadcasted_iota(jnp.int32, unit, 1)
    mask = (key_row // features == query_row // features) & (key_row % features < counts[1])
    for head in range(HEADS):
        lanes = slice(head * head_size, (head + 1) * head_size)
        for place in range(cells // UNIT):
            cols = slice(place * UNIT, (place + 1) * UNIT)
            scores = dot(heads[1, lanes, cols], heads[0, lanes, cols], TN) * score_scale
            scores = jnp.where(mask, scores, NEGATIVE)
            top = jnp.max(scores, axis=0, keepdims=True)
            powers = jnp.exp(scores - top)
            total = jnp.sum(powers, axis=0, keepdims=True)
            prob = powers * (1.0 / total)
            probs[head * (cells // UNIT) + place] = prob
            mixed[lanes, cols] = dot(heads[2, lanes, cols], prob.astype(BF)).astype(BF)
    for low in range(0, cells, ROWS):
        rows = slice(low, low + ROWS)
        part = x_one[rows] + dot(mixed[:, rows], weights[3], TN)
        x_two[rows] = part
        normal, scale = normalize(part)
        normal_two[rows] = normal
        scale_two[rows] = scale
        third[rows] = (normal * norms[4:5] + norms[5:6]).astype(BF)

    alive = first_sample < counts[0]

    @pl.when(jnp.logical_not(alive))
    def _():
        for low in range(0, hidden_width, width):
            cols = slice(low, low + width)
            hidden, _ = gelu_parts(dot(third[...], weight_in[:, cols]))
            x_two[...] += dot(hidden.astype(BF), weight_out[cols])
        d_out[...] = jnp.zeros_like(d_out)

    @pl.when(alive)
    def _():
        place = row_index((cells, 1))
        cell_live = (place % features < counts[1]) & (
            first_sample + place // features < counts[0]
        )
        grads = dot(order[...], cot_in[:, 0].reshape(cells, width))
        live_grad[...] = jnp.where(cell_live, grads, 0.0).astype(BF)
        for low in range(0, hidden_width, width):
            cols = slice(low, low + width)
            hidden, slope = gelu_parts(dot(third[...], weight_in[:, cols]))
            hidden = hidden.astype(BF)
            x_two[...] += dot(hidden, weight_out[cols])
            total_out[cols] += dot(hidden, live_grad[...], TN)
            d_pre = (dot(live_grad[...], weight_out[cols], NT) * slope).astype(BF)
            total_in[cols] += dot(d_pre, third[...], TN)
            d_third = dot(d_pre, weight_in[:, cols], NT)
            if low:
                grad_rows[...] += d_third
            else:
                grad_rows[...] = d_third
        for low in range(0, cells, ROWS):
            rows = slice(low, low + ROWS)
            normal = normal_two[rows]
            d_third = grad_rows[rows]
            norm_total[2:3] += column_sum(d_third * normal)
            norm_total[3:4] += column_sum(d_third)
            back = normalize_back(normal, scale_two[rows], d_third, norms[4:5])
            back = back + live_grad[rows].astype(F32)
            grad_rows[rows] = back
            live_grad[rows] = back.astype(BF)
        d_mix[...] = dot(weights[3], live_grad[...], NT).astype(BF)
        total_attn[3] += dot(mixed[...], live_grad[...])
        for head in range(HEADS):
            lanes = slice(head * head_size, (head + 1) * head_size)
            for place in range(cells // UNIT):
                cols = slice(place * UNIT, (place + 1) * UNIT)
                prob = probs[head * (cells // UNIT) + place]
                grads = d_mix[lanes, cols]
                shared = column_sum(grads.astype(F32) * mixed[lanes, cols].astype(F32))
                d_probs = dot(heads[2, lanes, cols], grads, TN)
                d_scores = (prob * (d_probs - shared)).astype(BF)
                d_query = dot(heads[1, lanes, cols], d_scores) * score_scale
                d_heads[0, lanes, cols] = d_query.astype(BF)
                d_key = dot(heads[0, lanes, cols], d_scores, NT) * score_scale
                d_heads[1, lanes, cols] = d_key.astype(BF)
                d_value = dot(grads, prob.astype(BF), NT)
                d_heads[2, lanes, cols] = d_value.astype(BF)
        for which in range(3):
            d_turned[which] = d_heads[which].T
        for which in range(3):
            total_attn[which] += dot(low_rows[...], d_turned[which], TN)
        for low in range(0, cells, ROWS):
            rows = slice(low, low + ROWS)
            d_second = dot(d_turned[0, rows], weights[0], NT)
            d_second = d_second + dot(d_turned[1, rows], weights[1], NT)
            d_second = d_second + dot(d_turned[2, rows], weights[2], NT)
            normal = normal_one[rows]
            norm_total[0:1] += column_sum(d_second * normal)
            norm_total[1:2] += column_sum(d_second)
            back = normalize_back(normal, scale_one[rows], d_second, norms[2:3])
            live_grad[rows] = (grad_rows[rows] + back).astype(BF)
        moved = dot(back_order[...], live_grad[...]).astype(BF)
        d_out[:, 0] = moved.reshape(devices, local, BLOCK, width)

    moved = dot(back_order[...], x_two[...].astype(BF)).astype(BF)
    y_out[:, 0] = moved.reshape(devices, local, BLOCK, width)

    @pl.when(step == pl.num_programs(0) - 1)
    def _():
        grad_in_out[...] = total_in[...].astype(BF)
        grad_out_out[...] = total_out[...].astype(BF)
        grad_attn_out[...] = total_attn[...].astype(BF)
        norm_out[...] = norm_total[...]


def whole(shape):
    zeros = (0,) * len(shape)
    return pl.BlockSpec(shape, lambda step: zeros, pipeline_mode=pl.Buffered(1))


def once(shape):
    zeros = (0,) * len(shape)
    return pl.BlockSpec(shape, lambda step: zeros)


def lead(shape):
    zeros = (0,) * (len(shape) - 1)
    return pl.BlockSpec((1,) + tuple(shape[1:]), lambda step: (step,) + zeros)


def call(body, grid, in_specs, outs, scratch, flops, name):
    return pl.pallas_call(
        body,
        grid=(grid,),
        in_specs=[pl.BlockSpec(memory_space=pltpu.SMEM)] + in_specs,
        out_specs=[spec for spec, _, _ in outs],
        out_shape=[jax.ShapeDtypeStruct(shape, kind) for _, shape, kind in outs],
        scratch_shapes=[pltpu.VMEM(shape, kind) for shape, kind in scratch],
        compiler_params=pltpu.CompilerParams(vmem_limit_bytes=VMEM_BYTES),
        cost_estimate=pl.CostEstimate(flops=flops, bytes_accessed=1 << 24, transcendentals=0),
        name=name,
    )


def run_sample_forward(counts, tokens, weights, norms, devices):
    local, samples, width = tokens.shape
    deals = samples // (devices * BLOCK)
    dealt = (devices, deals, local, BLOCK, width)
    square = (local, samples, width)
    three = (local, 3, width, samples)
    stats = (local, HEADS, samples)
    return call(
        sample_forward,
        local,
        [lead(square), whole((4, width, width)), whole(norms.shape)],
        [
            (
                pl.BlockSpec(
                    (devices, deals, 1, BLOCK, width), lambda step: (0, 0, step, 0, 0)
                ),
                dealt,
                BF,
            ),
            (lead(square), square, BF),
            (lead(three), three, BF),
            (lead(square), (local, width, samples), BF),
            (lead(stats), stats, F32),
        ],
        [((3, width, width), BF)],
        local * 8 * samples * width * (width + samples // 2),
        "sample_forward",
    )(counts, tokens, weights, norms)


def run_middle(counts, x_dealt, cot_dealt, weights, weight_in, weight_out, norms):
    devices, deals, local, _, width = x_dealt.shape
    cells = devices * local * BLOCK
    hidden_width = weight_in.shape[1]
    dealt = pl.BlockSpec(
        (devices, 1, local, BLOCK, width), lambda step: (0, step, 0, 0, 0)
    )
    square = (cells, width)
    turned = (width, cells)
    units = HEADS * (cells // UNIT)
    return call(
        middle,
        deals,
        [
            dealt,
            dealt,
            whole((4, width, width)),
            whole(weight_in.shape),
            whole(weight_out.shape),
            whole(norms.shape),
        ],
        [
            (dealt, x_dealt.shape, BF),
            (dealt, x_dealt.shape, BF),
            (once((hidden_width, width)), (hidden_width, width), BF),
            (once((hidden_width, width)), (hidden_width, width), BF),
            (once((4, width, width)), (4, width, width), BF),
            (once((4, width)), (4, width), F32),
        ],
        [
            ((3, width, width), BF),
            ((cells, cells), BF),
            ((cells, cells), BF),
            (square, F32),
            (square, F32),
            ((cells, 1), F32),
            (square, F32),
            ((cells, 1), F32),
            (square, F32),
            (square, BF),
            ((3,) + turned, BF),
            ((3,) + turned, BF),
            ((3,) + square, BF),
            (turned, BF),
            (turned, BF),
            ((units, UNIT, UNIT), F32),
            (square, BF),
            (square, BF),
            (square, F32),
            ((4, width, width), F32),
            ((hidden_width, width), F32),
            ((hidden_width, width), F32),
            ((4, width), F32),
        ],
        deals * cells * 6 * width * (4 * width + 2 * hidden_width),
        "middle",
    )(counts, x_dealt, cot_dealt, weights, weight_in, weight_out, norms)


def run_sample_backward(counts, d_dealt, tokens, first, heads, mixed, logs, weights, norms):
    devices, deals, local, _, width = d_dealt.shape
    samples = tokens.shape[1]
    square = (local, samples, width)
    three = (local, 3, width, samples)
    return call(
        sample_backward,
        local,
        [
            pl.BlockSpec((devices, deals, 1, BLOCK, width), lambda step: (0, 0, step, 0, 0)),
            lead(square),
            lead(square),
            lead(three),
            lead(mixed.shape),
            lead(logs.shape),
            whole((4, width, width)),
            whole(norms.shape),
        ],
        [
            (lead(square), square, BF),
            (once((4, width, width)), (4, width, width), BF),
            (once((2, width)), (2, width), F32),
        ],
        [
            ((samples, width), BF),
            ((width, samples), BF),
            ((3, width, samples), BF),
            ((3, samples, width), BF),
            ((4, width, width), F32),
            ((2, width), F32),
        ],
        local * 16 * samples * width * (width + samples),
        "sample_backward",
    )(counts, d_dealt, tokens, first, heads, mixed, logs, weights, norms)


def adam_step(weight, grad, first_m, second_m, rate):
    moment = BETA_ONE * first_m + (1.0 - BETA_ONE) * grad
    square = BETA_TWO * second_m + (1.0 - BETA_TWO) * grad * grad
    fix_one = 1.0 - BETA_ONE**STEP
    fix_two = 1.0 - BETA_TWO**STEP
    fresh = weight - rate * (
        moment / fix_one / (jnp.sqrt(square / fix_two) + ADAM_EPS) + DECAY * weight
    )
    return (fresh, moment, square)


def exchange(values, axis, groups=None):
    return lax.all_to_all(values, axis, 0, 0, axis_index_groups=groups, tiled=True)


def reduce_core(values):
    tasks = lax.axis_size("task")
    core = lax.axis_index("task") % 2
    pairs = [(place, place ^ 1) for place in range(tasks)]
    other = lax.dynamic_index_in_dim(values, 1 - core, 0, keepdims=False)
    mine = lax.dynamic_index_in_dim(values, core, 0, keepdims=False)
    came = lax.ppermute(other, "task", pairs)
    return (mine.astype(F32) + came.astype(F32)).astype(BF)


def reduce_feat(values):
    return jnp.sum(exchange(values, "feat").astype(F32), axis=0)


def reduce_chips(values):
    tasks = lax.axis_size("task")
    chips = tasks // 2
    chip = lax.axis_index("task") // 2
    if chips == 2:
        pairs = [(place, (place + 2) % tasks) for place in range(tasks)]
        other = lax.dynamic_index_in_dim(values, 1 - chip, 0, keepdims=False)
        mine = lax.dynamic_index_in_dim(values, chip, 0, keepdims=False)
        came = lax.ppermute(other, "task", pairs)
        return mine.astype(F32) + came.astype(F32)
    groups = [[2 * place + core for place in range(chips)] for core in range(2)]
    return jnp.sum(exchange(values, "task", groups).astype(F32), axis=0)


def total_of(values):
    count = lax.axis_size("task") * lax.axis_size("feat")
    copies = jnp.broadcast_to(values[None], (count,) + values.shape)
    return jnp.sum(exchange(copies, ("task", "feat")), axis=0)


def shards(
    tokens,
    cotangent,
    attn_weights,
    weight_in,
    weight_out,
    norm_params,
    master_attn,
    master_in,
    master_out,
    first_attn,
    first_in,
    first_out,
    first_norms,
    second_attn,
    second_in,
    second_out,
    second_norms,
    sample_count,
    feature_count,
):
    local, samples, width = tokens.shape[1:]
    devices = lax.axis_size("feat")
    tasks = lax.axis_size("task")
    chips = tasks // 2
    place = lax.axis_index("feat")
    deals = samples // (devices * BLOCK)
    counts = jnp.stack(
        [sample_count[0], feature_count[0], place * local, place]
    ).astype(jnp.int32)
    weights = attn_weights.reshape(8, width, width)
    weights_one, weights_two = weights[:4], weights[4:]

    dealt_cot = cotangent[0].reshape(local, deals, devices, BLOCK, width).transpose(2, 1, 0, 3, 4)
    came_cot = exchange(dealt_cot, "feat")
    dealt_x, first, heads, mixed, logs = run_sample_forward(
        counts, tokens[0], weights_one, norm_params, devices
    )
    came_x = exchange(dealt_x, "feat")
    dealt_y, dealt_d, grad_in, grad_out, grad_two, norms_two = run_middle(
        counts, came_x, came_cot, weights_two, weight_in, weight_out, norm_params
    )
    came_d = exchange(dealt_d, "feat")
    input_grad, grad_one, norms_one = run_sample_backward(
        counts, came_d, tokens[0], first, heads, mixed, logs, weights_one, norm_params
    )
    came_y = exchange(dealt_y, "feat")
    block_out = came_y.transpose(2, 1, 0, 3, 4).reshape(1, local, samples, width)

    own_ff = grad_in.shape[0] // (tasks * devices)
    both = jnp.concatenate(
        [
            grad_in.reshape(chips, 2, devices, own_ff, width),
            grad_out.reshape(chips, 2, devices, own_ff, width),
        ],
        axis=3,
    )
    both = reduce_core(jnp.moveaxis(both, 1, 0))
    both = reduce_chips(both).astype(BF)
    share_ff = reduce_feat(both)

    own_attn = attn_weights.shape[0] // (tasks * devices)
    halves = []
    for grad in (grad_one, grad_two):
        part = grad.reshape(chips // 2, 2, devices, own_attn, width)
        part = reduce_core(jnp.moveaxis(part, 1, 0))
        halves.append(reduce_feat(jnp.moveaxis(part, 1, 0)).astype(BF))
    share_attn = reduce_chips(jnp.concatenate(halves, axis=0))
    total_norms = total_of(jnp.concatenate([norms_one, norms_two], axis=0))

    share_in_turned, share_out = share_ff[:own_ff], share_ff[own_ff:]
    local_squares = jnp.sum(share_ff * share_ff) + jnp.sum(share_attn * share_attn)
    squares = total_of(jnp.full((8, 128), local_squares, F32))[0, 0]
    squares = squares + jnp.sum(total_norms * total_norms)
    grad_norm = jnp.sqrt(squares)
    factor = jnp.minimum(1.0, CLIP_AT / (grad_norm + 1e-06))
    new_attn, moment_attn, square_attn = adam_step(
        master_attn, factor * share_attn, first_attn, second_attn, RATE
    )
    new_in, moment_in, square_in = adam_step(
        master_in, factor * share_in_turned.T, first_in, second_in, RATE
    )
    new_out, moment_out, square_out = adam_step(
        master_out, factor * share_out, first_out, second_out, RATE
    )
    new_norms, moment_norms, square_norms = adam_step(
        norm_params, factor * total_norms, first_norms, second_norms, NORM_RATE
    )
    own = jnp.concatenate(
        [new_attn.astype(BF), new_in.astype(BF).T, new_out.astype(BF)], axis=0
    )
    copies = lax.all_gather(own, ("task", "feat"), axis=0, tiled=False)
    copy_attn = copies[:, :own_attn].reshape(-1, width)
    copy_in = copies[:, own_attn : own_attn + own_ff].reshape(-1, width).T
    copy_out = copies[:, own_attn + own_ff :].reshape(-1, width)
    return (
        block_out,
        input_grad[None],
        grad_norm.reshape(1),
        new_attn,
        new_in,
        new_out,
        new_norms,
        moment_attn,
        moment_in,
        moment_out,
        moment_norms,
        square_attn,
        square_in,
        square_out,
        square_norms,
        copy_attn,
        copy_in,
        copy_out,
    )


def solution(mesh):
    cells = P("task", "feat", None, None)
    rows = P(("task", "feat"), None)
    columns = P(None, ("task", "feat"))
    return jax.shard_map(
        shards,
        mesh=mesh,
        in_specs=(cells, cells, P(), P(), P(), P())
        + (rows, columns, rows)
        + (rows, columns, rows, P())
        + (rows, columns, rows, P())
        + (P("task"), P("task")),
        out_specs=(cells, cells, P())
        + (rows, columns, rows, P())
        + (rows, columns, rows, P())
        + (rows, columns, rows, P())
        + (P(), P(), P()),
        check_vma=False,
    )
```

time: 2150 us -> 626 us (0.29)
  waiting for transfers between devices: 1230 us -> 202 us
  matrix products: 362 us -> 0 us
  local copies, waits for them, and re-layouts: 358 us -> 26.5 us
  Pallas kernels: 0 us -> 187 us
  other arithmetic: 121 us -> 21.4 us
  starting transfers between devices: 0.29 us -> 85 us
  blocking collectives: 39.9 us -> 78.7 us
    all_gather x5 -> x1, waiting for transfers between devices: 510 us -> 12.3 us  [shards(): copies = lax.all_gather(own, ('task', 'feat'), axis=0, tiled=False)]
    reduce_scatter x1 -> x0, waiting for transfers between devices: 492 us -> none  [shards(): lax.psum_scatter(jnp.concatenate([d_key_block.reshape(feat_local * lax.ax...]
    dot_general x85 -> x0, matrix products: 362 us -> none  [the longest x31 82.4 us: matmul(): jnp.einsum('...d,de->...e', left, right, preferred_element_type=jnp.float32)]
    psum x1 -> x0, waiting for transfers between devices: 225 us -> none  [shards(): lax.psum((grad_attn, grad_in_w, grad_out_w, grad_norms), ('task', 'feat'))]
    pallas_call x0 -> x3, Pallas kernels: none -> 187 us  [the longest x1 102 us: run_middle(): call(middle, deals, [dealt, dealt, whole((4, width, width)), whole(weight...]
    all_to_all x0 -> x8, waiting for transfers between devices: none -> 155 us  [exchange(): lax.all_to_all(values, axis, 0, 0, axis_index_groups=groups, tiled=True)]
    reshape x6 -> x0, local copies, waits for them, and re-layouts: 154 us -> none  [the longest x1 46.7 us: shards(): value_four = value_all.reshape(feat_total, samples, head_count, head_size)]
    all_to_all x0 -> x1, blocking collectives: none -> 78.7 us  [exchange(): lax.all_to_all(values, axis, 0, 0, axis_index_groups=groups, tiled=True)]
  transfers between devices with their start and end apart: 7 -> 14, of which waited for: 7 -> 11; matrix products, arithmetic and copies ran while one was open for 9% -> 3% of each run, Pallas kernels for 0% -> 8%
where the time goes in v1:
time: 626 us; the launch traced here: 620 us
  waiting for transfers between devices  202 us (32%)
  Pallas kernels  187 us (30%)
  starting transfers between devices  85 us (14%)
  blocking collectives  78.7 us (13%)
  local copies, waits for them, and re-layouts  26.5 us (4%)
  other arithmetic  21.4 us (3%)
  between operations  19.7 us (3%)
    all_to_all x8, waiting for transfers between devices, exchange(): lax.all_to_all(values, axis, 0, 0, axis_index_groups=groups, tiled=True)  155 us
    pallas_call x1, Pallas kernels, run_middle(): call(middle, deals, [dealt, dealt, whole((4, width, width)), whole(weight...  102 us
    all_to_all x1, blocking collectives, exchange(): lax.all_to_all(values, axis, 0, 0, axis_index_groups=groups, tiled=True)  78.7 us
    all_to_all x8, starting transfers between devices, exchange(): lax.all_to_all(values, axis, 0, 0, axis_index_groups=groups, tiled=True)  51.6 us
    pallas_call x1, Pallas kernels, run_sample_backward(): call(sample_backward, local, [pl.BlockSpec((devices, deals, 1, BLOCK, wid...  48.8 us
    pallas_call x1, Pallas kernels, run_sample_forward(): call(sample_forward, local, [lead(square), whole((4, width, width)), whol...  35.6 us
    ppermute x2, starting transfers between devices, reduce_chips(): came = lax.ppermute(other, 'task', pairs)  33.1 us
    ppermute x2, waiting for transfers between devices, reduce_chips(): came = lax.ppermute(other, 'task', pairs)  29.7 us
  transfers between devices with their start and end apart: 14, of which 11 were waited for; matrix products, arithmetic and copies ran while one was open for 3% of the time, Pallas kernels for 8%

profile of v1, /device:TPU:0, one launch (start us, length us, event | category | flops | bytes accessed | tf_op | source)
XLA Modules:
  0.0 620.0 jit_solution(5134572966808172079)
XLA Ops:
  8.5 4.5 fusion.28
  13.0 0.6 pad_add_fusion.counts
  13.6 35.6 %sample_forward.1 = (bf16[8,4,4,16,512]{4,3,2,1,0:T(8,128)(2,1)}, bf16[4,512,512]{2,1,0:T(8,128)(2,1)}, bf16[4,3,512,512]{3,2,1,0:T(8,128)(2,1)}, bf16[4,512,512]{2,1,0:T(8,128)(2,1)}, f32[4,8,512]{2,1,0:T(8,128)}) custom-call(s32[4]{0:T(128)} %pad_add_fusion.counts, bf16[4,512,512]{2,1,0:T(8,128)(2,1)} %bitcast.95, bf16[4,512,512]{2,1,0:T(8,128)(2,1)} %bitcast.87, ...), custom_call_target="tpu_custom_call" | custom-call | flops 6442450944 | bytes 16777216 | tf_op jit(solution)/shard_map/sample_forward/pallas_call | solution.py:417
  49.2 7.4 %all-to-all-start = ((bf16[8,4,4,16,512]{4,3,2,1,0:T(8,128)(2,1)}), bf16[8,4,4,16,512]{4,3,2,1,0:T(8,128)(2,1)}, u32[]{:S(2)}, u32[]{:S(2)}) async-start(bf16[8,4,4,16,512]{4,3,2,1,0:T(8,128)(2,1)} %get-tuple-element.32), calls=%async_computation | async-start | bytes 4194304 | tf_op jit(solution)/shard_map/all_to_all | solution.py:547
  56.6 1.6 copy.59
  58.3 46.7 %all-to-all-done.x_in = bf16[8,4,4,16,512]{4,3,2,1,0:T(8,128)(2,1)} async-done(((bf16[8,4,4,16,512]{4,3,2,1,0:T(8,128)(2,1)}), bf16[8,4,4,16,512]{4,3,2,1,0:T(8,128)(2,1)}, u32[]{:S(2)}, u32[]{:S(2)}) %all-to-all-start) | async-done | bytes 2097184 | tf_op jit(solution)/shard_map/all_to_all | solution.py:547
  105.0 3.6 all-to-all-start.1
  108.6 48.4 %all-to-all-done.1.cot_in = bf16[8,4,4,16,512]{4,3,2,1,0:T(8,128)(2,1)S(1)} async-done(((bf16[8,4,4,16,512]{4,3,2,1,0:T(8,128)(2,1)}), bf16[8,4,4,16,512]{4,3,2,1,0:T(8,128)(2,1)S(1)}, u32[]{:S(2)}, u32[]{:S(2)}) %all-to-all-start.1) | async-done | bytes 2097184 | tf_op jit(solution)/shard_map/all_to_all | solution.py:547
  157.0 1.3 copy-done.6
  158.3 102.2 %middle.1 = (bf16[8,4,4,16,512]{4,3,2,1,0:T(8,128)(2,1)}, bf16[8,4,4,16,512]{4,3,2,1,0:T(8,128)(2,1)}, bf16[2048,512]{1,0:T(8,128)(2,1)}, bf16[2048,512]{1,0:T(8...) custom-call(s32[4]{0:T(128)} %pad_add_fusion.counts, bf16[8,4,4,16,512]{4,3,2,1,0:T(8,128)(2,1)} %all-to-all-done.x_in, ...), custom_call_target="tpu_custom_call" | custom-call | flops 38654705664 | bytes 16777216 | tf_op jit(solution)/shard_map/middle/pallas_call | solution.py:450
  260.6 1.3 dynamic-slice_bitcast_fusion
  261.9 0.1 collective-permute-start.3
  262.0 2.6 collective-permute-done.3
  264.7 1.0 copy-done.7
  265.6 3.0 fusion.9
  268.6 3.6 all-to-all-start.6
  272.2 2.7 fusion.2
  275.0 0.1 collective-permute-start
  275.1 23.4 %all-to-all-done.6 = bf16[8,1,128,512]{3,2,1,0:T(8,128)(2,1)S(1)} async-done(((bf16[8,1,128,512]{3,2,1,0:T(8,128)(2,1)}), bf16[8,1,128,512]{3,2,1,0:T(8,128)(2,1)S(1)}, u32[]{:S(2)}, u32[]{:S(2)}) %all-to-all-start.6) | async-done | bytes 1048608 | tf_op jit(solution)/shard_map/all_to_all | solution.py:547
  298.4 4.4 all-to-all-start.3
  302.8 2.5 fusion
  305.4 1.3 copy-done.2
  306.7 0.1 dynamic-slice_bitcast_fusion.2
  306.8 31.4 %collective-permute-start.1 = (bf16[8,128,512]{2,1,0:T(8,128)(2,1)S(1)}, bf16[8,128,512]{2,1,0:T(8,128)(2,1)S(1)}, u32[]{:S(2)}, u32[]{:S(2)}) collective-permute-start(bf16[8,128,512]{2,1,0:T(8,128)(2,1)S(1)} %dynamic-slice_bitcast_fusion.2), channel_id=1, source_target_pairs={{0,16},{8,24},{16,0},{24,8},{1,17},{9,25},{17,1},{25,9},{2,18},{10... | collective-permute-start | bytes 3145736 | tf_op jit(solution)/shard_map/ppermute | solution.py:572
  338.1 22.5 %collective-permute-done.1 = bf16[8,128,512]{2,1,0:T(8,128)(2,1)S(1)} collective-permute-done((bf16[8,128,512]{2,1,0:T(8,128)(2,1)S(1)}, bf16[8,128,512]{2,1,0:T(8,128)(2,1)S(1)}, u32[]{:S(2)}, u32[]{:S(2)}) %collective-permute-start.1) | collective-permute-done | bytes 1048608 | tf_op jit(solution)/shard_map/ppermute | solution.py:572
  360.6 2.5 fusion.7
  363.1 5.8 all-to-all-start.4
  368.9 48.8 %sample_backward.1 = (bf16[4,512,512]{2,1,0:T(8,128)(2,1)}, bf16[4,512,512]{2,1,0:T(8,128)(2,1)}, f32[2,512]{1,0:T(2,128)}) custom-call(s32[4]{0:T(128)} %pad_add_fusion.counts, bf16[8,4,4,16,512]{4,3,2,1,0:T(8,128)(2,1)} %all-to-all-done.3.d_x, bf16[4,512,512]{2,1,0:T(8,128)(2,1)} %bitcast.96, bf16[4,512,512]{2,1,0:T(8,128)(2,1)} %get-tuple-element.35.first, ...), custom_call_target="tpu_custom_call" | custom-call | flops 17179869184 | bytes 16777216 | tf_op jit(solution)/shard_map/sample_backward/pallas_call | solution.py:504
  417.7 1.5 dynamic-slice_bitcast_fusion.1
  419.2 0.1 collective-permute-start.2
  419.3 2.6 collective-permute-done.2
  421.9 1.3 fusion.8
  423.2 3.6 all-to-all-start.5
  426.8 26.2 %all-to-all-done.5 = bf16[8,1,128,512]{3,2,1,0:T(8,128)(2,1)S(1)} async-done(((bf16[8,1,128,512]{3,2,1,0:T(8,128)(2,1)}), bf16[8,1,128,512]{3,2,1,0:T(8,128)(2,1)S(1)}, u32[]{:S(2)}, u32[]{:S(2)}) %all-to-all-start.5) | async-done | bytes 1048608 | tf_op jit(solution)/shard_map/all_to_all | solution.py:547
  453.1 0.9 broadcast_in_dim.10
  453.9 20.6 %all-to-all-start.8 = ((f32[32,6,512]{2,1,0:T(8,128)}), f32[32,6,512]{2,1,0:T(8,128)}, u32[]{:S(2)}, u32[]{:S(2)}) async-start(f32[32,6,512]{2,1,0:T(8,128)} %broadcast_in_dim.10), calls=%async_computation.8 | async-start | bytes 1048576 | tf_op jit(solution)/shard_map/all_to_all | solution.py:547
  474.6 0.1 reduce_sum.86
  474.8 0.1 reduce_sum.84
  474.9 0.1 fusion.15
  475.0 1.8 collective-permute-start.4
  476.8 0.1 convert_reduce_fusion
  476.9 0.7 multiply_reduce_fusion.1
  477.6 7.2 %collective-permute-done.4 = bf16[128,512]{1,0:T(8,128)(2,1)S(1)} collective-permute-done((bf16[128,512]{1,0:T(8,128)(2,1)S(1)}, bf16[128,512]{1,0:T(8,128)(2,1)S(1)}, u32[]{:S(2)}, u32[]{:S(2)}) %collective-permute-start.4) | collective-permute-done | bytes 131104 | tf_op jit(solution)/shard_map/ppermute | solution.py:572
  484.8 0.7 multiply_reduce_fusion
  486.8 4.1 all-to-all-done.8
  490.9 0.7 broadcast_in_dim_broadcast_in_dim_broadcast_in_dim.3
  491.6 2.6 all-to-all-start.7
  494.2 0.0 all-gather.3.cloned.1.call-start
  494.2 1.1 reduce_sum.90
  495.3 0.6 multiply_reduce_fusion.2
  495.9 6.0 all-to-all-done.7
  501.9 0.5 slice.34
  503.9 0.8 convert_bitcast_fusion
  504.7 2.0 fusion.23
  506.7 1.0 fusion.20
  507.7 0.7 pad_maximum_fusion
  508.5 78.7 %all_to_all.45 = bf16[8,4,4,16,512]{4,3,2,1,0:T(8,128)(2,1)S(1)} all-to-all(bf16[8,4,4,16,512]{4,3,2,1,0:T(8,128)(2,1)S(1)} %copy-done.5), channel_id=1, replica_groups=mesh['task'=4,'feat'=8] {'feat'}, dimensions={0} | all-to-all | bytes 4194304 | tf_op jit(solution)/shard_map/all_to_all | solution.py:547
  587.2 1.5 copy.52
  588.7 0.6 multiply_subtract_fusion.3
  589.3 12.3 %all-gather.3.cloned.1.call-done = bf16[8192,512]{1,0:T(8,128)(2,1)} async-done(((bf16[256,512]{1,0:T(8,128)(2,1)}), bf16[8192,512]{1,0:T(8,128)(2,1)}) %all-gather.3.cloned.1.call-update) | async-done | bytes 8388624 | tf_op jit(solution)/shard_map/all_gather | solution.py:675
  601.6 4.9 slice.42
  606.5 1.2 copy-done
  607.8 1.7 fusion.27
  609.5 2.4 copy.56
  (40 shorter events, 0.2 us)
Async XLA Ops:
  49.2 7.4 %copy-start.4 = (bf16[1,4,512,512]{3,2,1,0:T(8,128)(2,1)S(1)}, bf16[1,4,512,512]{3,2,1,0:T(8,128)(2,1)}, u32[]{:S(2)}) copy-start(bf16[1,4,512,512]{3,2,1,0:T(8,128)(2,1)} %param.20) | copy-start | bytes 6291460
  49.2 55.7 %all-to-all-start = ((bf16[8,4,4,16,512]{4,3,2,1,0:T(8,128)(2,1)}), bf16[8,4,4,16,512]{4,3,2,1,0:T(8,128)(2,1)}, u32[]{:S(2)}, u32[]{:S(2)}) async-start(bf16[8,4,4,16,512]{4,3,2,1,0:T(8,128)(2,1)} %get-tuple-element.32), calls=%async_computation | async-start | bytes 4194304 | tf_op jit(solution)/shard_map/all_to_all | solution.py:547
  105.0 52.1 %all-to-all-start.1 = ((bf16[8,4,4,16,512]{4,3,2,1,0:T(8,128)(2,1)}), bf16[8,4,4,16,512]{4,3,2,1,0:T(8,128)(2,1)S(1)}, u32[]{:S(2)}, u32[]{:S(2)}) async-start(bf16[8,4,4,16,512]{4,3,2,1,0:T(8,128)(2,1)} %bitcast.71), calls=%async_computation.1 | async-start | bytes 4194304 | tf_op jit(solution)/shard_map/all_to_all | solution.py:547
  157.0 1.3 copy-start.6
  261.9 2.7 collective-permute-start.3
  264.7 1.0 copy-start.7
  265.6 6.6 %copy-start.1 = (bf16[2048,512]{1,0:T(8,128)(2,1)S(1)}, bf16[2048,512]{1,0:T(8,128)(2,1)}, u32[]{:S(2)}) copy-start(bf16[2048,512]{1,0:T(8,128)(2,1)} %get-tuple-element.40) | copy-start | bytes 6291460
  268.6 29.8 %all-to-all-start.6 = ((bf16[8,1,128,512]{3,2,1,0:T(8,128)(2,1)}), bf16[8,1,128,512]{3,2,1,0:T(8,128)(2,1)S(1)}, u32[]{:S(2)}, u32[]{:S(2)}) async-start(bf16[8,1,128,512]{3,2,1,0:T(8,128)(2,1)} %fusion.9), calls=%async_computation.6 | async-start | bytes 2097152 | tf_op jit(solution)/shard_map/all_to_all | solution.py:547
  275.0 27.8 %collective-permute-start = (bf16[2,8,128,512]{3,2,1,0:T(8,128)(2,1)}, bf16[2,8,128,512]{3,2,1,0:T(8,128)(2,1)}, u32[]{:S(2)}, u32[]{:S(2)}) collective-permute-start(bf16[2,8,128,512]{3,2,1,0:T(8,128)(2,1)} %fusion.2), channel_id=1, source_target_pairs={{0,8},{8,0},{16,24},{24,16},{1,9},{9,1},{17,25},{25,17},{2,10},{10... | collective-permute-start | bytes 6291464 | tf_op jit(solution)/shard_map/ppermute | solution.py:556
  298.4 64.7 %all-to-all-start.3 = ((bf16[8,4,4,16,512]{4,3,2,1,0:T(8,128)(2,1)}), bf16[8,4,4,16,512]{4,3,2,1,0:T(8,128)(2,1)}, u32[]{:S(2)}, u32[]{:S(2)}) async-start(bf16[8,4,4,16,512]{4,3,2,1,0:T(8,128)(2,1)} %get-tuple-element.34), calls=%async_computation.3 | async-start | bytes 4194304 | tf_op jit(solution)/shard_map/all_to_all | solution.py:547
  305.3 1.3 copy-start.2
  306.8 53.8 %collective-permute-start.1 = (bf16[8,128,512]{2,1,0:T(8,128)(2,1)S(1)}, bf16[8,128,512]{2,1,0:T(8,128)(2,1)S(1)}, u32[]{:S(2)}, u32[]{:S(2)}) collective-permute-start(bf16[8,128,512]{2,1,0:T(8,128)(2,1)S(1)} %dynamic-slice_bitcast_fusion.2), channel_id=1, source_target_pairs={{0,16},{8,24},{16,0},{24,8},{1,17},{9,25},{17,1},{25,9},{2,18},{10... | collective-permute-start | bytes 3145736 | tf_op jit(solution)/shard_map/ppermute | solution.py:572
  363.1 60.1 %all-to-all-start.4 = ((bf16[8,128,512]{2,1,0:T(8,128)(2,1)}), bf16[8,128,512]{2,1,0:T(8,128)(2,1)S(1)}, u32[]{:S(2)}, u32[]{:S(2)}) async-start(bf16[8,128,512]{2,1,0:T(8,128)(2,1)} %fusion.7), calls=%async_computation.4 | async-start | bytes 2097152 | tf_op jit(solution)/shard_map/all_to_all | solution.py:547
  417.7 4.2 copy-start.3
  419.2 2.7 collective-permute-start.2
  421.9 4.9 copy-start.17
  421.9 4.9 copy-start.18
  423.2 29.8 %all-to-all-start.5 = ((bf16[8,1,128,512]{3,2,1,0:T(8,128)(2,1)}), bf16[8,1,128,512]{3,2,1,0:T(8,128)(2,1)S(1)}, u32[]{:S(2)}, u32[]{:S(2)}) async-start(bf16[8,1,128,512]{3,2,1,0:T(8,128)(2,1)} %fusion.8), calls=%async_computation.5 | async-start | bytes 2097152 | tf_op jit(solution)/shard_map/all_to_all | solution.py:547
  453.9 37.0 %all-to-all-start.8 = ((f32[32,6,512]{2,1,0:T(8,128)}), f32[32,6,512]{2,1,0:T(8,128)}, u32[]{:S(2)}, u32[]{:S(2)}) async-start(f32[32,6,512]{2,1,0:T(8,128)} %broadcast_in_dim.10), calls=%async_computation.8 | async-start | bytes 1048576 | tf_op jit(solution)/shard_map/all_to_all | solution.py:547
  474.7 29.1 %copy-start.11 = (f32[512,64]{0,1:T(8,128)S(1)}, f32[512,64]{0,1:T(8,128)}, u32[]{:S(2)}) copy-start(f32[512,64]{0,1:T(8,128)} %param.26) | copy-start | bytes 393220
  474.8 29.1 %copy-start.12 = (f32[512,64]{0,1:T(8,128)S(1)}, f32[512,64]{0,1:T(8,128)}, u32[]{:S(2)}) copy-start(f32[512,64]{0,1:T(8,128)} %param.29) | copy-start | bytes 393220
  474.8 29.1 %copy-start.13 = (f32[512,64]{0,1:T(8,128)S(1)}, f32[512,64]{0,1:T(8,128)}, u32[]{:S(2)}) copy-start(f32[512,64]{0,1:T(8,128)} %param.33) | copy-start | bytes 393220
  475.0 9.8 %collective-permute-start.4 = (bf16[128,512]{1,0:T(8,128)(2,1)S(1)}, bf16[128,512]{1,0:T(8,128)(2,1)S(1)}, u32[]{:S(2)}, u32[]{:S(2)}) collective-permute-start(bf16[128,512]{1,0:T(8,128)(2,1)S(1)} %fusion.15), channel_id=1, source_target_pairs={{0,16},{8,24},{16,0},{24,8},{1,17},{9,25},{17,1},{25,9},{2,18},{10... | collective-permute-start | bytes 393224 | tf_op jit(solution)/shard_map/ppermute | solution.py:572
  476.9 29.7 %copy-start.8 = (f32[128,512]{1,0:T(8,128)S(1)}, f32[128,512]{1,0:T(8,128)}, u32[]{:S(2)}) copy-start(f32[128,512]{1,0:T(8,128)} %param.25) | copy-start | bytes 786436
  476.9 29.7 %copy-start.9 = (f32[128,512]{1,0:T(8,128)S(1)}, f32[128,512]{1,0:T(8,128)}, u32[]{:S(2)}) copy-start(f32[128,512]{1,0:T(8,128)} %param.28) | copy-start | bytes 786436
  476.9 29.7 %copy-start.10 = (f32[128,512]{1,0:T(8,128)S(1)}, f32[128,512]{1,0:T(8,128)}, u32[]{:S(2)}) copy-start(f32[128,512]{1,0:T(8,128)} %param.32) | copy-start | bytes 786436
  491.6 10.3 %all-to-all-start.7 = ((f32[32,8,128]{2,1,0:T(8,128)}), f32[32,8,128]{2,1,0:T(8,128)S(1)}, u32[]{:S(2)}, u32[]{:S(2)}) async-start(f32[32,8,128]{2,1,0:T(8,128)} %broadcast_in_dim_broadcast_in_dim_broadcast_in_dim.3), calls=%async_computation.7 | async-start | bytes 262144 | tf_op jit(solution)/shard_map/all_to_all | solution.py:547
  494.2 107.5 %all-gather.3.cloned.1.call-start = ((), (), s32[]{:S(2)}) async-start(), calls=%async_computation.9 | async-start | bytes 8650752 | tf_op jit(solution)/shard_map/all_gather | solution.py:675
  504.7 3.8 copy-start.5
  587.2 1.5 copy-start.14
  587.2 1.5 copy-start.15
  587.2 1.5 copy-start.16
  601.6 6.2 copy-start
Sparse Core Ops, SparseCore 0:
  508.6 92.9 all-gather.2

commit v2 on v1

--- a/solution.py
+++ b/solution.py
@@ -22,7 +22,7 @@
 BLOCK = 16
 UNIT = 128
 ROWS = 128
-QUERIES = 256
+QUERIES = 512
 VMEM_BYTES = 60 * 1024 * 1024
 
 BF = jnp.bfloat16
@@ -55,6 +55,15 @@
     return jnp.sum(values, axis=0, keepdims=True)
 
 
+def by_unit(units, one):
+    parts = [one(slice(place * UNIT, (place + 1) * UNIT)) for place in range(units)]
+    return jnp.concatenate(parts, axis=1)
+
+
+def scaled(values, head_size):
+    return (values.astype(BF).astype(F32) * head_size ** (-0.5)).astype(BF)
+
+
 def row_index(shape):
     return lax.broadcasted_iota(jnp.int32, shape, 0)
 
@@ -64,7 +73,6 @@
 ):
     samples, width = tokens.shape[1:]
     head_size = width // HEADS
-    score_scale = head_size ** (-0.5)
     group = x_out.shape[0] * BLOCK
 
     @pl.when(pl.program_id(0) == 0)
@@ -77,7 +85,8 @@
         normal, _ = normalize(tokens[0, rows].astype(F32))
         first_out[0, rows] = (normal * norms[0:1] + norms[1:2]).astype(BF)
     first = first_out[0]
-    for which in range(3):
+    heads_out[0, 0] = scaled(dot(turned[0], first, NT), head_size)
+    for which in range(1, 3):
         heads_out[0, which] = dot(turned[which], first, NT).astype(BF)
     live = row_index((samples, 1)) < counts[0]
     for head in range(HEADS):
@@ -86,7 +95,7 @@
         values = heads_out[0, 2, lanes]
         for low in range(0, samples, QUERIES):
             cols = slice(low, low + QUERIES)
-            scores = dot(keys, heads_out[0, 0, lanes, cols], TN) * score_scale
+            scores = dot(keys, heads_out[0, 0, lanes, cols], TN)
             scores = jnp.where(live, scores, NEGATIVE)
             top = jnp.max(scores, axis=0, keepdims=True)
             powers = jnp.exp(scores - top)
@@ -111,7 +120,8 @@
     weights,
     norms,
     grad_out,
-    weight_out,
+    keep_out,
+    send_out,
     norm_out,
     d_rows,
     d_mix,
@@ -142,33 +152,31 @@
         for low in range(0, samples, group):
             d_rows[low : low + group] = d_x[:, low // group, 0].reshape(group, width)
         d_mix[...] = dot(weights[3], d_rows[...], NT).astype(BF)
-        total[3] += dot(mixed[0], d_rows[...])
+        total[3 * width :] += dot(mixed[0], d_rows[...])
         live = row_index((samples, 1)) < counts[0]
-        for head in range(HEADS):
-            lanes = slice(head * head_size, (head + 1) * head_size)
-            keys = heads[0, 1, lanes]
-            values = heads[0, 2, lanes]
-            d_key = jnp.zeros((head_size, samples), F32)
-            d_value = jnp.zeros((head_size, samples), F32)
-            for low in range(0, samples, QUERIES):
-                cols = slice(low, low + QUERIES)
-                queries = heads[0, 0, lanes, cols]
-                grads = d_mix[lanes, cols]
-                shared = column_sum(grads.astype(F32) * mixed[0, lanes, cols].astype(F32))
-                scores = dot(keys, queries, TN) * score_scale
+        for pair in range(0, HEADS, 2):
+            d_keys, d_values = [], []
+            for head in (pair, pair + 1):
+                lanes = slice(head * head_size, (head + 1) * head_size)
+                keys = heads[0, 1, lanes]
+                values = heads[0, 2, lanes]
+                queries = heads[0, 0, lanes]
+                grads = d_mix[lanes]
+                shared = column_sum(grads.astype(F32) * mixed[0, lanes].astype(F32))
+                scores = dot(keys, queries, TN)
                 scores = jnp.where(live, scores, NEGATIVE)
-                probs = jnp.exp(scores - logs[0, head : head + 1, cols])
+                probs = jnp.exp(scores - logs[0, head : head + 1])
                 d_probs = dot(values, grads, TN)
                 d_scores = (probs * (d_probs - shared)).astype(BF)
-                d_heads[0, lanes, cols] = (dot(keys, d_scores) * score_scale).astype(BF)
-                d_key = d_key + dot(queries, d_scores, NT)
-                d_value = d_value + dot(grads, probs.astype(BF), NT)
-            d_heads[1, lanes] = (d_key * score_scale).astype(BF)
-            d_heads[2, lanes] = d_value.astype(BF)
+                d_heads[lanes] = (dot(keys, d_scores) * score_scale).astype(BF)
+                d_keys.append(dot(d_scores, queries, NT).astype(BF))
+                d_values.append(dot(probs.astype(BF), grads, NT).astype(BF))
+            lanes = slice(pair * head_size, (pair + 2) * head_size)
+            d_turned[1, :, lanes] = jnp.concatenate(d_keys, axis=1)
+            d_turned[2, :, lanes] = jnp.concatenate(d_values, axis=1)
+        d_turned[0] = d_heads[...].T
         for which in range(3):
-            d_turned[which] = d_heads[which].T
-        for which in range(3):
-            total[which] += dot(first[0], d_turned[which], TN)
+            total[which * width : (which + 1) * width] += dot(first[0], d_turned[which], TN)
         for low in range(0, samples, ROWS):
             rows = slice(low, low + ROWS)
             d_first = dot(d_turned[0, rows], weights[0], NT)
@@ -182,7 +190,8 @@
 
     @pl.when(step == pl.num_programs(0) - 1)
     def _():
-        weight_out[...] = total[...].astype(BF)
+        attention_parts(keep_out, total, counts[4], 0)
+        attention_parts(send_out, total, 1 - counts[4], 0)
         norm_out[...] = norm_total[...]
 
 
@@ -193,6 +202,22 @@
     half = 0.5 * (1.0 + curve)
     slope = half + (0.5 * root) * pre * (1.0 - curve * curve) * (1.0 + 3 * 0.044715 * square)
     return pre * half, slope
+
+
+def part_of(total, chip, core, owners, rows):
+    start = pl.multiple_of((chip * 2 + core) * (owners * rows), owners * rows)
+    part = total[pl.ds(start, owners * rows)].astype(BF)
+    return part.reshape(owners, rows, part.shape[-1])
+
+
+def attention_parts(where, total, core, low):
+    chips, owners = where.shape[:2]
+    half = total.shape[0] // (2 * chips * owners)
+    for pair in range(chips // 2):
+        part = part_of(total, pair, core, owners, 2 * half)
+        for piece in range(2):
+            rows = part[:, piece * half : (piece + 1) * half]
+            where[2 * pair + piece, :, low : low + half] = rows
 
 
 def middle(
@@ -205,9 +230,8 @@
     norms,
     y_out,
     d_out,
-    grad_in_out,
-    grad_out_out,
-    grad_attn_out,
+    keep_out,
+    send_out,
     norm_out,
     turned,
     order,
@@ -264,25 +288,25 @@
         normal_one[rows] = normal
         scale_one[rows] = scale
         low_rows[rows] = (normal * norms[2:3] + norms[3:4]).astype(BF)
-    for which in range(3):
+    heads[0] = scaled(dot(turned[0], low_rows[...], NT), head_size)
+    for which in range(1, 3):
         heads[which] = dot(turned[which], low_rows[...], NT).astype(BF)
 
-    unit = (UNIT, UNIT)
-    key_row = row_index(unit)
-    query_row = lax.broadcasted_iota(jnp.int32, unit, 1)
+    units = cells // UNIT
+    key_row = row_index((UNIT, cells))
+    query_row = lax.broadcasted_iota(jnp.int32, (UNIT, cells), 1) % UNIT
     mask = (key_row // features == query_row // features) & (key_row % features < counts[1])
     for head in range(HEADS):
         lanes = slice(head * head_size, (head + 1) * head_size)
-        for place in range(cells // UNIT):
-            cols = slice(place * UNIT, (place + 1) * UNIT)
-            scores = dot(heads[1, lanes, cols], heads[0, lanes, cols], TN) * score_scale
-            scores = jnp.where(mask, scores, NEGATIVE)
-            top = jnp.max(scores, axis=0, keepdims=True)
-            powers = jnp.exp(scores - top)
-            total = jnp.sum(powers, axis=0, keepdims=True)
-            prob = powers * (1.0 / total)
-            probs[head * (cells // UNIT) + place] = prob
-            mixed[lanes, cols] = dot(heads[2, lanes, cols], prob.astype(BF)).astype(BF)
+        scores = by_unit(units, lambda cols: dot(heads[1, lanes, cols], heads[0, lanes, cols], TN))
+        scores = jnp.where(mask, scores, NEGATIVE)
+        top = jnp.max(scores, axis=0, keepdims=True)
+        powers = jnp.exp(scores - top)
+        total = jnp.sum(powers, axis=0, keepdims=True)
+        prob = powers * (1.0 / total)
+        probs[head] = prob
+        prob = prob.astype(BF)
+        mixed[lanes] = by_unit(units, lambda cols: dot(heads[2, lanes, cols], prob[:, cols])).astype(BF)
     for low in range(0, cells, ROWS):
         rows = slice(low, low + ROWS)
         part = x_one[rows] + dot(mixed[:, rows], weights[3], TN)
@@ -334,26 +358,25 @@
             grad_rows[rows] = back
             live_grad[rows] = back.astype(BF)
         d_mix[...] = dot(weights[3], live_grad[...], NT).astype(BF)
-        total_attn[3] += dot(mixed[...], live_grad[...])
+        total_attn[3 * width :] += dot(mixed[...], live_grad[...])
         for head in range(HEADS):
             lanes = slice(head * head_size, (head + 1) * head_size)
-            for place in range(cells // UNIT):
-                cols = slice(place * UNIT, (place + 1) * UNIT)
-                prob = probs[head * (cells // UNIT) + place]
-                grads = d_mix[lanes, cols]
-                shared = column_sum(grads.astype(F32) * mixed[lanes, cols].astype(F32))
-                d_probs = dot(heads[2, lanes, cols], grads, TN)
-                d_scores = (prob * (d_probs - shared)).astype(BF)
-                d_query = dot(heads[1, lanes, cols], d_scores) * score_scale
-                d_heads[0, lanes, cols] = d_query.astype(BF)
-                d_key = dot(heads[0, lanes, cols], d_scores, NT) * score_scale
-                d_heads[1, lanes, cols] = d_key.astype(BF)
-                d_value = dot(grads, prob.astype(BF), NT)
-                d_heads[2, lanes, cols] = d_value.astype(BF)
+            prob = probs[head]
+            grads = d_mix[lanes]
+            shared = column_sum(grads.astype(F32) * mixed[lanes].astype(F32))
+            d_probs = by_unit(units, lambda cols: dot(heads[2, lanes, cols], grads[:, cols], TN))
+            d_scores = (prob * (d_probs - shared)).astype(BF)
+            low_prob = prob.astype(BF)
+            d_query = by_unit(units, lambda cols: dot(heads[1, lanes, cols], d_scores[:, cols]))
+            d_heads[0, lanes] = (d_query * score_scale).astype(BF)
+            d_key = by_unit(units, lambda cols: dot(heads[0, lanes, cols], d_scores[:, cols], NT))
+            d_heads[1, lanes] = d_key.astype(BF)
+            d_value = by_unit(units, lambda cols: dot(grads[:, cols], low_prob[:, cols], NT))
+            d_heads[2, lanes] = d_value.astype(BF)
         for which in range(3):
             d_turned[which] = d_heads[which].T
         for which in range(3):
-            total_attn[which] += dot(low_rows[...], d_turned[which], TN)
+            total_attn[which * width : (which + 1) * width] += dot(low_rows[...], d_turned[which], TN)
         for low in range(0, cells, ROWS):
             rows = slice(low, low + ROWS)
             d_second = dot(d_turned[0, rows], weights[0], NT)
@@ -372,9 +395,14 @@
 
     @pl.when(step == pl.num_programs(0) - 1)
     def _():
-        grad_in_out[...] = total_in[...].astype(BF)
-        grad_out_out[...] = total_out[...].astype(BF)
-        grad_attn_out[...] = total_attn[...].astype(BF)
+        chips, owners, rows, _ = keep_out.shape
+        own_ff = hidden_width // (2 * chips * owners)
+        for where, core in ((keep_out, counts[4]), (send_out, 1 - counts[4])):
+            for chip in range(chips):
+                for which, total in ((0, total_in), (1, total_out)):
+                    part = part_of(total, chip, core, owners, own_ff)
+                    where[chip, :, which * own_ff : (which + 1) * own_ff] = part
+            attention_parts(where, total_attn, core, 2 * own_ff)
         norm_out[...] = norm_total[...]
 
 
@@ -383,6 +411,14 @@
     return pl.BlockSpec(shape, lambda step: zeros, pipeline_mode=pl.Buffered(1))
 
 
+def half(shape, which):
+    return pl.BlockSpec(
+        (shape[0] // 2,) + tuple(shape[1:]),
+        lambda step: (which, 0, 0),
+        pipeline_mode=pl.Buffered(1),
+    )
+
+
 def once(shape):
     zeros = (0,) * len(shape)
     return pl.BlockSpec(shape, lambda step: zeros)
@@ -393,7 +429,7 @@
     return pl.BlockSpec((1,) + tuple(shape[1:]), lambda step: (step,) + zeros)
 
 
-def call(body, grid, in_specs, outs, scratch, flops, name):
+def call(body, grid, in_specs, outs, scratch, nanoseconds, name):
     return pl.pallas_call(
         body,
         grid=(grid,),
@@ -402,7 +438,9 @@
         out_shape=[jax.ShapeDtypeStruct(shape, kind) for _, shape, kind in outs],
         scratch_shapes=[pltpu.VMEM(shape, kind) for shape, kind in scratch],
         compiler_params=pltpu.CompilerParams(vmem_limit_bytes=VMEM_BYTES),
-        cost_estimate=pl.CostEstimate(flops=flops, bytes_accessed=1 << 24, transcendentals=0),
+        cost_estimate=pl.CostEstimate(
+            flops=nanoseconds * 1150000, bytes_accessed=1 << 24, transcendentals=0
+        ),
         name=name,
     )
 
@@ -417,7 +455,7 @@
     return call(
         sample_forward,
         local,
-        [lead(square), whole((4, width, width)), whole(norms.shape)],
+        [lead(square), half(weights.shape, 0), whole(norms.shape)],
         [
             (
                 pl.BlockSpec(
@@ -432,28 +470,28 @@
             (lead(stats), stats, F32),
         ],
         [((3, width, width), BF)],
-        local * 8 * samples * width * (width + samples // 2),
+        36000,
         "sample_forward",
     )(counts, tokens, weights, norms)
 
 
-def run_middle(counts, x_dealt, cot_dealt, weights, weight_in, weight_out, norms):
+def run_middle(counts, x_dealt, cot_dealt, weights, weight_in, weight_out, norms, chips):
     devices, deals, local, _, width = x_dealt.shape
     cells = devices * local * BLOCK
     hidden_width = weight_in.shape[1]
+    parts = (chips, devices, (hidden_width + 2 * width) // (chips * devices), width)
     dealt = pl.BlockSpec(
         (devices, 1, local, BLOCK, width), lambda step: (0, step, 0, 0, 0)
     )
     square = (cells, width)
     turned = (width, cells)
-    units = HEADS * (cells // UNIT)
     return call(
         middle,
         deals,
         [
             dealt,
             dealt,
-            whole((4, width, width)),
+            half(weights.shape, 1),
             whole(weight_in.shape),
             whole(weight_out.shape),
             whole(norms.shape),
@@ -461,9 +499,8 @@
         [
             (dealt, x_dealt.shape, BF),
             (dealt, x_dealt.shape, BF),
-            (once((hidden_width, width)), (hidden_width, width), BF),
-            (once((hidden_width, width)), (hidden_width, width), BF),
-            (once((4, width, width)), (4, width, width), BF),
+            (once(parts), parts, BF),
+            (once(parts), parts, BF),
             (once((4, width)), (4, width), F32),
         ],
         [
@@ -482,25 +519,28 @@
             ((3,) + square, BF),
             (turned, BF),
             (turned, BF),
-            ((units, UNIT, UNIT), F32),
+            ((HEADS, UNIT, cells), F32),
             (square, BF),
             (square, BF),
             (square, F32),
-            ((4, width, width), F32),
+            ((4 * width, width), F32),
             ((hidden_width, width), F32),
             ((hidden_width, width), F32),
             ((4, width), F32),
         ],
-        deals * cells * 6 * width * (4 * width + 2 * hidden_width),
+        90000,
         "middle",
     )(counts, x_dealt, cot_dealt, weights, weight_in, weight_out, norms)
 
 
-def run_sample_backward(counts, d_dealt, tokens, first, heads, mixed, logs, weights, norms):
+def run_sample_backward(
+    counts, d_dealt, tokens, first, heads, mixed, logs, weights, norms, chips
+):
     devices, deals, local, _, width = d_dealt.shape
     samples = tokens.shape[1]
     square = (local, samples, width)
     three = (local, 3, width, samples)
+    parts = (chips, devices, 4 * width // (2 * chips * devices), width)
     return call(
         sample_backward,
         local,
@@ -511,23 +551,24 @@
             lead(three),
             lead(mixed.shape),
             lead(logs.shape),
-            whole((4, width, width)),
+            half(weights.shape, 0),
             whole(norms.shape),
         ],
         [
             (lead(square), square, BF),
-            (once((4, width, width)), (4, width, width), BF),
+            (once(parts), parts, BF),
+            (once(parts), parts, BF),
             (once((2, width)), (2, width), F32),
         ],
         [
             ((samples, width), BF),
             ((width, samples), BF),
-            ((3, width, samples), BF),
+            ((width, samples), BF),
             ((3, samples, width), BF),
-            ((4, width, width), F32),
+            ((4 * width, width), F32),
             ((2, width), F32),
         ],
-        local * 16 * samples * width * (width + samples),
+        49000,
         "sample_backward",
     )(counts, d_dealt, tokens, first, heads, mixed, logs, weights, norms)
 
@@ -547,32 +588,53 @@
     return lax.all_to_all(values, axis, 0, 0, axis_index_groups=groups, tiled=True)
 
 
-def reduce_core(values):
-    tasks = lax.axis_size("task")
-    core = lax.axis_index("task") % 2
-    pairs = [(place, place ^ 1) for place in range(tasks)]
-    other = lax.dynamic_index_in_dim(values, 1 - core, 0, keepdims=False)
-    mine = lax.dynamic_index_in_dim(values, core, 0, keepdims=False)
-    came = lax.ppermute(other, "task", pairs)
-    return (mine.astype(F32) + came.astype(F32)).astype(BF)
+def task_pairs(hop):
+    return [(place, hop(place)) for place in range(lax.axis_size("task"))]
+
+
+def reduce_core(keep, send):
+    came = lax.ppermute(send, "task", task_pairs(lambda place: place ^ 1))
+    return (keep.astype(F32) + came.astype(F32)).astype(BF)
+
+
+def reduce_chips(values):
+    chips = values.shape[0]
+    chip = lax.axis_index("task") // 2
+    if chips == 2:
+        mine = lax.dynamic_index_in_dim(values, chip, 0, keepdims=False)
+        other = lax.dynamic_index_in_dim(values, 1 - chip, 0, keepdims=False)
+        came = lax.ppermute(other, "task", task_pairs(lambda place: place ^ 2))
+        return (mine.astype(F32) + came.astype(F32)).astype(BF)
+    groups = [[2 * place + core for place in range(chips)] for core in range(2)]
+    return jnp.sum(exchange(values, "task", groups).astype(F32), axis=0).astype(BF)
 
 
 def reduce_feat(values):
     return jnp.sum(exchange(values, "feat").astype(F32), axis=0)
 
 
-def reduce_chips(values):
-    tasks = lax.axis_size("task")
-    chips = tasks // 2
+def to_owners(one, two):
+    chips = lax.axis_size("task") // 2
     chip = lax.axis_index("task") // 2
-    if chips == 2:
-        pairs = [(place, (place + 2) % tasks) for place in range(tasks)]
-        other = lax.dynamic_index_in_dim(values, 1 - chip, 0, keepdims=False)
-        mine = lax.dynamic_index_in_dim(values, chip, 0, keepdims=False)
-        came = lax.ppermute(other, "task", pairs)
-        return mine.astype(F32) + came.astype(F32)
-    groups = [[2 * place + core for place in range(chips)] for core in range(2)]
-    return jnp.sum(exchange(values, "task", groups).astype(F32), axis=0)
+    even = chip % 2 == 0
+    stay, leave = jnp.where(even, one, two), jnp.where(even, two, one)
+
+    def target(chip, second):
+        return chip // 2 + (chips // 2 if second else 0)
+
+    def send(values, odd_second):
+        pairs = task_pairs(
+            lambda place: 2 * target(place // 2, (place // 2 % 2 == 1) == odd_second) + place % 2
+        )
+        return lax.ppermute(values, "task", pairs)
+
+    if chips > 2:
+        stay = send(stay, True)
+    leave = send(leave, False)
+    early = chip < chips // 2
+    return jnp.concatenate(
+        [jnp.where(early, stay, leave), jnp.where(early, leave, stay)], axis=0
+    )
 
 
 def total_of(values):
@@ -609,52 +671,43 @@
     place = lax.axis_index("feat")
     deals = samples // (devices * BLOCK)
     counts = jnp.stack(
-        [sample_count[0], feature_count[0], place * local, place]
+        [sample_count[0], feature_count[0], place * local, place, lax.axis_index("task") % 2]
     ).astype(jnp.int32)
     weights = attn_weights.reshape(8, width, width)
-    weights_one, weights_two = weights[:4], weights[4:]
 
     dealt_cot = cotangent[0].reshape(local, deals, devices, BLOCK, width).transpose(2, 1, 0, 3, 4)
     came_cot = exchange(dealt_cot, "feat")
     dealt_x, first, heads, mixed, logs = run_sample_forward(
-        counts, tokens[0], weights_one, norm_params, devices
+        counts, tokens[0], weights, norm_params, devices
     )
     came_x = exchange(dealt_x, "feat")
-    dealt_y, dealt_d, grad_in, grad_out, grad_two, norms_two = run_middle(
-        counts, came_x, came_cot, weights_two, weight_in, weight_out, norm_params
+    dealt_y, dealt_d, keep_two, send_two, norms_two = run_middle(
+        counts, came_x, came_cot, weights, weight_in, weight_out, norm_params, chips
     )
     came_d = exchange(dealt_d, "feat")
-    input_grad, grad_one, norms_one = run_sample_backward(
-        counts, came_d, tokens[0], first, heads, mixed, logs, weights_one, norm_params
-    )
+    part_two = reduce_chips(reduce_core(keep_two, send_two))
+    part_two, came_d = lax.optimization_barrier((part_two, came_d))
+    own_ff = weight_in.shape[1] // (tasks * devices)
+    own_attn = attn_weights.shape[0] // (tasks * devices)
+    share_two = reduce_feat(part_two)
+    input_grad, keep_one, send_one, norms_one = run_sample_backward(
+        counts, came_d, tokens[0], first, heads, mixed, logs, weights, norm_params, chips
+    )
+    share_two, send_one = lax.optimization_barrier((share_two, send_one))
+    share_one = reduce_feat(reduce_chips(reduce_core(keep_one, send_one)))
     came_y = exchange(dealt_y, "feat")
     block_out = came_y.transpose(2, 1, 0, 3, 4).reshape(1, local, samples, width)
 
-    own_ff = grad_in.shape[0] // (tasks * devices)
-    both = jnp.concatenate(
-        [
-            grad_in.reshape(chips, 2, devices, own_ff, width),
-            grad_out.reshape(chips, 2, devices, own_ff, width),
-        ],
-        axis=3,
-    )
-    both = reduce_core(jnp.moveaxis(both, 1, 0))
-    both = reduce_chips(both).astype(BF)
-    share_ff = reduce_feat(both)
-
-    own_attn = attn_weights.shape[0] // (tasks * devices)
-    halves = []
-    for grad in (grad_one, grad_two):
-        part = grad.reshape(chips // 2, 2, devices, own_attn, width)
-        part = reduce_core(jnp.moveaxis(part, 1, 0))
-        halves.append(reduce_feat(jnp.moveaxis(part, 1, 0)).astype(BF))
-    share_attn = reduce_chips(jnp.concatenate(halves, axis=0))
-    total_norms = total_of(jnp.concatenate([norms_one, norms_two], axis=0))
-
-    share_in_turned, share_out = share_ff[:own_ff], share_ff[own_ff:]
-    local_squares = jnp.sum(share_ff * share_ff) + jnp.sum(share_attn * share_attn)
-    squares = total_of(jnp.full((8, 128), local_squares, F32))[0, 0]
-    squares = squares + jnp.sum(total_norms * total_norms)
+    share_in_turned = share_two[:own_ff]
+    share_out = share_two[own_ff : 2 * own_ff]
+    share_attn = to_owners(share_one, share_two[2 * own_ff :])
+    local_squares = jnp.sum(share_one * share_one) + jnp.sum(share_two * share_two)
+    small = jnp.concatenate(
+        [norms_one, norms_two, jnp.full((2, width), local_squares, F32)], axis=0
+    )
+    small = total_of(small)
+    total_norms = small[:6]
+    squares = small[6, 0] + jnp.sum(total_norms * total_norms)
     grad_norm = jnp.sqrt(squares)
     factor = jnp.minimum(1.0, CLIP_AT / (grad_norm + 1e-06))
     new_attn, moment_attn, square_attn = adam_step(

time: 626 us -> 506 us (0.81)
  waiting for transfers between devices: 202 us -> 128 us
  blocking collectives: 78.7 us -> 125 us
  Pallas kernels: 187 us -> 142 us
  starting transfers between devices: 85 us -> 48 us
  local copies, waits for them, and re-layouts: 26.5 us -> 20.1 us
    all_to_all x8 -> x5, waiting for transfers between devices: 155 us -> 51.9 us  [exchange(): lax.all_to_all(values, axis, 0, 0, axis_index_groups=groups, tiled=True)]
    all_to_all x1 -> x2, blocking collectives: 78.7 us -> 125 us  [exchange(): lax.all_to_all(values, axis, 0, 0, axis_index_groups=groups, tiled=True)]
    pallas_call x2, Pallas kernels: 138 us -> 97.6 us  [the longest x1 72.7 us: run_middle(): call(middle, deals, [dealt, dealt, half(weights.shape, 1), whole(weight_i...]
    all_to_all x8 -> x5, starting transfers between devices: 51.6 us -> 23.8 us  [exchange(): lax.all_to_all(values, axis, 0, 0, axis_index_groups=groups, tiled=True)]
    ppermute x5, waiting for transfers between devices: 35 us -> 57.2 us  [the longest x2 50.7 us: reduce_chips(): came = lax.ppermute(other, 'task', task_pairs(lambda place: place ^ 2))]
    ppermute x5, starting transfers between devices: 33.3 us -> 24.2 us  [the longest x2 23.4 us: reduce_core(): came = lax.ppermute(send, 'task', task_pairs(lambda place: place ^ 1))]
  transfers between devices with their start and end apart: 14 -> 11, of which waited for: 11 -> 10; matrix products, arithmetic and copies ran while one was open for 3% -> 3% of each run, Pallas kernels for 8% -> 14%
where the time goes in v2:
time: 506 us; the launch traced here: 498 us
  Pallas kernels  142 us (28%)
  waiting for transfers between devices  128 us (25%)
  blocking collectives  125 us (25%)
  starting transfers between devices  48 us (9%)
  local copies, waits for them, and re-layouts  20.1 us (4%)
  between operations  19.6 us (4%)
  other arithmetic  15.6 us (3%)
    all_to_all x2, blocking collectives, exchange(): lax.all_to_all(values, axis, 0, 0, axis_index_groups=groups, tiled=True)  125 us
    pallas_call x1, Pallas kernels, run_middle(): call(middle, deals, [dealt, dealt, half(weights.shape, 1), whole(weight_i...  72.7 us
    all_to_all x5, waiting for transfers between devices, exchange(): lax.all_to_all(values, axis, 0, 0, axis_index_groups=groups, tiled=True)  51.9 us
    ppermute x2, waiting for transfers between devices, reduce_chips(): came = lax.ppermute(other, 'task', task_pairs(lambda place: place ^ 2))  50.7 us
    pallas_call x1, Pallas kernels, run_sample_backward(): call(sample_backward, local, [pl.BlockSpec((devices, deals, 1, BLOCK, wid...  44.5 us
    pallas_call x1, Pallas kernels, run_sample_forward(): call(sample_forward, local, [lead(square), half(weights.shape, 0), whole(...  24.9 us
    all_to_all x5, starting transfers between devices, exchange(): lax.all_to_all(values, axis, 0, 0, axis_index_groups=groups, tiled=True)  23.8 us
    ppermute x2, starting transfers between devices, reduce_core(): came = lax.ppermute(send, 'task', task_pairs(lambda place: place ^ 1))  23.4 us
  transfers between devices with their start and end apart: 11, of which 10 were waited for; matrix products, arithmetic and copies ran while one was open for 3% of the time, Pallas kernels for 14%

profile of v2, /device:TPU:0, one launch (start us, length us, event | category | flops | bytes accessed | tf_op | source)
XLA Modules:
  0.0 497.8 jit_solution(15334497321848189659)
XLA Ops:
  7.2 3.2 copy.45
  10.3 7.3 %all-to-all-start.1 = ((bf16[8,4,4,16,512]{4,3,2,1,0:T(8,128)(2,1)}), bf16[8,4,4,16,512]{4,3,2,1,0:T(8,128)(2,1)S(1)}, u32[]{:S(2)}, u32[]{:S(2)}) async-start(bf16[8,4,4,16,512]{4,3,2,1,0:T(8,128)(2,1)} %bitcast.38), calls=%async_computation.1 | async-start | bytes 4194304 | tf_op jit(solution)/shard_map/all_to_all | solution.py:588
  18.9 0.6 stack.15.counts
  19.5 24.9 %sample_forward.1 = (bf16[8,4,4,16,512]{4,3,2,1,0:T(8,128)(2,1)}, bf16[4,512,512]{2,1,0:T(8,128)(2,1)}, bf16[4,3,512,512]{3,2,1,0:T(8,128)(2,1)}, bf16[4,512,512]{2,1,0:T(8,128)(2,1)}, f32[4,8,512]{2,1,0:T(8,128)}) custom-call(s32[5]{0:T(128)} %stack.15.counts, bf16[4,512,512]{2,1,0:T(8,128)(2,1)} %bitcast.50, bf16[8,512,512]{2,1,0:T(8,128)(2,1)} %bitcast.47, ...), custom_call_target="tpu_custom_call" | custom-call | flops 41400000512 | bytes 16777216 | tf_op jit(solution)/shard_map/sample_forward/pallas_call | solution.py:455
  44.4 21.4 %all-to-all-done.1.cot_in = bf16[8,4,4,16,512]{4,3,2,1,0:T(8,128)(2,1)S(1)} async-done(((bf16[8,4,4,16,512]{4,3,2,1,0:T(8,128)(2,1)}), bf16[8,4,4,16,512]{4,3,2,1,0:T(8,128)(2,1)S(1)}, u32[]{:S(2)}, u32[]{:S(2)}) %all-to-all-start.1) | async-done | bytes 2097184 | tf_op jit(solution)/shard_map/all_to_all | solution.py:588
  65.8 52.2 %all_to_all.35.x_in = bf16[8,4,4,16,512]{4,3,2,1,0:T(8,128)(2,1)} all-to-all(bf16[8,4,4,16,512]{4,3,2,1,0:T(8,128)(2,1)} %get-tuple-element.36), channel_id=1, replica_groups=mesh['task'=4,'feat'=8] {'feat'}, dimensions={0} | all-to-all | bytes 4194304 | tf_op jit(solution)/shard_map/all_to_all | solution.py:588
  118.1 0.0 copy-done.3
  118.1 72.7 %middle.1 = (bf16[8,4,4,16,512]{4,3,2,1,0:T(8,128)(2,1)}, bf16[8,4,4,16,512]{4,3,2,1,0:T(8,128)(2,1)}, bf16[2,8,192,512]{3,2,1,0:T(8,128)(2,1)}, bf16[2,8,192,512]{3,2,1,0:T(8,128)(2,1)}, f32[4,512]{1,0:T(4,128)}) custom-call(s32[5]{0:T(128)} %stack.15.counts, bf16[8,4,4,16,512]{4,3,2,1,0:T(8,128)(2,1)} %all_to_all.35.x_in, ...), custom_call_target="tpu_custom_call" | custom-call | flops 103499997184 | bytes 16777216 | tf_op jit(solution)/shard_map/middle/pallas_call | solution.py:488
  190.8 23.3 %collective-permute-start = (bf16[2,8,192,512]{3,2,1,0:T(8,128)(2,1)}, bf16[2,8,192,512]{3,2,1,0:T(8,128)(2,1)S(1)}, u32[]{:S(2)}, u32[]{:S(2)}) collective-permute-start(bf16[2,8,192,512]{3,2,1,0:T(8,128)(2,1)} %get-tuple-element.39), channel_id=1, source_target_pairs={{0,8},{8,0},{16,24},{24,16},{1,9},{9,1},{17,25},{25,17},{2,10},{10... | collective-permute-start | bytes 9437192 | tf_op jit(solution)/shard_map/ppermute | solution.py:596
  214.1 4.4 all-to-all-start.3
  218.5 1.1 collective-permute-done
  219.6 1.7 copy-done.1
  221.3 3.9 add_convert_fusion
  225.2 1.3 dynamic-slice_bitcast_fusion
  226.6 0.0 collective-permute-start.1
  226.6 37.0 %collective-permute-done.1 = bf16[8,192,512]{2,1,0:T(8,128)(2,1)} collective-permute-done((bf16[8,192,512]{2,1,0:T(8,128)(2,1)}, bf16[8,192,512]{2,1,0:T(8,128)(2,1)}, u32[]{:S(2)}, u32[]{:S(2)}) %collective-permute-start.1) | collective-permute-done | bytes 1572896 | tf_op jit(solution)/shard_map/ppermute | solution.py:606
  263.5 3.0 fusion
  266.5 0.6 all-to-all-done.3.d_x
  267.1 3.6 all-to-all-start.4
  270.8 44.5 %sample_backward.1 = (bf16[4,512,512]{2,1,0:T(8,128)(2,1)}, bf16[2,8,64,512]{3,2,1,0:T(8,128)(2,1)}, bf16[2,8,64,512]{3,2,1,0:T(8,128)(2,1)}, f32[2,512]{1,0:T(2,128)}) custom-call(s32[5]{0:T(128)} %stack.15.counts, bf16[8,4,4,16,512]{4,3,2,1,0:T(8,128)(2,1)} %all-to-all-done.3.d_x, bf16[4,512,512]{2,1,0:T(8,128)(2,1)} %bitcast.51, ...), custom_call_target="tpu_custom_call" | custom-call | flops 56349999104 | bytes 16777216 | tf_op jit(solution)/shard_map/sample_backward/pallas_call | solution.py:544
  315.2 0.0 copy-start.4
  315.3 0.0 all-to-all-done.4
  315.3 0.2 convert_reduce_fusion
  315.5 0.1 collective-permute-start.2
  315.6 2.9 collective-permute-done.2
  318.4 0.0 copy-done.4
  318.4 0.3 add_convert_fusion.1
  318.8 0.1 dynamic-slice_bitcast_fusion.1
  318.8 0.0 copy-start.15
  318.8 0.0 copy-start.16
  318.8 0.3 collective-permute-start.3
  319.2 13.7 %collective-permute-done.3 = bf16[8,64,512]{2,1,0:T(8,128)(2,1)S(1)} collective-permute-done((bf16[8,64,512]{2,1,0:T(8,128)(2,1)S(1)}, bf16[8,64,512]{2,1,0:T(8,128)(2,1)S(1)}, u32[]{:S(2)}, u32[]{:S(2)}) %collective-permute-start.3) | collective-permute-done | bytes 524320 | tf_op jit(solution)/shard_map/ppermute | solution.py:606
  332.9 0.9 fusion.1
  333.8 4.9 all-to-all-start.5
  338.7 0.7 multiply_reduce_fusion
  339.4 13.6 %all-to-all-done.5 = bf16[8,64,512]{2,1,0:T(8,128)(2,1)S(1)} async-done(((bf16[8,64,512]{2,1,0:T(8,128)(2,1)}), bf16[8,64,512]{2,1,0:T(8,128)(2,1)S(1)}, u32[]{:S(2)}, u32[]{:S(2)}) %all-to-all-start.5) | async-done | bytes 524320 | tf_op jit(solution)/shard_map/all_to_all | solution.py:588
  353.0 0.1 convert_reduce_fusion.1
  353.1 0.6 multiply_reduce_fusion.1
  355.0 0.1 pad.7.clone
  355.1 0.0 copy-done.15
  355.1 0.0 copy-done.16
  355.1 0.1 maximum_maximum_fusion
  355.2 0.9 broadcast_in_dim.14
  356.0 3.6 all-to-all-start.6
  359.6 0.0 all-gather.3.cloned.1.call-start
  359.7 16.3 %all-to-all-done.6 = f32[32,8,512]{2,1,0:T(8,128)S(1)} async-done(((f32[32,8,512]{2,1,0:T(8,128)}), f32[32,8,512]{2,1,0:T(8,128)S(1)}, u32[]{:S(2)}, u32[]{:S(2)}) %all-to-all-start.6) | async-done | bytes 524320 | tf_op jit(solution)/shard_map/all_to_all | solution.py:588
  376.0 0.6 multiply_reduce_fusion.2
  376.6 0.5 slice.32
  378.5 0.0 copy-done.8
  378.6 0.8 fusion.11
  379.4 0.5 collective-permute-start.4
  379.9 1.9 convert_bitcast_fusion
  381.8 2.6 collective-permute-done.4
  384.4 1.0 fusion.7
  385.4 0.7 pad_maximum_fusion
  386.1 0.0 all-gather.3.cloned.1.call-update
  386.2 72.6 %all_to_all.36 = bf16[8,4,4,16,512]{4,3,2,1,0:T(8,128)(2,1)S(1)} all-to-all(bf16[8,4,4,16,512]{4,3,2,1,0:T(8,128)(2,1)S(1)} %copy-done.2), channel_id=1, replica_groups=mesh['task'=4,'feat'=8] {'feat'}, dimensions={0} | all-to-all | bytes 4194304 | tf_op jit(solution)/shard_map/all_to_all | solution.py:588
  458.8 1.5 copy.42
  460.3 0.6 multiply_subtract_fusion.3
  460.9 18.4 %all-gather.3.cloned.1.call-done = bf16[8192,512]{1,0:T(8,128)(2,1)} async-done(((bf16[256,512]{1,0:T(8,128)(2,1)}), bf16[8192,512]{1,0:T(8,128)(2,1)}) %all-gather.3.cloned.1.call-update) | async-done | bytes 8388624 | tf_op jit(solution)/shard_map/all_gather | solution.py:728
  479.3 4.9 slice.34
  484.3 1.2 copy-done
  485.5 1.7 fusion.14
  487.2 2.4 copy.43
  (27 shorter events, 0.1 us)
Async XLA Ops:
  10.3 55.5 %all-to-all-start.1 = ((bf16[8,4,4,16,512]{4,3,2,1,0:T(8,128)(2,1)}), bf16[8,4,4,16,512]{4,3,2,1,0:T(8,128)(2,1)S(1)}, u32[]{:S(2)}, u32[]{:S(2)}) async-start(bf16[8,4,4,16,512]{4,3,2,1,0:T(8,128)(2,1)} %bitcast.38), calls=%async_computation.1 | async-start | bytes 4194304 | tf_op jit(solution)/shard_map/all_to_all | solution.py:588
  65.8 52.3 %copy-start.3 = (bf16[8,4,4,16,512]{4,3,2,1,0:T(8,128)(2,1)}, bf16[8,4,4,16,512]{4,3,2,1,0:T(8,128)(2,1)S(1)}, u32[]{:S(2)}) copy-start(bf16[8,4,4,16,512]{4,3,2,1,0:T(8,128)(2,1)S(1)} %all-to-all-done.1.cot_in) | copy-start | bytes 6291460
  190.8 28.8 %collective-permute-start = (bf16[2,8,192,512]{3,2,1,0:T(8,128)(2,1)}, bf16[2,8,192,512]{3,2,1,0:T(8,128)(2,1)S(1)}, u32[]{:S(2)}, u32[]{:S(2)}) collective-permute-start(bf16[2,8,192,512]{3,2,1,0:T(8,128)(2,1)} %get-tuple-element.39), channel_id=1, source_target_pairs={{0,8},{8,0},{16,24},{24,16},{1,9},{9,1},{17,25},{25,17},{2,10},{10... | collective-permute-start | bytes 9437192 | tf_op jit(solution)/shard_map/ppermute | solution.py:596
  214.1 53.1 %all-to-all-start.3 = ((bf16[8,4,4,16,512]{4,3,2,1,0:T(8,128)(2,1)}), bf16[8,4,4,16,512]{4,3,2,1,0:T(8,128)(2,1)}, u32[]{:S(2)}, u32[]{:S(2)}) async-start(bf16[8,4,4,16,512]{4,3,2,1,0:T(8,128)(2,1)} %get-tuple-element.40), calls=%async_computation.3 | async-start | bytes 4194304 | tf_op jit(solution)/shard_map/all_to_all | solution.py:588
  219.6 1.7 copy-start.1
  226.6 37.0 %collective-permute-start.1 = (bf16[8,192,512]{2,1,0:T(8,128)(2,1)}, bf16[8,192,512]{2,1,0:T(8,128)(2,1)}, u32[]{:S(2)}, u32[]{:S(2)}) collective-permute-start(bf16[8,192,512]{2,1,0:T(8,128)(2,1)} %dynamic-slice_bitcast_fusion), channel_id=1, source_target_pairs={{0,16},{8,24},{16,0},{24,8},{1,17},{9,25},{17,1},{25,9},{2,18},{10... | collective-permute-start | bytes 4718600 | tf_op jit(solution)/shard_map/ppermute | solution.py:606
  267.1 48.1 %all-to-all-start.4 = ((bf16[8,192,512]{2,1,0:T(8,128)(2,1)}), bf16[8,192,512]{2,1,0:T(8,128)(2,1)S(1)}, u32[]{:S(2)}, u32[]{:S(2)}) async-start(bf16[8,192,512]{2,1,0:T(8,128)(2,1)} %fusion), calls=%async_computation.4 | async-start | bytes 3145728 | tf_op jit(solution)/shard_map/all_to_all | solution.py:588
  315.2 3.2 copy-start.4
  315.5 2.9 collective-permute-start.2
  318.8 36.3 %copy-start.15 = (f32[4,512]{1,0:T(4,128)S(1)}, f32[4,512]{1,0:T(4,128)}, u32[]{:S(2)}) copy-start(f32[4,512]{1,0:T(4,128)} %get-tuple-element.48) | copy-start | bytes 24580
  318.8 36.3 %copy-start.16 = (f32[2,512]{1,0:T(2,128)S(1)}, f32[2,512]{1,0:T(2,128)}, u32[]{:S(2)}) copy-start(f32[2,512]{1,0:T(2,128)} %get-tuple-element.47) | copy-start | bytes 12292
  318.8 14.0 %collective-permute-start.3 = (bf16[8,64,512]{2,1,0:T(8,128)(2,1)S(1)}, bf16[8,64,512]{2,1,0:T(8,128)(2,1)S(1)}, u32[]{:S(2)}, u32[]{:S(2)}) collective-permute-start(bf16[8,64,512]{2,1,0:T(8,128)(2,1)S(1)} %dynamic-slice_bitcast_fusion.1), channel_id=1, source_target_pairs={{0,16},{8,24},{16,0},{24,8},{1,17},{9,25},{17,1},{25,9},{2,18},{10... | collective-permute-start | bytes 1572872 | tf_op jit(solution)/shard_map/ppermute | solution.py:606
  333.8 44.7 %copy-start.8 = (f32[64,512]{1,0:T(8,128)S(1)}, f32[64,512]{1,0:T(8,128)}, u32[]{:S(2)}) copy-start(f32[64,512]{1,0:T(8,128)} %param.27) | copy-start | bytes 393220
  333.8 44.7 %copy-start.9 = (f32[64,512]{1,0:T(8,128)S(1)}, f32[64,512]{1,0:T(8,128)}, u32[]{:S(2)}) copy-start(f32[64,512]{1,0:T(8,128)} %param.30) | copy-start | bytes 393220
  333.8 44.7 %copy-start.10 = (f32[64,512]{1,0:T(8,128)S(1)}, f32[64,512]{1,0:T(8,128)}, u32[]{:S(2)}) copy-start(f32[64,512]{1,0:T(8,128)} %param.34) | copy-start | bytes 393220
  333.8 19.2 %all-to-all-start.5 = ((bf16[8,64,512]{2,1,0:T(8,128)(2,1)}), bf16[8,64,512]{2,1,0:T(8,128)(2,1)S(1)}, u32[]{:S(2)}, u32[]{:S(2)}) async-start(bf16[8,64,512]{2,1,0:T(8,128)(2,1)} %fusion.1), calls=%async_computation.5 | async-start | bytes 1048576 | tf_op jit(solution)/shard_map/all_to_all | solution.py:588
  339.4 40.5 %copy-start.11 = (f32[512,64]{0,1:T(8,128)S(1)}, f32[512,64]{0,1:T(8,128)}, u32[]{:S(2)}) copy-start(f32[512,64]{0,1:T(8,128)} %param.26) | copy-start | bytes 393220
  356.0 28.4 %copy-start.5 = (f32[128,512]{1,0:T(8,128)S(1)}, f32[128,512]{1,0:T(8,128)}, u32[]{:S(2)}) copy-start(f32[128,512]{1,0:T(8,128)} %param.25) | copy-start | bytes 786436
  356.0 28.4 %copy-start.6 = (f32[128,512]{1,0:T(8,128)S(1)}, f32[128,512]{1,0:T(8,128)}, u32[]{:S(2)}) copy-start(f32[128,512]{1,0:T(8,128)} %param.28) | copy-start | bytes 786436
  356.0 28.4 %copy-start.7 = (f32[128,512]{1,0:T(8,128)S(1)}, f32[128,512]{1,0:T(8,128)}, u32[]{:S(2)}) copy-start(f32[128,512]{1,0:T(8,128)} %param.32) | copy-start | bytes 786436
  356.0 20.0 %all-to-all-start.6 = ((f32[32,8,512]{2,1,0:T(8,128)}), f32[32,8,512]{2,1,0:T(8,128)S(1)}, u32[]{:S(2)}, u32[]{:S(2)}) async-start(f32[32,8,512]{2,1,0:T(8,128)} %broadcast_in_dim.14), calls=%async_computation.6 | async-start | bytes 1048576 | tf_op jit(solution)/shard_map/all_to_all | solution.py:588
  359.6 119.7 %all-gather.3.cloned.1.call-start = ((), (), s32[]{:S(2)}) async-start(), calls=%async_computation.7 | async-start | bytes 8650752 | tf_op jit(solution)/shard_map/all_gather | solution.py:728
  379.4 6.8 %copy-start.2 = (bf16[8,4,4,16,512]{4,3,2,1,0:T(8,128)(2,1)S(1)}, bf16[8,4,4,16,512]{4,3,2,1,0:T(8,128)(2,1)}, u32[]{:S(2)}) copy-start(bf16[8,4,4,16,512]{4,3,2,1,0:T(8,128)(2,1)} %get-tuple-element.37) | copy-start | bytes 6291460
  379.4 5.0 collective-permute-start.4
  458.8 1.5 copy-start.12
  458.8 1.5 copy-start.13
  458.8 1.5 copy-start.14
  479.3 6.2 %copy-start = (bf16[8192,512]{1,0:T(8,128)(2,1)S(1)}, bf16[8192,512]{1,0:T(8,128)(2,1)}, u32[]{:S(2)}) copy-start(bf16[8192,512]{1,0:T(8,128)(2,1)} %all-gather.3.cloned.1.call-done) | copy-start | bytes 25165828
Sparse Core Ops, SparseCore 0:
  386.3 93.0 all-gather.2

commit v3 on v2

--- a/solution.py
+++ b/solution.py
@@ -23,6 +23,7 @@
 UNIT = 128
 ROWS = 128
 QUERIES = 512
+UNROLL = 2
 VMEM_BYTES = 60 * 1024 * 1024
 
 BF = jnp.bfloat16
@@ -64,16 +65,23 @@
     return (values.astype(BF).astype(F32) * head_size ** (-0.5)).astype(BF)
 
 
+def block_of(place, size):
+    return pl.ds(pl.multiple_of(place * size, size), size)
+
+
 def row_index(shape):
     return lax.broadcasted_iota(jnp.int32, shape, 0)
 
 
-def sample_forward(
-    counts, tokens, weights, norms, x_out, first_out, heads_out, mixed_out, log_out, turned
-):
+def sample_forward(late, counts, tokens, cotangent, weights, norms, x_out, *rest):
+    if late:
+        late_out, *rest = rest
+    first_out, heads_out, mixed_out, log_out, turned = rest
     samples, width = tokens.shape[1:]
     head_size = width // HEADS
-    group = x_out.shape[0] * BLOCK
+    early = x_out.shape[1]
+    dealt = (x_out.shape[0], BLOCK, width)
+    group = dealt[0] * BLOCK
 
     @pl.when(pl.program_id(0) == 0)
     def _():
@@ -106,42 +114,42 @@
     for low in range(0, samples, group):
         rows = slice(low, low + group)
         part = tokens[0, rows].astype(F32) + dot(mixed_out[0, :, rows], weights[3], TN)
-        x_out[:, low // group, 0] = part.astype(BF).reshape(group // BLOCK, BLOCK, width)
-
-
-def sample_backward(
-    counts,
-    d_x,
-    tokens,
-    first,
-    heads,
-    mixed,
-    logs,
-    weights,
-    norms,
-    grad_out,
-    keep_out,
-    send_out,
-    norm_out,
-    d_rows,
-    d_mix,
-    d_heads,
-    d_turned,
-    total,
-    norm_total,
-):
+        part = part.astype(BF).reshape(dealt)
+        if low // group < early:
+            x_out[:, low // group, 0] = part
+        else:
+            late_out[:, 0, low // group - early, 0] = part
+            late_out[:, 1, low // group - early, 0] = cotangent[0, rows].reshape(dealt)
+
+
+def sample_backward(offset, early, opening, closing, counts, *refs):
+    if early:
+        d_early, *refs = refs
+    d_late, tokens, first, heads, mixed, logs, weights, norms, *refs = refs
+    if not opening:
+        _, total_in, norm_total_in, *refs = refs
+    grad_out, *refs = refs
+    if closing:
+        keep_out, send_out, norm_out, *refs = refs
+    else:
+        total_out, norm_out, *refs = refs
+    d_rows, d_mix, d_heads, d_turned, total, norm_total = refs
     samples, width = tokens.shape[1:]
     head_size = width // HEADS
     score_scale = head_size ** (-0.5)
-    group = d_x.shape[0] * BLOCK
+    group = d_late.shape[0] * BLOCK
     step = pl.program_id(0)
 
     @pl.when(step == 0)
     def _():
-        total[...] = jnp.zeros_like(total)
-        norm_total[...] = jnp.zeros_like(norm_total)
-
-    feature_live = counts[2] + step < counts[1]
+        if opening:
+            total[...] = jnp.zeros_like(total)
+            norm_total[...] = jnp.zeros_like(norm_total)
+        else:
+            total[...] = total_in[...]
+            norm_total[...] = norm_total_in[...]
+
+    feature_live = counts[2] + offset + step < counts[1]
 
     @pl.when(jnp.logical_not(feature_live))
     def _():
@@ -150,7 +158,9 @@
     @pl.when(feature_live)
     def _():
         for low in range(0, samples, group):
-            d_rows[low : low + group] = d_x[:, low // group, 0].reshape(group, width)
+            deal = low // group
+            part = d_early[:, deal, 0] if deal < early else d_late[:, deal - early, 0]
+            d_rows[low : low + group] = part.reshape(group, width)
         d_mix[...] = dot(weights[3], d_rows[...], NT).astype(BF)
         total[3 * width :] += dot(mixed[0], d_rows[...])
         live = row_index((samples, 1)) < counts[0]
@@ -190,8 +200,11 @@
 
     @pl.when(step == pl.num_programs(0) - 1)
     def _():
-        attention_parts(keep_out, total, counts[4], 0)
-        attention_parts(send_out, total, 1 - counts[4], 0)
+        if closing:
+            attention_parts(keep_out, total, counts[4], 0)
+            attention_parts(send_out, total, 1 - counts[4], 0)
+        else:
+            total_out[...] = total[...]
         norm_out[...] = norm_total[...]
 
 
@@ -220,43 +233,32 @@
             where[2 * pair + piece, :, low : low + half] = rows
 
 
-def middle(
-    counts,
-    x_in,
-    cot_in,
-    weights,
-    weight_in,
-    weight_out,
-    norms,
-    y_out,
-    d_out,
-    keep_out,
-    send_out,
-    norm_out,
-    turned,
-    order,
-    back_order,
-    x_one,
-    normal_one,
-    scale_one,
-    normal_two,
-    scale_two,
-    x_two,
-    low_rows,
-    heads,
-    d_heads,
-    d_turned,
-    mixed,
-    d_mix,
-    probs,
-    live_grad,
-    third,
-    grad_rows,
-    total_attn,
-    total_in,
-    total_out,
-    norm_total,
-):
+def middle(offset, opening, closing, groups, counts, *refs):
+    refs = list(refs)
+
+    def take(count):
+        return [refs.pop(0) for _ in range(count)]
+
+    x_in, cot_in, weights, weight_in, weight_out, norms = take(6)
+    if not opening:
+        held = take(3)
+        (norm_held,) = take(1)
+    if closing:
+        d_outs = take(groups)
+        y_out, keep_out, send_out, norm_out = take(4)
+    else:
+        (both_out,) = take(1)
+        given = take(3)
+        (norm_out,) = take(1)
+    turned, order, back_order, x_one, normal_one, scale_one, normal_two, scale_two = take(8)
+    x_two, low_rows, heads, d_heads, d_turned, mixed, d_mix, probs, live_grad = take(9)
+    third, grad_rows, *totals, norm_total, copied = take(7)
+    total_attn, total_in, total_out = totals
+    if not opening:
+        loads = [
+            pltpu.make_async_copy(source, target, copied.at[place])
+            for place, (source, target) in enumerate(zip(held, totals))
+        ]
     devices, _, local, _, width = x_in.shape
     features = devices * local
     cells = features * BLOCK
@@ -264,10 +266,13 @@
     score_scale = head_size ** (-0.5)
     hidden_width = weight_in.shape[1]
     step = pl.program_id(0)
-    first_sample = (step * devices + counts[3]) * BLOCK
+    first_sample = ((offset + step) * devices + counts[3]) * BLOCK
 
     @pl.when(step == 0)
     def _():
+        if not opening:
+            for load in loads:
+                load.start()
         for which in range(3):
             turned[which] = weights[which].T
         here = row_index((cells, cells))
@@ -276,10 +281,12 @@
         order[...] = jnp.where(source == there, 1.0, 0.0).astype(BF)
         source = (here % BLOCK) * features + here // BLOCK
         back_order[...] = jnp.where(source == there, 1.0, 0.0).astype(BF)
-        total_attn[...] = jnp.zeros_like(total_attn)
-        total_in[...] = jnp.zeros_like(total_in)
-        total_out[...] = jnp.zeros_like(total_out)
-        norm_total[...] = jnp.zeros_like(norm_total)
+        if opening:
+            for total in totals:
+                total[...] = jnp.zeros_like(total)
+            norm_total[...] = jnp.zeros_like(norm_total)
+        else:
+            norm_total[...] = norm_held[...]
 
     x_one[...] = dot(order[...], x_in[:, 0].reshape(cells, width))
     for low in range(0, cells, ROWS):
@@ -316,15 +323,33 @@
         scale_two[rows] = scale
         third[rows] = (normal * norms[4:5] + norms[5:6]).astype(BF)
 
+    if not opening:
+
+        @pl.when(step == 0)
+        def _():
+            for load in loads:
+                load.wait()
+
+    def write_d(values):
+        if not closing:
+            both_out[:, 0, 0] = values
+            return
+        count = local // groups
+        for place, d_out in enumerate(d_outs):
+            d_out[:, 0] = values[:, place * count : (place + 1) * count]
+
     alive = first_sample < counts[0]
 
     @pl.when(jnp.logical_not(alive))
     def _():
-        for low in range(0, hidden_width, width):
-            cols = slice(low, low + width)
+
+        @pl.loop(0, hidden_width // width)
+        def _(block):
+            cols = block_of(block, width)
             hidden, _ = gelu_parts(dot(third[...], weight_in[:, cols]))
             x_two[...] += dot(hidden.astype(BF), weight_out[cols])
-        d_out[...] = jnp.zeros_like(d_out)
+
+        write_d(jnp.zeros((devices, local, BLOCK, width), BF))
 
     @pl.when(alive)
     def _():
@@ -334,19 +359,20 @@
         )
         grads = dot(order[...], cot_in[:, 0].reshape(cells, width))
         live_grad[...] = jnp.where(cell_live, grads, 0.0).astype(BF)
-        for low in range(0, hidden_width, width):
-            cols = slice(low, low + width)
+        grad_rows[...] = jnp.zeros_like(grad_rows)
+
+        @pl.loop(0, hidden_width // width)
+        def _(block):
+            cols = block_of(block, width)
             hidden, slope = gelu_parts(dot(third[...], weight_in[:, cols]))
             hidden = hidden.astype(BF)
             x_two[...] += dot(hidden, weight_out[cols])
             total_out[cols] += dot(hidden, live_grad[...], TN)
             d_pre = (dot(live_grad[...], weight_out[cols], NT) * slope).astype(BF)
             total_in[cols] += dot(d_pre, third[...], TN)
-            d_third = dot(d_pre, weight_in[:, cols], NT)
-            if low:
-                grad_rows[...] += d_third
-            else:
-                grad_rows[...] = d_third
+            grad_rows[...] += dot(d_pre, weight_in[:, cols], NT)
+
+
         for low in range(0, cells, ROWS):
             rows = slice(low, low + ROWS)
             normal = normal_two[rows]
@@ -388,21 +414,35 @@
             back = normalize_back(normal, scale_one[rows], d_second, norms[2:3])
             live_grad[rows] = (grad_rows[rows] + back).astype(BF)
         moved = dot(back_order[...], live_grad[...]).astype(BF)
-        d_out[:, 0] = moved.reshape(devices, local, BLOCK, width)
+        write_d(moved.reshape(devices, local, BLOCK, width))
 
     moved = dot(back_order[...], x_two[...].astype(BF)).astype(BF)
-    y_out[:, 0] = moved.reshape(devices, local, BLOCK, width)
+    moved = moved.reshape(devices, local, BLOCK, width)
+    if closing:
+        y_out[:, 0] = moved
+    else:
+        both_out[:, 1, 0] = moved
 
     @pl.when(step == pl.num_programs(0) - 1)
     def _():
-        chips, owners, rows, _ = keep_out.shape
-        own_ff = hidden_width // (2 * chips * owners)
-        for where, core in ((keep_out, counts[4]), (send_out, 1 - counts[4])):
-            for chip in range(chips):
-                for which, total in ((0, total_in), (1, total_out)):
-                    part = part_of(total, chip, core, owners, own_ff)
-                    where[chip, :, which * own_ff : (which + 1) * own_ff] = part
-            attention_parts(where, total_attn, core, 2 * own_ff)
+        if closing:
+            chips, owners, rows, _ = keep_out.shape
+            own_ff = hidden_width // (2 * chips * owners)
+            for where, core in ((keep_out, counts[4]), (send_out, 1 - counts[4])):
+                for chip in range(chips):
+                    for which, total in ((0, total_in), (1, total_out)):
+                        part = part_of(total, chip, core, owners, own_ff)
+                        where[chip, :, which * own_ff : (which + 1) * own_ff] = part
+                attention_parts(where, total_attn, core, 2 * own_ff)
+        else:
+            stores = [
+                pltpu.make_async_copy(source, target, copied.at[place])
+                for place, (source, target) in enumerate(zip(totals, given))
+            ]
+            for store in stores:
+                store.start()
+            for store in stores:
+                store.wait()
         norm_out[...] = norm_total[...]
 
 
@@ -429,80 +469,132 @@
     return pl.BlockSpec((1,) + tuple(shape[1:]), lambda step: (step,) + zeros)
 
 
-def call(body, grid, in_specs, outs, scratch, nanoseconds, name):
+def call(body, grid, ins, outs, scratch, nanoseconds, name, aliases=None):
     return pl.pallas_call(
         body,
         grid=(grid,),
-        in_specs=[pl.BlockSpec(memory_space=pltpu.SMEM)] + in_specs,
+        in_specs=[pl.BlockSpec(memory_space=pltpu.SMEM)] + [spec for spec, _ in ins[1:]],
         out_specs=[spec for spec, _, _ in outs],
         out_shape=[jax.ShapeDtypeStruct(shape, kind) for _, shape, kind in outs],
-        scratch_shapes=[pltpu.VMEM(shape, kind) for shape, kind in scratch],
+        scratch_shapes=[
+            pltpu.SemaphoreType.DMA((3,)) if kind is None else pltpu.VMEM(shape, kind)
+            for shape, kind in scratch
+        ],
+        input_output_aliases=aliases or {},
         compiler_params=pltpu.CompilerParams(vmem_limit_bytes=VMEM_BYTES),
         cost_estimate=pl.CostEstimate(
             flops=nanoseconds * 1150000, bytes_accessed=1 << 24, transcendentals=0
         ),
         name=name,
-    )
-
-
-def run_sample_forward(counts, tokens, weights, norms, devices):
+    )(ins[0][1], *[value for _, value in ins[1:]])
+
+
+ANYWHERE = pl.BlockSpec(memory_space=pl.ANY)
+
+
+def run_sample_forward(counts, tokens, cotangent, weights, norms, devices, early):
     local, samples, width = tokens.shape
-    deals = samples // (devices * BLOCK)
-    dealt = (devices, deals, local, BLOCK, width)
+    late = samples // (devices * BLOCK) - early
     square = (local, samples, width)
     three = (local, 3, width, samples)
     stats = (local, HEADS, samples)
-    return call(
-        sample_forward,
-        local,
-        [lead(square), half(weights.shape, 0), whole(norms.shape)],
-        [
+    outs = [
+        (
+            pl.BlockSpec((devices, early, 1, BLOCK, width), lambda step: (0, 0, step, 0, 0)),
+            (devices, early, local, BLOCK, width),
+            BF,
+        )
+    ]
+    if late:
+        outs.append(
             (
                 pl.BlockSpec(
-                    (devices, deals, 1, BLOCK, width), lambda step: (0, 0, step, 0, 0)
+                    (devices, 2, late, 1, BLOCK, width), lambda step: (0, 0, 0, step, 0, 0)
                 ),
-                dealt,
+                (devices, 2, late, local, BLOCK, width),
                 BF,
-            ),
-            (lead(square), square, BF),
-            (lead(three), three, BF),
-            (lead(square), (local, width, samples), BF),
-            (lead(stats), stats, F32),
+            )
+        )
+    outs = outs + [
+        (lead(square), square, BF),
+        (lead(three), three, BF),
+        (lead(square), (local, width, samples), BF),
+        (lead(stats), stats, F32),
+    ]
+    return call(
+        functools.partial(sample_forward, late),
+        local,
+        [
+            (None, counts),
+            (lead(square), tokens),
+            (lead(square), cotangent),
+            (half(weights.shape, 0), weights),
+            (whole(norms.shape), norms),
         ],
+        outs,
         [((3, width, width), BF)],
-        36000,
+        25000,
         "sample_forward",
-    )(counts, tokens, weights, norms)
-
-
-def run_middle(counts, x_dealt, cot_dealt, weights, weight_in, weight_out, norms, chips):
-    devices, deals, local, _, width = x_dealt.shape
+    )
+
+
+def run_middle(counts, x_dealt, cot_dealt, weights, weight_in, weight_out, norms, chips, offset, held, groups):
+    array, which = x_dealt
+    devices = array.shape[0]
+    deals, local, _, width = array.shape[-4:]
     cells = devices * local * BLOCK
     hidden_width = weight_in.shape[1]
     parts = (chips, devices, (hidden_width + 2 * width) // (chips * devices), width)
-    dealt = pl.BlockSpec(
-        (devices, 1, local, BLOCK, width), lambda step: (0, step, 0, 0, 0)
-    )
+
+    def dealt(which):
+        if which is None:
+            return pl.BlockSpec(
+                (devices, 1, local, BLOCK, width), lambda step: (0, step, 0, 0, 0)
+            )
+        return pl.BlockSpec(
+            (devices, None, 1, local, BLOCK, width),
+            lambda step: (0, which, step, 0, 0, 0),
+        )
+
+    ins = [
+        (None, counts),
+        (dealt(x_dealt[1]), x_dealt[0]),
+        (dealt(cot_dealt[1]), cot_dealt[0]),
+        (half(weights.shape, 1), weights),
+        (whole(weight_in.shape), weight_in),
+        (whole(weight_out.shape), weight_out),
+        (whole(norms.shape), norms),
+    ]
+    sums = [(4 * width, width), (hidden_width, width), (hidden_width, width)]
+    norm_sums = (4, width)
+    if held is not None:
+        ins = ins + [(ANYWHERE, value) for value in held[:3]] + [(whole(norm_sums), held[3])]
+    if groups:
+        few = (devices, deals, local // groups, BLOCK, width)
+        piece = pl.BlockSpec((devices, 1) + few[2:], lambda step: (0, step, 0, 0, 0))
+        outs = [(piece, few, BF)] * groups + [
+            (dealt(None), (devices, deals, local, BLOCK, width), BF),
+            (once(parts), parts, BF),
+            (once(parts), parts, BF),
+        ]
+    else:
+        outs = [
+            (
+                pl.BlockSpec(
+                    (devices, 2, 1, local, BLOCK, width), lambda step: (0, 0, step, 0, 0, 0)
+                ),
+                (devices, 2, deals, local, BLOCK, width),
+                BF,
+            )
+        ] + [(ANYWHERE, shape, F32) for shape in sums]
+    outs.append((once(norm_sums), norm_sums, F32))
     square = (cells, width)
     turned = (width, cells)
     return call(
-        middle,
+        functools.partial(middle, offset, held is None, bool(groups), groups),
         deals,
-        [
-            dealt,
-            dealt,
-            half(weights.shape, 1),
-            whole(weight_in.shape),
-            whole(weight_out.shape),
-            whole(norms.shape),
-        ],
-        [
-            (dealt, x_dealt.shape, BF),
-            (dealt, x_dealt.shape, BF),
-            (once(parts), parts, BF),
-            (once(parts), parts, BF),
-            (once((4, width)), (4, width), F32),
-        ],
+        ins,
+        outs,
         [
             ((3, width, width), BF),
             ((cells, cells), BF),
@@ -523,54 +615,72 @@
             (square, BF),
             (square, BF),
             (square, F32),
-            ((4 * width, width), F32),
-            ((hidden_width, width), F32),
-            ((hidden_width, width), F32),
-            ((4, width), F32),
-        ],
-        90000,
+        ]
+        + [(shape, F32) for shape in sums]
+        + [(norm_sums, F32), ((3,), None)],
+        deals * 23000,
         "middle",
-    )(counts, x_dealt, cot_dealt, weights, weight_in, weight_out, norms)
-
-
-def run_sample_backward(
-    counts, d_dealt, tokens, first, heads, mixed, logs, weights, norms, chips
-):
-    devices, deals, local, _, width = d_dealt.shape
-    samples = tokens.shape[1]
-    square = (local, samples, width)
-    three = (local, 3, width, samples)
+    )
+
+
+def run_sample_backward(counts, d_early, d_late, saved, weights, norms, chips, offset, held, closing):
+    devices, late, count, _, width = d_late.shape
+    tokens = saved[0]
+    local, samples, _ = tokens.shape
+    early = 0 if d_early is None else d_early.shape[2]
     parts = (chips, devices, 4 * width // (2 * chips * devices), width)
+
+    def moved(shape):
+        zeros = (0,) * (len(shape) - 1)
+        return pl.BlockSpec((1,) + tuple(shape[1:]), lambda step: (step + offset,) + zeros)
+
+    ins = [(None, counts)]
+    if early:
+        ins.append(
+            (
+                pl.BlockSpec(
+                    (devices, None, early, 1, BLOCK, width),
+                    lambda step: (0, 0, 0, step + offset, 0, 0),
+                ),
+                d_early,
+            )
+        )
+    ins.append(
+        (
+            pl.BlockSpec((devices, late, 1, BLOCK, width), lambda step: (0, 0, step, 0, 0)),
+            d_late,
+        )
+    )
+    ins = ins + [(moved(value.shape), value) for value in saved]
+    ins = ins + [(half(weights.shape, 0), weights), (whole(norms.shape), norms)]
+    sums, norm_sums = (4 * width, width), (2, width)
+    aliases = {}
+    if held is not None:
+        aliases = {len(ins): 0}
+        ins = ins + [(ANYWHERE, held[0]), (whole(sums), held[1]), (whole(norm_sums), held[2])]
+    outs = [(moved(tokens.shape), tokens.shape, BF)]
+    if closing:
+        outs = outs + [(once(parts), parts, BF), (once(parts), parts, BF)]
+    else:
+        outs = outs + [(once(sums), sums, F32)]
+    outs.append((once(norm_sums), norm_sums, F32))
     return call(
-        sample_backward,
-        local,
-        [
-            pl.BlockSpec((devices, deals, 1, BLOCK, width), lambda step: (0, 0, step, 0, 0)),
-            lead(square),
-            lead(square),
-            lead(three),
-            lead(mixed.shape),
-            lead(logs.shape),
-            half(weights.shape, 0),
-            whole(norms.shape),
-        ],
-        [
-            (lead(square), square, BF),
-            (once(parts), parts, BF),
-            (once(parts), parts, BF),
-            (once((2, width)), (2, width), F32),
-        ],
+        functools.partial(sample_backward, offset, early, held is None, closing),
+        count,
+        ins,
+        outs,
         [
             ((samples, width), BF),
             ((width, samples), BF),
             ((width, samples), BF),
             ((3, samples, width), BF),
-            ((4 * width, width), F32),
-            ((2, width), F32),
+            (sums, F32),
+            (norm_sums, F32),
         ],
-        49000,
+        count * 11000,
         "sample_backward",
-    )(counts, d_dealt, tokens, first, heads, mixed, logs, weights, norms)
+        aliases,
+    )
 
 
 def adam_step(weight, grad, first_m, second_m, rate):
@@ -675,27 +785,75 @@
     ).astype(jnp.int32)
     weights = attn_weights.reshape(8, width, width)
 
-    dealt_cot = cotangent[0].reshape(local, deals, devices, BLOCK, width).transpose(2, 1, 0, 3, 4)
-    came_cot = exchange(dealt_cot, "feat")
-    dealt_x, first, heads, mixed, logs = run_sample_forward(
-        counts, tokens[0], weights, norm_params, devices
-    )
-    came_x = exchange(dealt_x, "feat")
-    dealt_y, dealt_d, keep_two, send_two, norms_two = run_middle(
-        counts, came_x, came_cot, weights, weight_in, weight_out, norm_params, chips
-    )
-    came_d = exchange(dealt_d, "feat")
-    part_two = reduce_chips(reduce_core(keep_two, send_two))
-    part_two, came_d = lax.optimization_barrier((part_two, came_d))
+    early = max(deals // 2, 1)
+    late = deals - early
+    groups = 2 if late and local % 2 == 0 else 1
     own_ff = weight_in.shape[1] // (tasks * devices)
     own_attn = attn_weights.shape[0] // (tasks * devices)
+
+    def dealt(values):
+        count = values.shape[1] // (devices * BLOCK)
+        values = values.reshape(local, count, devices, BLOCK, width)
+        return values.transpose(2, 1, 0, 3, 4)
+
+    came_cot = exchange(dealt(cotangent[0, :, : early * devices * BLOCK]), "feat")
+    dealt_x, *rest = run_sample_forward(
+        counts, tokens[0], cotangent[0], weights, norm_params, devices, early
+    )
+    came_cot, dealt_x, *rest = lax.optimization_barrier((came_cot, dealt_x, *rest))
+    saved = [tokens[0]] + rest[-4:]
+    came_x = exchange(dealt_x, "feat")
+    shared = (weights, weight_in, weight_out, norm_params, chips)
+    came_both = None
+    if late:
+        dealt_late, came_x = lax.optimization_barrier((rest[0], came_x))
+        came_late = exchange(dealt_late, "feat")
+        dealt_both, *held = run_middle(
+            counts, (came_x, None), (came_cot, None), *shared, 0, None, 0
+        )
+        *dealt_d, dealt_y, keep_two, send_two, norms_two = run_middle(
+            counts, (came_late, 0), (came_late, 1), *shared, early, held, groups
+        )
+        came_both = exchange(dealt_both, "feat")
+        came_both, dealt_d, dealt_y, keep_two, send_two, norms_two = lax.optimization_barrier(
+            (came_both, dealt_d, dealt_y, keep_two, send_two, norms_two)
+        )
+    else:
+        *dealt_d, dealt_y, keep_two, send_two, norms_two = run_middle(
+            counts, (came_x, None), (came_cot, None), *shared, 0, None, groups
+        )
+    part_two = reduce_chips(reduce_core(keep_two, send_two))
+    came_d = exchange(dealt_d[0], "feat")
+    if groups == 2:
+        dealt_d[1], came_d = lax.optimization_barrier((dealt_d[1], came_d))
+        came_last = exchange(dealt_d[1], "feat")
+        held = run_sample_backward(
+            counts, came_both, came_d, saved, weights, norm_params, chips, 0, None, False
+        )
+        came_d, held = lax.optimization_barrier((came_last, held))
+    else:
+        held = None
+    part_two, came_d = lax.optimization_barrier((part_two, came_d))
     share_two = reduce_feat(part_two)
     input_grad, keep_one, send_one, norms_one = run_sample_backward(
-        counts, came_d, tokens[0], first, heads, mixed, logs, weights, norm_params, chips
-    )
-    share_two, send_one = lax.optimization_barrier((share_two, send_one))
+        counts,
+        came_both,
+        came_d,
+        saved,
+        weights,
+        norm_params,
+        chips,
+        0 if held is None else local // 2,
+        held,
+        True,
+    )
+    share_two, input_grad, keep_one, send_one, norms_one = lax.optimization_barrier(
+        (share_two, input_grad, keep_one, send_one, norms_one)
+    )
     share_one = reduce_feat(reduce_chips(reduce_core(keep_one, send_one)))
     came_y = exchange(dealt_y, "feat")
+    if late:
+        came_y = jnp.concatenate([came_both[:, 1], came_y], axis=1)
     block_out = came_y.transpose(2, 1, 0, 3, 4).reshape(1, local, samples, width)
 
     share_in_turned = share_two[:own_ff]

time: 506 us -> 477 us (0.943)
  blocking collectives: 125 us -> 31.4 us
  Pallas kernels: 142 us -> 180 us
  waiting for transfers between devices: 128 us -> 159 us
    all_to_all x2 -> x1, blocking collectives: 125 us -> 31.4 us  [exchange(): lax.all_to_all(values, axis, 0, 0, axis_index_groups=groups, tiled=True)]
    pallas_call x3 -> x5, Pallas kernels: 142 us -> 180 us  [call(): pl.pallas_call(body, grid=(grid,), in_specs=[pl.BlockSpec(memory_space=pl...]
    all_to_all x5 -> x9, waiting for transfers between devices: 51.9 us -> 83.6 us  [exchange(): lax.all_to_all(values, axis, 0, 0, axis_index_groups=groups, tiled=True)]
    all_gather x1, waiting for transfers between devices: 18.4 us -> 45.4 us  [shards(): copies = lax.all_gather(own, ('task', 'feat'), axis=0, tiled=False)]
    ppermute x2, waiting for transfers between devices: 50.7 us -> 23.9 us  [reduce_chips(): came = lax.ppermute(other, 'task', task_pairs(lambda place: place ^ 2))]
    ppermute x2, starting transfers between devices: 23.4 us -> 0.14 us  [reduce_core(): came = lax.ppermute(send, 'task', task_pairs(lambda place: place ^ 1))]
    all_to_all x5 -> x9, starting transfers between devices: 23.8 us -> 42.8 us  [exchange(): lax.all_to_all(values, axis, 0, 0, axis_index_groups=groups, tiled=True)]
  transfers between devices with their start and end apart: 11 -> 15, of which waited for: 10 -> 10; matrix products, arithmetic and copies ran while one was open for 3% -> 3% of each run, Pallas kernels for 14% -> 38%
where the time goes in v3:
time: 477 us; the launch traced here: 471 us
  Pallas kernels  180 us (38%)
  waiting for transfers between devices  159 us (33%)
  starting transfers between devices  44.1 us (9%)
  blocking collectives  31.4 us (7%)
  local copies, waits for them, and re-layouts  20 us (4%)
  between operations  19.8 us (4%)
  other arithmetic  16 us (3%)
    pallas_call x5, Pallas kernels, call(): pl.pallas_call(body, grid=(grid,), in_specs=[pl.BlockSpec(memory_space=pl...  180 us
    all_to_all x9, waiting for transfers between devices, exchange(): lax.all_to_all(values, axis, 0, 0, axis_index_groups=groups, tiled=True)  83.6 us
    all_gather x1, waiting for transfers between devices, shards(): copies = lax.all_gather(own, ('task', 'feat'), axis=0, tiled=False)  45.4 us
    all_to_all x9, starting transfers between devices, exchange(): lax.all_to_all(values, axis, 0, 0, axis_index_groups=groups, tiled=True)  42.8 us
    all_to_all x1, blocking collectives, exchange(): lax.all_to_all(values, axis, 0, 0, axis_index_groups=groups, tiled=True)  31.4 us
    ppermute x2, waiting for transfers between devices, reduce_chips(): came = lax.ppermute(other, 'task', task_pairs(lambda place: place ^ 2))  23.9 us
  transfers between devices with their start and end apart: 15, of which 10 were waited for; matrix products, arithmetic and copies ran while one was open for 3% of the time, Pallas kernels for 38%

profile of v3, /device:TPU:0, one launch (start us, length us, event | category | flops | bytes accessed | tf_op | source)
XLA Modules:
  0.0 470.8 jit_solution(7010202641139962223)
XLA Ops:
  7.2 0.0 slice-start
  7.2 1.2 slice-done
  8.4 1.1 copy.46
  9.5 7.3 %all-to-all-start = ((bf16[8,2,4,16,512]{4,3,2,1,0:T(8,128)(2,1)}), bf16[8,2,4,16,512]{4,3,2,1,0:T(8,128)(2,1)S(1)}, u32[]{:S(2)}, u32[]{:S(2)}) async-start(bf16[8,2,4,16,512]{4,3,2,1,0:T(8,128)(2,1)} %bitcast.42), calls=%async_computation | async-start | bytes 2097152 | tf_op jit(solution)/shard_map/all_to_all | solution.py:698
  18.0 0.6 stack.15.counts
  18.6 25.1 %sample_forward.1 = (bf16[8,2,4,16,512]{4,3,2,1,0:T(8,128)(2,1)}, bf16[8,2,2,4,16,512]{5,4,3,2,1,0:T(8,128)(2,1)}, bf16[4,512,512]{2,1,0:T(8,128)(2,1)}, bf16[4,...) custom-call(s32[5]{0:T(128)} %stack.15.counts, bf16[4,512,512]{2,1,0:T(8,128)(2,1)} %bitcast.56, ...), custom_call_target="tpu_custom_call" | custom-call | flops 28750000128 | bytes 16777216 | tf_op jit(solution)/shard_map/sample_forward/pallas_call | solution.py:473
  43.8 31.4 %all_to_all.50.refs_0_ = bf16[8,2,4,16,512]{4,3,2,1,0:T(8,128)(2,1)} all-to-all(bf16[8,2,4,16,512]{4,3,2,1,0:T(8,128)(2,1)} %get-tuple-element.78), channel_id=1, replica_groups=mesh['task'=4,'feat'=8] {'feat'}, dimensions={0} | all-to-all | bytes 2097152 | tf_op jit(solution)/shard_map/all_to_all | solution.py:698
  75.2 3.6 all-to-all-start.3
  78.8 53.4 %middle.2 = (bf16[8,2,2,4,16,512]{5,4,3,2,1,0:T(8,128)(2,1)}, f32[2048,512]{1,0:T(8,128)}, f32[2048,512]{1,0:T(8,128)}, f32[2048,512]{1,0:T(8,128)}, f32[4,512]{1,0:T(4,128)}) custom-call(s32[5]{0:T(128)} %stack.15.counts, bf16[8,2,4,16,512]{4,3,2,1,0:T(8,128)(2,1)} %all_to_all.50.refs_0_, bf16[8,2,4,16,512]{4,3,2,1,0:T(8,128)(2,1)} %copy-done.5, ...), custom_call_target="tpu_custom_call" | custom-call | flops 52899999744 | bytes 16777216 | tf_op jit(solution)/shard_map/middle/pallas_call | solution.py:473
  132.2 0.0 copy-start.3
  132.2 1.3 copy-done.3
  133.5 5.9 %all-to-all-start.2 = ((bf16[8,2,2,4,16,512]{5,4,3,2,1,0:T(8,128)(2,1)}), bf16[8,2,2,4,16,512]{5,4,3,2,1,0:T(8,128)(2,1)S(1)}, u32[]{:S(2)}, u32[]{:S(2)}) async-start(bf16[8,2,2,4,16,512]{5,4,3,2,1,0:T(8,128)(2,1)} %get-tuple-element.81), calls=%async_computation.2 | async-start | bytes 4194304 | tf_op jit(solution)/shard_map/all_to_all | solution.py:698
  139.4 50.4 %middle.3 = (bf16[8,2,2,16,512]{4,3,2,1,0:T(8,128)(2,1)}, bf16[8,2,2,16,512]{4,3,2,1,0:T(8,128)(2,1)}, bf16[8,2,4,16,512]{4,3,2,1,0:T(8,128)(2,1)}, bf16[2,8,192...) custom-call(s32[5]{0:T(128)} %stack.15.counts, ...), custom_call_target="tpu_custom_call" | custom-call | flops 52899999744 | bytes 16777216 | tf_op jit(solution)/shard_map/middle/pallas_call | solution.py:473
  189.8 0.1 collective-permute-start
  189.9 6.0 %all-to-all-start.5 = ((bf16[8,2,2,16,512]{4,3,2,1,0:T(8,128)(2,1)}), bf16[8,2,2,16,512]{4,3,2,1,0:T(8,128)(2,1)S(1)}, u32[]{:S(2)}, u32[]{:S(2)}) async-start(bf16[8,2,2,16,512]{4,3,2,1,0:T(8,128)(2,1)} %get-tuple-element.98), calls=%async_computation.5 | async-start | bytes 1048576 | tf_op jit(solution)/shard_map/all_to_all | solution.py:698
  195.9 15.1 %all-to-all-done.5.refs_1_ = bf16[8,2,2,16,512]{4,3,2,1,0:T(8,128)(2,1)S(1)} async-done(((bf16[8,2,2,16,512]{4,3,2,1,0:T(8,128)(2,1)}), bf16[8,2,2,16,512]{4,3,2,1,0:T(8,128)(2,1)S(1)}, u32[]{:S(2)}, u32[]{:S(2)}) %all-to-all-start.5) | async-done | bytes 524320 | tf_op jit(solution)/shard_map/all_to_all | solution.py:698
  211.0 4.1 all-to-all-start.6
  215.2 3.9 add_convert_fusion
  219.1 1.4 dynamic-slice_bitcast_fusion
  220.5 25.3 %sample_backward.2 = (bf16[4,512,512]{2,1,0:T(8,128)(2,1)}, f32[2048,512]{1,0:T(8,128)}, f32[2,512]{1,0:T(2,128)}) custom-call(s32[5]{0:T(128)} %stack.15.counts, bf16[8,2,2,4,16,512]{5,4,3,2,1,0:T(8,128)(2,1)} %copy-done.1, bf16[8,2,2,16,512]{4,3,2,1,0:T(8,128)(2,1)} %copy-done.6, bf16[4,512,512]{2,1,0:T(8,128)(2,1)} %bitcast.57, ...), custom_call_target="tpu_custom_call" | custom-call | flops 25300000768 | bytes 16777216 | tf_op jit(solution)/shard_map/sample_backward/pallas_call | solution.py:473
  245.8 10.5 %collective-permute-done.1 = bf16[8,192,512]{2,1,0:T(8,128)(2,1)} collective-permute-done((bf16[8,192,512]{2,1,0:T(8,128)(2,1)}, bf16[8,192,512]{2,1,0:T(8,128)(2,1)}, u32[]{:S(2)}, u32[]{:S(2)}) %collective-permute-start.1) | collective-permute-done | bytes 1572896 | tf_op jit(solution)/shard_map/ppermute | solution.py:716
  256.3 3.0 fusion
  259.4 5.9 %all-to-all-start.7 = ((bf16[8,192,512]{2,1,0:T(8,128)(2,1)}), bf16[8,192,512]{2,1,0:T(8,128)(2,1)S(1)}, u32[]{:S(2)}, u32[]{:S(2)}) async-start(bf16[8,192,512]{2,1,0:T(8,128)(2,1)} %fusion), calls=%async_computation.7 | async-start | bytes 3145728 | tf_op jit(solution)/shard_map/all_to_all | solution.py:698
  265.3 26.0 %sample_backward.3 = (bf16[4,512,512]{2,1,0:T(8,128)(2,1)}, bf16[2,8,64,512]{3,2,1,0:T(8,128)(2,1)}, bf16[2,8,64,512]{3,2,1,0:T(8,128)(2,1)}, f32[2,512]{1,0:T(2,128)}) custom-call(s32[5]{0:T(128)} %stack.15.counts, bf16[8,2,2,4,16,512]{5,4,3,2,1,0:T(8,128)(2,1)} %copy-done.1, ...), custom_call_target="tpu_custom_call", output_to_operand_aliasing={{0}: (10, {})} | custom-call | flops 25300000768 | bytes 16777216 | tf_op jit(solution)/shard_map/sample_backward/pallas_call | solution.py:473
  291.3 9.5 %all-to-all-done.7 = bf16[8,192,512]{2,1,0:T(8,128)(2,1)S(1)} async-done(((bf16[8,192,512]{2,1,0:T(8,128)(2,1)}), bf16[8,192,512]{2,1,0:T(8,128)(2,1)S(1)}, u32[]{:S(2)}, u32[]{:S(2)}) %all-to-all-start.7) | async-done | bytes 1572896 | tf_op jit(solution)/shard_map/all_to_all | solution.py:698
  300.8 0.2 convert_reduce_fusion
  301.0 0.1 collective-permute-start.2
  301.1 2.9 collective-permute-done.2
  304.0 0.3 add_convert_fusion.1
  304.3 0.1 dynamic-slice_bitcast_fusion.1
  304.4 0.6 collective-permute-start.3
  305.0 13.4 %collective-permute-done.3 = bf16[8,64,512]{2,1,0:T(8,128)(2,1)S(1)} collective-permute-done((bf16[8,64,512]{2,1,0:T(8,128)(2,1)S(1)}, bf16[8,64,512]{2,1,0:T(8,128)(2,1)S(1)}, u32[]{:S(2)}, u32[]{:S(2)}) %collective-permute-start.3) | collective-permute-done | bytes 524320 | tf_op jit(solution)/shard_map/ppermute | solution.py:716
  318.4 0.9 fusion.1
  319.4 3.6 all-to-all-start.8
  323.0 0.7 multiply_reduce_fusion
  323.7 13.5 %all-to-all-done.8 = bf16[8,64,512]{2,1,0:T(8,128)(2,1)S(1)} async-done(((bf16[8,64,512]{2,1,0:T(8,128)(2,1)}), bf16[8,64,512]{2,1,0:T(8,128)(2,1)S(1)}, u32[]{:S(2)}, u32[]{:S(2)}) %all-to-all-start.8) | async-done | bytes 524320 | tf_op jit(solution)/shard_map/all_to_all | solution.py:698
  337.2 0.1 convert_reduce_fusion.1
  337.3 0.6 multiply_reduce_fusion.1
  339.2 0.1 pad.7.clone
  339.3 0.1 maximum_maximum_fusion
  339.4 0.9 broadcast_in_dim.14
  340.2 2.7 all-to-all-start.9
  343.0 0.0 all-gather.3.cloned.1.call-start
  343.0 16.3 %all-to-all-done.9 = f32[32,8,512]{2,1,0:T(8,128)S(1)} async-done(((f32[32,8,512]{2,1,0:T(8,128)}), f32[32,8,512]{2,1,0:T(8,128)S(1)}, u32[]{:S(2)}, u32[]{:S(2)}) %all-to-all-start.9) | async-done | bytes 524320 | tf_op jit(solution)/shard_map/all_to_all | solution.py:698
  359.4 0.6 multiply_reduce_fusion.2
  360.0 0.5 slice.40
  361.9 0.8 fusion.11
  362.7 0.5 collective-permute-start.4
  363.3 0.8 convert_bitcast_fusion
  364.1 3.6 collective-permute-done.4
  367.8 1.0 fusion.7
  368.8 0.7 pad_maximum_fusion
  369.5 0.0 all-gather.3.cloned.1.call-update
  369.5 3.6 all-to-all-start.4
  373.1 1.1 slice_bitcast_fusion
  374.2 29.2 %all-to-all-done.4 = bf16[8,2,4,16,512]{4,3,2,1,0:T(8,128)(2,1)S(1)} async-done(((bf16[8,2,4,16,512]{4,3,2,1,0:T(8,128)(2,1)}), bf16[8,2,4,16,512]{4,3,2,1,0:T(8,128)(2,1)S(1)}, u32[]{:S(2)}, u32[]{:S(2)}) %all-to-all-start.4) | async-done | bytes 1048608 | tf_op jit(solution)/shard_map/all_to_all | solution.py:698
  403.3 1.4 maximum_bitcast_fusion
  404.8 1.5 copy.43
  406.3 0.6 multiply_subtract_fusion.3
  406.9 45.4 %all-gather.3.cloned.1.call-done = bf16[8192,512]{1,0:T(8,128)(2,1)} async-done(((bf16[256,512]{1,0:T(8,128)(2,1)}), bf16[8192,512]{1,0:T(8,128)(2,1)}) %all-gather.3.cloned.1.call-update) | async-done | bytes 8388624 | tf_op jit(solution)/shard_map/all_gather | solution.py:886
  452.4 4.9 %slice.42 = bf16[32,128,512]{2,1,0:T(8,128)(2,1)} slice(bf16[32,256,512]{2,1,0:T(8,128)(2,1)} %bitcast.43), slice={[0:32], [0:128], [0:512]} | slice | bytes 8388608 | tf_op jit(solution)/shard_map/slice | solution.py:887
  457.3 1.2 copy-done
  458.5 1.7 fusion.14
  460.2 2.4 copy.44
  (48 shorter events, 0.2 us)
Async XLA Ops:
  7.2 1.2 slice-start
  9.5 34.3 %all-to-all-start = ((bf16[8,2,4,16,512]{4,3,2,1,0:T(8,128)(2,1)}), bf16[8,2,4,16,512]{4,3,2,1,0:T(8,128)(2,1)S(1)}, u32[]{:S(2)}, u32[]{:S(2)}) async-start(bf16[8,2,4,16,512]{4,3,2,1,0:T(8,128)(2,1)} %bitcast.42), calls=%async_computation | async-start | bytes 2097152 | tf_op jit(solution)/shard_map/all_to_all | solution.py:698
  43.8 31.4 %copy-start.5 = (bf16[8,2,4,16,512]{4,3,2,1,0:T(8,128)(2,1)}, bf16[8,2,4,16,512]{4,3,2,1,0:T(8,128)(2,1)S(1)}, u32[]{:S(2)}) copy-start(bf16[8,2,4,16,512]{4,3,2,1,0:T(8,128)(2,1)S(1)} %all-to-all-done.refs_1_) | copy-start | bytes 3145732
  75.2 57.0 %all-to-all-start.3 = ((bf16[8,2,2,4,16,512]{5,4,3,2,1,0:T(8,128)(2,1)}), bf16[8,2,2,4,16,512]{5,4,3,2,1,0:T(8,128)(2,1)S(1)}, u32[]{:S(2)}, u32[]{:S(2)}) async-start(bf16[8,2,2,4,16,512]{5,4,3,2,1,0:T(8,128)(2,1)} %get-tuple-element.82), calls=%async_computation.3 | async-start | bytes 4194304 | tf_op jit(solution)/shard_map/all_to_all | solution.py:698
  132.2 1.3 copy-start.3
  133.5 56.3 %all-to-all-start.2 = ((bf16[8,2,2,4,16,512]{5,4,3,2,1,0:T(8,128)(2,1)}), bf16[8,2,2,4,16,512]{5,4,3,2,1,0:T(8,128)(2,1)S(1)}, u32[]{:S(2)}, u32[]{:S(2)}) async-start(bf16[8,2,2,4,16,512]{5,4,3,2,1,0:T(8,128)(2,1)} %get-tuple-element.81), calls=%async_computation.2 | async-start | bytes 4194304 | tf_op jit(solution)/shard_map/all_to_all | solution.py:698
  189.8 25.4 %copy-start.1 = (bf16[8,2,2,4,16,512]{5,4,3,2,1,0:T(8,128)(2,1)}, bf16[8,2,2,4,16,512]{5,4,3,2,1,0:T(8,128)(2,1)S(1)}, u32[]{:S(2)}) copy-start(bf16[8,2,2,4,16,512]{5,4,3,2,1,0:T(8,128)(2,1)S(1)} %all-to-all-done.2.refs_0_) | copy-start | bytes 6291460
  189.8 25.4 %collective-permute-start = (bf16[2,8,192,512]{3,2,1,0:T(8,128)(2,1)}, bf16[2,8,192,512]{3,2,1,0:T(8,128)(2,1)}, u32[]{:S(2)}, u32[]{:S(2)}) collective-permute-start(bf16[2,8,192,512]{3,2,1,0:T(8,128)(2,1)} %get-tuple-element.96), channel_id=1, source_target_pairs={{0,8},{8,0},{16,24},{24,16},{1,9},{9,1},{17,25},{25,17},{2,10},{10... | collective-permute-start | bytes 9437192 | tf_op jit(solution)/shard_map/ppermute | solution.py:706
  189.9 21.1 %all-to-all-start.5 = ((bf16[8,2,2,16,512]{4,3,2,1,0:T(8,128)(2,1)}), bf16[8,2,2,16,512]{4,3,2,1,0:T(8,128)(2,1)S(1)}, u32[]{:S(2)}, u32[]{:S(2)}) async-start(bf16[8,2,2,16,512]{4,3,2,1,0:T(8,128)(2,1)} %get-tuple-element.98), calls=%async_computation.5 | async-start | bytes 1048576 | tf_op jit(solution)/shard_map/all_to_all | solution.py:698
  211.0 4.2 copy-start.6
  211.0 34.8 %all-to-all-start.6 = ((bf16[8,2,2,16,512]{4,3,2,1,0:T(8,128)(2,1)}), bf16[8,2,2,16,512]{4,3,2,1,0:T(8,128)(2,1)}, u32[]{:S(2)}, u32[]{:S(2)}) async-start(bf16[8,2,2,16,512]{4,3,2,1,0:T(8,128)(2,1)} %get-tuple-element.99), calls=%async_computation.6 | async-start | bytes 1048576 | tf_op jit(solution)/shard_map/all_to_all | solution.py:698
  220.5 35.9 %collective-permute-start.1 = (bf16[8,192,512]{2,1,0:T(8,128)(2,1)}, bf16[8,192,512]{2,1,0:T(8,128)(2,1)}, u32[]{:S(2)}, u32[]{:S(2)}) collective-permute-start(bf16[8,192,512]{2,1,0:T(8,128)(2,1)} %dynamic-slice_bitcast_fusion), channel_id=1, source_target_pairs={{0,16},{8,24},{16,0},{24,8},{1,17},{9,25},{17,1},{25,9},{2,18},{10... | collective-permute-start | bytes 4718600 | tf_op jit(solution)/shard_map/ppermute | solution.py:716
  259.4 41.4 %all-to-all-start.7 = ((bf16[8,192,512]{2,1,0:T(8,128)(2,1)}), bf16[8,192,512]{2,1,0:T(8,128)(2,1)S(1)}, u32[]{:S(2)}, u32[]{:S(2)}) async-start(bf16[8,192,512]{2,1,0:T(8,128)(2,1)} %fusion), calls=%async_computation.7 | async-start | bytes 3145728 | tf_op jit(solution)/shard_map/all_to_all | solution.py:698
  291.3 12.7 %copy-start.4 = (bf16[2,8,64,512]{3,2,1,0:T(8,128)(2,1)S(1)}, bf16[2,8,64,512]{3,2,1,0:T(8,128)(2,1)}, u32[]{:S(2)}) copy-start(bf16[2,8,64,512]{3,2,1,0:T(8,128)(2,1)} %get-tuple-element.121) | copy-start | bytes 3145732
  301.0 2.9 collective-permute-start.2
  304.4 34.9 %copy-start.19 = (f32[4,512]{1,0:T(4,128)S(1)}, f32[4,512]{1,0:T(4,128)}, u32[]{:S(2)}) copy-start(f32[4,512]{1,0:T(4,128)} %get-tuple-element.120) | copy-start | bytes 24580
  304.4 34.9 %copy-start.20 = (f32[2,512]{1,0:T(2,128)S(1)}, f32[2,512]{1,0:T(2,128)}, u32[]{:S(2)}) copy-start(f32[2,512]{1,0:T(2,128)} %get-tuple-element.119) | copy-start | bytes 12292
  304.4 14.0 %collective-permute-start.3 = (bf16[8,64,512]{2,1,0:T(8,128)(2,1)S(1)}, bf16[8,64,512]{2,1,0:T(8,128)(2,1)S(1)}, u32[]{:S(2)}, u32[]{:S(2)}) collective-permute-start(bf16[8,64,512]{2,1,0:T(8,128)(2,1)S(1)} %dynamic-slice_bitcast_fusion.1), channel_id=1, source_target_pairs={{0,16},{8,24},{16,0},{24,8},{1,17},{9,25},{17,1},{25,9},{2,18},{10... | collective-permute-start | bytes 1572872 | tf_op jit(solution)/shard_map/ppermute | solution.py:716
  319.3 42.5 %copy-start.10 = (f32[64,512]{1,0:T(8,128)S(1)}, f32[64,512]{1,0:T(8,128)}, u32[]{:S(2)}) copy-start(f32[64,512]{1,0:T(8,128)} %param.27) | copy-start | bytes 393220
  319.4 42.5 %copy-start.11 = (f32[64,512]{1,0:T(8,128)S(1)}, f32[64,512]{1,0:T(8,128)}, u32[]{:S(2)}) copy-start(f32[64,512]{1,0:T(8,128)} %param.30) | copy-start | bytes 393220
  319.4 42.5 %copy-start.12 = (f32[64,512]{1,0:T(8,128)S(1)}, f32[64,512]{1,0:T(8,128)}, u32[]{:S(2)}) copy-start(f32[64,512]{1,0:T(8,128)} %param.34) | copy-start | bytes 393220
  319.4 17.8 %all-to-all-start.8 = ((bf16[8,64,512]{2,1,0:T(8,128)(2,1)}), bf16[8,64,512]{2,1,0:T(8,128)(2,1)S(1)}, u32[]{:S(2)}, u32[]{:S(2)}) async-start(bf16[8,64,512]{2,1,0:T(8,128)(2,1)} %fusion.1), calls=%async_computation.8 | async-start | bytes 1048576 | tf_op jit(solution)/shard_map/all_to_all | solution.py:698
  323.7 39.6 %copy-start.13 = (f32[512,64]{0,1:T(8,128)S(1)}, f32[512,64]{0,1:T(8,128)}, u32[]{:S(2)}) copy-start(f32[512,64]{0,1:T(8,128)} %param.26) | copy-start | bytes 393220
  323.7 39.6 %copy-start.14 = (f32[512,64]{0,1:T(8,128)S(1)}, f32[512,64]{0,1:T(8,128)}, u32[]{:S(2)}) copy-start(f32[512,64]{0,1:T(8,128)} %param.29) | copy-start | bytes 393220
  323.7 39.6 %copy-start.15 = (f32[512,64]{0,1:T(8,128)S(1)}, f32[512,64]{0,1:T(8,128)}, u32[]{:S(2)}) copy-start(f32[512,64]{0,1:T(8,128)} %param.33) | copy-start | bytes 393220
  340.2 27.5 %copy-start.7 = (f32[128,512]{1,0:T(8,128)S(1)}, f32[128,512]{1,0:T(8,128)}, u32[]{:S(2)}) copy-start(f32[128,512]{1,0:T(8,128)} %param.25) | copy-start | bytes 786436
  340.2 27.5 %copy-start.8 = (f32[128,512]{1,0:T(8,128)S(1)}, f32[128,512]{1,0:T(8,128)}, u32[]{:S(2)}) copy-start(f32[128,512]{1,0:T(8,128)} %param.28) | copy-start | bytes 786436
  340.2 27.5 %copy-start.9 = (f32[128,512]{1,0:T(8,128)S(1)}, f32[128,512]{1,0:T(8,128)}, u32[]{:S(2)}) copy-start(f32[128,512]{1,0:T(8,128)} %param.32) | copy-start | bytes 786436
  340.2 19.1 %all-to-all-start.9 = ((f32[32,8,512]{2,1,0:T(8,128)}), f32[32,8,512]{2,1,0:T(8,128)S(1)}, u32[]{:S(2)}, u32[]{:S(2)}) async-start(f32[32,8,512]{2,1,0:T(8,128)} %broadcast_in_dim.14), calls=%async_computation.9 | async-start | bytes 1048576 | tf_op jit(solution)/shard_map/all_to_all | solution.py:698
  343.0 109.4 %all-gather.3.cloned.1.call-start = ((), (), s32[]{:S(2)}) async-start(), calls=%async_computation.10 | async-start | bytes 8650752 | tf_op jit(solution)/shard_map/all_gather | solution.py:886
  362.7 5.0 %collective-permute-start.4 = (f32[64,512]{1,0:T(8,128)S(1)}, f32[64,512]{1,0:T(8,128)S(1)}, u32[]{:S(2)}, u32[]{:S(2)}) collective-permute-start(f32[64,512]{1,0:T(8,128)S(1)} %get-tuple-element.179), channel_id=1, source_target_pairs={{0,16},{8,24},{16,0},{24,8},{1,17},{9,25},{17,1},{25,9},{2,18},{10... | collective-permute-start | bytes 393224 | tf_op jit(solution)/shard_map/ppermute | solution.py:739
  367.7 5.3 %copy-start.2 = (bf16[8,2,2,4,16,512]{5,4,3,2,1,0:T(8,128)(2,1)S(1)}, bf16[8,2,2,4,16,512]{5,4,3,2,1,0:T(8,128)(2,1)}, u32[]{:S(2)}) copy-start(bf16[8,2,2,4,16,512]{5,4,3,2,1,0:T(8,128)(2,1)} %copy-done.1) | copy-start | bytes 6291460
  369.5 33.8 %all-to-all-start.4 = ((bf16[8,2,4,16,512]{4,3,2,1,0:T(8,128)(2,1)}), bf16[8,2,4,16,512]{4,3,2,1,0:T(8,128)(2,1)S(1)}, u32[]{:S(2)}, u32[]{:S(2)}) async-start(bf16[8,2,4,16,512]{4,3,2,1,0:T(8,128)(2,1)} %get-tuple-element.94), calls=%async_computation.4 | async-start | bytes 2097152 | tf_op jit(solution)/shard_map/all_to_all | solution.py:698
  404.8 1.5 copy-start.16
  404.8 1.5 copy-start.17
  404.8 1.5 copy-start.18
  452.4 6.2 %copy-start = (bf16[8192,512]{1,0:T(8,128)(2,1)S(1)}, bf16[8192,512]{1,0:T(8,128)(2,1)}, u32[]{:S(2)}) copy-start(bf16[8192,512]{1,0:T(8,128)(2,1)} %all-gather.3.cloned.1.call-done) | copy-start | bytes 25165828
Sparse Core Ops, SparseCore 0:
  369.6 82.6 all-gather.2

commit v4 on v3

--- a/solution.py
+++ b/solution.py
@@ -698,23 +698,48 @@
     return lax.all_to_all(values, axis, 0, 0, axis_index_groups=groups, tiled=True)
 
 
-def task_pairs(hop):
-    return [(place, hop(place)) for place in range(lax.axis_size("task"))]
+def moved_by(values, axis, hop):
+    pairs = [(place, hop(place)) for place in range(lax.axis_size(axis))]
+    return lax.ppermute(values, axis, pairs)
+
+
+def other_core(values):
+    return moved_by(values, "task", lambda place: place ^ 1)
+
+
+def along_y(values, shift):
+    tasks = lax.axis_size("task")
+    return moved_by(values, "task", lambda place: (place + 2 * shift) % tasks)
+
+
+def along_x(values):
+    return moved_by(values, "feat", lambda place: place ^ 1)
+
+
+def along_z(values, shift):
+    devices = lax.axis_size("feat")
+    return moved_by(values, "feat", lambda place: (place + 2 * shift) % devices)
 
 
 def reduce_core(keep, send):
-    came = lax.ppermute(send, "task", task_pairs(lambda place: place ^ 1))
+    came = other_core(send)
     return (keep.astype(F32) + came.astype(F32)).astype(BF)
 
 
-def reduce_chips(values):
+def chip_parts(values):
+    if values.shape[0] != 2:
+        return (values,)
+    chip = lax.axis_index("task") // 2
+    return tuple(
+        lax.dynamic_index_in_dim(values, place, 0, keepdims=False) for place in (chip, 1 - chip)
+    )
+
+
+def reduce_chips(parts):
+    if len(parts) == 2:
+        return (parts[0].astype(F32) + along_y(parts[1], 1).astype(F32)).astype(BF)
+    (values,) = parts
     chips = values.shape[0]
-    chip = lax.axis_index("task") // 2
-    if chips == 2:
-        mine = lax.dynamic_index_in_dim(values, chip, 0, keepdims=False)
-        other = lax.dynamic_index_in_dim(values, 1 - chip, 0, keepdims=False)
-        came = lax.ppermute(other, "task", task_pairs(lambda place: place ^ 2))
-        return (mine.astype(F32) + came.astype(F32)).astype(BF)
     groups = [[2 * place + core for place in range(chips)] for core in range(2)]
     return jnp.sum(exchange(values, "task", groups).astype(F32), axis=0).astype(BF)
 
@@ -733,10 +758,11 @@
         return chip // 2 + (chips // 2 if second else 0)
 
     def send(values, odd_second):
-        pairs = task_pairs(
-            lambda place: 2 * target(place // 2, (place // 2 % 2 == 1) == odd_second) + place % 2
-        )
-        return lax.ppermute(values, "task", pairs)
+        return moved_by(
+            values,
+            "task",
+            lambda place: 2 * target(place // 2, (place // 2 % 2 == 1) == odd_second) + place % 2,
+        )
 
     if chips > 2:
         stay = send(stay, True)
@@ -747,10 +773,126 @@
     )
 
 
+def place_copies(chips, layers, table, *refs):
+    count = 2 * chips
+    near, far = refs[:count], refs[count : count + 4]
+    *halves, attn_out, in_out, out_out, block_out, pair, copied = refs[count + 4 :]
+    step = pl.program_id(0)
+    moves = []
+    for half in halves:
+        for deal in range(half.shape[-4]):
+            for feature in range(half.shape[-3]):
+                index = (slice(None),) + (1,) * (len(half.shape) - 5) + (deal, feature)
+                place = len(moves)
+                target = block_out.at[feature, place // half.shape[-3]]
+                moves.append(pltpu.make_async_copy(half.at[index], target, copied.at[place]))
+
+    @pl.when(step == 0)
+    def _():
+        for move in moves:
+            move.start()
+    side, layer = table[count], table[count + 1]
+    rows = near[0].shape[2]
+    half = far[0].shape[1] // 2
+
+    def owner(other, behind):
+        return ((layer + layers - behind) % layers) * 2 + (side ^ other)
+
+    for place in range(count):
+
+        @pl.when(step == place)
+        def _():
+            core, chip = place // chips, place % chips
+            for other in range(2):
+                for behind in range(layers):
+                    at = owner(other, behind)
+                    attn_out[block_of(at, rows)] = near[place][other, behind]
+                    part = far[core * 2 + other]
+                    pair[block_of(at, half)] = part[chip * layers + behind, :half]
+                    out_out[block_of(at, half)] = part[chip * layers + behind, half:]
+
+    in_out[...] = pair[...].T
+
+    @pl.when(step == count - 1)
+    def _():
+        for move in moves:
+            move.wait()
+
+
+def gather_layers(own_attn, own_ff):
+    layers = lax.axis_size("feat") // 2
+    nears = [own_attn] + [along_z(own_attn, shift) for shift in range(1, layers)]
+    fars = [own_ff] + [along_z(own_ff, shift) for shift in range(1, layers)]
+    return jnp.stack(nears), jnp.stack(fars)
+
+
+def gather_rest(nears, fars, came_halves):
+    layers, rows_near, width = nears.shape
+    rows_far = fars.shape[1]
+    chips = lax.axis_size("task") // 2
+    task, place = lax.axis_index("task"), lax.axis_index("feat")
+    near = jnp.stack([nears, along_x(nears)])
+    far = jnp.concatenate([fars] + [along_y(fars, shift) for shift in range(1, chips)])
+    nears = [near] + [along_y(near, shift) for shift in range(1, chips)]
+    fars = [far, along_x(far)]
+    nears = nears + [other_core(value) for value in nears]
+    fars = fars + [other_core(value) for value in fars]
+    steps = jnp.arange(2 * chips, dtype=jnp.int32)
+    chip = (task // 2 - steps) % chips
+    core = (task % 2) ^ (steps // chips)
+    table = jnp.concatenate([chip * 2 + core, jnp.stack([place % 2, place // 2])])
+    total = 2 * chips
+    owned = 2 * layers
+    devices, _, local, _, _ = came_halves[-1].shape
+    deals = sum(value.shape[-4] for value in came_halves)
+
+    def held(value):
+        zeros = (0,) * value.ndim
+        return pl.BlockSpec(
+            value.shape, lambda step, table: zeros, pipeline_mode=pl.Buffered(1)
+        )
+
+    return pl.pallas_call(
+        functools.partial(place_copies, chips, layers),
+        grid_spec=pltpu.PrefetchScalarGridSpec(
+            num_scalar_prefetch=1,
+            grid=(total,),
+            in_specs=[held(value) for value in nears + fars] + [ANYWHERE] * len(came_halves),
+            out_specs=[
+                pl.BlockSpec((owned * rows_near, width), lambda step, table: (table[step], 0)),
+                pl.BlockSpec(
+                    (width, owned * rows_far // 2), lambda step, table: (0, table[step])
+                ),
+                pl.BlockSpec(
+                    (owned * rows_far // 2, width), lambda step, table: (table[step], 0)
+                ),
+                ANYWHERE,
+            ],
+            scratch_shapes=[
+                pltpu.VMEM((owned * rows_far // 2, width), BF),
+                pltpu.SemaphoreType.DMA((deals * local,)),
+            ],
+        ),
+        out_shape=[
+            jax.ShapeDtypeStruct((total * owned * rows_near, width), BF),
+            jax.ShapeDtypeStruct((width, total * owned * rows_far // 2), BF),
+            jax.ShapeDtypeStruct((total * owned * rows_far // 2, width), BF),
+            jax.ShapeDtypeStruct((local, deals, devices, BLOCK, width), BF),
+        ],
+        compiler_params=pltpu.CompilerParams(vmem_limit_bytes=40 * 1024 * 1024),
+        name="place_copies",
+    )(table.astype(jnp.int32), *nears, *fars, *came_halves)
+
+
 def total_of(values):
-    count = lax.axis_size("task") * lax.axis_size("feat")
-    copies = jnp.broadcast_to(values[None], (count,) + values.shape)
-    return jnp.sum(exchange(copies, ("task", "feat")), axis=0)
+    values = values + other_core(values)
+    chips = lax.axis_size("task") // 2
+    values = sum([along_y(values, shift) for shift in range(1, chips)], values)
+    bit = 1
+    while bit < lax.axis_size("feat"):
+        values = values + moved_by(values, "feat", lambda place: place ^ bit)
+        bit *= 2
+    return values
 
 
 def shards(
@@ -822,18 +964,21 @@
         *dealt_d, dealt_y, keep_two, send_two, norms_two = run_middle(
             counts, (came_x, None), (came_cot, None), *shared, 0, None, groups
         )
-    part_two = reduce_chips(reduce_core(keep_two, send_two))
     came_d = exchange(dealt_d[0], "feat")
+    parts_two = chip_parts(reduce_core(keep_two, send_two))
+    came_d, _ = lax.optimization_barrier((came_d, parts_two))
     if groups == 2:
         dealt_d[1], came_d = lax.optimization_barrier((dealt_d[1], came_d))
         came_last = exchange(dealt_d[1], "feat")
         held = run_sample_backward(
             counts, came_both, came_d, saved, weights, norm_params, chips, 0, None, False
         )
-        came_d, held = lax.optimization_barrier((came_last, held))
+        kept, *parts_two = parts_two
+        came_d, held, kept = lax.optimization_barrier((came_last, held, kept))
+        parts_two = (kept, *parts_two)
     else:
         held = None
-    part_two, came_d = lax.optimization_barrier((part_two, came_d))
+    part_two, came_d = lax.optimization_barrier((reduce_chips(parts_two), came_d))
     share_two = reduce_feat(part_two)
     input_grad, keep_one, send_one, norms_one = run_sample_backward(
         counts,
@@ -850,20 +995,20 @@
     share_two, input_grad, keep_one, send_one, norms_one = lax.optimization_barrier(
         (share_two, input_grad, keep_one, send_one, norms_one)
     )
-    share_one = reduce_feat(reduce_chips(reduce_core(keep_one, send_one)))
-    came_y = exchange(dealt_y, "feat")
-    if late:
-        came_y = jnp.concatenate([came_both[:, 1], came_y], axis=1)
-    block_out = came_y.transpose(2, 1, 0, 3, 4).reshape(1, local, samples, width)
-
+    share_one = reduce_feat(reduce_chips(chip_parts(reduce_core(keep_one, send_one))))
     share_in_turned = share_two[:own_ff]
     share_out = share_two[own_ff : 2 * own_ff]
-    share_attn = to_owners(share_one, share_two[2 * own_ff :])
+    share_one, dealt_y = lax.optimization_barrier((share_one, dealt_y))
+    came_y = exchange(dealt_y, "feat")
     local_squares = jnp.sum(share_one * share_one) + jnp.sum(share_two * share_two)
     small = jnp.concatenate(
         [norms_one, norms_two, jnp.full((2, width), local_squares, F32)], axis=0
     )
-    small = total_of(small)
+    small, part_one, part_two = lax.optimization_barrier(
+        (small, share_one, share_two[2 * own_ff :])
+    )
+    share_attn = to_owners(part_one, part_two)
+    small, share_attn, came_y = lax.optimization_barrier((total_of(small), share_attn, came_y))
     total_norms = small[:6]
     squares = small[6, 0] + jnp.sum(total_norms * total_norms)
     grad_norm = jnp.sqrt(squares)
@@ -880,13 +1025,11 @@
     new_norms, moment_norms, square_norms = adam_step(
         norm_params, factor * total_norms, first_norms, second_norms, NORM_RATE
     )
-    own = jnp.concatenate(
-        [new_attn.astype(BF), new_in.astype(BF).T, new_out.astype(BF)], axis=0
-    )
-    copies = lax.all_gather(own, ("task", "feat"), axis=0, tiled=False)
-    copy_attn = copies[:, :own_attn].reshape(-1, width)
-    copy_in = copies[:, own_attn : own_attn + own_ff].reshape(-1, width).T
-    copy_out = copies[:, own_attn + own_ff :].reshape(-1, width)
+    own_both = jnp.concatenate([new_in.astype(BF).T, new_out.astype(BF)], axis=0)
+    nears, fars = gather_layers(new_attn.astype(BF), own_both)
+    came_halves = [came_y] if came_both is None else [came_both, came_y]
+    copy_attn, copy_in, copy_out, block_out = gather_rest(nears, fars, came_halves)
+    block_out = block_out.reshape(1, local, samples, width)
     return (
         block_out,
         input_grad[None],

time: 477 us -> 423 us (0.89)
  waiting for transfers between devices: 159 us -> 87.1 us
  starting transfers between devices: 44.1 us -> 61.9 us
  blocking collectives: 31.4 us -> 48.8 us
  between operations: 19.8 us -> 6.44 us
  local copies, waits for them, and re-layouts: 20 us -> 9.88 us
  Pallas kernels: 180 us -> 189 us
    all_to_all x9 -> x7, waiting for transfers between devices: 83.6 us -> 20.8 us  [exchange(): lax.all_to_all(values, axis, 0, 0, axis_index_groups=groups, tiled=True)]
    all_gather x1 -> x0, waiting for transfers between devices: 45.4 us -> none  [shards(): copies = lax.all_gather(own, ('task', 'feat'), axis=0, tiled=False)]
    ppermute x5 -> x24, waiting for transfers between devices: 30.4 us -> 66.3 us  [moved_by(): return lax.ppermute(values, axis, pairs)]
    ppermute x5 -> x24, starting transfers between devices: 1.3 us -> 27.2 us  [moved_by(): return lax.ppermute(values, axis, pairs)]
    all_to_all x1 -> x2, blocking collectives: 31.4 us -> 48.8 us  [exchange(): lax.all_to_all(values, axis, 0, 0, axis_index_groups=groups, tiled=True)]
    pallas_call x0 -> x1, Pallas kernels: none -> 8.43 us  [gather_rest(): pl.pallas_call(functools.partial(place_copies, chips, layers), grid_spec=...]
    all_to_all x9 -> x7, starting transfers between devices: 42.8 us -> 34.7 us  [exchange(): lax.all_to_all(values, axis, 0, 0, axis_index_groups=groups, tiled=True)]
    slice x2 -> x1, local copies, waits for them, and re-layouts: 6.63 us -> 0.01 us  [shards(): share_two[2 * own_ff:]]
  transfers between devices with their start and end apart: 15 -> 31, of which waited for: 10 -> 16; matrix products, arithmetic and copies ran while one was open for 3% -> 4% of each run, Pallas kernels for 38% -> 43%
where the time goes in v4:
time: 423 us; the launch traced here: 417 us
  Pallas kernels  189 us (45%)
  waiting for transfers between devices  87.1 us (21%)
  starting transfers between devices  61.9 us (15%)
  blocking collectives  48.8 us (12%)
  other arithmetic  14.7 us (3%)
  local copies, waits for them, and re-layouts  9.88 us (2%)
  between operations  6.44 us (2%)
    pallas_call x5, Pallas kernels, call(): pl.pallas_call(body, grid=(grid,), in_specs=[pl.BlockSpec(memory_space=pl...  180 us
    ppermute x24, waiting for transfers between devices, moved_by(): return lax.ppermute(values, axis, pairs)  66.3 us
    all_to_all x2, blocking collectives, exchange(): lax.all_to_all(values, axis, 0, 0, axis_index_groups=groups, tiled=True)  48.8 us
    all_to_all x7, starting transfers between devices, exchange(): lax.all_to_all(values, axis, 0, 0, axis_index_groups=groups, tiled=True)  34.7 us
    ppermute x24, starting transfers between devices, moved_by(): return lax.ppermute(values, axis, pairs)  27.2 us
    all_to_all x7, waiting for transfers between devices, exchange(): lax.all_to_all(values, axis, 0, 0, axis_index_groups=groups, tiled=True)  20.8 us
  transfers between devices with their start and end apart: 31, of which 16 were waited for; matrix products, arithmetic and copies ran while one was open for 4% of the time, Pallas kernels for 43%

profile of v4, /device:TPU:0, one launch (start us, length us, event | category | flops | bytes accessed | tf_op | source)
XLA Modules:
  0.0 417.4 jit_solution(15239048346448674000)
XLA Ops:
  0.7 1.2 slice-done
  1.9 1.1 copy.40
  2.9 7.3 %all-to-all-start = ((bf16[8,2,4,16,512]{4,3,2,1,0:T(8,128)(2,1)}), bf16[8,2,4,16,512]{4,3,2,1,0:T(8,128)(2,1)S(1)}, u32[]{:S(2)}, u32[]{:S(2)}) async-start(bf16[8,2,4,16,512]{4,3,2,1,0:T(8,128)(2,1)} %bitcast.49), calls=%async_computation | async-start | bytes 2097152 | tf_op jit(solution)/shard_map/all_to_all | solution.py:698
  11.5 0.6 stack.62.counts
  12.1 25.1 %sample_forward.1 = (bf16[8,2,4,16,512]{4,3,2,1,0:T(8,128)(2,1)}, bf16[8,2,2,4,16,512]{5,4,3,2,1,0:T(8,128)(2,1)}, bf16[4,512,512]{2,1,0:T(8,128)(2,1)}, bf16[4,...) custom-call(s32[5]{0:T(128)} %stack.62.counts, bf16[4,512,512]{2,1,0:T(8,128)(2,1)} %bitcast.65, ...), custom_call_target="tpu_custom_call" | custom-call | flops 28750000128 | bytes 16777216 | tf_op jit(solution)/shard_map/sample_forward/pallas_call | solution.py:473
  37.3 31.4 %all_to_all.45.refs_0_ = bf16[8,2,4,16,512]{4,3,2,1,0:T(8,128)(2,1)} all-to-all(bf16[8,2,4,16,512]{4,3,2,1,0:T(8,128)(2,1)} %get-tuple-element.92), channel_id=1, replica_groups=mesh['task'=4,'feat'=8] {'feat'}, dimensions={0} | all-to-all | bytes 2097152 | tf_op jit(solution)/shard_map/all_to_all | solution.py:698
  68.6 3.6 all-to-all-start.3
  72.2 53.3 %middle.2 = (bf16[8,2,2,4,16,512]{5,4,3,2,1,0:T(8,128)(2,1)}, f32[2048,512]{1,0:T(8,128)}, f32[2048,512]{1,0:T(8,128)}, f32[2048,512]{1,0:T(8,128)}, f32[4,512]{1,0:T(4,128)}) custom-call(s32[5]{0:T(128)} %stack.62.counts, bf16[8,2,4,16,512]{4,3,2,1,0:T(8,128)(2,1)} %all_to_all.45.refs_0_, bf16[8,2,4,16,512]{4,3,2,1,0:T(8,128)(2,1)} %copy-done.5, ...), custom_call_target="tpu_custom_call" | custom-call | flops 52899999744 | bytes 16777216 | tf_op jit(solution)/shard_map/middle/pallas_call | solution.py:473
  125.6 1.3 copy-done.3
  126.9 5.9 %all-to-all-start.2 = ((bf16[8,2,2,4,16,512]{5,4,3,2,1,0:T(8,128)(2,1)}), bf16[8,2,2,4,16,512]{5,4,3,2,1,0:T(8,128)(2,1)S(1)}, u32[]{:S(2)}, u32[]{:S(2)}) async-start(bf16[8,2,2,4,16,512]{5,4,3,2,1,0:T(8,128)(2,1)} %get-tuple-element.95), calls=%async_computation.2 | async-start | bytes 4194304 | tf_op jit(solution)/shard_map/all_to_all | solution.py:698
  132.9 50.4 %middle.3 = (bf16[8,2,2,16,512]{4,3,2,1,0:T(8,128)(2,1)}, bf16[8,2,2,16,512]{4,3,2,1,0:T(8,128)(2,1)}, bf16[8,2,4,16,512]{4,3,2,1,0:T(8,128)(2,1)}, bf16[2,8,192...) custom-call(s32[5]{0:T(128)} %stack.62.counts, ...), custom_call_target="tpu_custom_call" | custom-call | flops 52899999744 | bytes 16777216 | tf_op jit(solution)/shard_map/middle/pallas_call | solution.py:473
  183.4 6.0 %all-to-all-start.4 = ((bf16[8,2,2,16,512]{4,3,2,1,0:T(8,128)(2,1)}), bf16[8,2,2,16,512]{4,3,2,1,0:T(8,128)(2,1)}, u32[]{:S(2)}, u32[]{:S(2)}) async-start(bf16[8,2,2,16,512]{4,3,2,1,0:T(8,128)(2,1)} %get-tuple-element.108), calls=%async_computation.4 | async-start | bytes 1048576 | tf_op jit(solution)/shard_map/all_to_all | solution.py:698
  189.4 3.9 add_convert_fusion
  193.3 2.0 dynamic-slice_bitcast_fusion.1
  195.3 9.3 %all-to-all-done.4.refs_1_ = bf16[8,2,2,16,512]{4,3,2,1,0:T(8,128)(2,1)} async-done(((bf16[8,2,2,16,512]{4,3,2,1,0:T(8,128)(2,1)}), bf16[8,2,2,16,512]{4,3,2,1,0:T(8,128)(2,1)}, u32[]{:S(2)}, u32[]{:S(2)}) %all-to-all-start.4) | async-done | bytes 524320 | tf_op jit(solution)/shard_map/all_to_all | solution.py:698
  204.6 4.2 all-to-all-start.5
  208.8 25.4 %sample_backward.2 = (bf16[4,512,512]{2,1,0:T(8,128)(2,1)}, f32[2048,512]{1,0:T(8,128)}, f32[2,512]{1,0:T(2,128)}) custom-call(s32[5]{0:T(128)} %stack.62.counts, bf16[8,2,2,4,16,512]{5,4,3,2,1,0:T(8,128)(2,1)} %copy-done, bf16[8,2,2,16,512]{4,3,2,1,0:T(8,128)(2,1)} %all-to-all-done.4.refs_1_, bf16[4,512,512]{2,1,0:T(8,128)(2,1)} %bitcast.66, ...), custom_call_target="tpu_custom_call" | custom-call | flops 25300000768 | bytes 16777216 | tf_op jit(solution)/shard_map/sample_backward/pallas_call | solution.py:473
  234.2 1.7 add_convert_fusion.1
  236.0 3.9 all-to-all-start.6
  239.9 26.0 %sample_backward.3 = (bf16[4,512,512]{2,1,0:T(8,128)(2,1)}, bf16[2,8,64,512]{3,2,1,0:T(8,128)(2,1)}, bf16[2,8,64,512]{3,2,1,0:T(8,128)(2,1)}, f32[2,512]{1,0:T(2,128)}) custom-call(s32[5]{0:T(128)} %stack.62.counts, bf16[8,2,2,4,16,512]{5,4,3,2,1,0:T(8,128)(2,1)} %copy-done, ...), custom_call_target="tpu_custom_call", output_to_operand_aliasing={{0}: (10, {})} | custom-call | flops 25300000768 | bytes 16777216 | tf_op jit(solution)/shard_map/sample_backward/pallas_call | solution.py:473
  265.9 11.5 %all-to-all-done.6 = bf16[8,192,512]{2,1,0:T(8,128)(2,1)S(1)} async-done(((bf16[8,192,512]{2,1,0:T(8,128)(2,1)}), bf16[8,192,512]{2,1,0:T(8,128)(2,1)S(1)}, u32[]{:S(2)}, u32[]{:S(2)}) %all-to-all-start.6) | async-done | bytes 1572896 | tf_op jit(solution)/shard_map/all_to_all | solution.py:698
  277.7 2.9 collective-permute-done.2
  281.0 14.0 %collective-permute-done.3 = bf16[8,64,512]{2,1,0:T(8,128)(2,1)S(1)} collective-permute-done((bf16[8,64,512]{2,1,0:T(8,128)(2,1)S(1)}, bf16[8,64,512]{2,1,0:T(8,128)(2,1)S(1)}, u32[]{:S(2)}, u32[]{:S(2)}) %collective-permute-start.3) | collective-permute-done | bytes 524320 | tf_op jit(solution)/shard_map/ppermute | solution.py:703
  295.1 17.4 %all_to_all.46 = bf16[8,64,512]{2,1,0:T(8,128)(2,1)S(1)} all-to-all(bf16[8,64,512]{2,1,0:T(8,128)(2,1)S(1)} %fusion), channel_id=1, replica_groups=mesh['task'=4,'feat'=8] {'feat'}, dimensions={0} | all-to-all | bytes 1048576 | tf_op jit(solution)/shard_map/all_to_all | solution.py:698
  312.6 3.8 all-to-all-start.8
  316.5 0.7 multiply_reduce_fusion
  317.2 0.6 multiply_reduce_fusion.1
  319.3 0.7 collective-permute-start.9
  320.0 1.2 collective-permute-done.4
  321.1 1.4 collective-permute-start.5
  322.6 2.3 collective-permute-done.5
  324.9 2.0 collective-permute-start.6
  326.9 2.1 collective-permute-done.6
  329.0 2.2 collective-permute-start.7
  331.1 2.1 collective-permute-done.7
  333.3 4.9 %collective-permute-start.8 = (f32[8,512]{1,0:T(8,128)S(1)}, f32[8,512]{1,0:T(8,128)S(1)}, u32[]{:S(2)}, u32[]{:S(2)}) collective-permute-start(f32[8,512]{1,0:T(8,128)S(1)} %add.144), channel_id=1, source_target_pairs={{0,4},{1,5},{2,6},{3,7},{4,0},{5,1},{6,2},{7,3},{8,12},{9,13},{10,... | collective-permute-start | bytes 49160 | tf_op jit(solution)/shard_map/ppermute | solution.py:703
  338.2 4.4 %collective-permute-done.8 = f32[8,512]{1,0:T(8,128)S(1)} collective-permute-done((f32[8,512]{1,0:T(8,128)S(1)}, f32[8,512]{1,0:T(8,128)S(1)}, u32[]{:S(2)}, u32[]{:S(2)}) %collective-permute-start.8) | collective-permute-done | bytes 16416 | tf_op jit(solution)/shard_map/ppermute | solution.py:703
  342.7 0.5 slice.20
  343.2 0.6 multiply_reduce_fusion.2
  345.2 1.0 fusion.17
  346.3 0.7 collective-permute-start.12
  347.0 1.5 collective-permute-start.10
  348.5 0.8 fusion.15
  349.3 1.7 convert_bitcast_fusion
  351.1 2.0 collective-permute-start.17
  353.1 0.9 collective-permute-start.18
  354.0 2.7 collective-permute-start.19
  356.7 0.7 constant_dynamic-update-slice_fusion.4
  357.4 6.8 %collective-permute-done.11 = bf16[128,512]{1,0:T(8,128)(2,1)S(1)} collective-permute-done((bf16[128,512]{1,0:T(8,128)(2,1)S(1)}, bf16[128,512]{1,0:T(8,128)(2,1)S(1)}, u32[]{:S(2)}, u32[]{:S(2)}) %collective-permute-start.11) | collective-permute-done | bytes 131104 | tf_op jit(solution)/shard_map/ppermute | solution.py:703
  364.3 2.5 collective-permute-start.13
  367.1 0.9 collective-permute-start.20
  368.0 0.7 constant_dynamic-update-slice_fusion.3
  368.7 0.7 constant_dynamic-update-slice_fusion.2
  369.3 0.7 constant_dynamic-update-slice_fusion.1
  370.0 7.7 %collective-permute-done.13 = bf16[4,128,512]{2,1,0:T(8,128)(2,1)S(1)} collective-permute-done((bf16[4,128,512]{2,1,0:T(8,128)(2,1)S(1)}, bf16[4,128,512]{2,1,0:T(8,128)(2,1)S(1)}, u32[]{:S(2)}, u32[]{:S(2)}) %collective-permute-start.13) | collective-permute-done | bytes 524320 | tf_op jit(solution)/shard_map/ppermute | solution.py:703
  377.6 1.1 pad_maximum_fusion.refs_0_
  378.8 0.8 collective-permute-start.14
  379.9 0.9 constant_dynamic-update-slice_fusion.refs_4_
  380.8 3.3 collective-permute-start.21
  384.6 17.9 %collective-permute-done.14.refs_1_ = bf16[2,4,128,512]{3,2,1,0:T(8,128)(2,1)} collective-permute-done((bf16[2,4,128,512]{3,2,1,0:T(8,128)(2,1)}, bf16[2,4,128,512]{3,2,1,0:T(8,128)(2,1)}, u32[]{:S(2)}, u32[]{:S(2)}) %collective-permute-start.14) | collective-permute-done | bytes 1048608 | tf_op jit(solution)/shard_map/ppermute | solution.py:703
  402.4 2.2 collective-permute-done.21.refs_5_
  404.7 0.6 multiply_subtract_fusion.3
  405.4 2.2 collective-permute-done.23.refs_7_
  407.6 8.4 %place_copies.1 = (bf16[4096,512]{1,0:T(8,128)(2,1)}, bf16[512,2048]{1,0:T(8,128)(2,1)}, bf16[2048,512]{1,0:T(8,128)(2,1)}, bf16[4,4,8,16,512]{4,3,2,1,0:T(8,128)(2,1)}) custom-call(s32[6]{0:T(128)S(1)} %pad_add_fusion.table, bf16[2,4,128,512]{3,2,1,0:T(8,128)(2,1)} %pad_maximum_fusion.refs_0_, bf16[2,4,128,512]{3,2,1,0:T(8,128)(2,1)} %collective-permute-done.14.refs_1_, ...), custom_call_target="tpu_custom_call" | custom-call | tf_op jit(solution)/shard_map/place_copies/pallas_call | solution.py:855
  (87 shorter events, 2.8 us)
Async XLA Ops:
  0.7 1.2 slice-start
  2.9 34.3 %all-to-all-start = ((bf16[8,2,4,16,512]{4,3,2,1,0:T(8,128)(2,1)}), bf16[8,2,4,16,512]{4,3,2,1,0:T(8,128)(2,1)S(1)}, u32[]{:S(2)}, u32[]{:S(2)}) async-start(bf16[8,2,4,16,512]{4,3,2,1,0:T(8,128)(2,1)} %bitcast.49), calls=%async_computation | async-start | bytes 2097152 | tf_op jit(solution)/shard_map/all_to_all | solution.py:698
  37.3 31.4 %copy-start.5 = (bf16[8,2,4,16,512]{4,3,2,1,0:T(8,128)(2,1)}, bf16[8,2,4,16,512]{4,3,2,1,0:T(8,128)(2,1)S(1)}, u32[]{:S(2)}) copy-start(bf16[8,2,4,16,512]{4,3,2,1,0:T(8,128)(2,1)S(1)} %all-to-all-done.refs_1_) | copy-start | bytes 3145732
  68.6 57.0 %all-to-all-start.3 = ((bf16[8,2,2,4,16,512]{5,4,3,2,1,0:T(8,128)(2,1)}), bf16[8,2,2,4,16,512]{5,4,3,2,1,0:T(8,128)(2,1)S(1)}, u32[]{:S(2)}, u32[]{:S(2)}) async-start(bf16[8,2,2,4,16,512]{5,4,3,2,1,0:T(8,128)(2,1)} %get-tuple-element.96), calls=%async_computation.3 | async-start | bytes 4194304 | tf_op jit(solution)/shard_map/all_to_all | solution.py:698
  125.6 1.3 copy-start.3
  126.9 56.3 %all-to-all-start.2 = ((bf16[8,2,2,4,16,512]{5,4,3,2,1,0:T(8,128)(2,1)}), bf16[8,2,2,4,16,512]{5,4,3,2,1,0:T(8,128)(2,1)S(1)}, u32[]{:S(2)}, u32[]{:S(2)}) async-start(bf16[8,2,2,4,16,512]{5,4,3,2,1,0:T(8,128)(2,1)} %get-tuple-element.95), calls=%async_computation.2 | async-start | bytes 4194304 | tf_op jit(solution)/shard_map/all_to_all | solution.py:698
  183.3 10.0 %copy-start = (bf16[8,2,2,4,16,512]{5,4,3,2,1,0:T(8,128)(2,1)}, bf16[8,2,2,4,16,512]{5,4,3,2,1,0:T(8,128)(2,1)S(1)}, u32[]{:S(2)}) copy-start(bf16[8,2,2,4,16,512]{5,4,3,2,1,0:T(8,128)(2,1)S(1)} %all-to-all-done.2.refs_0_.refs_8_) | copy-start | bytes 6291460
  183.3 6.1 %collective-permute-start = (bf16[2,8,192,512]{3,2,1,0:T(8,128)(2,1)}, bf16[2,8,192,512]{3,2,1,0:T(8,128)(2,1)}, u32[]{:S(2)}, u32[]{:S(2)}) collective-permute-start(bf16[2,8,192,512]{3,2,1,0:T(8,128)(2,1)} %get-tuple-element.110), channel_id=1, source_target_pairs={{0,8},{8,0},{16,24},{24,16},{1,9},{9,1},{17,25},{25,17},{2,10},{10... | collective-permute-start | bytes 9437192 | tf_op jit(solution)/shard_map/ppermute | solution.py:703
  183.4 21.3 %all-to-all-start.4 = ((bf16[8,2,2,16,512]{4,3,2,1,0:T(8,128)(2,1)}), bf16[8,2,2,16,512]{4,3,2,1,0:T(8,128)(2,1)}, u32[]{:S(2)}, u32[]{:S(2)}) async-start(bf16[8,2,2,16,512]{4,3,2,1,0:T(8,128)(2,1)} %get-tuple-element.108), calls=%async_computation.4 | async-start | bytes 1048576 | tf_op jit(solution)/shard_map/all_to_all | solution.py:698
  195.3 38.9 %collective-permute-start.1 = (bf16[8,192,512]{2,1,0:T(8,128)(2,1)}, bf16[8,192,512]{2,1,0:T(8,128)(2,1)S(1)}, u32[]{:S(2)}, u32[]{:S(2)}) collective-permute-start(bf16[8,192,512]{2,1,0:T(8,128)(2,1)} %get-tuple-element.168), channel_id=1, source_target_pairs={{0,16},{8,24},{16,0},{24,8},{1,17},{9,25},{17,1},{25,9},{2,18},{10... | collective-permute-start | bytes 4718600 | tf_op jit(solution)/shard_map/ppermute | solution.py:703
  204.6 29.6 %all-to-all-start.5 = ((bf16[8,2,2,16,512]{4,3,2,1,0:T(8,128)(2,1)}), bf16[8,2,2,16,512]{4,3,2,1,0:T(8,128)(2,1)}, u32[]{:S(2)}, u32[]{:S(2)}) async-start(bf16[8,2,2,16,512]{4,3,2,1,0:T(8,128)(2,1)} %get-tuple-element.112), calls=%async_computation.5 | async-start | bytes 1048576 | tf_op jit(solution)/shard_map/all_to_all | solution.py:698
  208.8 25.5 %copy-start.2 = (bf16[8,192,512]{2,1,0:T(8,128)(2,1)S(1)}, bf16[8,192,512]{2,1,0:T(8,128)(2,1)}, u32[]{:S(2)}) copy-start(bf16[8,192,512]{2,1,0:T(8,128)(2,1)} %get-tuple-element.122) | copy-start | bytes 4718596
  236.0 41.4 %all-to-all-start.6 = ((bf16[8,192,512]{2,1,0:T(8,128)(2,1)}), bf16[8,192,512]{2,1,0:T(8,128)(2,1)S(1)}, u32[]{:S(2)}, u32[]{:S(2)}) async-start(bf16[8,192,512]{2,1,0:T(8,128)(2,1)} %add_convert_fusion.1), calls=%async_computation.6 | async-start | bytes 3145728 | tf_op jit(solution)/shard_map/all_to_all | solution.py:698
  265.9 14.7 %copy-start.4 = (bf16[2,8,64,512]{3,2,1,0:T(8,128)(2,1)S(1)}, bf16[2,8,64,512]{3,2,1,0:T(8,128)(2,1)}, u32[]{:S(2)}) copy-start(bf16[2,8,64,512]{3,2,1,0:T(8,128)(2,1)} %get-tuple-element.135) | copy-start | bytes 3145732
  277.6 2.9 collective-permute-start.2
  280.9 14.0 %collective-permute-start.3 = (bf16[8,64,512]{2,1,0:T(8,128)(2,1)S(1)}, bf16[8,64,512]{2,1,0:T(8,128)(2,1)S(1)}, u32[]{:S(2)}, u32[]{:S(2)}) collective-permute-start(bf16[8,64,512]{2,1,0:T(8,128)(2,1)S(1)} %dynamic-slice_bitcast_fusion.2), channel_id=1, source_target_pairs={{0,16},{8,24},{16,0},{24,8},{1,17},{9,25},{17,1},{25,9},{2,18},{10... | collective-permute-start | bytes 1572872 | tf_op jit(solution)/shard_map/ppermute | solution.py:703
  295.1 24.1 %copy-start.17 = (f32[4,512]{1,0:T(4,128)S(1)}, f32[4,512]{1,0:T(4,128)}, u32[]{:S(2)}) copy-start(f32[4,512]{1,0:T(4,128)} %get-tuple-element.134) | copy-start | bytes 24580
  295.1 24.1 %copy-start.18 = (f32[2,512]{1,0:T(2,128)S(1)}, f32[2,512]{1,0:T(2,128)}, u32[]{:S(2)}) copy-start(f32[2,512]{1,0:T(2,128)} %get-tuple-element.133) | copy-start | bytes 12292
  312.6 32.6 %copy-start.6 = (f32[128,512]{1,0:T(8,128)S(1)}, f32[128,512]{1,0:T(8,128)}, u32[]{:S(2)}) copy-start(f32[128,512]{1,0:T(8,128)} %param.25) | copy-start | bytes 786436
  312.6 32.6 %copy-start.7 = (f32[128,512]{1,0:T(8,128)S(1)}, f32[128,512]{1,0:T(8,128)}, u32[]{:S(2)}) copy-start(f32[128,512]{1,0:T(8,128)} %param.28) | copy-start | bytes 786436
  312.6 32.6 %copy-start.8 = (f32[128,512]{1,0:T(8,128)S(1)}, f32[128,512]{1,0:T(8,128)}, u32[]{:S(2)}) copy-start(f32[128,512]{1,0:T(8,128)} %param.32) | copy-start | bytes 786436
  312.6 30.1 %all-to-all-start.8 = ((bf16[8,2,4,16,512]{4,3,2,1,0:T(8,128)(2,1)}), bf16[8,2,4,16,512]{4,3,2,1,0:T(8,128)(2,1)S(1)}, u32[]{:S(2)}, u32[]{:S(2)}) async-start(bf16[8,2,4,16,512]{4,3,2,1,0:T(8,128)(2,1)} %get-tuple-element.143), calls=%async_computation.8 | async-start | bytes 2097152 | tf_op jit(solution)/shard_map/all_to_all | solution.py:698
  316.4 32.1 %copy-start.9 = (f32[64,512]{1,0:T(8,128)S(1)}, f32[64,512]{1,0:T(8,128)}, u32[]{:S(2)}) copy-start(f32[64,512]{1,0:T(8,128)} %param.27) | copy-start | bytes 393220
  316.4 32.1 %copy-start.10 = (f32[64,512]{1,0:T(8,128)S(1)}, f32[64,512]{1,0:T(8,128)}, u32[]{:S(2)}) copy-start(f32[64,512]{1,0:T(8,128)} %param.30) | copy-start | bytes 393220
  316.5 32.1 %copy-start.11 = (f32[64,512]{1,0:T(8,128)S(1)}, f32[64,512]{1,0:T(8,128)}, u32[]{:S(2)}) copy-start(f32[64,512]{1,0:T(8,128)} %param.34) | copy-start | bytes 393220
  319.3 23.3 %collective-permute-start.9 = (f32[64,512]{1,0:T(8,128)S(1)}, f32[64,512]{1,0:T(8,128)S(1)}, u32[]{:S(2)}, u32[]{:S(2)}) collective-permute-start(f32[64,512]{1,0:T(8,128)S(1)} %broadcast_select_fusion), channel_id=1, source_target_pairs={{0,16},{8,24},{16,0},{24,8},{1,17},{9,25},{17,1},{25,9},{2,18},{10... | collective-permute-start | bytes 393224 | tf_op jit(solution)/shard_map/ppermute | solution.py:703
  320.0 1.2 collective-permute-start.4
  321.1 3.7 collective-permute-start.5
  324.9 4.1 collective-permute-start.6
  329.0 4.3 %collective-permute-start.7 = (f32[8,512]{1,0:T(8,128)S(1)}, f32[8,512]{1,0:T(8,128)S(1)}, u32[]{:S(2)}, u32[]{:S(2)}) collective-permute-start(f32[8,512]{1,0:T(8,128)S(1)} %add.143), channel_id=1, source_target_pairs={{0,2},{1,3},{2,0},{3,1},{4,6},{5,7},{6,4},{7,5},{8,10},{9,11},{10,... | collective-permute-start | bytes 49160 | tf_op jit(solution)/shard_map/ppermute | solution.py:703
  333.3 9.3 %collective-permute-start.8 = (f32[8,512]{1,0:T(8,128)S(1)}, f32[8,512]{1,0:T(8,128)S(1)}, u32[]{:S(2)}, u32[]{:S(2)}) collective-permute-start(f32[8,512]{1,0:T(8,128)S(1)} %add.144), channel_id=1, source_target_pairs={{0,4},{1,5},{2,6},{3,7},{4,0},{5,1},{6,2},{7,3},{8,12},{9,13},{10,... | collective-permute-start | bytes 49160 | tf_op jit(solution)/shard_map/ppermute | solution.py:703
  338.2 11.1 %copy-start.12 = (f32[512,64]{0,1:T(8,128)S(1)}, f32[512,64]{0,1:T(8,128)}, u32[]{:S(2)}) copy-start(f32[512,64]{0,1:T(8,128)} %param.26) | copy-start | bytes 393220
  338.2 11.1 %copy-start.13 = (f32[512,64]{0,1:T(8,128)S(1)}, f32[512,64]{0,1:T(8,128)}, u32[]{:S(2)}) copy-start(f32[512,64]{0,1:T(8,128)} %param.29) | copy-start | bytes 393220
  346.3 7.7 %collective-permute-start.12 = (bf16[128,512]{1,0:T(8,128)(2,1)S(1)}, bf16[128,512]{1,0:T(8,128)(2,1)S(1)}, u32[]{:S(2)}, u32[]{:S(2)}) collective-permute-start(bf16[128,512]{1,0:T(8,128)(2,1)S(1)} %get-tuple-element.163), channel_id=1, source_target_pairs={{0,6},{1,7},{2,0},{3,1},{4,2},{5,3},{6,4},{7,5},{8,14},{9,15},{10,... | collective-permute-start | bytes 393224 | tf_op jit(solution)/shard_map/ppermute | solution.py:703
  347.0 17.2 %collective-permute-start.11 = (bf16[128,512]{1,0:T(8,128)(2,1)S(1)}, bf16[128,512]{1,0:T(8,128)(2,1)S(1)}, u32[]{:S(2)}, u32[]{:S(2)}) collective-permute-start(bf16[128,512]{1,0:T(8,128)(2,1)S(1)} %get-tuple-element.163), channel_id=1, source_target_pairs={{0,4},{1,5},{2,6},{3,7},{4,0},{5,1},{6,2},{7,3},{8,12},{9,13},{10,... | collective-permute-start | bytes 393224 | tf_op jit(solution)/shard_map/ppermute | solution.py:703
  347.0 17.2 %collective-permute-start.10 = (bf16[128,512]{1,0:T(8,128)(2,1)S(1)}, bf16[128,512]{1,0:T(8,128)(2,1)S(1)}, u32[]{:S(2)}, u32[]{:S(2)}) collective-permute-start(bf16[128,512]{1,0:T(8,128)(2,1)S(1)} %get-tuple-element.163), channel_id=1, source_target_pairs={{0,2},{1,3},{2,4},{3,5},{4,6},{5,7},{6,0},{7,1},{8,10},{9,11},{10,... | collective-permute-start | bytes 393224 | tf_op jit(solution)/shard_map/ppermute | solution.py:703
  351.1 15.7 %collective-permute-start.17 = (bf16[128,512]{1,0:T(8,128)(2,1)S(1)}, bf16[128,512]{1,0:T(8,128)(2,1)S(1)}, u32[]{:S(2)}, u32[]{:S(2)}) collective-permute-start(bf16[128,512]{1,0:T(8,128)(2,1)S(1)} %get-tuple-element.174), channel_id=1, source_target_pairs={{0,2},{1,3},{2,4},{3,5},{4,6},{5,7},{6,0},{7,1},{8,10},{9,11},{10,... | collective-permute-start | bytes 393224 | tf_op jit(solution)/shard_map/ppermute | solution.py:703
  353.1 13.9 %collective-permute-start.18 = (bf16[128,512]{1,0:T(8,128)(2,1)S(1)}, bf16[128,512]{1,0:T(8,128)(2,1)S(1)}, u32[]{:S(2)}, u32[]{:S(2)}) collective-permute-start(bf16[128,512]{1,0:T(8,128)(2,1)S(1)} %get-tuple-element.174), channel_id=1, source_target_pairs={{0,4},{1,5},{2,6},{3,7},{4,0},{5,1},{6,2},{7,3},{8,12},{9,13},{10,... | collective-permute-start | bytes 393224 | tf_op jit(solution)/shard_map/ppermute | solution.py:703
  354.0 13.0 %collective-permute-start.19 = (bf16[128,512]{1,0:T(8,128)(2,1)S(1)}, bf16[128,512]{1,0:T(8,128)(2,1)S(1)}, u32[]{:S(2)}, u32[]{:S(2)}) collective-permute-start(bf16[128,512]{1,0:T(8,128)(2,1)S(1)} %get-tuple-element.174), channel_id=1, source_target_pairs={{0,6},{1,7},{2,0},{3,1},{4,2},{5,3},{6,4},{7,5},{8,14},{9,15},{10,... | collective-permute-start | bytes 393224 | tf_op jit(solution)/shard_map/ppermute | solution.py:703
  364.3 13.4 %collective-permute-start.13 = (bf16[4,128,512]{2,1,0:T(8,128)(2,1)S(1)}, bf16[4,128,512]{2,1,0:T(8,128)(2,1)S(1)}, u32[]{:S(2)}, u32[]{:S(2)}) collective-permute-start(bf16[4,128,512]{2,1,0:T(8,128)(2,1)S(1)} %get-tuple-element.170), channel_id=1, source_target_pairs={{0,1},{1,0},{2,3},{3,2},{4,5},{5,4},{6,7},{7,6},{8,9},{9,8},{10,11... | collective-permute-start | bytes 1572872 | tf_op jit(solution)/shard_map/ppermute | solution.py:703
  367.1 37.7 %copy-start.14 = (f32[6,512]{1,0:T(8,128)S(1)}, f32[6,512]{1,0:T(8,128)}, u32[]{:S(2)}) copy-start(f32[6,512]{1,0:T(8,128)} %refs_8_.3) | copy-start | bytes 36868
  367.1 37.7 %copy-start.15 = (f32[6,512]{1,0:T(8,128)S(1)}, f32[6,512]{1,0:T(8,128)}, u32[]{:S(2)}) copy-start(f32[6,512]{1,0:T(8,128)} %param.31) | copy-start | bytes 36868
  367.1 37.6 %copy-start.16 = (f32[6,512]{1,0:T(8,128)S(1)}, f32[6,512]{1,0:T(8,128)}, u32[]{:S(2)}) copy-start(f32[6,512]{1,0:T(8,128)} %param.35) | copy-start | bytes 36868
  367.1 40.5 %copy-start.1 = (bf16[8,2,2,4,16,512]{5,4,3,2,1,0:T(8,128)(2,1)S(1)}, bf16[8,2,2,4,16,512]{5,4,3,2,1,0:T(8,128)(2,1)}, u32[]{:S(2)}) copy-start(bf16[8,2,2,4,16,512]{5,4,3,2,1,0:T(8,128)(2,1)} %copy-done) | copy-start | bytes 6291460
  367.1 12.8 %collective-permute-start.20 = (bf16[4,128,512]{2,1,0:T(8,128)(2,1)S(1)}, bf16[4,128,512]{2,1,0:T(8,128)(2,1)S(1)}, u32[]{:S(2)}, u32[]{:S(2)}) collective-permute-start(bf16[4,128,512]{2,1,0:T(8,128)(2,1)S(1)} %pad_maximum_fusion.2), channel_id=1, source_target_pairs={{0,16},{8,24},{16,0},{24,8},{1,17},{9,25},{17,1},{25,9},{2,18},{10... | collective-permute-start | bytes 1572872 | tf_op jit(solution)/shard_map/ppermute | solution.py:703
  378.8 23.7 %collective-permute-start.14 = (bf16[2,4,128,512]{3,2,1,0:T(8,128)(2,1)}, bf16[2,4,128,512]{3,2,1,0:T(8,128)(2,1)}, u32[]{:S(2)}, u32[]{:S(2)}) collective-permute-start(bf16[2,4,128,512]{3,2,1,0:T(8,128)(2,1)} %pad_maximum_fusion.refs_0_), channel_id=1, source_target_pairs={{0,16},{8,24},{16,0},{24,8},{1,17},{9,25},{17,1},{25,9},{2,18},{10... | collective-permute-start | bytes 3145736 | tf_op jit(solution)/shard_map/ppermute | solution.py:703
  380.8 23.9 %collective-permute-start.21 = (bf16[8,128,512]{2,1,0:T(8,128)(2,1)}, bf16[8,128,512]{2,1,0:T(8,128)(2,1)}, u32[]{:S(2)}, u32[]{:S(2)}) collective-permute-start(bf16[8,128,512]{2,1,0:T(8,128)(2,1)} %constant_dynamic-update-slice_fusion.refs_4_), channel_id=1, source_target_pairs={{0,1},{1,0},{2,3},{3,2},{4,5},{5,4},{6,7},{7,6},{8,9},{9,8},{10,11... | collective-permute-start | bytes 3145736 | tf_op jit(solution)/shard_map/ppermute | solution.py:703
  384.1 21.3 %collective-permute-start.15 = (bf16[2,4,128,512]{3,2,1,0:T(8,128)(2,1)}, bf16[2,4,128,512]{3,2,1,0:T(8,128)(2,1)}, u32[]{:S(2)}, u32[]{:S(2)}) collective-permute-start(bf16[2,4,128,512]{3,2,1,0:T(8,128)(2,1)} %pad_maximum_fusion.refs_0_), channel_id=1, source_target_pairs={{0,8},{8,0},{16,24},{24,16},{1,9},{9,1},{17,25},{25,17},{2,10},{10... | collective-permute-start | bytes 3145736 | tf_op jit(solution)/shard_map/ppermute | solution.py:703
  384.1 21.3 %collective-permute-start.22 = (bf16[8,128,512]{2,1,0:T(8,128)(2,1)}, bf16[8,128,512]{2,1,0:T(8,128)(2,1)}, u32[]{:S(2)}, u32[]{:S(2)}) collective-permute-start(bf16[8,128,512]{2,1,0:T(8,128)(2,1)} %constant_dynamic-update-slice_fusion.refs_4_), channel_id=1, source_target_pairs={{0,8},{8,0},{16,24},{24,16},{1,9},{9,1},{17,25},{25,17},{2,10},{10... | collective-permute-start | bytes 3145736 | tf_op jit(solution)/shard_map/ppermute | solution.py:703
  402.4 3.0 collective-permute-start.16
  404.6 3.0 collective-permute-start.23

commit v5 on v4

--- a/solution.py
+++ b/solution.py
@@ -726,26 +726,49 @@
     return (keep.astype(F32) + came.astype(F32)).astype(BF)
 
 
-def chip_parts(values):
-    if values.shape[0] != 2:
-        return (values,)
-    chip = lax.axis_index("task") // 2
-    return tuple(
-        lax.dynamic_index_in_dim(values, place, 0, keepdims=False) for place in (chip, 1 - chip)
-    )
-
-
-def reduce_chips(parts):
-    if len(parts) == 2:
-        return (parts[0].astype(F32) + along_y(parts[1], 1).astype(F32)).astype(BF)
-    (values,) = parts
-    chips = values.shape[0]
-    groups = [[2 * place + core for place in range(chips)] for core in range(2)]
-    return jnp.sum(exchange(values, "task", groups).astype(F32), axis=0).astype(BF)
-
-
-def reduce_feat(values):
-    return jnp.sum(exchange(values, "feat").astype(F32), axis=0)
+def in_plane(values, up, across):
+    tasks, devices = lax.axis_size("task"), lax.axis_size("feat")
+    pairs = [
+        (task * devices + place, (task + 2 * up) % tasks * devices + (place ^ across))
+        for task in range(tasks)
+        for place in range(devices)
+    ]
+    return lax.ppermute(values, ("task", "feat"), pairs)
+
+
+def plane_parts(values):
+    chips, devices = values.shape[:2]
+    values = values.reshape((chips, devices // 2, 2) + values.shape[2:])
+    chip, side = lax.axis_index("task") // 2, lax.axis_index("feat") % 2
+    parts = []
+    for up in range(chips):
+        part = lax.dynamic_index_in_dim(values, (chip + up) % chips, 0, keepdims=False)
+        for across in range(2):
+            parts.append(lax.dynamic_index_in_dim(part, side ^ across, 1, keepdims=False))
+    return parts
+
+
+def reduce_plane(parts):
+    total = parts[0].astype(F32)
+    for place, part in enumerate(parts[1:], 1):
+        total = total + in_plane(part, place // 2, place % 2).astype(F32)
+    return total.astype(BF)
+
+
+def layer_parts(values):
+    layers = values.shape[0]
+    layer = lax.axis_index("feat") // 2
+    return [
+        lax.dynamic_index_in_dim(values, (layer + shift) % layers, 0, keepdims=False)
+        for shift in range(layers)
+    ]
+
+
+def reduce_layers(parts):
+    total = parts[0].astype(F32)
+    for shift, part in enumerate(parts[1:], 1):
+        total = total + along_z(part, shift).astype(F32)
+    return total
 
 
 def to_owners(one, two):
@@ -965,7 +988,7 @@
             counts, (came_x, None), (came_cot, None), *shared, 0, None, groups
         )
     came_d = exchange(dealt_d[0], "feat")
-    parts_two = chip_parts(reduce_core(keep_two, send_two))
+    parts_two = plane_parts(reduce_core(keep_two, send_two))
     came_d, _ = lax.optimization_barrier((came_d, parts_two))
     if groups == 2:
         dealt_d[1], came_d = lax.optimization_barrier((dealt_d[1], came_d))
@@ -973,13 +996,11 @@
         held = run_sample_backward(
             counts, came_both, came_d, saved, weights, norm_params, chips, 0, None, False
         )
-        kept, *parts_two = parts_two
-        came_d, held, kept = lax.optimization_barrier((came_last, held, kept))
-        parts_two = (kept, *parts_two)
+        came_d, held, parts_two[0] = lax.optimization_barrier((came_last, held, parts_two[0]))
     else:
         held = None
-    part_two, came_d = lax.optimization_barrier((reduce_chips(parts_two), came_d))
-    share_two = reduce_feat(part_two)
+    part_two, came_d = lax.optimization_barrier((reduce_plane(parts_two), came_d))
+    came_two = exchange(part_two, "feat", [list(range(side, devices, 2)) for side in range(2)])
     input_grad, keep_one, send_one, norms_one = run_sample_backward(
         counts,
         came_both,
@@ -992,10 +1013,11 @@
         held,
         True,
     )
-    share_two, input_grad, keep_one, send_one, norms_one = lax.optimization_barrier(
-        (share_two, input_grad, keep_one, send_one, norms_one)
-    )
-    share_one = reduce_feat(reduce_chips(chip_parts(reduce_core(keep_one, send_one))))
+    came_two, input_grad, keep_one, send_one, norms_one = lax.optimization_barrier(
+        (came_two, input_grad, keep_one, send_one, norms_one)
+    )
+    share_two = jnp.sum(came_two.astype(F32), axis=0)
+    share_one = reduce_layers(layer_parts(reduce_plane(plane_parts(reduce_core(keep_one, send_one)))))
     share_in_turned = share_two[:own_ff]
     share_out = share_two[own_ff : 2 * own_ff]
     share_one, dealt_y = lax.optimization_barrier((share_one, dealt_y))

time: 423 us -> 408 us (0.965)
  blocking collectives: 48.8 us -> 31.4 us
  starting transfers between devices: 61.9 us -> 74.2 us
  waiting for transfers between devices: 87.1 us -> 82.5 us
    all_to_all x2 -> x1, blocking collectives: 48.8 us -> 31.4 us  [exchange(): lax.all_to_all(values, axis, 0, 0, axis_index_groups=groups, tiled=True)]
    ppermute x0 -> x6, waiting for transfers between devices: none -> 10.6 us  [in_plane(): return lax.ppermute(values, ('task', 'feat'), pairs)]
    all_to_all x7, waiting for transfers between devices: 20.8 us -> 11.2 us  [exchange(): lax.all_to_all(values, axis, 0, 0, axis_index_groups=groups, tiled=True)]
    ppermute x0 -> x6, starting transfers between devices: none -> 7.03 us  [in_plane(): return lax.ppermute(values, ('task', 'feat'), pairs)]
    ppermute x24 -> x25, waiting for transfers between devices: 66.3 us -> 60.8 us  [moved_by(): return lax.ppermute(values, axis, pairs)]
    ppermute x24 -> x25, starting transfers between devices: 27.2 us -> 31.3 us  [moved_by(): return lax.ppermute(values, axis, pairs)]
  transfers between devices with their start and end apart: 31 -> 38, of which waited for: 16 -> 20; matrix products, arithmetic and copies ran while one was open for 4% -> 3% of each run, Pallas kernels for 43% -> 45%
where the time goes in v5:
time: 408 us; the launch traced here: 401 us
  Pallas kernels  185 us (45%)
  waiting for transfers between devices  82.5 us (20%)
  starting transfers between devices  74.2 us (18%)
  blocking collectives  31.4 us (8%)
  other arithmetic  15.1 us (4%)
  between operations  6.5 us (2%)
  local copies, waits for them, and re-layouts  6.31 us (2%)
    pallas_call x5, Pallas kernels, call(): pl.pallas_call(body, grid=(grid,), in_specs=[pl.BlockSpec(memory_space=pl...  180 us
    ppermute x25, waiting for transfers between devices, moved_by(): return lax.ppermute(values, axis, pairs)  60.8 us
    all_to_all x7, starting transfers between devices, exchange(): lax.all_to_all(values, axis, 0, 0, axis_index_groups=groups, tiled=True)  35.9 us
    all_to_all x1, blocking collectives, exchange(): lax.all_to_all(values, axis, 0, 0, axis_index_groups=groups, tiled=True)  31.4 us
    ppermute x25, starting transfers between devices, moved_by(): return lax.ppermute(values, axis, pairs)  31.3 us
    all_to_all x7, waiting for transfers between devices, exchange(): lax.all_to_all(values, axis, 0, 0, axis_index_groups=groups, tiled=True)  11.2 us
    ppermute x6, waiting for transfers between devices, in_plane(): return lax.ppermute(values, ('task', 'feat'), pairs)  10.6 us
  transfers between devices with their start and end apart: 38, of which 20 were waited for; matrix products, arithmetic and copies ran while one was open for 3% of the time, Pallas kernels for 45%

profile of v5, /device:TPU:0, one launch (start us, length us, event | category | flops | bytes accessed | tf_op | source)
XLA Modules:
  0.0 401.1 jit_solution(3682194573243500473)
XLA Ops:
  0.7 1.2 slice-done
  1.9 1.1 copy.42
  2.9 7.3 %all-to-all-start = ((bf16[8,2,4,16,512]{4,3,2,1,0:T(8,128)(2,1)}), bf16[8,2,4,16,512]{4,3,2,1,0:T(8,128)(2,1)S(1)}, u32[]{:S(2)}, u32[]{:S(2)}) async-start(bf16[8,2,4,16,512]{4,3,2,1,0:T(8,128)(2,1)} %bitcast.71), calls=%async_computation | async-start | bytes 2097152 | tf_op jit(solution)/shard_map/all_to_all | solution.py:698
  12.1 25.1 %sample_forward.1 = (bf16[8,2,4,16,512]{4,3,2,1,0:T(8,128)(2,1)}, bf16[8,2,2,4,16,512]{5,4,3,2,1,0:T(8,128)(2,1)}, bf16[4,512,512]{2,1,0:T(8,128)(2,1)}, bf16[4,...) custom-call(s32[5]{0:T(128)} %stack.62.counts, bf16[4,512,512]{2,1,0:T(8,128)(2,1)} %bitcast.90, ...), custom_call_target="tpu_custom_call" | custom-call | flops 28750000128 | bytes 16777216 | tf_op jit(solution)/shard_map/sample_forward/pallas_call | solution.py:473
  37.3 31.4 %all_to_all.40.refs_0_ = bf16[8,2,4,16,512]{4,3,2,1,0:T(8,128)(2,1)} all-to-all(bf16[8,2,4,16,512]{4,3,2,1,0:T(8,128)(2,1)} %get-tuple-element.92), channel_id=1, replica_groups=mesh['task'=4,'feat'=8] {'feat'}, dimensions={0} | all-to-all | bytes 2097152 | tf_op jit(solution)/shard_map/all_to_all | solution.py:698
  68.6 3.6 all-to-all-start.3
  72.2 53.3 %middle.2 = (bf16[8,2,2,4,16,512]{5,4,3,2,1,0:T(8,128)(2,1)}, f32[2048,512]{1,0:T(8,128)}, f32[2048,512]{1,0:T(8,128)}, f32[2048,512]{1,0:T(8,128)}, f32[4,512]{1,0:T(4,128)}) custom-call(s32[5]{0:T(128)} %stack.62.counts, bf16[8,2,4,16,512]{4,3,2,1,0:T(8,128)(2,1)} %all_to_all.40.refs_0_, bf16[8,2,4,16,512]{4,3,2,1,0:T(8,128)(2,1)} %copy-done.3, ...), custom_call_target="tpu_custom_call" | custom-call | flops 52899999744 | bytes 16777216 | tf_op jit(solution)/shard_map/middle/pallas_call | solution.py:473
  125.6 1.3 copy-done.2
  126.9 5.9 %all-to-all-start.2 = ((bf16[8,2,2,4,16,512]{5,4,3,2,1,0:T(8,128)(2,1)}), bf16[8,2,2,4,16,512]{5,4,3,2,1,0:T(8,128)(2,1)S(1)}, u32[]{:S(2)}, u32[]{:S(2)}) async-start(bf16[8,2,2,4,16,512]{5,4,3,2,1,0:T(8,128)(2,1)} %get-tuple-element.95), calls=%async_computation.2 | async-start | bytes 4194304 | tf_op jit(solution)/shard_map/all_to_all | solution.py:698
  132.9 50.3 %middle.3 = (bf16[8,2,2,16,512]{4,3,2,1,0:T(8,128)(2,1)}, bf16[8,2,2,16,512]{4,3,2,1,0:T(8,128)(2,1)}, bf16[8,2,4,16,512]{4,3,2,1,0:T(8,128)(2,1)}, bf16[2,8,192...) custom-call(s32[5]{0:T(128)} %stack.62.counts, ...), custom_call_target="tpu_custom_call" | custom-call | flops 52899999744 | bytes 16777216 | tf_op jit(solution)/shard_map/middle/pallas_call | solution.py:473
  183.3 6.0 %all-to-all-start.4 = ((bf16[8,2,2,16,512]{4,3,2,1,0:T(8,128)(2,1)}), bf16[8,2,2,16,512]{4,3,2,1,0:T(8,128)(2,1)}, u32[]{:S(2)}, u32[]{:S(2)}) async-start(bf16[8,2,2,16,512]{4,3,2,1,0:T(8,128)(2,1)} %get-tuple-element.108), calls=%async_computation.4 | async-start | bytes 1048576 | tf_op jit(solution)/shard_map/all_to_all | solution.py:698
  189.3 3.9 add_convert_fusion
  193.2 1.3 dynamic-slice_bitcast_fusion.3
  194.5 3.5 collective-permute-start.2
  198.0 6.6 %all-to-all-done.4.refs_1_ = bf16[8,2,2,16,512]{4,3,2,1,0:T(8,128)(2,1)} async-done(((bf16[8,2,2,16,512]{4,3,2,1,0:T(8,128)(2,1)}), bf16[8,2,2,16,512]{4,3,2,1,0:T(8,128)(2,1)}, u32[]{:S(2)}, u32[]{:S(2)}) %all-to-all-start.4) | async-done | bytes 524320 | tf_op jit(solution)/shard_map/all_to_all | solution.py:698
  204.6 4.2 %all-to-all-start.5 = ((bf16[8,2,2,16,512]{4,3,2,1,0:T(8,128)(2,1)}), bf16[8,2,2,16,512]{4,3,2,1,0:T(8,128)(2,1)}, u32[]{:S(2)}, u32[]{:S(2)}) async-start(bf16[8,2,2,16,512]{4,3,2,1,0:T(8,128)(2,1)} %get-tuple-element.112), calls=%async_computation.5 | async-start | bytes 1048576 | tf_op jit(solution)/shard_map/all_to_all | solution.py:698
  208.7 25.3 %sample_backward.2 = (bf16[4,512,512]{2,1,0:T(8,128)(2,1)}, f32[2048,512]{1,0:T(8,128)}, f32[2,512]{1,0:T(2,128)}) custom-call(s32[5]{0:T(128)} %stack.62.counts, bf16[8,2,2,4,16,512]{5,4,3,2,1,0:T(8,128)(2,1)} %copy-done, bf16[8,2,2,16,512]{4,3,2,1,0:T(8,128)(2,1)} %all-to-all-done.4.refs_1_, bf16[4,512,512]{2,1,0:T(8,128)(2,1)} %bitcast.91, ...), custom_call_target="tpu_custom_call" | custom-call | flops 25300000768 | bytes 16777216 | tf_op jit(solution)/shard_map/sample_backward/pallas_call | solution.py:473
  234.1 4.6 %all-to-all-done.5.refs_1_ = bf16[8,2,2,16,512]{4,3,2,1,0:T(8,128)(2,1)} async-done(((bf16[8,2,2,16,512]{4,3,2,1,0:T(8,128)(2,1)}), bf16[8,2,2,16,512]{4,3,2,1,0:T(8,128)(2,1)}, u32[]{:S(2)}, u32[]{:S(2)}) %all-to-all-start.5) | async-done | bytes 524320 | tf_op jit(solution)/shard_map/all_to_all | solution.py:698
  238.7 2.7 add_convert_fusion.2
  241.3 4.8 %all-to-all-start.6 = ((bf16[4,192,512]{2,1,0:T(8,128)(2,1)}), bf16[4,192,512]{2,1,0:T(8,128)(2,1)S(1)}, u32[]{:S(2)}, u32[]{:S(2)}) async-start(bf16[4,192,512]{2,1,0:T(8,128)(2,1)} %add_convert_fusion.2), calls=%async_computation.6 | async-start | bytes 1572864 | tf_op jit(solution)/shard_map/all_to_all | solution.py:698
  246.1 25.9 %sample_backward.3 = (bf16[4,512,512]{2,1,0:T(8,128)(2,1)}, bf16[2,8,64,512]{3,2,1,0:T(8,128)(2,1)}, bf16[2,8,64,512]{3,2,1,0:T(8,128)(2,1)}, f32[2,512]{1,0:T(2,128)}) custom-call(s32[5]{0:T(128)} %stack.62.counts, bf16[8,2,2,4,16,512]{5,4,3,2,1,0:T(8,128)(2,1)} %copy-done, ...), custom_call_target="tpu_custom_call", output_to_operand_aliasing={{0}: (10, {})} | custom-call | flops 25300000768 | bytes 16777216 | tf_op jit(solution)/shard_map/sample_backward/pallas_call | solution.py:473
  272.1 2.9 collective-permute-done.4
  274.9 1.5 add_convert_fusion.1
  276.6 1.9 collective-permute-start.6
  278.6 1.5 collective-permute-start.5
  280.1 6.6 %collective-permute-done.7 = bf16[4,64,512]{2,1,0:T(8,128)(2,1)S(1)} collective-permute-done((bf16[4,64,512]{2,1,0:T(8,128)(2,1)S(1)}, bf16[4,64,512]{2,1,0:T(8,128)(2,1)S(1)}, u32[]{:S(2)}, u32[]{:S(2)}) %collective-permute-start.7) | collective-permute-done | bytes 262176 | tf_op jit(solution)/shard_map/ppermute | solution.py:736
  286.7 3.9 collective-permute-done.6
  290.9 3.1 collective-permute-start.10
  294.0 1.1 collective-permute-start.8
  295.1 1.4 collective-permute-done.10
  296.5 3.8 collective-permute-done.9
  300.4 4.2 %all-to-all-start.7 = ((bf16[8,2,4,16,512]{4,3,2,1,0:T(8,128)(2,1)}), bf16[8,2,4,16,512]{4,3,2,1,0:T(8,128)(2,1)S(1)}, u32[]{:S(2)}, u32[]{:S(2)}) async-start(bf16[8,2,4,16,512]{4,3,2,1,0:T(8,128)(2,1)} %get-tuple-element.143), calls=%async_computation.7 | async-start | bytes 2097152 | tf_op jit(solution)/shard_map/all_to_all | solution.py:698
  304.7 0.7 multiply_reduce_fusion
  307.6 0.9 collective-permute-start.16
  308.4 1.2 collective-permute-done.11
  309.6 1.2 collective-permute-start.12
  310.8 2.5 collective-permute-done.12
  313.4 1.9 collective-permute-start.13
  315.3 2.1 collective-permute-done.13
  317.4 1.9 collective-permute-start.14
  319.3 2.0 collective-permute-done.14
  321.3 5.0 %collective-permute-start.15 = (f32[8,512]{1,0:T(8,128)S(1)}, f32[8,512]{1,0:T(8,128)S(1)}, u32[]{:S(2)}, u32[]{:S(2)}) collective-permute-start(f32[8,512]{1,0:T(8,128)S(1)} %add.287), channel_id=1, source_target_pairs={{0,4},{1,5},{2,6},{3,7},{4,0},{5,1},{6,2},{7,3},{8,12},{9,13},{10,... | collective-permute-start | bytes 49160 | tf_op jit(solution)/shard_map/ppermute | solution.py:703
  326.3 4.4 %collective-permute-done.15 = f32[8,512]{1,0:T(8,128)S(1)} collective-permute-done((f32[8,512]{1,0:T(8,128)S(1)}, f32[8,512]{1,0:T(8,128)S(1)}, u32[]{:S(2)}, u32[]{:S(2)}) %collective-permute-start.15) | collective-permute-done | bytes 16416 | tf_op jit(solution)/shard_map/ppermute | solution.py:703
  333.3 1.0 fusion.20
  334.3 0.7 collective-permute-start.19
  335.0 1.8 collective-permute-start.17
  336.8 0.8 fusion.18
  337.6 1.8 convert_bitcast_fusion
  339.4 2.0 collective-permute-start.24
  341.4 0.9 collective-permute-start.25
  342.3 2.7 collective-permute-start.26
  345.1 7.0 %collective-permute-done.18 = bf16[128,512]{1,0:T(8,128)(2,1)S(1)} collective-permute-done((bf16[128,512]{1,0:T(8,128)(2,1)S(1)}, bf16[128,512]{1,0:T(8,128)(2,1)S(1)}, u32[]{:S(2)}, u32[]{:S(2)}) %collective-permute-start.18) | collective-permute-done | bytes 131104 | tf_op jit(solution)/shard_map/ppermute | solution.py:703
  352.2 2.4 collective-permute-start.20
  355.0 1.1 collective-permute-start.27
  356.2 9.0 %collective-permute-done.20 = bf16[4,128,512]{2,1,0:T(8,128)(2,1)S(1)} collective-permute-done((bf16[4,128,512]{2,1,0:T(8,128)(2,1)S(1)}, bf16[4,128,512]{2,1,0:T(8,128)(2,1)S(1)}, u32[]{:S(2)}, u32[]{:S(2)}) %collective-permute-start.20) | collective-permute-done | bytes 524320 | tf_op jit(solution)/shard_map/ppermute | solution.py:703
  365.3 1.4 collective-permute-start.21
  366.7 3.2 collective-permute-done.27
  370.0 2.4 collective-permute-start.28
  372.9 17.6 %collective-permute-done.21.refs_1_ = bf16[2,4,128,512]{3,2,1,0:T(8,128)(2,1)S(1)} collective-permute-done((bf16[2,4,128,512]{3,2,1,0:T(8,128)(2,1)S(1)}, bf16[2,4,128,512]{3,2,1,0:T(8,128)(2,1)S(1)}, u32[]{:S(2)}, u32[]{:S(2)}) %collective-permute-start.21) | collective-permute-done | bytes 1048608 | tf_op jit(solution)/shard_map/ppermute | solution.py:703
  390.5 0.9 collective-permute-done.28.refs_5_
  391.5 0.6 multiply_subtract_fusion.3
  392.1 1.0 collective-permute-done.23.refs_3_
  393.1 1.5 collective-permute-done.30.refs_7_
  394.6 5.0 %place_copies.1 = (bf16[4096,512]{1,0:T(8,128)(2,1)}, bf16[512,2048]{1,0:T(8,128)(2,1)}, bf16[2048,512]{1,0:T(8,128)(2,1)}, bf16[4,4,8,16,512]{4,3,2,1,0:T(8,128)(2,1)}) custom-call(s32[6]{0:T(128)S(1)} %pad_add_fusion.table, bf16[2,4,128,512]{3,2,1,0:T(8,128)(2,1)S(1)} %pad_maximum_fusion.refs_0_, ...), custom_call_target="tpu_custom_call" | custom-call | tf_op jit(solution)/shard_map/place_copies/pallas_call | solution.py:878
  (95 shorter events, 4.6 us)
Async XLA Ops:
  0.7 1.2 slice-start
  2.9 34.3 %all-to-all-start = ((bf16[8,2,4,16,512]{4,3,2,1,0:T(8,128)(2,1)}), bf16[8,2,4,16,512]{4,3,2,1,0:T(8,128)(2,1)S(1)}, u32[]{:S(2)}, u32[]{:S(2)}) async-start(bf16[8,2,4,16,512]{4,3,2,1,0:T(8,128)(2,1)} %bitcast.71), calls=%async_computation | async-start | bytes 2097152 | tf_op jit(solution)/shard_map/all_to_all | solution.py:698
  37.3 31.4 %copy-start.3 = (bf16[8,2,4,16,512]{4,3,2,1,0:T(8,128)(2,1)}, bf16[8,2,4,16,512]{4,3,2,1,0:T(8,128)(2,1)S(1)}, u32[]{:S(2)}) copy-start(bf16[8,2,4,16,512]{4,3,2,1,0:T(8,128)(2,1)S(1)} %all-to-all-done.refs_1_) | copy-start | bytes 3145732
  68.6 57.0 %all-to-all-start.3 = ((bf16[8,2,2,4,16,512]{5,4,3,2,1,0:T(8,128)(2,1)}), bf16[8,2,2,4,16,512]{5,4,3,2,1,0:T(8,128)(2,1)S(1)}, u32[]{:S(2)}, u32[]{:S(2)}) async-start(bf16[8,2,2,4,16,512]{5,4,3,2,1,0:T(8,128)(2,1)} %get-tuple-element.96), calls=%async_computation.3 | async-start | bytes 4194304 | tf_op jit(solution)/shard_map/all_to_all | solution.py:698
  125.6 1.3 copy-start.2
  126.9 56.3 %all-to-all-start.2 = ((bf16[8,2,2,4,16,512]{5,4,3,2,1,0:T(8,128)(2,1)}), bf16[8,2,2,4,16,512]{5,4,3,2,1,0:T(8,128)(2,1)S(1)}, u32[]{:S(2)}, u32[]{:S(2)}) async-start(bf16[8,2,2,4,16,512]{5,4,3,2,1,0:T(8,128)(2,1)} %get-tuple-element.95), calls=%async_computation.2 | async-start | bytes 4194304 | tf_op jit(solution)/shard_map/all_to_all | solution.py:698
  183.2 10.0 %copy-start = (bf16[8,2,2,4,16,512]{5,4,3,2,1,0:T(8,128)(2,1)}, bf16[8,2,2,4,16,512]{5,4,3,2,1,0:T(8,128)(2,1)S(1)}, u32[]{:S(2)}) copy-start(bf16[8,2,2,4,16,512]{5,4,3,2,1,0:T(8,128)(2,1)S(1)} %all-to-all-done.2.refs_0_.refs_8_) | copy-start | bytes 6291460
  183.2 6.1 %collective-permute-start = (bf16[2,8,192,512]{3,2,1,0:T(8,128)(2,1)}, bf16[2,8,192,512]{3,2,1,0:T(8,128)(2,1)}, u32[]{:S(2)}, u32[]{:S(2)}) collective-permute-start(bf16[2,8,192,512]{3,2,1,0:T(8,128)(2,1)} %get-tuple-element.110), channel_id=1, source_target_pairs={{0,8},{8,0},{16,24},{24,16},{1,9},{9,1},{17,25},{25,17},{2,10},{10... | collective-permute-start | bytes 9437192 | tf_op jit(solution)/shard_map/ppermute | solution.py:703
  183.3 21.3 %all-to-all-start.4 = ((bf16[8,2,2,16,512]{4,3,2,1,0:T(8,128)(2,1)}), bf16[8,2,2,16,512]{4,3,2,1,0:T(8,128)(2,1)}, u32[]{:S(2)}, u32[]{:S(2)}) async-start(bf16[8,2,2,16,512]{4,3,2,1,0:T(8,128)(2,1)} %get-tuple-element.108), calls=%async_computation.4 | async-start | bytes 1048576 | tf_op jit(solution)/shard_map/all_to_all | solution.py:698
  194.5 44.2 %collective-permute-start.3 = (bf16[4,192,512]{2,1,0:T(8,128)(2,1)}, bf16[4,192,512]{2,1,0:T(8,128)(2,1)S(1)}, u32[]{:S(2)}, u32[]{:S(2)}) collective-permute-start(bf16[4,192,512]{2,1,0:T(8,128)(2,1)} %get-tuple-element.168), channel_id=1, source_target_pairs={{0,17},{1,16},{2,19},{3,18},{4,21},{5,20},{6,23},{7,22},{8,25},{9,... | collective-permute-start | bytes 2359304 | tf_op jit(solution)/shard_map/ppermute | solution.py:736
  194.5 44.2 %collective-permute-start.2 = (bf16[4,192,512]{2,1,0:T(8,128)(2,1)S(1)}, bf16[4,192,512]{2,1,0:T(8,128)(2,1)}, u32[]{:S(2)}, u32[]{:S(2)}) collective-permute-start(bf16[4,192,512]{2,1,0:T(8,128)(2,1)S(1)} %get-tuple-element.169), channel_id=1, source_target_pairs={{0,16},{1,17},{2,18},{3,19},{4,20},{5,21},{6,22},{7,23},{8,24},{9,... | collective-permute-start | bytes 2359304 | tf_op jit(solution)/shard_map/ppermute | solution.py:736
  198.0 40.7 %collective-permute-start.1 = (bf16[4,192,512]{2,1,0:T(8,128)(2,1)S(1)}, bf16[4,192,512]{2,1,0:T(8,128)(2,1)}, u32[]{:S(2)}, u32[]{:S(2)}) collective-permute-start(bf16[4,192,512]{2,1,0:T(8,128)(2,1)S(1)} %get-tuple-element.170), channel_id=1, source_target_pairs={{0,1},{1,0},{2,3},{3,2},{4,5},{5,4},{6,7},{7,6},{8,9},{9,8},{10,11... | collective-permute-start | bytes 2359304 | tf_op jit(solution)/shard_map/ppermute | solution.py:736
  204.6 34.1 %all-to-all-start.5 = ((bf16[8,2,2,16,512]{4,3,2,1,0:T(8,128)(2,1)}), bf16[8,2,2,16,512]{4,3,2,1,0:T(8,128)(2,1)}, u32[]{:S(2)}, u32[]{:S(2)}) async-start(bf16[8,2,2,16,512]{4,3,2,1,0:T(8,128)(2,1)} %get-tuple-element.112), calls=%async_computation.5 | async-start | bytes 1048576 | tf_op jit(solution)/shard_map/all_to_all | solution.py:698
  241.3 30.7 %all-to-all-start.6 = ((bf16[4,192,512]{2,1,0:T(8,128)(2,1)}), bf16[4,192,512]{2,1,0:T(8,128)(2,1)S(1)}, u32[]{:S(2)}, u32[]{:S(2)}) async-start(bf16[4,192,512]{2,1,0:T(8,128)(2,1)} %add_convert_fusion.2), calls=%async_computation.6 | async-start | bytes 1572864 | tf_op jit(solution)/shard_map/all_to_all | solution.py:698
  272.0 2.9 collective-permute-start.4
  276.6 10.2 %collective-permute-start.7 = (bf16[4,64,512]{2,1,0:T(8,128)(2,1)S(1)}, bf16[4,64,512]{2,1,0:T(8,128)(2,1)S(1)}, u32[]{:S(2)}, u32[]{:S(2)}) collective-permute-start(bf16[4,64,512]{2,1,0:T(8,128)(2,1)S(1)} %get-tuple-element.172), channel_id=1, source_target_pairs={{0,17},{1,16},{2,19},{3,18},{4,21},{5,20},{6,23},{7,22},{8,25},{9,... | collective-permute-start | bytes 786440 | tf_op jit(solution)/shard_map/ppermute | solution.py:736
  276.6 14.0 %collective-permute-start.6 = (bf16[4,64,512]{2,1,0:T(8,128)(2,1)S(1)}, bf16[4,64,512]{2,1,0:T(8,128)(2,1)S(1)}, u32[]{:S(2)}, u32[]{:S(2)}) collective-permute-start(bf16[4,64,512]{2,1,0:T(8,128)(2,1)S(1)} %get-tuple-element.173), channel_id=1, source_target_pairs={{0,16},{1,17},{2,18},{3,19},{4,20},{5,21},{6,22},{7,23},{8,24},{9,... | collective-permute-start | bytes 786440 | tf_op jit(solution)/shard_map/ppermute | solution.py:736
  278.6 12.1 %collective-permute-start.5 = (bf16[4,64,512]{2,1,0:T(8,128)(2,1)S(1)}, bf16[4,64,512]{2,1,0:T(8,128)(2,1)S(1)}, u32[]{:S(2)}, u32[]{:S(2)}) collective-permute-start(bf16[4,64,512]{2,1,0:T(8,128)(2,1)S(1)} %get-tuple-element.171), channel_id=1, source_target_pairs={{0,1},{1,0},{2,3},{3,2},{4,5},{5,4},{6,7},{7,6},{8,9},{9,8},{10,11... | collective-permute-start | bytes 786440 | tf_op jit(solution)/shard_map/ppermute | solution.py:736
  290.9 5.7 %collective-permute-start.10 = (bf16[64,512]{1,0:T(8,128)(2,1)S(1)}, bf16[64,512]{1,0:T(8,128)(2,1)S(1)}, u32[]{:S(2)}, u32[]{:S(2)}) collective-permute-start(bf16[64,512]{1,0:T(8,128)(2,1)S(1)} %get-tuple-element.179), channel_id=1, source_target_pairs={{0,6},{1,7},{2,0},{3,1},{4,2},{5,3},{6,4},{7,5},{8,14},{9,15},{10,... | collective-permute-start | bytes 196616 | tf_op jit(solution)/shard_map/ppermute | solution.py:703
  294.0 6.3 %collective-permute-start.9 = (bf16[64,512]{1,0:T(8,128)(2,1)S(1)}, bf16[64,512]{1,0:T(8,128)(2,1)S(1)}, u32[]{:S(2)}, u32[]{:S(2)}) collective-permute-start(bf16[64,512]{1,0:T(8,128)(2,1)S(1)} %get-tuple-element.180), channel_id=1, source_target_pairs={{0,4},{1,5},{2,6},{3,7},{4,0},{5,1},{6,2},{7,3},{8,12},{9,13},{10,... | collective-permute-start | bytes 196616 | tf_op jit(solution)/shard_map/ppermute | solution.py:703
  294.0 6.3 %collective-permute-start.8 = (bf16[64,512]{1,0:T(8,128)(2,1)S(1)}, bf16[64,512]{1,0:T(8,128)(2,1)S(1)}, u32[]{:S(2)}, u32[]{:S(2)}) collective-permute-start(bf16[64,512]{1,0:T(8,128)(2,1)S(1)} %get-tuple-element.178), channel_id=1, source_target_pairs={{0,2},{1,3},{2,4},{3,5},{4,6},{5,7},{6,0},{7,1},{8,10},{9,11},{10,... | collective-permute-start | bytes 196616 | tf_op jit(solution)/shard_map/ppermute | solution.py:703
  300.3 7.1 %copy-start.14 = (f32[4,512]{1,0:T(4,128)S(1)}, f32[4,512]{1,0:T(4,128)}, u32[]{:S(2)}) copy-start(f32[4,512]{1,0:T(4,128)} %get-tuple-element.134) | copy-start | bytes 24580
  300.3 7.1 %copy-start.15 = (f32[2,512]{1,0:T(2,128)S(1)}, f32[2,512]{1,0:T(2,128)}, u32[]{:S(2)}) copy-start(f32[2,512]{1,0:T(2,128)} %get-tuple-element.133) | copy-start | bytes 12292
  300.4 30.4 %all-to-all-start.7 = ((bf16[8,2,4,16,512]{4,3,2,1,0:T(8,128)(2,1)}), bf16[8,2,4,16,512]{4,3,2,1,0:T(8,128)(2,1)S(1)}, u32[]{:S(2)}, u32[]{:S(2)}) async-start(bf16[8,2,4,16,512]{4,3,2,1,0:T(8,128)(2,1)} %get-tuple-element.143), calls=%async_computation.7 | async-start | bytes 2097152 | tf_op jit(solution)/shard_map/all_to_all | solution.py:698
  304.5 28.7 %copy-start.4 = (f32[128,512]{1,0:T(8,128)S(1)}, f32[128,512]{1,0:T(8,128)}, u32[]{:S(2)}) copy-start(f32[128,512]{1,0:T(8,128)} %param.25) | copy-start | bytes 786436
  304.5 28.7 %copy-start.5 = (f32[128,512]{1,0:T(8,128)S(1)}, f32[128,512]{1,0:T(8,128)}, u32[]{:S(2)}) copy-start(f32[128,512]{1,0:T(8,128)} %param.28) | copy-start | bytes 786436
  304.6 28.7 %copy-start.6 = (f32[128,512]{1,0:T(8,128)S(1)}, f32[128,512]{1,0:T(8,128)}, u32[]{:S(2)}) copy-start(f32[128,512]{1,0:T(8,128)} %param.32) | copy-start | bytes 786436
  304.7 32.1 %copy-start.7 = (f32[64,512]{1,0:T(8,128)S(1)}, f32[64,512]{1,0:T(8,128)}, u32[]{:S(2)}) copy-start(f32[64,512]{1,0:T(8,128)} %param.27) | copy-start | bytes 393220
  304.7 32.1 %copy-start.8 = (f32[64,512]{1,0:T(8,128)S(1)}, f32[64,512]{1,0:T(8,128)}, u32[]{:S(2)}) copy-start(f32[64,512]{1,0:T(8,128)} %param.30) | copy-start | bytes 393220
  304.7 32.1 %copy-start.9 = (f32[64,512]{1,0:T(8,128)S(1)}, f32[64,512]{1,0:T(8,128)}, u32[]{:S(2)}) copy-start(f32[64,512]{1,0:T(8,128)} %param.34) | copy-start | bytes 393220
  307.6 23.1 %collective-permute-start.16 = (f32[64,512]{1,0:T(8,128)S(1)}, f32[64,512]{1,0:T(8,128)S(1)}, u32[]{:S(2)}, u32[]{:S(2)}) collective-permute-start(f32[64,512]{1,0:T(8,128)S(1)} %broadcast_select_fusion), channel_id=1, source_target_pairs={{0,16},{8,24},{16,0},{24,8},{1,17},{9,25},{17,1},{25,9},{2,18},{10... | collective-permute-start | bytes 393224 | tf_op jit(solution)/shard_map/ppermute | solution.py:703
  308.4 1.2 collective-permute-start.11
  309.6 3.7 collective-permute-start.12
  313.4 4.0 %collective-permute-start.13 = (f32[8,512]{1,0:T(8,128)S(1)}, f32[8,512]{1,0:T(8,128)S(1)}, u32[]{:S(2)}, u32[]{:S(2)}) collective-permute-start(f32[8,512]{1,0:T(8,128)S(1)} %add.285), channel_id=1, source_target_pairs={{0,1},{1,0},{2,3},{3,2},{4,5},{5,4},{6,7},{7,6},{8,9},{9,8},{10,11... | collective-permute-start | bytes 49160 | tf_op jit(solution)/shard_map/ppermute | solution.py:703
  317.4 3.9 collective-permute-start.14
  321.3 9.3 %collective-permute-start.15 = (f32[8,512]{1,0:T(8,128)S(1)}, f32[8,512]{1,0:T(8,128)S(1)}, u32[]{:S(2)}, u32[]{:S(2)}) collective-permute-start(f32[8,512]{1,0:T(8,128)S(1)} %add.287), channel_id=1, source_target_pairs={{0,4},{1,5},{2,6},{3,7},{4,0},{5,1},{6,2},{7,3},{8,12},{9,13},{10,... | collective-permute-start | bytes 49160 | tf_op jit(solution)/shard_map/ppermute | solution.py:703
  326.3 11.3 %copy-start.10 = (f32[512,64]{0,1:T(8,128)S(1)}, f32[512,64]{0,1:T(8,128)}, u32[]{:S(2)}) copy-start(f32[512,64]{0,1:T(8,128)} %param.26) | copy-start | bytes 393220
  334.3 8.0 %collective-permute-start.19 = (bf16[128,512]{1,0:T(8,128)(2,1)S(1)}, bf16[128,512]{1,0:T(8,128)(2,1)S(1)}, u32[]{:S(2)}, u32[]{:S(2)}) collective-permute-start(bf16[128,512]{1,0:T(8,128)(2,1)S(1)} %get-tuple-element.163), channel_id=1, source_target_pairs={{0,6},{1,7},{2,0},{3,1},{4,2},{5,3},{6,4},{7,5},{8,14},{9,15},{10,... | collective-permute-start | bytes 393224 | tf_op jit(solution)/shard_map/ppermute | solution.py:703
  335.0 17.1 %collective-permute-start.18 = (bf16[128,512]{1,0:T(8,128)(2,1)S(1)}, bf16[128,512]{1,0:T(8,128)(2,1)S(1)}, u32[]{:S(2)}, u32[]{:S(2)}) collective-permute-start(bf16[128,512]{1,0:T(8,128)(2,1)S(1)} %get-tuple-element.163), channel_id=1, source_target_pairs={{0,4},{1,5},{2,6},{3,7},{4,0},{5,1},{6,2},{7,3},{8,12},{9,13},{10,... | collective-permute-start | bytes 393224 | tf_op jit(solution)/shard_map/ppermute | solution.py:703
  335.0 17.1 %collective-permute-start.17 = (bf16[128,512]{1,0:T(8,128)(2,1)S(1)}, bf16[128,512]{1,0:T(8,128)(2,1)S(1)}, u32[]{:S(2)}, u32[]{:S(2)}) collective-permute-start(bf16[128,512]{1,0:T(8,128)(2,1)S(1)} %get-tuple-element.163), channel_id=1, source_target_pairs={{0,2},{1,3},{2,4},{3,5},{4,6},{5,7},{6,0},{7,1},{8,10},{9,11},{10,... | collective-permute-start | bytes 393224 | tf_op jit(solution)/shard_map/ppermute | solution.py:703
  339.4 15.2 %collective-permute-start.24 = (bf16[128,512]{1,0:T(8,128)(2,1)S(1)}, bf16[128,512]{1,0:T(8,128)(2,1)S(1)}, u32[]{:S(2)}, u32[]{:S(2)}) collective-permute-start(bf16[128,512]{1,0:T(8,128)(2,1)S(1)} %get-tuple-element.182), channel_id=1, source_target_pairs={{0,2},{1,3},{2,4},{3,5},{4,6},{5,7},{6,0},{7,1},{8,10},{9,11},{10,... | collective-permute-start | bytes 393224 | tf_op jit(solution)/shard_map/ppermute | solution.py:703
  341.4 13.5 %collective-permute-start.25 = (bf16[128,512]{1,0:T(8,128)(2,1)S(1)}, bf16[128,512]{1,0:T(8,128)(2,1)S(1)}, u32[]{:S(2)}, u32[]{:S(2)}) collective-permute-start(bf16[128,512]{1,0:T(8,128)(2,1)S(1)} %get-tuple-element.182), channel_id=1, source_target_pairs={{0,4},{1,5},{2,6},{3,7},{4,0},{5,1},{6,2},{7,3},{8,12},{9,13},{10,... | collective-permute-start | bytes 393224 | tf_op jit(solution)/shard_map/ppermute | solution.py:703
  342.3 12.6 %collective-permute-start.26 = (bf16[128,512]{1,0:T(8,128)(2,1)S(1)}, bf16[128,512]{1,0:T(8,128)(2,1)S(1)}, u32[]{:S(2)}, u32[]{:S(2)}) collective-permute-start(bf16[128,512]{1,0:T(8,128)(2,1)S(1)} %get-tuple-element.182), channel_id=1, source_target_pairs={{0,6},{1,7},{2,0},{3,1},{4,2},{5,3},{6,4},{7,5},{8,14},{9,15},{10,... | collective-permute-start | bytes 393224 | tf_op jit(solution)/shard_map/ppermute | solution.py:703
  352.2 13.0 %collective-permute-start.20 = (bf16[4,128,512]{2,1,0:T(8,128)(2,1)S(1)}, bf16[4,128,512]{2,1,0:T(8,128)(2,1)S(1)}, u32[]{:S(2)}, u32[]{:S(2)}) collective-permute-start(bf16[4,128,512]{2,1,0:T(8,128)(2,1)S(1)} %get-tuple-element.175), channel_id=1, source_target_pairs={{0,1},{1,0},{2,3},{3,2},{4,5},{5,4},{6,7},{7,6},{8,9},{9,8},{10,11... | collective-permute-start | bytes 1572872 | tf_op jit(solution)/shard_map/ppermute | solution.py:703
  355.0 36.5 %copy-start.11 = (f32[6,512]{1,0:T(8,128)S(1)}, f32[6,512]{1,0:T(8,128)}, u32[]{:S(2)}) copy-start(f32[6,512]{1,0:T(8,128)} %refs_8_.3) | copy-start | bytes 36868
  355.0 36.5 %copy-start.12 = (f32[6,512]{1,0:T(8,128)S(1)}, f32[6,512]{1,0:T(8,128)}, u32[]{:S(2)}) copy-start(f32[6,512]{1,0:T(8,128)} %param.31) | copy-start | bytes 36868
  355.0 36.5 %copy-start.13 = (f32[6,512]{1,0:T(8,128)S(1)}, f32[6,512]{1,0:T(8,128)}, u32[]{:S(2)}) copy-start(f32[6,512]{1,0:T(8,128)} %param.35) | copy-start | bytes 36868
  355.0 39.6 %copy-start.1 = (bf16[8,2,2,4,16,512]{5,4,3,2,1,0:T(8,128)(2,1)S(1)}, bf16[8,2,2,4,16,512]{5,4,3,2,1,0:T(8,128)(2,1)}, u32[]{:S(2)}) copy-start(bf16[8,2,2,4,16,512]{5,4,3,2,1,0:T(8,128)(2,1)} %copy-done) | copy-start | bytes 6291460
  355.0 14.9 %collective-permute-start.27 = (bf16[4,128,512]{2,1,0:T(8,128)(2,1)S(1)}, bf16[4,128,512]{2,1,0:T(8,128)(2,1)S(1)}, u32[]{:S(2)}, u32[]{:S(2)}) collective-permute-start(bf16[4,128,512]{2,1,0:T(8,128)(2,1)S(1)} %pad_maximum_fusion.2), channel_id=1, source_target_pairs={{0,16},{8,24},{16,0},{24,8},{1,17},{9,25},{17,1},{25,9},{2,18},{10... | collective-permute-start | bytes 1572872 | tf_op jit(solution)/shard_map/ppermute | solution.py:703
  365.3 25.2 %collective-permute-start.21 = (bf16[2,4,128,512]{3,2,1,0:T(8,128)(2,1)S(1)}, bf16[2,4,128,512]{3,2,1,0:T(8,128)(2,1)S(1)}, u32[]{:S(2)}, u32[]{:S(2)}) collective-permute-start(bf16[2,4,128,512]{3,2,1,0:T(8,128)(2,1)S(1)} %pad_maximum_fusion.refs_0_), channel_id=1, source_target_pairs={{0,16},{8,24},{16,0},{24,8},{1,17},{9,25},{17,1},{25,9},{2,18},{10... | collective-permute-start | bytes 3145736 | tf_op jit(solution)/shard_map/ppermute | solution.py:703
  370.0 21.4 %collective-permute-start.28 = (bf16[8,128,512]{2,1,0:T(8,128)(2,1)S(1)}, bf16[8,128,512]{2,1,0:T(8,128)(2,1)S(1)}, u32[]{:S(2)}, u32[]{:S(2)}) collective-permute-start(bf16[8,128,512]{2,1,0:T(8,128)(2,1)S(1)} %constant_dynamic-update-slice_fusion.refs_4_), channel_id=1, source_target_pairs={{0,1},{1,0},{2,3},{3,2},{4,5},{5,4},{6,7},{7,6},{8,9},{9,8},{10,11... | collective-permute-start | bytes 3145736 | tf_op jit(solution)/shard_map/ppermute | solution.py:703
  372.4 19.7 %collective-permute-start.22 = (bf16[2,4,128,512]{3,2,1,0:T(8,128)(2,1)S(1)}, bf16[2,4,128,512]{3,2,1,0:T(8,128)(2,1)S(1)}, u32[]{:S(2)}, u32[]{:S(2)}) collective-permute-start(bf16[2,4,128,512]{3,2,1,0:T(8,128)(2,1)S(1)} %pad_maximum_fusion.refs_0_), channel_id=1, source_target_pairs={{0,8},{8,0},{16,24},{24,16},{1,9},{9,1},{17,25},{25,17},{2,10},{10... | collective-permute-start | bytes 3145736 | tf_op jit(solution)/shard_map/ppermute | solution.py:703
  372.4 19.7 %collective-permute-start.29 = (bf16[8,128,512]{2,1,0:T(8,128)(2,1)S(1)}, bf16[8,128,512]{2,1,0:T(8,128)(2,1)S(1)}, u32[]{:S(2)}, u32[]{:S(2)}) collective-permute-start(bf16[8,128,512]{2,1,0:T(8,128)(2,1)S(1)} %constant_dynamic-update-slice_fusion.refs_4_), channel_id=1, source_target_pairs={{0,8},{8,0},{16,24},{24,16},{1,9},{9,1},{17,25},{25,17},{2,10},{10... | collective-permute-start | bytes 3145736 | tf_op jit(solution)/shard_map/ppermute | solution.py:703
  390.5 2.7 collective-permute-start.23
  391.4 3.3 collective-permute-start.30

commit v6 on v5

--- a/solution.py
+++ b/solution.py
@@ -952,7 +952,7 @@
 
     early = max(deals // 2, 1)
     late = deals - early
-    groups = 2 if late and local % 2 == 0 else 1
+    groups = 1
     own_ff = weight_in.shape[1] // (tasks * devices)
     own_attn = attn_weights.shape[0] // (tasks * devices)
 
@@ -989,39 +989,21 @@
         )
     came_d = exchange(dealt_d[0], "feat")
     parts_two = plane_parts(reduce_core(keep_two, send_two))
-    came_d, _ = lax.optimization_barrier((came_d, parts_two))
-    if groups == 2:
-        dealt_d[1], came_d = lax.optimization_barrier((dealt_d[1], came_d))
-        came_last = exchange(dealt_d[1], "feat")
-        held = run_sample_backward(
-            counts, came_both, came_d, saved, weights, norm_params, chips, 0, None, False
-        )
-        came_d, held, parts_two[0] = lax.optimization_barrier((came_last, held, parts_two[0]))
-    else:
-        held = None
-    part_two, came_d = lax.optimization_barrier((reduce_plane(parts_two), came_d))
-    came_two = exchange(part_two, "feat", [list(range(side, devices, 2)) for side in range(2)])
+    parts_two, dealt_y, came_d = lax.optimization_barrier((parts_two, dealt_y, came_d))
+    came_y = exchange(dealt_y, "feat")
     input_grad, keep_one, send_one, norms_one = run_sample_backward(
-        counts,
-        came_both,
-        came_d,
-        saved,
-        weights,
-        norm_params,
-        chips,
-        0 if held is None else local // 2,
-        held,
-        True,
-    )
-    came_two, input_grad, keep_one, send_one, norms_one = lax.optimization_barrier(
-        (came_two, input_grad, keep_one, send_one, norms_one)
-    )
-    share_two = jnp.sum(came_two.astype(F32), axis=0)
-    share_one = reduce_layers(layer_parts(reduce_plane(plane_parts(reduce_core(keep_one, send_one)))))
+        counts, came_both, came_d, saved, weights, norm_params, chips, 0, None, True
+    )
+    parts_two[0], came_y, input_grad, keep_one, send_one, norms_one = lax.optimization_barrier(
+        (parts_two[0], came_y, input_grad, keep_one, send_one, norms_one)
+    )
+    parts_two = layer_parts(reduce_plane(parts_two))
+    parts_two, keep_one, send_one = lax.optimization_barrier((parts_two, keep_one, send_one))
+    parts_one = layer_parts(reduce_plane(plane_parts(reduce_core(keep_one, send_one))))
+    share_two, parts_one = lax.optimization_barrier((reduce_layers(parts_two), parts_one))
+    share_one = reduce_layers(parts_one)
     share_in_turned = share_two[:own_ff]
     share_out = share_two[own_ff : 2 * own_ff]
-    share_one, dealt_y = lax.optimization_barrier((share_one, dealt_y))
-    came_y = exchange(dealt_y, "feat")
     local_squares = jnp.sum(share_one * share_one) + jnp.sum(share_two * share_two)
     small = jnp.concatenate(
         [norms_one, norms_two, jnp.full((2, width), local_squares, F32)], axis=0
@@ -1030,7 +1012,7 @@
         (small, share_one, share_two[2 * own_ff :])
     )
     share_attn = to_owners(part_one, part_two)
-    small, share_attn, came_y = lax.optimization_barrier((total_of(small), share_attn, came_y))
+    small, share_attn = lax.optimization_barrier((total_of(small), share_attn))
     total_norms = small[:6]
     squares = small[6, 0] + jnp.sum(total_norms * total_norms)
     grad_norm = jnp.sqrt(squares)

time: 408 us -> 397 us (0.973)
  Pallas kernels: 185 us -> 153 us
  waiting for transfers between devices: 82.5 us -> 111 us
  starting transfers between devices: 74.2 us -> 68.2 us
    pallas_call x5 -> x4, Pallas kernels: 180 us -> 148 us  [call(): pl.pallas_call(body, grid=(grid,), in_specs=[pl.BlockSpec(memory_space=pl...]
    all_to_all x7 -> x5, waiting for transfers between devices: 11.2 us -> 39.8 us  [exchange(): lax.all_to_all(values, axis, 0, 0, axis_index_groups=groups, tiled=True)]
    all_to_all x7 -> x5, starting transfers between devices: 35.9 us -> 23.9 us  [exchange(): lax.all_to_all(values, axis, 0, 0, axis_index_groups=groups, tiled=True)]
    ppermute x6, waiting for transfers between devices: 10.6 us -> 0.17 us  [in_plane(): return lax.ppermute(values, ('task', 'feat'), pairs)]
    ppermute x25 -> x28, waiting for transfers between devices: 60.8 us -> 70.7 us  [moved_by(): return lax.ppermute(values, axis, pairs)]
    ppermute x6, starting transfers between devices: 7.03 us -> 14.8 us  [in_plane(): return lax.ppermute(values, ('task', 'feat'), pairs)]
    ppermute x25 -> x28, starting transfers between devices: 31.3 us -> 29.5 us  [moved_by(): return lax.ppermute(values, axis, pairs)]
  transfers between devices with their start and end apart: 38 -> 39, of which waited for: 20 -> 18; matrix products, arithmetic and copies ran while one was open for 3% -> 3% of each run, Pallas kernels for 45% -> 38%
where the time goes in v6:
time: 397 us; the launch traced here: 392 us
  Pallas kernels  153 us (39%)
  waiting for transfers between devices  111 us (28%)
  starting transfers between devices  68.2 us (17%)
  blocking collectives  31.4 us (8%)
  other arithmetic  15.2 us (4%)
  local copies, waits for them, and re-layouts  7.46 us (2%)
  between operations  6.62 us (2%)
    pallas_call x4, Pallas kernels, call(): pl.pallas_call(body, grid=(grid,), in_specs=[pl.BlockSpec(memory_space=pl...  148 us
    ppermute x28, waiting for transfers between devices, moved_by(): return lax.ppermute(values, axis, pairs)  70.7 us
    all_to_all x5, waiting for transfers between devices, exchange(): lax.all_to_all(values, axis, 0, 0, axis_index_groups=groups, tiled=True)  39.8 us
    all_to_all x1, blocking collectives, exchange(): lax.all_to_all(values, axis, 0, 0, axis_index_groups=groups, tiled=True)  31.4 us
    ppermute x28, starting transfers between devices, moved_by(): return lax.ppermute(values, axis, pairs)  29.5 us
    all_to_all x5, starting transfers between devices, exchange(): lax.all_to_all(values, axis, 0, 0, axis_index_groups=groups, tiled=True)  23.9 us
    ppermute x6, starting transfers between devices, in_plane(): return lax.ppermute(values, ('task', 'feat'), pairs)  14.8 us
  transfers between devices with their start and end apart: 39, of which 18 were waited for; matrix products, arithmetic and copies ran while one was open for 3% of the time, Pallas kernels for 38%

profile of v6, /device:TPU:0, one launch (start us, length us, event | category | flops | bytes accessed | tf_op | source)
XLA Modules:
  0.0 392.2 jit_solution(11288518590534544155)
XLA Ops:
  0.7 1.2 slice-done
  1.9 1.1 copy.42
  2.9 7.3 %all-to-all-start = ((bf16[8,2,4,16,512]{4,3,2,1,0:T(8,128)(2,1)}), bf16[8,2,4,16,512]{4,3,2,1,0:T(8,128)(2,1)S(1)}, u32[]{:S(2)}, u32[]{:S(2)}) async-start(bf16[8,2,4,16,512]{4,3,2,1,0:T(8,128)(2,1)} %bitcast.77), calls=%async_computation | async-start | bytes 2097152 | tf_op jit(solution)/shard_map/all_to_all | solution.py:698
  11.5 0.6 stack.62.counts
  12.1 25.1 %sample_forward.1 = (bf16[8,2,4,16,512]{4,3,2,1,0:T(8,128)(2,1)}, bf16[8,2,2,4,16,512]{5,4,3,2,1,0:T(8,128)(2,1)}, bf16[4,512,512]{2,1,0:T(8,128)(2,1)}, bf16[4,...) custom-call(s32[5]{0:T(128)} %stack.62.counts, bf16[4,512,512]{2,1,0:T(8,128)(2,1)} %bitcast.95, ...), custom_call_target="tpu_custom_call" | custom-call | flops 28750000128 | bytes 16777216 | tf_op jit(solution)/shard_map/sample_forward/pallas_call | solution.py:473
  37.3 31.4 %all_to_all.30.refs_0_ = bf16[8,2,4,16,512]{4,3,2,1,0:T(8,128)(2,1)} all-to-all(bf16[8,2,4,16,512]{4,3,2,1,0:T(8,128)(2,1)} %get-tuple-element.92), channel_id=1, replica_groups=mesh['task'=4,'feat'=8] {'feat'}, dimensions={0} | all-to-all | bytes 2097152 | tf_op jit(solution)/shard_map/all_to_all | solution.py:698
  68.6 3.6 all-to-all-start.3
  72.2 53.3 %middle.2 = (bf16[8,2,2,4,16,512]{5,4,3,2,1,0:T(8,128)(2,1)}, f32[2048,512]{1,0:T(8,128)}, f32[2048,512]{1,0:T(8,128)}, f32[2048,512]{1,0:T(8,128)}, f32[4,512]{1,0:T(4,128)}) custom-call(s32[5]{0:T(128)} %stack.62.counts, bf16[8,2,4,16,512]{4,3,2,1,0:T(8,128)(2,1)} %all_to_all.30.refs_0_, bf16[8,2,4,16,512]{4,3,2,1,0:T(8,128)(2,1)} %copy-done.5, ...), custom_call_target="tpu_custom_call" | custom-call | flops 52899999744 | bytes 16777216 | tf_op jit(solution)/shard_map/middle/pallas_call | solution.py:473
  125.6 1.3 copy-done.2
  126.9 5.9 %all-to-all-start.2 = ((bf16[8,2,2,4,16,512]{5,4,3,2,1,0:T(8,128)(2,1)}), bf16[8,2,2,4,16,512]{5,4,3,2,1,0:T(8,128)(2,1)S(1)}, u32[]{:S(2)}, u32[]{:S(2)}) async-start(bf16[8,2,2,4,16,512]{5,4,3,2,1,0:T(8,128)(2,1)} %get-tuple-element.95), calls=%async_computation.2 | async-start | bytes 4194304 | tf_op jit(solution)/shard_map/all_to_all | solution.py:698
  132.8 24.6 %middle.3 = (bf16[8,2,4,16,512]{4,3,2,1,0:T(8,128)(2,1)}, bf16[8,2,4,16,512]{4,3,2,1,0:T(8,128)(2,1)}, bf16[2,8,192,512]{3,2,1,0:T(8,128)(2,1)}, bf16[2,8,192,512]{3,2,1,0:T(8,128)(2,1)}, f32[4,512]{1,0:T(4,128)}) custom-call(s32[5]{0:T(128)} %stack.62.counts, bf16[8,2,2,4,16,512]{5,4,3,2,1,0:T(8,128)(2,1)} %copy-done.2, ...), custom_call_target="tpu_custom_call" | custom-call | flops 52899999744 | bytes 16777216 | tf_op jit(solution)/shard_map/middle/pallas_call | solution.py:473
  157.5 21.0 %all-to-all-done.2.refs_0_.refs_8_ = bf16[8,2,2,4,16,512]{5,4,3,2,1,0:T(8,128)(2,1)S(1)} async-done(((bf16[8,2,2,4,16,512]{5,4,3,2,1,0:T(8,128)(2,1)}), bf16[8,2,2,4,16,512]{5,4,3,2,1,0:T(8,128)(2,1)S(1)}, u32[]{:S(2)}, u32[]{:S(2)}) %all-to-all-start.2) | async-done | bytes 2097184 | tf_op jit(solution)/shard_map/all_to_all | solution.py:698
  178.5 3.6 all-to-all-start.4
  182.2 2.3 collective-permute-done
  184.5 3.9 add_convert_fusion
  188.4 1.5 dynamic-slice_bitcast_fusion
  189.9 18.8 %all-to-all-done.4.refs_1_ = bf16[8,2,4,16,512]{4,3,2,1,0:T(8,128)(2,1)S(1)} async-done(((bf16[8,2,4,16,512]{4,3,2,1,0:T(8,128)(2,1)}), bf16[8,2,4,16,512]{4,3,2,1,0:T(8,128)(2,1)S(1)}, u32[]{:S(2)}, u32[]{:S(2)}) %all-to-all-start.4) | async-done | bytes 1048608 | tf_op jit(solution)/shard_map/all_to_all | solution.py:698
  208.7 3.6 all-to-all-start.5
  212.3 10.0 %collective-permute-start.3 = (bf16[4,192,512]{2,1,0:T(8,128)(2,1)}, bf16[4,192,512]{2,1,0:T(8,128)(2,1)}, u32[]{:S(2)}, u32[]{:S(2)}) collective-permute-start(bf16[4,192,512]{2,1,0:T(8,128)(2,1)} %get-tuple-element.127), channel_id=1, source_target_pairs={{0,17},{1,16},{2,19},{3,18},{4,21},{5,20},{6,23},{7,22},{8,25},{9,... | collective-permute-start | bytes 2359304 | tf_op jit(solution)/shard_map/ppermute | solution.py:736
  222.3 0.6 collective-permute-start.1
  222.9 44.5 %sample_backward.1 = (bf16[4,512,512]{2,1,0:T(8,128)(2,1)}, bf16[2,8,64,512]{3,2,1,0:T(8,128)(2,1)}, bf16[2,8,64,512]{3,2,1,0:T(8,128)(2,1)}, f32[2,512]{1,0:T(2,128)}) custom-call(s32[5]{0:T(128)} %stack.62.counts, bf16[8,2,2,4,16,512]{5,4,3,2,1,0:T(8,128)(2,1)} %copy-done, bf16[8,2,4,16,512]{4,3,2,1,0:T(8,128)(2,1)} %copy-done.4, ...), custom_call_target="tpu_custom_call" | custom-call | flops 50600001536 | bytes 16777216 | tf_op jit(solution)/shard_map/sample_backward/pallas_call | solution.py:473
  267.5 2.2 add_convert_fusion.2
  269.8 3.3 collective-permute-start.6
  273.1 1.3 collective-permute-start.4
  274.8 0.9 dynamic-slice_bitcast_fusion.6
  275.7 1.5 collective-permute-start.10
  277.2 1.4 collective-permute-start.9
  278.7 1.2 collective-permute-start.8
  279.9 10.8 %collective-permute-done.5 = bf16[192,512]{1,0:T(8,128)(2,1)S(1)} collective-permute-done((bf16[192,512]{1,0:T(8,128)(2,1)S(1)}, bf16[192,512]{1,0:T(8,128)(2,1)S(1)}, u32[]{:S(2)}, u32[]{:S(2)}) %collective-permute-start.5) | collective-permute-done | bytes 196640 | tf_op jit(solution)/shard_map/ppermute | solution.py:703
  291.0 1.2 fusion.2
  292.2 2.4 collective-permute-start.13
  294.6 0.8 collective-permute-start.12
  295.5 1.4 collective-permute-start.11
  296.9 0.7 multiply_reduce_fusion
  297.6 4.3 %collective-permute-done.12 = bf16[64,512]{1,0:T(8,128)(2,1)S(1)} collective-permute-done((bf16[64,512]{1,0:T(8,128)(2,1)S(1)}, bf16[64,512]{1,0:T(8,128)(2,1)S(1)}, u32[]{:S(2)}, u32[]{:S(2)}) %collective-permute-start.12) | collective-permute-done | bytes 65568 | tf_op jit(solution)/shard_map/ppermute | solution.py:703
  301.9 0.6 multiply_reduce_fusion.1
  304.0 4.0 %collective-permute-start.19 = (f32[64,512]{1,0:T(8,128)S(1)}, f32[64,512]{1,0:T(8,128)}, u32[]{:S(2)}, u32[]{:S(2)}) collective-permute-start(f32[64,512]{1,0:T(8,128)S(1)} %broadcast_select_fusion), channel_id=1, source_target_pairs={{0,16},{8,24},{16,0},{24,8},{1,17},{9,25},{17,1},{25,9},{2,18},{10... | collective-permute-start | bytes 393224 | tf_op jit(solution)/shard_map/ppermute | solution.py:703
  308.0 1.2 collective-permute-done.14
  309.3 3.7 collective-permute-done.15
  313.0 1.7 collective-permute-start.16
  314.7 2.0 collective-permute-done.16
  316.7 3.7 collective-permute-done.17
  320.5 4.6 %collective-permute-done.18 = f32[8,512]{1,0:T(8,128)S(1)} collective-permute-done((f32[8,512]{1,0:T(8,128)S(1)}, f32[8,512]{1,0:T(8,128)S(1)}, u32[]{:S(2)}, u32[]{:S(2)}) %collective-permute-start.18) | collective-permute-done | bytes 16416 | tf_op jit(solution)/shard_map/ppermute | solution.py:703
  325.1 0.9 broadcast_select_fusion.3
  326.6 0.6 multiply_reduce_fusion.2
  328.6 1.0 fusion.19
  329.6 1.5 collective-permute-start.21
  331.6 0.8 fusion.17
  332.5 1.7 convert_bitcast_fusion
  334.2 1.5 collective-permute-start.27
  335.7 2.4 collective-permute-start.28
  338.1 2.0 collective-permute-start.29
  340.1 6.3 %collective-permute-done.21 = bf16[128,512]{1,0:T(8,128)(2,1)S(1)} collective-permute-done((bf16[128,512]{1,0:T(8,128)(2,1)S(1)}, bf16[128,512]{1,0:T(8,128)(2,1)S(1)}, u32[]{:S(2)}, u32[]{:S(2)}) %collective-permute-start.21) | collective-permute-done | bytes 131104 | tf_op jit(solution)/shard_map/ppermute | solution.py:703
  346.5 1.8 collective-permute-start.23
  348.7 0.9 collective-permute-start.30
  349.6 6.1 %collective-permute-done.23 = bf16[4,128,512]{2,1,0:T(8,128)(2,1)S(1)} collective-permute-done((bf16[4,128,512]{2,1,0:T(8,128)(2,1)S(1)}, bf16[4,128,512]{2,1,0:T(8,128)(2,1)S(1)}, u32[]{:S(2)}, u32[]{:S(2)}) %collective-permute-start.23) | collective-permute-done | bytes 524320 | tf_op jit(solution)/shard_map/ppermute | solution.py:703
  355.9 0.9 collective-permute-start.24
  356.7 6.9 %collective-permute-done.30 = bf16[4,128,512]{2,1,0:T(8,128)(2,1)S(1)} collective-permute-done((bf16[4,128,512]{2,1,0:T(8,128)(2,1)S(1)}, bf16[4,128,512]{2,1,0:T(8,128)(2,1)S(1)}, u32[]{:S(2)}, u32[]{:S(2)}) %collective-permute-start.30) | collective-permute-done | bytes 524320 | tf_op jit(solution)/shard_map/ppermute | solution.py:703
  363.6 1.8 collective-permute-start.31
  366.0 15.7 %collective-permute-done.24.refs_1_ = bf16[2,4,128,512]{3,2,1,0:T(8,128)(2,1)S(1)} collective-permute-done((bf16[2,4,128,512]{3,2,1,0:T(8,128)(2,1)S(1)}, bf16[2,4,128,512]{3,2,1,0:T(8,128)(2,1)S(1)}, u32[]{:S(2)}, u32[]{:S(2)}) %collective-permute-start.24) | collective-permute-done | bytes 1048608 | tf_op jit(solution)/shard_map/ppermute | solution.py:703
  382.3 0.6 multiply_subtract_fusion.3
  382.9 1.4 collective-permute-done.26.refs_3_
  384.3 1.5 collective-permute-done.33.refs_7_
  385.8 5.0 %place_copies.1 = (bf16[4096,512]{1,0:T(8,128)(2,1)}, bf16[512,2048]{1,0:T(8,128)(2,1)}, bf16[2048,512]{1,0:T(8,128)(2,1)}, bf16[4,4,8,16,512]{4,3,2,1,0:T(8,128)(2,1)}) custom-call(s32[6]{0:T(128)S(1)} %pad_add_fusion.table, bf16[2,4,128,512]{3,2,1,0:T(8,128)(2,1)S(1)} %pad_maximum_fusion.refs_0_, ...), custom_call_target="tpu_custom_call" | custom-call | tf_op jit(solution)/shard_map/place_copies/pallas_call | solution.py:878
  (104 shorter events, 4.0 us)
Async XLA Ops:
  0.7 1.2 slice-start
  2.9 34.3 %all-to-all-start = ((bf16[8,2,4,16,512]{4,3,2,1,0:T(8,128)(2,1)}), bf16[8,2,4,16,512]{4,3,2,1,0:T(8,128)(2,1)S(1)}, u32[]{:S(2)}, u32[]{:S(2)}) async-start(bf16[8,2,4,16,512]{4,3,2,1,0:T(8,128)(2,1)} %bitcast.77), calls=%async_computation | async-start | bytes 2097152 | tf_op jit(solution)/shard_map/all_to_all | solution.py:698
  37.3 31.4 %copy-start.5 = (bf16[8,2,4,16,512]{4,3,2,1,0:T(8,128)(2,1)}, bf16[8,2,4,16,512]{4,3,2,1,0:T(8,128)(2,1)S(1)}, u32[]{:S(2)}) copy-start(bf16[8,2,4,16,512]{4,3,2,1,0:T(8,128)(2,1)S(1)} %all-to-all-done.refs_1_) | copy-start | bytes 3145732
  68.6 57.0 %all-to-all-start.3 = ((bf16[8,2,2,4,16,512]{5,4,3,2,1,0:T(8,128)(2,1)}), bf16[8,2,2,4,16,512]{5,4,3,2,1,0:T(8,128)(2,1)S(1)}, u32[]{:S(2)}, u32[]{:S(2)}) async-start(bf16[8,2,2,4,16,512]{5,4,3,2,1,0:T(8,128)(2,1)} %get-tuple-element.96), calls=%async_computation.3 | async-start | bytes 4194304 | tf_op jit(solution)/shard_map/all_to_all | solution.py:698
  125.6 1.3 copy-start.2
  126.9 51.5 %all-to-all-start.2 = ((bf16[8,2,2,4,16,512]{5,4,3,2,1,0:T(8,128)(2,1)}), bf16[8,2,2,4,16,512]{5,4,3,2,1,0:T(8,128)(2,1)S(1)}, u32[]{:S(2)}, u32[]{:S(2)}) async-start(bf16[8,2,2,4,16,512]{5,4,3,2,1,0:T(8,128)(2,1)} %get-tuple-element.95), calls=%async_computation.2 | async-start | bytes 4194304 | tf_op jit(solution)/shard_map/all_to_all | solution.py:698
  178.5 9.9 %copy-start = (bf16[8,2,2,4,16,512]{5,4,3,2,1,0:T(8,128)(2,1)}, bf16[8,2,2,4,16,512]{5,4,3,2,1,0:T(8,128)(2,1)S(1)}, u32[]{:S(2)}) copy-start(bf16[8,2,2,4,16,512]{5,4,3,2,1,0:T(8,128)(2,1)S(1)} %all-to-all-done.2.refs_0_.refs_8_) | copy-start | bytes 6291460
  178.5 6.0 %collective-permute-start = (bf16[2,8,192,512]{3,2,1,0:T(8,128)(2,1)}, bf16[2,8,192,512]{3,2,1,0:T(8,128)(2,1)}, u32[]{:S(2)}, u32[]{:S(2)}) collective-permute-start(bf16[2,8,192,512]{3,2,1,0:T(8,128)(2,1)} %get-tuple-element.107), channel_id=1, source_target_pairs={{0,8},{8,0},{16,24},{24,16},{1,9},{9,1},{17,25},{25,17},{2,10},{10... | collective-permute-start | bytes 9437192 | tf_op jit(solution)/shard_map/ppermute | solution.py:703
  178.5 30.2 %all-to-all-start.4 = ((bf16[8,2,4,16,512]{4,3,2,1,0:T(8,128)(2,1)}), bf16[8,2,4,16,512]{4,3,2,1,0:T(8,128)(2,1)S(1)}, u32[]{:S(2)}, u32[]{:S(2)}) async-start(bf16[8,2,4,16,512]{4,3,2,1,0:T(8,128)(2,1)} %get-tuple-element.109), calls=%async_computation.4 | async-start | bytes 2097152 | tf_op jit(solution)/shard_map/all_to_all | solution.py:698
  208.7 14.2 %copy-start.4 = (bf16[8,2,4,16,512]{4,3,2,1,0:T(8,128)(2,1)}, bf16[8,2,4,16,512]{4,3,2,1,0:T(8,128)(2,1)S(1)}, u32[]{:S(2)}) copy-start(bf16[8,2,4,16,512]{4,3,2,1,0:T(8,128)(2,1)S(1)} %all-to-all-done.4.refs_1_) | copy-start | bytes 3145732
  208.7 58.8 %all-to-all-start.5 = ((bf16[8,2,4,16,512]{4,3,2,1,0:T(8,128)(2,1)}), bf16[8,2,4,16,512]{4,3,2,1,0:T(8,128)(2,1)S(1)}, u32[]{:S(2)}, u32[]{:S(2)}) async-start(bf16[8,2,4,16,512]{4,3,2,1,0:T(8,128)(2,1)} %get-tuple-element.111), calls=%async_computation.5 | async-start | bytes 2097152 | tf_op jit(solution)/shard_map/all_to_all | solution.py:698
  212.3 55.2 %collective-permute-start.3 = (bf16[4,192,512]{2,1,0:T(8,128)(2,1)}, bf16[4,192,512]{2,1,0:T(8,128)(2,1)}, u32[]{:S(2)}, u32[]{:S(2)}) collective-permute-start(bf16[4,192,512]{2,1,0:T(8,128)(2,1)} %get-tuple-element.127), channel_id=1, source_target_pairs={{0,17},{1,16},{2,19},{3,18},{4,21},{5,20},{6,23},{7,22},{8,25},{9,... | collective-permute-start | bytes 2359304 | tf_op jit(solution)/shard_map/ppermute | solution.py:736
  222.3 45.1 %collective-permute-start.2 = (bf16[4,192,512]{2,1,0:T(8,128)(2,1)}, bf16[4,192,512]{2,1,0:T(8,128)(2,1)}, u32[]{:S(2)}, u32[]{:S(2)}) collective-permute-start(bf16[4,192,512]{2,1,0:T(8,128)(2,1)} %get-tuple-element.126), channel_id=1, source_target_pairs={{0,16},{1,17},{2,18},{3,19},{4,20},{5,21},{6,22},{7,23},{8,24},{9,... | collective-permute-start | bytes 2359304 | tf_op jit(solution)/shard_map/ppermute | solution.py:736
  222.3 45.1 %collective-permute-start.1 = (bf16[4,192,512]{2,1,0:T(8,128)(2,1)}, bf16[4,192,512]{2,1,0:T(8,128)(2,1)}, u32[]{:S(2)}, u32[]{:S(2)}) collective-permute-start(bf16[4,192,512]{2,1,0:T(8,128)(2,1)} %get-tuple-element.125), channel_id=1, source_target_pairs={{0,1},{1,0},{2,3},{3,2},{4,5},{5,4},{6,7},{7,6},{8,9},{9,8},{10,11... | collective-permute-start | bytes 2359304 | tf_op jit(solution)/shard_map/ppermute | solution.py:736
  267.4 2.3 copy-start.19
  267.4 7.0 %copy-start.3 = (bf16[2,8,64,512]{3,2,1,0:T(8,128)(2,1)S(1)}, bf16[2,8,64,512]{3,2,1,0:T(8,128)(2,1)}, u32[]{:S(2)}) copy-start(bf16[2,8,64,512]{3,2,1,0:T(8,128)(2,1)} %get-tuple-element.134) | copy-start | bytes 3145732
  269.7 4.7 %collective-permute-start.7 = (bf16[2,8,64,512]{3,2,1,0:T(8,128)(2,1)S(1)}, bf16[2,8,64,512]{3,2,1,0:T(8,128)(2,1)S(1)}, u32[]{:S(2)}, u32[]{:S(2)}) collective-permute-start(bf16[2,8,64,512]{3,2,1,0:T(8,128)(2,1)S(1)} %copy-done.19), channel_id=1, source_target_pairs={{0,8},{8,0},{16,24},{24,16},{1,9},{9,1},{17,25},{25,17},{2,10},{10... | collective-permute-start | bytes 3145736 | tf_op jit(solution)/shard_map/ppermute | solution.py:703
  269.8 8.9 %collective-permute-start.6 = (bf16[192,512]{1,0:T(8,128)(2,1)S(1)}, bf16[192,512]{1,0:T(8,128)(2,1)S(1)}, u32[]{:S(2)}, u32[]{:S(2)}) collective-permute-start(bf16[192,512]{1,0:T(8,128)(2,1)S(1)} %get-tuple-element.133), channel_id=1, source_target_pairs={{0,6},{1,7},{2,0},{3,1},{4,2},{5,3},{6,4},{7,5},{8,14},{9,15},{10,... | collective-permute-start | bytes 589832 | tf_op jit(solution)/shard_map/ppermute | solution.py:703
  273.1 17.5 %collective-permute-start.5 = (bf16[192,512]{1,0:T(8,128)(2,1)S(1)}, bf16[192,512]{1,0:T(8,128)(2,1)S(1)}, u32[]{:S(2)}, u32[]{:S(2)}) collective-permute-start(bf16[192,512]{1,0:T(8,128)(2,1)S(1)} %get-tuple-element.132), channel_id=1, source_target_pairs={{0,4},{1,5},{2,6},{3,7},{4,0},{5,1},{6,2},{7,3},{8,12},{9,13},{10,... | collective-permute-start | bytes 589832 | tf_op jit(solution)/shard_map/ppermute | solution.py:703
  273.1 17.5 %collective-permute-start.4 = (bf16[192,512]{1,0:T(8,128)(2,1)S(1)}, bf16[192,512]{1,0:T(8,128)(2,1)S(1)}, u32[]{:S(2)}, u32[]{:S(2)}) collective-permute-start(bf16[192,512]{1,0:T(8,128)(2,1)S(1)} %get-tuple-element.131), channel_id=1, source_target_pairs={{0,2},{1,3},{2,4},{3,5},{4,6},{5,7},{6,0},{7,1},{8,10},{9,11},{10,... | collective-permute-start | bytes 589832 | tf_op jit(solution)/shard_map/ppermute | solution.py:703
  275.7 28.2 %copy-start.17 = (f32[4,512]{1,0:T(4,128)S(1)}, f32[4,512]{1,0:T(4,128)}, u32[]{:S(2)}) copy-start(f32[4,512]{1,0:T(4,128)} %get-tuple-element.123) | copy-start | bytes 24580
  275.7 28.2 %copy-start.18 = (f32[2,512]{1,0:T(2,128)S(1)}, f32[2,512]{1,0:T(2,128)}, u32[]{:S(2)}) copy-start(f32[2,512]{1,0:T(2,128)} %get-tuple-element.122) | copy-start | bytes 12292
  275.7 15.1 %collective-permute-start.10 = (bf16[4,64,512]{2,1,0:T(8,128)(2,1)}, bf16[4,64,512]{2,1,0:T(8,128)(2,1)S(1)}, u32[]{:S(2)}, u32[]{:S(2)}) collective-permute-start(bf16[4,64,512]{2,1,0:T(8,128)(2,1)} %get-tuple-element.174), channel_id=1, source_target_pairs={{0,17},{1,16},{2,19},{3,18},{4,21},{5,20},{6,23},{7,22},{8,25},{9,... | collective-permute-start | bytes 786440 | tf_op jit(solution)/shard_map/ppermute | solution.py:736
  277.2 13.6 %collective-permute-start.9 = (bf16[4,64,512]{2,1,0:T(8,128)(2,1)}, bf16[4,64,512]{2,1,0:T(8,128)(2,1)}, u32[]{:S(2)}, u32[]{:S(2)}) collective-permute-start(bf16[4,64,512]{2,1,0:T(8,128)(2,1)} %get-tuple-element.175), channel_id=1, source_target_pairs={{0,16},{1,17},{2,18},{3,19},{4,20},{5,21},{6,22},{7,23},{8,24},{9,... | collective-permute-start | bytes 786440 | tf_op jit(solution)/shard_map/ppermute | solution.py:736
  278.7 12.3 %collective-permute-start.8 = (bf16[4,64,512]{2,1,0:T(8,128)(2,1)}, bf16[4,64,512]{2,1,0:T(8,128)(2,1)}, u32[]{:S(2)}, u32[]{:S(2)}) collective-permute-start(bf16[4,64,512]{2,1,0:T(8,128)(2,1)} %get-tuple-element.173), channel_id=1, source_target_pairs={{0,1},{1,0},{2,3},{3,2},{4,5},{5,4},{6,7},{7,6},{8,9},{9,8},{10,11... | collective-permute-start | bytes 786440 | tf_op jit(solution)/shard_map/ppermute | solution.py:736
  290.8 37.8 %copy-start.6 = (f32[128,512]{1,0:T(8,128)S(1)}, f32[128,512]{1,0:T(8,128)}, u32[]{:S(2)}) copy-start(f32[128,512]{1,0:T(8,128)} %param.25) | copy-start | bytes 786436
  290.8 37.8 %copy-start.7 = (f32[128,512]{1,0:T(8,128)S(1)}, f32[128,512]{1,0:T(8,128)}, u32[]{:S(2)}) copy-start(f32[128,512]{1,0:T(8,128)} %param.28) | copy-start | bytes 786436
  290.8 37.8 %copy-start.8 = (f32[128,512]{1,0:T(8,128)S(1)}, f32[128,512]{1,0:T(8,128)}, u32[]{:S(2)}) copy-start(f32[128,512]{1,0:T(8,128)} %param.32) | copy-start | bytes 786436
  292.2 5.4 %collective-permute-start.13 = (bf16[64,512]{1,0:T(8,128)(2,1)S(1)}, bf16[64,512]{1,0:T(8,128)(2,1)S(1)}, u32[]{:S(2)}, u32[]{:S(2)}) collective-permute-start(bf16[64,512]{1,0:T(8,128)(2,1)S(1)} %get-tuple-element.139), channel_id=1, source_target_pairs={{0,6},{1,7},{2,0},{3,1},{4,2},{5,3},{6,4},{7,5},{8,14},{9,15},{10,... | collective-permute-start | bytes 196616 | tf_op jit(solution)/shard_map/ppermute | solution.py:703
  294.6 7.3 %collective-permute-start.12 = (bf16[64,512]{1,0:T(8,128)(2,1)S(1)}, bf16[64,512]{1,0:T(8,128)(2,1)S(1)}, u32[]{:S(2)}, u32[]{:S(2)}) collective-permute-start(bf16[64,512]{1,0:T(8,128)(2,1)S(1)} %get-tuple-element.138), channel_id=1, source_target_pairs={{0,4},{1,5},{2,6},{3,7},{4,0},{5,1},{6,2},{7,3},{8,12},{9,13},{10,... | collective-permute-start | bytes 196616 | tf_op jit(solution)/shard_map/ppermute | solution.py:703
  295.5 6.5 %collective-permute-start.11 = (bf16[64,512]{1,0:T(8,128)(2,1)S(1)}, bf16[64,512]{1,0:T(8,128)(2,1)S(1)}, u32[]{:S(2)}, u32[]{:S(2)}) collective-permute-start(bf16[64,512]{1,0:T(8,128)(2,1)S(1)} %get-tuple-element.137), channel_id=1, source_target_pairs={{0,2},{1,3},{2,4},{3,5},{4,6},{5,7},{6,0},{7,1},{8,10},{9,11},{10,... | collective-permute-start | bytes 196616 | tf_op jit(solution)/shard_map/ppermute | solution.py:703
  297.6 34.1 %copy-start.9 = (f32[64,512]{1,0:T(8,128)S(1)}, f32[64,512]{1,0:T(8,128)}, u32[]{:S(2)}) copy-start(f32[64,512]{1,0:T(8,128)} %param.27) | copy-start | bytes 393220
  297.6 34.1 %copy-start.10 = (f32[64,512]{1,0:T(8,128)S(1)}, f32[64,512]{1,0:T(8,128)}, u32[]{:S(2)}) copy-start(f32[64,512]{1,0:T(8,128)} %param.30) | copy-start | bytes 393220
  297.6 34.1 %copy-start.11 = (f32[64,512]{1,0:T(8,128)S(1)}, f32[64,512]{1,0:T(8,128)}, u32[]{:S(2)}) copy-start(f32[64,512]{1,0:T(8,128)} %param.34) | copy-start | bytes 393220
  304.0 21.0 %collective-permute-start.19 = (f32[64,512]{1,0:T(8,128)S(1)}, f32[64,512]{1,0:T(8,128)}, u32[]{:S(2)}, u32[]{:S(2)}) collective-permute-start(f32[64,512]{1,0:T(8,128)S(1)} %broadcast_select_fusion), channel_id=1, source_target_pairs={{0,16},{8,24},{16,0},{24,8},{1,17},{9,25},{17,1},{25,9},{2,18},{10... | collective-permute-start | bytes 393224 | tf_op jit(solution)/shard_map/ppermute | solution.py:703
  308.0 1.2 collective-permute-start.14
  309.2 3.7 collective-permute-start.15
  313.0 3.7 collective-permute-start.16
  316.7 3.7 collective-permute-start.17
  320.5 4.6 %collective-permute-start.18 = (f32[8,512]{1,0:T(8,128)S(1)}, f32[8,512]{1,0:T(8,128)S(1)}, u32[]{:S(2)}, u32[]{:S(2)}) collective-permute-start(f32[8,512]{1,0:T(8,128)S(1)} %add.311), channel_id=1, source_target_pairs={{0,4},{1,5},{2,6},{3,7},{4,0},{5,1},{6,2},{7,3},{8,12},{9,13},{10,... | collective-permute-start | bytes 49160 | tf_op jit(solution)/shard_map/ppermute | solution.py:703
  320.5 12.0 %copy-start.12 = (f32[512,64]{0,1:T(8,128)S(1)}, f32[512,64]{0,1:T(8,128)}, u32[]{:S(2)}) copy-start(f32[512,64]{0,1:T(8,128)} %param.26) | copy-start | bytes 393220
  320.5 12.0 %copy-start.13 = (f32[512,64]{0,1:T(8,128)S(1)}, f32[512,64]{0,1:T(8,128)}, u32[]{:S(2)}) copy-start(f32[512,64]{0,1:T(8,128)} %param.29) | copy-start | bytes 393220
  329.6 8.5 %collective-permute-start.22 = (bf16[128,512]{1,0:T(8,128)(2,1)S(1)}, bf16[128,512]{1,0:T(8,128)(2,1)S(1)}, u32[]{:S(2)}, u32[]{:S(2)}) collective-permute-start(bf16[128,512]{1,0:T(8,128)(2,1)S(1)} %get-tuple-element.163), channel_id=1, source_target_pairs={{0,6},{1,7},{2,0},{3,1},{4,2},{5,3},{6,4},{7,5},{8,14},{9,15},{10,... | collective-permute-start | bytes 393224 | tf_op jit(solution)/shard_map/ppermute | solution.py:703
  329.6 16.8 %collective-permute-start.21 = (bf16[128,512]{1,0:T(8,128)(2,1)S(1)}, bf16[128,512]{1,0:T(8,128)(2,1)S(1)}, u32[]{:S(2)}, u32[]{:S(2)}) collective-permute-start(bf16[128,512]{1,0:T(8,128)(2,1)S(1)} %get-tuple-element.163), channel_id=1, source_target_pairs={{0,4},{1,5},{2,6},{3,7},{4,0},{5,1},{6,2},{7,3},{8,12},{9,13},{10,... | collective-permute-start | bytes 393224 | tf_op jit(solution)/shard_map/ppermute | solution.py:703
  331.1 15.4 %collective-permute-start.20 = (bf16[128,512]{1,0:T(8,128)(2,1)S(1)}, bf16[128,512]{1,0:T(8,128)(2,1)S(1)}, u32[]{:S(2)}, u32[]{:S(2)}) collective-permute-start(bf16[128,512]{1,0:T(8,128)(2,1)S(1)} %get-tuple-element.163), channel_id=1, source_target_pairs={{0,2},{1,3},{2,4},{3,5},{4,6},{5,7},{6,0},{7,1},{8,10},{9,11},{10,... | collective-permute-start | bytes 393224 | tf_op jit(solution)/shard_map/ppermute | solution.py:703
  334.2 14.2 %collective-permute-start.27 = (bf16[128,512]{1,0:T(8,128)(2,1)S(1)}, bf16[128,512]{1,0:T(8,128)(2,1)S(1)}, u32[]{:S(2)}, u32[]{:S(2)}) collective-permute-start(bf16[128,512]{1,0:T(8,128)(2,1)S(1)} %get-tuple-element.189), channel_id=1, source_target_pairs={{0,2},{1,3},{2,4},{3,5},{4,6},{5,7},{6,0},{7,1},{8,10},{9,11},{10,... | collective-permute-start | bytes 393224 | tf_op jit(solution)/shard_map/ppermute | solution.py:703
  335.7 12.9 %collective-permute-start.28 = (bf16[128,512]{1,0:T(8,128)(2,1)S(1)}, bf16[128,512]{1,0:T(8,128)(2,1)S(1)}, u32[]{:S(2)}, u32[]{:S(2)}) collective-permute-start(bf16[128,512]{1,0:T(8,128)(2,1)S(1)} %get-tuple-element.189), channel_id=1, source_target_pairs={{0,4},{1,5},{2,6},{3,7},{4,0},{5,1},{6,2},{7,3},{8,12},{9,13},{10,... | collective-permute-start | bytes 393224 | tf_op jit(solution)/shard_map/ppermute | solution.py:703
  338.1 10.5 %collective-permute-start.29 = (bf16[128,512]{1,0:T(8,128)(2,1)S(1)}, bf16[128,512]{1,0:T(8,128)(2,1)S(1)}, u32[]{:S(2)}, u32[]{:S(2)}) collective-permute-start(bf16[128,512]{1,0:T(8,128)(2,1)S(1)} %get-tuple-element.189), channel_id=1, source_target_pairs={{0,6},{1,7},{2,0},{3,1},{4,2},{5,3},{6,4},{7,5},{8,14},{9,15},{10,... | collective-permute-start | bytes 393224 | tf_op jit(solution)/shard_map/ppermute | solution.py:703
  346.5 9.2 %collective-permute-start.23 = (bf16[4,128,512]{2,1,0:T(8,128)(2,1)S(1)}, bf16[4,128,512]{2,1,0:T(8,128)(2,1)S(1)}, u32[]{:S(2)}, u32[]{:S(2)}) collective-permute-start(bf16[4,128,512]{2,1,0:T(8,128)(2,1)S(1)} %get-tuple-element.181), channel_id=1, source_target_pairs={{0,1},{1,0},{2,3},{3,2},{4,5},{5,4},{6,7},{7,6},{8,9},{9,8},{10,11... | collective-permute-start | bytes 1572872 | tf_op jit(solution)/shard_map/ppermute | solution.py:703
  348.6 33.6 %copy-start.14 = (f32[6,512]{1,0:T(8,128)S(1)}, f32[6,512]{1,0:T(8,128)}, u32[]{:S(2)}) copy-start(f32[6,512]{1,0:T(8,128)} %refs_8_.1) | copy-start | bytes 36868
  348.6 33.6 %copy-start.15 = (f32[6,512]{1,0:T(8,128)S(1)}, f32[6,512]{1,0:T(8,128)}, u32[]{:S(2)}) copy-start(f32[6,512]{1,0:T(8,128)} %param.31) | copy-start | bytes 36868
  348.7 33.6 %copy-start.16 = (f32[6,512]{1,0:T(8,128)S(1)}, f32[6,512]{1,0:T(8,128)}, u32[]{:S(2)}) copy-start(f32[6,512]{1,0:T(8,128)} %param.35) | copy-start | bytes 36868
  348.7 37.1 %copy-start.1 = (bf16[8,2,2,4,16,512]{5,4,3,2,1,0:T(8,128)(2,1)S(1)}, bf16[8,2,2,4,16,512]{5,4,3,2,1,0:T(8,128)(2,1)}, u32[]{:S(2)}) copy-start(bf16[8,2,2,4,16,512]{5,4,3,2,1,0:T(8,128)(2,1)} %copy-done) | copy-start | bytes 6291460
  348.7 14.9 %collective-permute-start.30 = (bf16[4,128,512]{2,1,0:T(8,128)(2,1)S(1)}, bf16[4,128,512]{2,1,0:T(8,128)(2,1)S(1)}, u32[]{:S(2)}, u32[]{:S(2)}) collective-permute-start(bf16[4,128,512]{2,1,0:T(8,128)(2,1)S(1)} %pad_maximum_fusion.2), channel_id=1, source_target_pairs={{0,16},{8,24},{16,0},{24,8},{1,17},{9,25},{17,1},{25,9},{2,18},{10... | collective-permute-start | bytes 1572872 | tf_op jit(solution)/shard_map/ppermute | solution.py:703
  355.9 25.8 %collective-permute-start.24 = (bf16[2,4,128,512]{3,2,1,0:T(8,128)(2,1)S(1)}, bf16[2,4,128,512]{3,2,1,0:T(8,128)(2,1)S(1)}, u32[]{:S(2)}, u32[]{:S(2)}) collective-permute-start(bf16[2,4,128,512]{3,2,1,0:T(8,128)(2,1)S(1)} %pad_maximum_fusion.refs_0_), channel_id=1, source_target_pairs={{0,16},{8,24},{16,0},{24,8},{1,17},{9,25},{17,1},{25,9},{2,18},{10... | collective-permute-start | bytes 3145736 | tf_op jit(solution)/shard_map/ppermute | solution.py:703
  363.6 18.0 %collective-permute-start.31 = (bf16[8,128,512]{2,1,0:T(8,128)(2,1)S(1)}, bf16[8,128,512]{2,1,0:T(8,128)(2,1)S(1)}, u32[]{:S(2)}, u32[]{:S(2)}) collective-permute-start(bf16[8,128,512]{2,1,0:T(8,128)(2,1)S(1)} %constant_dynamic-update-slice_fusion.refs_4_), channel_id=1, source_target_pairs={{0,1},{1,0},{2,3},{3,2},{4,5},{5,4},{6,7},{7,6},{8,9},{9,8},{10,11... | collective-permute-start | bytes 3145736 | tf_op jit(solution)/shard_map/ppermute | solution.py:703
  365.5 17.5 %collective-permute-start.25 = (bf16[2,4,128,512]{3,2,1,0:T(8,128)(2,1)S(1)}, bf16[2,4,128,512]{3,2,1,0:T(8,128)(2,1)S(1)}, u32[]{:S(2)}, u32[]{:S(2)}) collective-permute-start(bf16[2,4,128,512]{3,2,1,0:T(8,128)(2,1)S(1)} %pad_maximum_fusion.refs_0_), channel_id=1, source_target_pairs={{0,8},{8,0},{16,24},{24,16},{1,9},{9,1},{17,25},{25,17},{2,10},{10... | collective-permute-start | bytes 3145736 | tf_op jit(solution)/shard_map/ppermute | solution.py:703
  365.5 17.5 %collective-permute-start.32 = (bf16[8,128,512]{2,1,0:T(8,128)(2,1)S(1)}, bf16[8,128,512]{2,1,0:T(8,128)(2,1)S(1)}, u32[]{:S(2)}, u32[]{:S(2)}) collective-permute-start(bf16[8,128,512]{2,1,0:T(8,128)(2,1)S(1)} %constant_dynamic-update-slice_fusion.refs_4_), channel_id=1, source_target_pairs={{0,8},{8,0},{16,24},{24,16},{1,9},{9,1},{17,25},{25,17},{2,10},{10... | collective-permute-start | bytes 3145736 | tf_op jit(solution)/shard_map/ppermute | solution.py:703
  381.7 2.7 collective-permute-start.26
  381.7 4.2 %collective-permute-start.33 = (bf16[8,128,512]{2,1,0:T(8,128)(2,1)S(1)}, bf16[8,128,512]{2,1,0:T(8,128)(2,1)S(1)}, u32[]{:S(2)}, u32[]{:S(2)}) collective-permute-start(bf16[8,128,512]{2,1,0:T(8,128)(2,1)S(1)} %collective-permute-done.31.refs_5_), channel_id=1, source_target_pairs={{0,8},{8,0},{16,24},{24,16},{1,9},{9,1},{17,25},{25,17},{2,10},{10... | collective-permute-start | bytes 3145736 | tf_op jit(solution)/shard_map/ppermute | solution.py:703

commit v7 on v6

--- a/solution.py
+++ b/solution.py
@@ -122,34 +122,82 @@
             late_out[:, 1, low // group - early, 0] = cotangent[0, rows].reshape(dealt)
 
 
-def sample_backward(offset, early, opening, closing, counts, *refs):
+def heads_back(heads, mixed, logs, d_mix, rows, live, d_query, add):
+    width = d_mix.shape[0]
+    head_size = width // HEADS
+    for pair in range(0, HEADS, 2):
+        d_keys, d_values = [], []
+        for head in (pair, pair + 1):
+            lanes = slice(head * head_size, (head + 1) * head_size)
+            keys = heads[0, 1, lanes]
+            values = heads[0, 2, lanes]
+            queries = heads[0, 0, lanes, rows]
+            grads = d_mix[lanes]
+            shared = column_sum(grads.astype(F32) * mixed[0, lanes, rows].astype(F32))
+            scores = jnp.where(live, dot(keys, queries, TN), NEGATIVE)
+            probs = jnp.exp(scores - logs[0, head : head + 1, rows])
+            d_probs = dot(values, grads, TN)
+            d_scores = (probs * (d_probs - shared)).astype(BF)
+            d_query[lanes] = (dot(keys, d_scores) * head_size ** (-0.5)).astype(BF)
+            d_keys.append(dot(d_scores, queries, NT))
+            d_values.append(dot(probs.astype(BF), grads, NT))
+        lanes = slice(pair * head_size, (pair + 2) * head_size)
+        add(lanes, jnp.concatenate(d_keys, axis=1), jnp.concatenate(d_values, axis=1))
+
+
+def sample_backward_early(
+    counts, d_early, heads, mixed, logs, weights, query_out, sums_out, weight_out, d_rows, d_mix, d_query, total
+):
+    samples = mixed.shape[2]
+    width = d_mix.shape[0]
+    group = d_early.shape[0] * BLOCK
+    rows = slice(0, d_rows.shape[0])
+    step = pl.program_id(0)
+
+    @pl.when(step == 0)
+    def _():
+        total[...] = jnp.zeros_like(total)
+
+    @pl.when(counts[2] + step < counts[1])
+    def _():
+        for deal in range(d_early.shape[1]):
+            part = d_early[:, deal, 0].reshape(group, width)
+            d_rows[deal * group : (deal + 1) * group] = part
+        d_mix[...] = dot(weights[3], d_rows[...], NT).astype(BF)
+        total[...] += dot(mixed[0, :, rows], d_rows[...])
+        live = row_index((samples, 1)) < counts[0]
+
+        def add(lanes, d_keys, d_values):
+            sums_out[0, 0, :, lanes] = d_keys
+            sums_out[0, 1, :, lanes] = d_values
+
+        heads_back(heads, mixed, logs, d_mix, rows, live, d_query, add)
+        query_out[0] = d_query[...].T
+
+    @pl.when(step == pl.num_programs(0) - 1)
+    def _():
+        weight_out[...] = total[...]
+
+
+def sample_backward(early, counts, *refs):
     if early:
-        d_early, *refs = refs
+        d_early, query_held, sums_held, weight_held, *refs = refs
     d_late, tokens, first, heads, mixed, logs, weights, norms, *refs = refs
-    if not opening:
-        _, total_in, norm_total_in, *refs = refs
-    grad_out, *refs = refs
-    if closing:
-        keep_out, send_out, norm_out, *refs = refs
-    else:
-        total_out, norm_out, *refs = refs
-    d_rows, d_mix, d_heads, d_turned, total, norm_total = refs
+    grad_out, keep_out, send_out, norm_out, d_rows, d_mix, d_query, d_turned, total, norm_total = refs
     samples, width = tokens.shape[1:]
-    head_size = width // HEADS
-    score_scale = head_size ** (-0.5)
     group = d_late.shape[0] * BLOCK
+    start = early * group
+    rows = slice(start, samples)
     step = pl.program_id(0)
 
     @pl.when(step == 0)
     def _():
-        if opening:
-            total[...] = jnp.zeros_like(total)
-            norm_total[...] = jnp.zeros_like(norm_total)
-        else:
-            total[...] = total_in[...]
-            norm_total[...] = norm_total_in[...]
-
-    feature_live = counts[2] + offset + step < counts[1]
+        total[...] = jnp.zeros_like(total)
+        if early:
+            total[3 * width :] = weight_held[...]
+        norm_total[...] = jnp.zeros_like(norm_total)
+
+    feature_live = counts[2] + step < counts[1]
 
     @pl.when(jnp.logical_not(feature_live))
     def _():
@@ -161,50 +209,38 @@
             deal = low // group
             part = d_early[:, deal, 0] if deal < early else d_late[:, deal - early, 0]
             d_rows[low : low + group] = part.reshape(group, width)
-        d_mix[...] = dot(weights[3], d_rows[...], NT).astype(BF)
-        total[3 * width :] += dot(mixed[0], d_rows[...])
+        d_mix[...] = dot(weights[3], d_rows[rows], NT).astype(BF)
+        total[3 * width :] += dot(mixed[0, :, rows], d_rows[rows])
         live = row_index((samples, 1)) < counts[0]
-        for pair in range(0, HEADS, 2):
-            d_keys, d_values = [], []
-            for head in (pair, pair + 1):
-                lanes = slice(head * head_size, (head + 1) * head_size)
-                keys = heads[0, 1, lanes]
-                values = heads[0, 2, lanes]
-                queries = heads[0, 0, lanes]
-                grads = d_mix[lanes]
-                shared = column_sum(grads.astype(F32) * mixed[0, lanes].astype(F32))
-                scores = dot(keys, queries, TN)
-                scores = jnp.where(live, scores, NEGATIVE)
-                probs = jnp.exp(scores - logs[0, head : head + 1])
-                d_probs = dot(values, grads, TN)
-                d_scores = (probs * (d_probs - shared)).astype(BF)
-                d_heads[lanes] = (dot(keys, d_scores) * score_scale).astype(BF)
-                d_keys.append(dot(d_scores, queries, NT).astype(BF))
-                d_values.append(dot(probs.astype(BF), grads, NT).astype(BF))
-            lanes = slice(pair * head_size, (pair + 2) * head_size)
-            d_turned[1, :, lanes] = jnp.concatenate(d_keys, axis=1)
-            d_turned[2, :, lanes] = jnp.concatenate(d_values, axis=1)
-        d_turned[0] = d_heads[...].T
+
+        def add(lanes, d_keys, d_values):
+            if early:
+                d_keys = d_keys + sums_held[0, 0, :, lanes]
+                d_values = d_values + sums_held[0, 1, :, lanes]
+            d_turned[1, :, lanes] = d_keys.astype(BF)
+            d_turned[2, :, lanes] = d_values.astype(BF)
+
+        heads_back(heads, mixed, logs, d_mix, rows, live, d_query, add)
+        d_turned[0, rows] = d_query[...].T
+        if early:
+            d_turned[0, :start] = query_held[0]
         for which in range(3):
             total[which * width : (which + 1) * width] += dot(first[0], d_turned[which], TN)
         for low in range(0, samples, ROWS):
-            rows = slice(low, low + ROWS)
-            d_first = dot(d_turned[0, rows], weights[0], NT)
-            d_first = d_first + dot(d_turned[1, rows], weights[1], NT)
-            d_first = d_first + dot(d_turned[2, rows], weights[2], NT)
-            normal, scale = normalize(tokens[0, rows].astype(F32))
+            part = slice(low, low + ROWS)
+            d_first = dot(d_turned[0, part], weights[0], NT)
+            d_first = d_first + dot(d_turned[1, part], weights[1], NT)
+            d_first = d_first + dot(d_turned[2, part], weights[2], NT)
+            normal, scale = normalize(tokens[0, part].astype(F32))
             norm_total[0:1] += column_sum(d_first * normal)
             norm_total[1:2] += column_sum(d_first)
             back = normalize_back(normal, scale, d_first, norms[0:1])
-            grad_out[0, rows] = (d_rows[rows].astype(F32) + back).astype(BF)
+            grad_out[0, part] = (d_rows[part].astype(F32) + back).astype(BF)
 
     @pl.when(step == pl.num_programs(0) - 1)
     def _():
-        if closing:
-            attention_parts(keep_out, total, counts[4], 0)
-            attention_parts(send_out, total, 1 - counts[4], 0)
-        else:
-            total_out[...] = total[...]
+        attention_parts(keep_out, total, counts[4], 0)
+        attention_parts(send_out, total, 1 - counts[4], 0)
         norm_out[...] = norm_total[...]
 
 
@@ -623,63 +659,81 @@
     )
 
 
-def run_sample_backward(counts, d_early, d_late, saved, weights, norms, chips, offset, held, closing):
-    devices, late, count, _, width = d_late.shape
+def run_sample_backward_early(counts, both, saved, weights):
+    devices, _, early, local, _, width = both.shape
+    _, _, heads, mixed, logs = saved
+    samples = mixed.shape[2]
+    queries = (local, early * devices * BLOCK, width)
+    sums = (local, 2, samples, width)
+    return call(
+        sample_backward_early,
+        local,
+        [(None, counts), (early_spec(both), both)]
+        + [(lead(value.shape), value) for value in (heads, mixed, logs)]
+        + [(half(weights.shape, 0), weights)],
+        [
+            (lead(queries), queries, BF),
+            (lead(sums), sums, F32),
+            (once((width, width)), (width, width), F32),
+        ],
+        [
+            (queries[1:], BF),
+            ((width, queries[1]), BF),
+            ((width, queries[1]), BF),
+            ((width, width), F32),
+        ],
+        22000,
+        "sample_backward_early",
+    )
+
+
+def early_spec(both):
+    devices, _, early, _, _, width = both.shape
+    return pl.BlockSpec(
+        (devices, None, early, 1, BLOCK, width), lambda step: (0, 0, 0, step, 0, 0)
+    )
+
+
+def run_sample_backward(counts, both, held, d_late, saved, weights, norms, chips):
+    devices, late, local, _, width = d_late.shape
     tokens = saved[0]
-    local, samples, _ = tokens.shape
-    early = 0 if d_early is None else d_early.shape[2]
+    samples = tokens.shape[1]
+    early = 0 if both is None else both.shape[2]
+    start = early * devices * BLOCK
     parts = (chips, devices, 4 * width // (2 * chips * devices), width)
-
-    def moved(shape):
-        zeros = (0,) * (len(shape) - 1)
-        return pl.BlockSpec((1,) + tuple(shape[1:]), lambda step: (step + offset,) + zeros)
-
     ins = [(None, counts)]
     if early:
-        ins.append(
-            (
-                pl.BlockSpec(
-                    (devices, None, early, 1, BLOCK, width),
-                    lambda step: (0, 0, 0, step + offset, 0, 0),
-                ),
-                d_early,
-            )
-        )
+        query, sums, weight = held
+        ins = ins + [(early_spec(both), both), (lead(query.shape), query), (lead(sums.shape), sums)]
+        ins.append((whole(weight.shape), weight))
     ins.append(
         (
             pl.BlockSpec((devices, late, 1, BLOCK, width), lambda step: (0, 0, step, 0, 0)),
             d_late,
         )
     )
-    ins = ins + [(moved(value.shape), value) for value in saved]
+    ins = ins + [(lead(value.shape), value) for value in saved]
     ins = ins + [(half(weights.shape, 0), weights), (whole(norms.shape), norms)]
-    sums, norm_sums = (4 * width, width), (2, width)
-    aliases = {}
-    if held is not None:
-        aliases = {len(ins): 0}
-        ins = ins + [(ANYWHERE, held[0]), (whole(sums), held[1]), (whole(norm_sums), held[2])]
-    outs = [(moved(tokens.shape), tokens.shape, BF)]
-    if closing:
-        outs = outs + [(once(parts), parts, BF), (once(parts), parts, BF)]
-    else:
-        outs = outs + [(once(sums), sums, F32)]
-    outs.append((once(norm_sums), norm_sums, F32))
     return call(
-        functools.partial(sample_backward, offset, early, held is None, closing),
-        count,
+        functools.partial(sample_backward, early),
+        local,
         ins,
-        outs,
+        [
+            (lead(tokens.shape), tokens.shape, BF),
+            (once(parts), parts, BF),
+            (once(parts), parts, BF),
+            (once((2, width)), (2, width), F32),
+        ],
         [
             ((samples, width), BF),
-            ((width, samples), BF),
-            ((width, samples), BF),
+            ((width, samples - start), BF),
+            ((width, samples - start), BF),
             ((3, samples, width), BF),
-            (sums, F32),
-            (norm_sums, F32),
+            ((4 * width, width), F32),
+            ((2, width), F32),
         ],
-        count * 11000,
+        30000,
         "sample_backward",
-        aliases,
     )
 
 
@@ -989,10 +1043,14 @@
         )
     came_d = exchange(dealt_d[0], "feat")
     parts_two = plane_parts(reduce_core(keep_two, send_two))
-    parts_two, dealt_y, came_d = lax.optimization_barrier((parts_two, dealt_y, came_d))
+    held = None
+    if late:
+        came_both, _ = lax.optimization_barrier((came_both, parts_two))
+        held = run_sample_backward_early(counts, came_both, saved, weights)
+    dealt_y, came_d, held = lax.optimization_barrier((dealt_y, came_d, held))
     came_y = exchange(dealt_y, "feat")
     input_grad, keep_one, send_one, norms_one = run_sample_backward(
-        counts, came_both, came_d, saved, weights, norm_params, chips, 0, None, True
+        counts, came_both, held, came_d, saved, weights, norm_params, chips
     )
     parts_two[0], came_y, input_grad, keep_one, send_one, norms_one = lax.optimization_barrier(
         (parts_two[0], came_y, input_grad, keep_one, send_one, norms_one)

time: 397 us -> 384 us (0.967)
  waiting for transfers between devices: 111 us -> 70.8 us
  Pallas kernels: 153 us -> 187 us
  starting transfers between devices: 68.2 us -> 60.9 us
    all_to_all x5, waiting for transfers between devices: 39.8 us -> 0.01 us  [exchange(): lax.all_to_all(values, axis, 0, 0, axis_index_groups=groups, tiled=True)]
    pallas_call x4 -> x5, Pallas kernels: 148 us -> 182 us  [call(): pl.pallas_call(body, grid=(grid,), in_specs=[pl.BlockSpec(memory_space=pl...]
    ppermute x6, starting transfers between devices: 14.8 us -> 7.88 us  [in_plane(): return lax.ppermute(values, ('task', 'feat'), pairs)]
  transfers between devices with their start and end apart: 39 -> 39, of which waited for: 18 -> 14; matrix products, arithmetic and copies ran while one was open for 3% -> 3% of each run, Pallas kernels for 38% -> 48%
where the time goes in v7:
time: 384 us; the launch traced here: 380 us
  Pallas kernels  187 us (49%)
  waiting for transfers between devices  70.8 us (18%)
  starting transfers between devices  60.9 us (16%)
  blocking collectives  31.4 us (8%)
  other arithmetic  15.3 us (4%)
  local copies, waits for them, and re-layouts  7.44 us (2%)
  between operations  6.61 us (2%)
    pallas_call x5, Pallas kernels, call(): pl.pallas_call(body, grid=(grid,), in_specs=[pl.BlockSpec(memory_space=pl...  182 us
    ppermute x28, waiting for transfers between devices, moved_by(): return lax.ppermute(values, axis, pairs)  70.8 us
    all_to_all x1, blocking collectives, exchange(): lax.all_to_all(values, axis, 0, 0, axis_index_groups=groups, tiled=True)  31.4 us
    ppermute x28, starting transfers between devices, moved_by(): return lax.ppermute(values, axis, pairs)  26.6 us
    all_to_all x5, starting transfers between devices, exchange(): lax.all_to_all(values, axis, 0, 0, axis_index_groups=groups, tiled=True)  26.3 us
    ppermute x6, starting transfers between devices, in_plane(): return lax.ppermute(values, ('task', 'feat'), pairs)  7.88 us
  transfers between devices with their start and end apart: 39, of which 14 were waited for; matrix products, arithmetic and copies ran while one was open for 3% of the time, Pallas kernels for 48%

profile of v7, /device:TPU:0, one launch (start us, length us, event | category | flops | bytes accessed | tf_op | source)
XLA Modules:
  0.0 379.6 jit_solution(3686680945914097205)
XLA Ops:
  0.7 1.2 slice-done
  1.9 1.1 copy.42
  2.9 7.3 %all-to-all-start = ((bf16[8,2,4,16,512]{4,3,2,1,0:T(8,128)(2,1)}), bf16[8,2,4,16,512]{4,3,2,1,0:T(8,128)(2,1)S(1)}, u32[]{:S(2)}, u32[]{:S(2)}) async-start(bf16[8,2,4,16,512]{4,3,2,1,0:T(8,128)(2,1)} %bitcast.77), calls=%async_computation | async-start | bytes 2097152 | tf_op jit(solution)/shard_map/all_to_all | solution.py:752
  12.1 25.1 %sample_forward.1 = (bf16[8,2,4,16,512]{4,3,2,1,0:T(8,128)(2,1)}, bf16[8,2,2,4,16,512]{5,4,3,2,1,0:T(8,128)(2,1)}, bf16[4,512,512]{2,1,0:T(8,128)(2,1)}, bf16[4,...) custom-call(s32[5]{0:T(128)} %stack.62.counts, bf16[4,512,512]{2,1,0:T(8,128)(2,1)} %bitcast.96, ...), custom_call_target="tpu_custom_call" | custom-call | flops 28750000128 | bytes 16777216 | tf_op jit(solution)/shard_map/sample_forward/pallas_call | solution.py:509
  37.3 31.4 %all_to_all.30.refs_0_ = bf16[8,2,4,16,512]{4,3,2,1,0:T(8,128)(2,1)} all-to-all(bf16[8,2,4,16,512]{4,3,2,1,0:T(8,128)(2,1)} %get-tuple-element.95), channel_id=1, replica_groups=mesh['task'=4,'feat'=8] {'feat'}, dimensions={0} | all-to-all | bytes 2097152 | tf_op jit(solution)/shard_map/all_to_all | solution.py:752
  68.6 3.6 all-to-all-start.3
  72.2 53.3 %middle.2 = (bf16[8,2,2,4,16,512]{5,4,3,2,1,0:T(8,128)(2,1)}, f32[2048,512]{1,0:T(8,128)}, f32[2048,512]{1,0:T(8,128)}, f32[2048,512]{1,0:T(8,128)}, f32[4,512]{1,0:T(4,128)}) custom-call(s32[5]{0:T(128)} %stack.62.counts, bf16[8,2,4,16,512]{4,3,2,1,0:T(8,128)(2,1)} %all_to_all.30.refs_0_, bf16[8,2,4,16,512]{4,3,2,1,0:T(8,128)(2,1)} %copy-done.4, ...), custom_call_target="tpu_custom_call" | custom-call | flops 52899999744 | bytes 16777216 | tf_op jit(solution)/shard_map/middle/pallas_call | solution.py:509
  125.5 1.3 copy-done.2
  126.8 5.9 %all-to-all-start.2 = ((bf16[8,2,2,4,16,512]{5,4,3,2,1,0:T(8,128)(2,1)}), bf16[8,2,2,4,16,512]{5,4,3,2,1,0:T(8,128)(2,1)S(1)}, u32[]{:S(2)}, u32[]{:S(2)}) async-start(bf16[8,2,2,4,16,512]{5,4,3,2,1,0:T(8,128)(2,1)} %get-tuple-element.98), calls=%async_computation.2 | async-start | bytes 4194304 | tf_op jit(solution)/shard_map/all_to_all | solution.py:752
  132.7 50.3 %middle.3 = (bf16[8,2,4,16,512]{4,3,2,1,0:T(8,128)(2,1)}, bf16[8,2,4,16,512]{4,3,2,1,0:T(8,128)(2,1)}, bf16[2,8,192,512]{3,2,1,0:T(8,128)(2,1)}, bf16[2,8,192,512]{3,2,1,0:T(8,128)(2,1)}, f32[4,512]{1,0:T(4,128)}) custom-call(s32[5]{0:T(128)} %stack.62.counts, bf16[8,2,2,4,16,512]{5,4,3,2,1,0:T(8,128)(2,1)} %copy-done.2, ...), custom_call_target="tpu_custom_call" | custom-call | flops 52899999744 | bytes 16777216 | tf_op jit(solution)/shard_map/middle/pallas_call | solution.py:509
  183.4 6.0 %all-to-all-start.4 = ((bf16[8,2,4,16,512]{4,3,2,1,0:T(8,128)(2,1)}), bf16[8,2,4,16,512]{4,3,2,1,0:T(8,128)(2,1)S(1)}, u32[]{:S(2)}, u32[]{:S(2)}) async-start(bf16[8,2,4,16,512]{4,3,2,1,0:T(8,128)(2,1)} %get-tuple-element.112), calls=%async_computation.4 | async-start | bytes 2097152 | tf_op jit(solution)/shard_map/all_to_all | solution.py:752
  189.4 3.9 %add_convert_fusion = bf16[2,8,192,512]{3,2,1,0:T(8,128)(2,1)S(1)} fusion(bf16[2,8,192,512]{3,2,1,0:T(8,128)(2,1)} %collective-permute-done, bf16[2,8,192,512]{3,2,1,0:T(8,128)(2,1)} %get-tuple-element.109), kind=kLoop, calls=%fused_computation | loop fusion | flops 6291456 | bytes 9437184 | tf_op jit(solution)/shard_map/convert_element_type | solution.py:780
  193.3 1.5 dynamic-slice_bitcast_fusion
  194.8 2.8 collective-permute-start.3
  197.6 0.7 collective-permute-start.2
  198.3 20.2 %sample_backward_early.1 = (bf16[4,256,512]{2,1,0:T(8,128)(2,1)}, f32[4,2,512,512]{3,2,1,0:T(8,128)}, f32[512,512]{1,0:T(8,128)}) custom-call(s32[5]{0:T(128)} %stack.62.counts, bf16[8,2,2,4,16,512]{5,4,3,2,1,0:T(8,128)(2,1)} %copy-done, bf16[4,3,512,512]{3,2,1,0:T(8,128)(2,1)} %get-tuple-element.115.heads.refs_7_, ...), custom_call_target="tpu_custom_call" | custom-call | flops 25300000768 | bytes 16777216 | tf_op jit(solution)/shard_map/sample_backward_early/pallas_call | solution.py:509
  218.5 3.6 all-to-all-start.5
  222.1 33.3 %sample_backward.1 = (bf16[4,512,512]{2,1,0:T(8,128)(2,1)}, bf16[2,8,64,512]{3,2,1,0:T(8,128)(2,1)}, bf16[2,8,64,512]{3,2,1,0:T(8,128)(2,1)}, f32[2,512]{1,0:T(2,128)}) custom-call(s32[5]{0:T(128)} %stack.62.counts, bf16[8,2,2,4,16,512]{5,4,3,2,1,0:T(8,128)(2,1)} %copy-done, bf16[4,256,512]{2,1,0:T(8,128)(2,1)} %get-tuple-element.122.refs_1_, ...), custom_call_target="tpu_custom_call" | custom-call | flops 34500001792 | bytes 16777216 | tf_op jit(solution)/shard_map/sample_backward/pallas_call | solution.py:509
  255.5 2.2 add_convert_fusion.2
  257.7 1.3 collective-permute-start.7
  259.0 3.5 collective-permute-start.6
  262.5 1.1 collective-permute-start.4
  264.0 0.9 dynamic-slice_bitcast_fusion.6
  264.9 2.9 collective-permute-start.9
  267.9 1.5 collective-permute-start.8
  269.4 10.3 %collective-permute-done.5 = bf16[192,512]{1,0:T(8,128)(2,1)S(1)} collective-permute-done((bf16[192,512]{1,0:T(8,128)(2,1)S(1)}, bf16[192,512]{1,0:T(8,128)(2,1)S(1)}, u32[]{:S(2)}, u32[]{:S(2)}) %collective-permute-start.5) | collective-permute-done | bytes 196640 | tf_op jit(solution)/shard_map/ppermute | solution.py:757
  279.9 1.2 fusion.2
  281.1 2.3 collective-permute-start.13
  283.4 0.8 collective-permute-start.12
  284.3 1.6 collective-permute-start.11
  285.9 0.7 multiply_reduce_fusion
  286.6 4.1 %collective-permute-done.12 = bf16[64,512]{1,0:T(8,128)(2,1)S(1)} collective-permute-done((bf16[64,512]{1,0:T(8,128)(2,1)S(1)}, bf16[64,512]{1,0:T(8,128)(2,1)S(1)}, u32[]{:S(2)}, u32[]{:S(2)}) %collective-permute-start.12) | collective-permute-done | bytes 65568 | tf_op jit(solution)/shard_map/ppermute | solution.py:757
  290.7 0.6 multiply_reduce_fusion.1
  292.9 1.6 collective-permute-start.19
  294.5 1.2 collective-permute-done.14
  296.2 3.2 collective-permute-done.15
  299.7 3.5 collective-permute-done.16
  303.1 3.7 collective-permute-done.17
  306.9 1.1 collective-permute-start.18
  308.0 3.5 collective-permute-done.18
  311.5 0.9 broadcast_select_fusion.3
  313.0 0.6 multiply_reduce_fusion.2
  315.0 1.0 fusion.19
  316.0 0.6 collective-permute-start.22
  316.7 0.8 collective-permute-start.21
  317.5 1.7 collective-permute-start.20
  319.2 0.8 fusion.17
  320.0 1.7 convert_bitcast_fusion
  321.8 1.0 collective-permute-start.27
  322.8 1.7 collective-permute-start.28
  324.5 2.0 collective-permute-start.29
  326.5 6.6 %collective-permute-done.21 = bf16[128,512]{1,0:T(8,128)(2,1)S(1)} collective-permute-done((bf16[128,512]{1,0:T(8,128)(2,1)S(1)}, bf16[128,512]{1,0:T(8,128)(2,1)S(1)}, u32[]{:S(2)}, u32[]{:S(2)}) %collective-permute-start.21) | collective-permute-done | bytes 131104 | tf_op jit(solution)/shard_map/ppermute | solution.py:757
  333.2 0.7 collective-permute-start.23
  333.9 1.7 collective-permute-done.28
  335.7 1.0 collective-permute-start.30
  336.8 5.7 %collective-permute-done.23 = bf16[4,128,512]{2,1,0:T(8,128)(2,1)S(1)} collective-permute-done((bf16[4,128,512]{2,1,0:T(8,128)(2,1)S(1)}, bf16[4,128,512]{2,1,0:T(8,128)(2,1)S(1)}, u32[]{:S(2)}, u32[]{:S(2)}) %collective-permute-start.23) | collective-permute-done | bytes 524320 | tf_op jit(solution)/shard_map/ppermute | solution.py:757
  342.5 1.0 collective-permute-start.24
  343.5 7.1 %collective-permute-done.30 = bf16[4,128,512]{2,1,0:T(8,128)(2,1)S(1)} collective-permute-done((bf16[4,128,512]{2,1,0:T(8,128)(2,1)S(1)}, bf16[4,128,512]{2,1,0:T(8,128)(2,1)S(1)}, u32[]{:S(2)}, u32[]{:S(2)}) %collective-permute-start.30) | collective-permute-done | bytes 524320 | tf_op jit(solution)/shard_map/ppermute | solution.py:757
  350.7 0.7 collective-permute-start.31
  351.9 17.2 %collective-permute-done.24.refs_1_ = bf16[2,4,128,512]{3,2,1,0:T(8,128)(2,1)S(1)} collective-permute-done((bf16[2,4,128,512]{3,2,1,0:T(8,128)(2,1)S(1)}, bf16[2,4,128,512]{3,2,1,0:T(8,128)(2,1)S(1)}, u32[]{:S(2)}, u32[]{:S(2)}) %collective-permute-start.24) | collective-permute-done | bytes 1048608 | tf_op jit(solution)/shard_map/ppermute | solution.py:757
  369.7 0.6 multiply_subtract_fusion.3
  370.4 1.4 collective-permute-done.26.refs_3_
  371.8 1.5 collective-permute-done.33.refs_7_
  373.3 5.0 %place_copies.1 = (bf16[4096,512]{1,0:T(8,128)(2,1)}, bf16[512,2048]{1,0:T(8,128)(2,1)}, bf16[2048,512]{1,0:T(8,128)(2,1)}, bf16[4,4,8,16,512]{4,3,2,1,0:T(8,128)(2,1)}) custom-call(s32[6]{0:T(128)S(1)} %pad_add_fusion.table, bf16[2,4,128,512]{3,2,1,0:T(8,128)(2,1)S(1)} %pad_maximum_fusion.refs_0_, ...), custom_call_target="tpu_custom_call" | custom-call | tf_op jit(solution)/shard_map/place_copies/pallas_call | solution.py:932
  (105 shorter events, 4.4 us)
Async XLA Ops:
  0.7 1.2 slice-start
  2.9 34.3 %all-to-all-start = ((bf16[8,2,4,16,512]{4,3,2,1,0:T(8,128)(2,1)}), bf16[8,2,4,16,512]{4,3,2,1,0:T(8,128)(2,1)S(1)}, u32[]{:S(2)}, u32[]{:S(2)}) async-start(bf16[8,2,4,16,512]{4,3,2,1,0:T(8,128)(2,1)} %bitcast.77), calls=%async_computation | async-start | bytes 2097152 | tf_op jit(solution)/shard_map/all_to_all | solution.py:752
  37.3 31.4 %copy-start.4 = (bf16[8,2,4,16,512]{4,3,2,1,0:T(8,128)(2,1)}, bf16[8,2,4,16,512]{4,3,2,1,0:T(8,128)(2,1)S(1)}, u32[]{:S(2)}) copy-start(bf16[8,2,4,16,512]{4,3,2,1,0:T(8,128)(2,1)S(1)} %all-to-all-done.refs_1_) | copy-start | bytes 3145732
  68.6 56.9 %all-to-all-start.3 = ((bf16[8,2,2,4,16,512]{5,4,3,2,1,0:T(8,128)(2,1)}), bf16[8,2,2,4,16,512]{5,4,3,2,1,0:T(8,128)(2,1)S(1)}, u32[]{:S(2)}, u32[]{:S(2)}) async-start(bf16[8,2,2,4,16,512]{5,4,3,2,1,0:T(8,128)(2,1)} %get-tuple-element.99), calls=%async_computation.3 | async-start | bytes 4194304 | tf_op jit(solution)/shard_map/all_to_all | solution.py:752
  125.5 1.3 copy-start.2
  126.8 56.3 %all-to-all-start.2 = ((bf16[8,2,2,4,16,512]{5,4,3,2,1,0:T(8,128)(2,1)}), bf16[8,2,2,4,16,512]{5,4,3,2,1,0:T(8,128)(2,1)S(1)}, u32[]{:S(2)}, u32[]{:S(2)}) async-start(bf16[8,2,2,4,16,512]{5,4,3,2,1,0:T(8,128)(2,1)} %get-tuple-element.98), calls=%async_computation.2 | async-start | bytes 4194304 | tf_op jit(solution)/shard_map/all_to_all | solution.py:752
  183.1 10.2 %copy-start = (bf16[8,2,2,4,16,512]{5,4,3,2,1,0:T(8,128)(2,1)}, bf16[8,2,2,4,16,512]{5,4,3,2,1,0:T(8,128)(2,1)S(1)}, u32[]{:S(2)}) copy-start(bf16[8,2,2,4,16,512]{5,4,3,2,1,0:T(8,128)(2,1)S(1)} %all-to-all-done.2.d_early.refs_0_.refs_8_) | copy-start | bytes 6291460
  183.1 6.3 %collective-permute-start = (bf16[2,8,192,512]{3,2,1,0:T(8,128)(2,1)}, bf16[2,8,192,512]{3,2,1,0:T(8,128)(2,1)}, u32[]{:S(2)}, u32[]{:S(2)}) collective-permute-start(bf16[2,8,192,512]{3,2,1,0:T(8,128)(2,1)} %get-tuple-element.110), channel_id=1, source_target_pairs={{0,8},{8,0},{16,24},{24,16},{1,9},{9,1},{17,25},{25,17},{2,10},{10... | collective-permute-start | bytes 9437192 | tf_op jit(solution)/shard_map/ppermute | solution.py:757
  183.4 35.1 %all-to-all-start.4 = ((bf16[8,2,4,16,512]{4,3,2,1,0:T(8,128)(2,1)}), bf16[8,2,4,16,512]{4,3,2,1,0:T(8,128)(2,1)S(1)}, u32[]{:S(2)}, u32[]{:S(2)}) async-start(bf16[8,2,4,16,512]{4,3,2,1,0:T(8,128)(2,1)} %get-tuple-element.112), calls=%async_computation.4 | async-start | bytes 2097152 | tf_op jit(solution)/shard_map/all_to_all | solution.py:752
  194.8 60.6 %collective-permute-start.3 = (bf16[4,192,512]{2,1,0:T(8,128)(2,1)}, bf16[4,192,512]{2,1,0:T(8,128)(2,1)}, u32[]{:S(2)}, u32[]{:S(2)}) collective-permute-start(bf16[4,192,512]{2,1,0:T(8,128)(2,1)} %get-tuple-element.175), channel_id=1, source_target_pairs={{0,17},{1,16},{2,19},{3,18},{4,21},{5,20},{6,23},{7,22},{8,25},{9,... | collective-permute-start | bytes 2359304 | tf_op jit(solution)/shard_map/ppermute | solution.py:790
  197.6 57.9 %collective-permute-start.2 = (bf16[4,192,512]{2,1,0:T(8,128)(2,1)}, bf16[4,192,512]{2,1,0:T(8,128)(2,1)}, u32[]{:S(2)}, u32[]{:S(2)}) collective-permute-start(bf16[4,192,512]{2,1,0:T(8,128)(2,1)} %get-tuple-element.176), channel_id=1, source_target_pairs={{0,16},{1,17},{2,18},{3,19},{4,20},{5,21},{6,22},{7,23},{8,24},{9,... | collective-permute-start | bytes 2359304 | tf_op jit(solution)/shard_map/ppermute | solution.py:790
  198.3 57.2 %collective-permute-start.1 = (bf16[4,192,512]{2,1,0:T(8,128)(2,1)}, bf16[4,192,512]{2,1,0:T(8,128)(2,1)}, u32[]{:S(2)}, u32[]{:S(2)}) collective-permute-start(bf16[4,192,512]{2,1,0:T(8,128)(2,1)} %get-tuple-element.177), channel_id=1, source_target_pairs={{0,1},{1,0},{2,3},{3,2},{4,5},{5,4},{6,7},{7,6},{8,9},{9,8},{10,11... | collective-permute-start | bytes 2359304 | tf_op jit(solution)/shard_map/ppermute | solution.py:790
  218.5 3.6 copy-start.5
  218.5 36.9 %all-to-all-start.5 = ((bf16[8,2,4,16,512]{4,3,2,1,0:T(8,128)(2,1)}), bf16[8,2,4,16,512]{4,3,2,1,0:T(8,128)(2,1)S(1)}, u32[]{:S(2)}, u32[]{:S(2)}) async-start(bf16[8,2,4,16,512]{4,3,2,1,0:T(8,128)(2,1)} %get-tuple-element.121), calls=%async_computation.5 | async-start | bytes 2097152 | tf_op jit(solution)/shard_map/all_to_all | solution.py:752
  255.4 2.3 copy-start.19
  255.4 8.2 %copy-start.3 = (bf16[2,8,64,512]{3,2,1,0:T(8,128)(2,1)S(1)}, bf16[2,8,64,512]{3,2,1,0:T(8,128)(2,1)}, u32[]{:S(2)}) copy-start(bf16[2,8,64,512]{3,2,1,0:T(8,128)(2,1)} %get-tuple-element.140) | copy-start | bytes 3145732
  257.7 6.0 %collective-permute-start.7 = (bf16[2,8,64,512]{3,2,1,0:T(8,128)(2,1)S(1)}, bf16[2,8,64,512]{3,2,1,0:T(8,128)(2,1)S(1)}, u32[]{:S(2)}, u32[]{:S(2)}) collective-permute-start(bf16[2,8,64,512]{3,2,1,0:T(8,128)(2,1)S(1)} %copy-done.19), channel_id=1, source_target_pairs={{0,8},{8,0},{16,24},{24,16},{1,9},{9,1},{17,25},{25,17},{2,10},{10... | collective-permute-start | bytes 3145736 | tf_op jit(solution)/shard_map/ppermute | solution.py:757
  259.0 8.9 %collective-permute-start.6 = (bf16[192,512]{1,0:T(8,128)(2,1)S(1)}, bf16[192,512]{1,0:T(8,128)(2,1)S(1)}, u32[]{:S(2)}, u32[]{:S(2)}) collective-permute-start(bf16[192,512]{1,0:T(8,128)(2,1)S(1)} %get-tuple-element.139), channel_id=1, source_target_pairs={{0,6},{1,7},{2,0},{3,1},{4,2},{5,3},{6,4},{7,5},{8,14},{9,15},{10,... | collective-permute-start | bytes 589832 | tf_op jit(solution)/shard_map/ppermute | solution.py:757
  262.5 17.1 %collective-permute-start.5 = (bf16[192,512]{1,0:T(8,128)(2,1)S(1)}, bf16[192,512]{1,0:T(8,128)(2,1)S(1)}, u32[]{:S(2)}, u32[]{:S(2)}) collective-permute-start(bf16[192,512]{1,0:T(8,128)(2,1)S(1)} %get-tuple-element.138), channel_id=1, source_target_pairs={{0,4},{1,5},{2,6},{3,7},{4,0},{5,1},{6,2},{7,3},{8,12},{9,13},{10,... | collective-permute-start | bytes 589832 | tf_op jit(solution)/shard_map/ppermute | solution.py:757
  262.5 17.1 %collective-permute-start.4 = (bf16[192,512]{1,0:T(8,128)(2,1)S(1)}, bf16[192,512]{1,0:T(8,128)(2,1)S(1)}, u32[]{:S(2)}, u32[]{:S(2)}) collective-permute-start(bf16[192,512]{1,0:T(8,128)(2,1)S(1)} %get-tuple-element.137), channel_id=1, source_target_pairs={{0,2},{1,3},{2,4},{3,5},{4,6},{5,7},{6,0},{7,1},{8,10},{9,11},{10,... | collective-permute-start | bytes 589832 | tf_op jit(solution)/shard_map/ppermute | solution.py:757
  264.9 27.8 %copy-start.17 = (f32[4,512]{1,0:T(4,128)S(1)}, f32[4,512]{1,0:T(4,128)}, u32[]{:S(2)}) copy-start(f32[4,512]{1,0:T(4,128)} %get-tuple-element.132) | copy-start | bytes 24580
  264.9 27.8 %copy-start.18 = (f32[2,512]{1,0:T(2,128)S(1)}, f32[2,512]{1,0:T(2,128)}, u32[]{:S(2)}) copy-start(f32[2,512]{1,0:T(2,128)} %get-tuple-element.131) | copy-start | bytes 12292
  264.9 14.9 %collective-permute-start.10 = (bf16[4,64,512]{2,1,0:T(8,128)(2,1)}, bf16[4,64,512]{2,1,0:T(8,128)(2,1)S(1)}, u32[]{:S(2)}, u32[]{:S(2)}) collective-permute-start(bf16[4,64,512]{2,1,0:T(8,128)(2,1)} %get-tuple-element.180), channel_id=1, source_target_pairs={{0,17},{1,16},{2,19},{3,18},{4,21},{5,20},{6,23},{7,22},{8,25},{9,... | collective-permute-start | bytes 786440 | tf_op jit(solution)/shard_map/ppermute | solution.py:790
  264.9 14.9 %collective-permute-start.9 = (bf16[4,64,512]{2,1,0:T(8,128)(2,1)}, bf16[4,64,512]{2,1,0:T(8,128)(2,1)}, u32[]{:S(2)}, u32[]{:S(2)}) collective-permute-start(bf16[4,64,512]{2,1,0:T(8,128)(2,1)} %get-tuple-element.181), channel_id=1, source_target_pairs={{0,16},{1,17},{2,18},{3,19},{4,20},{5,21},{6,22},{7,23},{8,24},{9,... | collective-permute-start | bytes 786440 | tf_op jit(solution)/shard_map/ppermute | solution.py:790
  267.9 11.9 %collective-permute-start.8 = (bf16[4,64,512]{2,1,0:T(8,128)(2,1)}, bf16[4,64,512]{2,1,0:T(8,128)(2,1)}, u32[]{:S(2)}, u32[]{:S(2)}) collective-permute-start(bf16[4,64,512]{2,1,0:T(8,128)(2,1)} %get-tuple-element.179), channel_id=1, source_target_pairs={{0,1},{1,0},{2,3},{3,2},{4,5},{5,4},{6,7},{7,6},{8,9},{9,8},{10,11... | collective-permute-start | bytes 786440 | tf_op jit(solution)/shard_map/ppermute | solution.py:790
  279.8 35.2 %copy-start.6 = (f32[128,512]{1,0:T(8,128)S(1)}, f32[128,512]{1,0:T(8,128)}, u32[]{:S(2)}) copy-start(f32[128,512]{1,0:T(8,128)} %param.25) | copy-start | bytes 786436
  279.8 35.2 %copy-start.7 = (f32[128,512]{1,0:T(8,128)S(1)}, f32[128,512]{1,0:T(8,128)}, u32[]{:S(2)}) copy-start(f32[128,512]{1,0:T(8,128)} %param.28) | copy-start | bytes 786436
  279.8 35.2 %copy-start.8 = (f32[128,512]{1,0:T(8,128)S(1)}, f32[128,512]{1,0:T(8,128)}, u32[]{:S(2)}) copy-start(f32[128,512]{1,0:T(8,128)} %param.32) | copy-start | bytes 786436
  281.1 5.5 %collective-permute-start.13 = (bf16[64,512]{1,0:T(8,128)(2,1)S(1)}, bf16[64,512]{1,0:T(8,128)(2,1)S(1)}, u32[]{:S(2)}, u32[]{:S(2)}) collective-permute-start(bf16[64,512]{1,0:T(8,128)(2,1)S(1)} %get-tuple-element.145), channel_id=1, source_target_pairs={{0,6},{1,7},{2,0},{3,1},{4,2},{5,3},{6,4},{7,5},{8,14},{9,15},{10,... | collective-permute-start | bytes 196616 | tf_op jit(solution)/shard_map/ppermute | solution.py:757
  283.4 7.3 %collective-permute-start.12 = (bf16[64,512]{1,0:T(8,128)(2,1)S(1)}, bf16[64,512]{1,0:T(8,128)(2,1)S(1)}, u32[]{:S(2)}, u32[]{:S(2)}) collective-permute-start(bf16[64,512]{1,0:T(8,128)(2,1)S(1)} %get-tuple-element.144), channel_id=1, source_target_pairs={{0,4},{1,5},{2,6},{3,7},{4,0},{5,1},{6,2},{7,3},{8,12},{9,13},{10,... | collective-permute-start | bytes 196616 | tf_op jit(solution)/shard_map/ppermute | solution.py:757
  284.3 6.5 %collective-permute-start.11 = (bf16[64,512]{1,0:T(8,128)(2,1)S(1)}, bf16[64,512]{1,0:T(8,128)(2,1)S(1)}, u32[]{:S(2)}, u32[]{:S(2)}) collective-permute-start(bf16[64,512]{1,0:T(8,128)(2,1)S(1)} %get-tuple-element.143), channel_id=1, source_target_pairs={{0,2},{1,3},{2,4},{3,5},{4,6},{5,7},{6,0},{7,1},{8,10},{9,11},{10,... | collective-permute-start | bytes 196616 | tf_op jit(solution)/shard_map/ppermute | solution.py:757
  286.6 32.6 %copy-start.9 = (f32[64,512]{1,0:T(8,128)S(1)}, f32[64,512]{1,0:T(8,128)}, u32[]{:S(2)}) copy-start(f32[64,512]{1,0:T(8,128)} %param.27) | copy-start | bytes 393220
  286.6 32.6 %copy-start.10 = (f32[64,512]{1,0:T(8,128)S(1)}, f32[64,512]{1,0:T(8,128)}, u32[]{:S(2)}) copy-start(f32[64,512]{1,0:T(8,128)} %param.30) | copy-start | bytes 393220
  286.6 32.6 %copy-start.11 = (f32[64,512]{1,0:T(8,128)S(1)}, f32[64,512]{1,0:T(8,128)}, u32[]{:S(2)}) copy-start(f32[64,512]{1,0:T(8,128)} %param.34) | copy-start | bytes 393220
  292.9 18.7 %collective-permute-start.19 = (f32[64,512]{1,0:T(8,128)S(1)}, f32[64,512]{1,0:T(8,128)}, u32[]{:S(2)}, u32[]{:S(2)}) collective-permute-start(f32[64,512]{1,0:T(8,128)S(1)} %broadcast_select_fusion), channel_id=1, source_target_pairs={{0,16},{8,24},{16,0},{24,8},{1,17},{9,25},{17,1},{25,9},{2,18},{10... | collective-permute-start | bytes 393224 | tf_op jit(solution)/shard_map/ppermute | solution.py:757
  294.5 1.2 collective-permute-start.14
  295.6 3.7 collective-permute-start.15
  299.4 3.7 collective-permute-start.16
  303.1 3.7 collective-permute-start.17
  306.9 4.6 %collective-permute-start.18 = (f32[8,512]{1,0:T(8,128)S(1)}, f32[8,512]{1,0:T(8,128)S(1)}, u32[]{:S(2)}, u32[]{:S(2)}) collective-permute-start(f32[8,512]{1,0:T(8,128)S(1)} %add.311), channel_id=1, source_target_pairs={{0,4},{1,5},{2,6},{3,7},{4,0},{5,1},{6,2},{7,3},{8,12},{9,13},{10,... | collective-permute-start | bytes 49160 | tf_op jit(solution)/shard_map/ppermute | solution.py:757
  308.0 12.0 %copy-start.12 = (f32[512,64]{0,1:T(8,128)S(1)}, f32[512,64]{0,1:T(8,128)}, u32[]{:S(2)}) copy-start(f32[512,64]{0,1:T(8,128)} %param.26) | copy-start | bytes 393220
  308.0 12.0 %copy-start.13 = (f32[512,64]{0,1:T(8,128)S(1)}, f32[512,64]{0,1:T(8,128)}, u32[]{:S(2)}) copy-start(f32[512,64]{0,1:T(8,128)} %param.29) | copy-start | bytes 393220
  316.0 8.5 %collective-permute-start.22 = (bf16[128,512]{1,0:T(8,128)(2,1)S(1)}, bf16[128,512]{1,0:T(8,128)(2,1)S(1)}, u32[]{:S(2)}, u32[]{:S(2)}) collective-permute-start(bf16[128,512]{1,0:T(8,128)(2,1)S(1)} %get-tuple-element.169), channel_id=1, source_target_pairs={{0,6},{1,7},{2,0},{3,1},{4,2},{5,3},{6,4},{7,5},{8,14},{9,15},{10,... | collective-permute-start | bytes 393224 | tf_op jit(solution)/shard_map/ppermute | solution.py:757
  316.7 16.4 %collective-permute-start.21 = (bf16[128,512]{1,0:T(8,128)(2,1)S(1)}, bf16[128,512]{1,0:T(8,128)(2,1)S(1)}, u32[]{:S(2)}, u32[]{:S(2)}) collective-permute-start(bf16[128,512]{1,0:T(8,128)(2,1)S(1)} %get-tuple-element.169), channel_id=1, source_target_pairs={{0,4},{1,5},{2,6},{3,7},{4,0},{5,1},{6,2},{7,3},{8,12},{9,13},{10,... | collective-permute-start | bytes 393224 | tf_op jit(solution)/shard_map/ppermute | solution.py:757
  317.5 15.6 %collective-permute-start.20 = (bf16[128,512]{1,0:T(8,128)(2,1)S(1)}, bf16[128,512]{1,0:T(8,128)(2,1)S(1)}, u32[]{:S(2)}, u32[]{:S(2)}) collective-permute-start(bf16[128,512]{1,0:T(8,128)(2,1)S(1)} %get-tuple-element.169), channel_id=1, source_target_pairs={{0,2},{1,3},{2,4},{3,5},{4,6},{5,7},{6,0},{7,1},{8,10},{9,11},{10,... | collective-permute-start | bytes 393224 | tf_op jit(solution)/shard_map/ppermute | solution.py:757
  321.8 12.2 %collective-permute-start.27 = (bf16[128,512]{1,0:T(8,128)(2,1)S(1)}, bf16[128,512]{1,0:T(8,128)(2,1)S(1)}, u32[]{:S(2)}, u32[]{:S(2)}) collective-permute-start(bf16[128,512]{1,0:T(8,128)(2,1)S(1)} %get-tuple-element.195), channel_id=1, source_target_pairs={{0,2},{1,3},{2,4},{3,5},{4,6},{5,7},{6,0},{7,1},{8,10},{9,11},{10,... | collective-permute-start | bytes 393224 | tf_op jit(solution)/shard_map/ppermute | solution.py:757
  322.8 12.8 %collective-permute-start.28 = (bf16[128,512]{1,0:T(8,128)(2,1)S(1)}, bf16[128,512]{1,0:T(8,128)(2,1)S(1)}, u32[]{:S(2)}, u32[]{:S(2)}) collective-permute-start(bf16[128,512]{1,0:T(8,128)(2,1)S(1)} %get-tuple-element.195), channel_id=1, source_target_pairs={{0,4},{1,5},{2,6},{3,7},{4,0},{5,1},{6,2},{7,3},{8,12},{9,13},{10,... | collective-permute-start | bytes 393224 | tf_op jit(solution)/shard_map/ppermute | solution.py:757
  324.5 11.1 %collective-permute-start.29 = (bf16[128,512]{1,0:T(8,128)(2,1)S(1)}, bf16[128,512]{1,0:T(8,128)(2,1)S(1)}, u32[]{:S(2)}, u32[]{:S(2)}) collective-permute-start(bf16[128,512]{1,0:T(8,128)(2,1)S(1)} %get-tuple-element.195), channel_id=1, source_target_pairs={{0,6},{1,7},{2,0},{3,1},{4,2},{5,3},{6,4},{7,5},{8,14},{9,15},{10,... | collective-permute-start | bytes 393224 | tf_op jit(solution)/shard_map/ppermute | solution.py:757
  333.2 9.2 %collective-permute-start.23 = (bf16[4,128,512]{2,1,0:T(8,128)(2,1)S(1)}, bf16[4,128,512]{2,1,0:T(8,128)(2,1)S(1)}, u32[]{:S(2)}, u32[]{:S(2)}) collective-permute-start(bf16[4,128,512]{2,1,0:T(8,128)(2,1)S(1)} %get-tuple-element.187), channel_id=1, source_target_pairs={{0,1},{1,0},{2,3},{3,2},{4,5},{5,4},{6,7},{7,6},{8,9},{9,8},{10,11... | collective-permute-start | bytes 1572872 | tf_op jit(solution)/shard_map/ppermute | solution.py:757
  335.7 34.0 %copy-start.14 = (f32[6,512]{1,0:T(8,128)S(1)}, f32[6,512]{1,0:T(8,128)}, u32[]{:S(2)}) copy-start(f32[6,512]{1,0:T(8,128)} %refs_11_.1) | copy-start | bytes 36868
  335.7 34.0 %copy-start.15 = (f32[6,512]{1,0:T(8,128)S(1)}, f32[6,512]{1,0:T(8,128)}, u32[]{:S(2)}) copy-start(f32[6,512]{1,0:T(8,128)} %param.31) | copy-start | bytes 36868
  335.7 34.0 %copy-start.16 = (f32[6,512]{1,0:T(8,128)S(1)}, f32[6,512]{1,0:T(8,128)}, u32[]{:S(2)}) copy-start(f32[6,512]{1,0:T(8,128)} %param.35) | copy-start | bytes 36868
  335.7 37.5 %copy-start.1 = (bf16[8,2,2,4,16,512]{5,4,3,2,1,0:T(8,128)(2,1)S(1)}, bf16[8,2,2,4,16,512]{5,4,3,2,1,0:T(8,128)(2,1)}, u32[]{:S(2)}) copy-start(bf16[8,2,2,4,16,512]{5,4,3,2,1,0:T(8,128)(2,1)} %copy-done) | copy-start | bytes 6291460
  335.7 14.9 %collective-permute-start.30 = (bf16[4,128,512]{2,1,0:T(8,128)(2,1)S(1)}, bf16[4,128,512]{2,1,0:T(8,128)(2,1)S(1)}, u32[]{:S(2)}, u32[]{:S(2)}) collective-permute-start(bf16[4,128,512]{2,1,0:T(8,128)(2,1)S(1)} %pad_maximum_fusion.2), channel_id=1, source_target_pairs={{0,16},{8,24},{16,0},{24,8},{1,17},{9,25},{17,1},{25,9},{2,18},{10... | collective-permute-start | bytes 1572872 | tf_op jit(solution)/shard_map/ppermute | solution.py:757
  342.5 26.6 %collective-permute-start.24 = (bf16[2,4,128,512]{3,2,1,0:T(8,128)(2,1)S(1)}, bf16[2,4,128,512]{3,2,1,0:T(8,128)(2,1)S(1)}, u32[]{:S(2)}, u32[]{:S(2)}) collective-permute-start(bf16[2,4,128,512]{3,2,1,0:T(8,128)(2,1)S(1)} %pad_maximum_fusion.refs_0_), channel_id=1, source_target_pairs={{0,16},{8,24},{16,0},{24,8},{1,17},{9,25},{17,1},{25,9},{2,18},{10... | collective-permute-start | bytes 3145736 | tf_op jit(solution)/shard_map/ppermute | solution.py:757
  350.7 18.4 %collective-permute-start.31 = (bf16[8,128,512]{2,1,0:T(8,128)(2,1)S(1)}, bf16[8,128,512]{2,1,0:T(8,128)(2,1)S(1)}, u32[]{:S(2)}, u32[]{:S(2)}) collective-permute-start(bf16[8,128,512]{2,1,0:T(8,128)(2,1)S(1)} %constant_dynamic-update-slice_fusion.refs_4_), channel_id=1, source_target_pairs={{0,1},{1,0},{2,3},{3,2},{4,5},{5,4},{6,7},{7,6},{8,9},{9,8},{10,11... | collective-permute-start | bytes 3145736 | tf_op jit(solution)/shard_map/ppermute | solution.py:757
  351.4 19.0 %collective-permute-start.25 = (bf16[2,4,128,512]{3,2,1,0:T(8,128)(2,1)S(1)}, bf16[2,4,128,512]{3,2,1,0:T(8,128)(2,1)S(1)}, u32[]{:S(2)}, u32[]{:S(2)}) collective-permute-start(bf16[2,4,128,512]{3,2,1,0:T(8,128)(2,1)S(1)} %pad_maximum_fusion.refs_0_), channel_id=1, source_target_pairs={{0,8},{8,0},{16,24},{24,16},{1,9},{9,1},{17,25},{25,17},{2,10},{10... | collective-permute-start | bytes 3145736 | tf_op jit(solution)/shard_map/ppermute | solution.py:757
  351.4 19.0 %collective-permute-start.32 = (bf16[8,128,512]{2,1,0:T(8,128)(2,1)S(1)}, bf16[8,128,512]{2,1,0:T(8,128)(2,1)S(1)}, u32[]{:S(2)}, u32[]{:S(2)}) collective-permute-start(bf16[8,128,512]{2,1,0:T(8,128)(2,1)S(1)} %constant_dynamic-update-slice_fusion.refs_4_), channel_id=1, source_target_pairs={{0,8},{8,0},{16,24},{24,16},{1,9},{9,1},{17,25},{25,17},{2,10},{10... | collective-permute-start | bytes 3145736 | tf_op jit(solution)/shard_map/ppermute | solution.py:757
  369.1 2.7 collective-permute-start.26
  369.1 4.2 %collective-permute-start.33 = (bf16[8,128,512]{2,1,0:T(8,128)(2,1)S(1)}, bf16[8,128,512]{2,1,0:T(8,128)(2,1)S(1)}, u32[]{:S(2)}, u32[]{:S(2)}) collective-permute-start(bf16[8,128,512]{2,1,0:T(8,128)(2,1)S(1)} %collective-permute-done.31.refs_5_), channel_id=1, source_target_pairs={{0,8},{8,0},{16,24},{24,16},{1,9},{9,1},{17,25},{25,17},{2,10},{10... | collective-permute-start | bytes 3145736 | tf_op jit(solution)/shard_map/ppermute | solution.py:757

commit v8 on v7

--- a/solution.py
+++ b/solution.py
@@ -275,6 +275,7 @@
     def take(count):
         return [refs.pop(0) for _ in range(count)]
 
+    step = pl.program_id(0)
     x_in, cot_in, weights, weight_in, weight_out, norms = take(6)
     if not opening:
         held = take(3)
@@ -295,13 +296,18 @@
             pltpu.make_async_copy(source, target, copied.at[place])
             for place, (source, target) in enumerate(zip(held, totals))
         ]
+    if not closing:
+        stores = [
+            pltpu.make_async_copy(source, target, copied.at[place])
+            for place, (source, target) in enumerate(zip(totals, given))
+        ]
+        last = step == pl.num_programs(0) - 1
     devices, _, local, _, width = x_in.shape
     features = devices * local
     cells = features * BLOCK
     head_size = width // HEADS
     score_scale = head_size ** (-0.5)
     hidden_width = weight_in.shape[1]
-    step = pl.program_id(0)
     first_sample = ((offset + step) * devices + counts[3]) * BLOCK
 
     @pl.when(step == 0)
@@ -386,6 +392,12 @@
             x_two[...] += dot(hidden.astype(BF), weight_out[cols])
 
         write_d(jnp.zeros((devices, local, BLOCK, width), BF))
+        if not closing:
+
+            @pl.when(last)
+            def _():
+                for store in stores[1:]:
+                    store.start()
 
     @pl.when(alive)
     def _():
@@ -407,6 +419,13 @@
             d_pre = (dot(live_grad[...], weight_out[cols], NT) * slope).astype(BF)
             total_in[cols] += dot(d_pre, third[...], TN)
             grad_rows[...] += dot(d_pre, weight_in[:, cols], NT)
+
+        if not closing:
+
+            @pl.when(last)
+            def _():
+                for store in stores[1:]:
+                    store.start()
 
 
         for low in range(0, cells, ROWS):
@@ -471,12 +490,7 @@
                         where[chip, :, which * own_ff : (which + 1) * own_ff] = part
                 attention_parts(where, total_attn, core, 2 * own_ff)
         else:
-            stores = [
-                pltpu.make_async_copy(source, target, copied.at[place])
-                for place, (source, target) in enumerate(zip(totals, given))
-            ]
-            for store in stores:
-                store.start()
+            stores[0].start()
             for store in stores:
                 store.wait()
         norm_out[...] = norm_total[...]
@@ -961,15 +975,22 @@
     )(table.astype(jnp.int32), *nears, *fars, *came_halves)
 
 
+def by_halves(parts):
+    while len(parts) > 1:
+        half_way = len(parts) // 2
+        parts = [one + two for one, two in zip(parts[:half_way], parts[half_way:])]
+    return parts[0]
+
+
 def total_of(values):
+    chips, layers = lax.axis_size("task") // 2, lax.axis_size("feat") // 2
     values = values + other_core(values)
-    chips = lax.axis_size("task") // 2
-    values = sum([along_y(values, shift) for shift in range(1, chips)], values)
-    bit = 1
-    while bit < lax.axis_size("feat"):
-        values = values + moved_by(values, "feat", lambda place: place ^ bit)
-        bit *= 2
-    return values
+    rows = []
+    for up in range(chips):
+        near = in_plane(values, up, 0) if up else values
+        rows.append(near + in_plane(values, up, 1))
+    values = by_halves(rows)
+    return by_halves([values] + [along_z(values, shift) for shift in range(1, layers)])
 
 
 def shards(

time: 384 us -> 379 us (0.987)
  starting transfers between devices: 60.9 us -> 67.7 us
  waiting for transfers between devices: 70.8 us -> 64.5 us
    ppermute x28 -> x27, waiting for transfers between devices: 70.8 us -> 57.3 us  [moved_by(): return lax.ppermute(values, axis, pairs)]
    ppermute x6 -> x9, waiting for transfers between devices: 0.02 us -> 7.14 us  [in_plane(): return lax.ppermute(values, ('task', 'feat'), pairs)]
    ppermute x6 -> x9, starting transfers between devices: 7.88 us -> 13.6 us  [in_plane(): return lax.ppermute(values, ('task', 'feat'), pairs)]
    ppermute x28 -> x27, starting transfers between devices: 26.6 us -> 27.8 us  [moved_by(): return lax.ppermute(values, axis, pairs)]
  transfers between devices with their start and end apart: 39 -> 41, of which waited for: 14 -> 19; matrix products, arithmetic and copies ran while one was open for 3% -> 3% of each run, Pallas kernels for 48% -> 48%
where the time goes in v8:
time: 379 us; the launch traced here: 374 us
  Pallas kernels  185 us (49%)
  starting transfers between devices  67.7 us (18%)
  waiting for transfers between devices  64.5 us (17%)
  blocking collectives  31.4 us (8%)
  other arithmetic  12.4 us (3%)
  between operations  6.67 us (2%)
  local copies, waits for them, and re-layouts  6.58 us (2%)
    pallas_call x5, Pallas kernels, call(): pl.pallas_call(body, grid=(grid,), in_specs=[pl.BlockSpec(memory_space=pl...  180 us
    ppermute x27, waiting for transfers between devices, moved_by(): return lax.ppermute(values, axis, pairs)  57.3 us
    all_to_all x1, blocking collectives, exchange(): lax.all_to_all(values, axis, 0, 0, axis_index_groups=groups, tiled=True)  31.4 us
    ppermute x27, starting transfers between devices, moved_by(): return lax.ppermute(values, axis, pairs)  27.8 us
    all_to_all x5, starting transfers between devices, exchange(): lax.all_to_all(values, axis, 0, 0, axis_index_groups=groups, tiled=True)  26.4 us
    ppermute x9, starting transfers between devices, in_plane(): return lax.ppermute(values, ('task', 'feat'), pairs)  13.6 us
  transfers between devices with their start and end apart: 41, of which 19 were waited for; matrix products, arithmetic and copies ran while one was open for 3% of the time, Pallas kernels for 48%

profile of v8, /device:TPU:0, one launch (start us, length us, event | category | flops | bytes accessed | tf_op | source)
XLA Modules:
  0.0 373.8 jit_solution(14493237093007907856)
XLA Ops:
  0.7 1.2 slice-done
  1.9 1.1 copy.42
  2.9 7.3 %all-to-all-start = ((bf16[8,2,4,16,512]{4,3,2,1,0:T(8,128)(2,1)}), bf16[8,2,4,16,512]{4,3,2,1,0:T(8,128)(2,1)S(1)}, u32[]{:S(2)}, u32[]{:S(2)}) async-start(bf16[8,2,4,16,512]{4,3,2,1,0:T(8,128)(2,1)} %bitcast.77), calls=%async_computation | async-start | bytes 2097152 | tf_op jit(solution)/shard_map/all_to_all | solution.py:766
  11.5 0.6 stack.62.counts
  12.1 25.1 %sample_forward.1 = (bf16[8,2,4,16,512]{4,3,2,1,0:T(8,128)(2,1)}, bf16[8,2,2,4,16,512]{5,4,3,2,1,0:T(8,128)(2,1)}, bf16[4,512,512]{2,1,0:T(8,128)(2,1)}, bf16[4,...) custom-call(s32[5]{0:T(128)} %stack.62.counts, bf16[4,512,512]{2,1,0:T(8,128)(2,1)} %bitcast.96, ...), custom_call_target="tpu_custom_call" | custom-call | flops 28750000128 | bytes 16777216 | tf_op jit(solution)/shard_map/sample_forward/pallas_call | solution.py:523
  37.3 31.4 %all_to_all.30.refs_0_ = bf16[8,2,4,16,512]{4,3,2,1,0:T(8,128)(2,1)} all-to-all(bf16[8,2,4,16,512]{4,3,2,1,0:T(8,128)(2,1)} %get-tuple-element.95), channel_id=1, replica_groups=mesh['task'=4,'feat'=8] {'feat'}, dimensions={0} | all-to-all | bytes 2097152 | tf_op jit(solution)/shard_map/all_to_all | solution.py:766
  68.6 3.6 all-to-all-start.3
  72.2 50.6 %middle.2 = (bf16[8,2,2,4,16,512]{5,4,3,2,1,0:T(8,128)(2,1)}, f32[2048,512]{1,0:T(8,128)}, f32[2048,512]{1,0:T(8,128)}, f32[2048,512]{1,0:T(8,128)}, f32[4,512]{1,0:T(4,128)}) custom-call(s32[5]{0:T(128)} %stack.62.counts, bf16[8,2,4,16,512]{4,3,2,1,0:T(8,128)(2,1)} %all_to_all.30.refs_0_, bf16[8,2,4,16,512]{4,3,2,1,0:T(8,128)(2,1)} %copy-done.4, ...), custom_call_target="tpu_custom_call" | custom-call | flops 52899999744 | bytes 16777216 | tf_op jit(solution)/shard_map/middle/pallas_call | solution.py:523
  122.9 1.3 copy-done.2
  124.2 5.9 %all-to-all-start.2 = ((bf16[8,2,2,4,16,512]{5,4,3,2,1,0:T(8,128)(2,1)}), bf16[8,2,2,4,16,512]{5,4,3,2,1,0:T(8,128)(2,1)S(1)}, u32[]{:S(2)}, u32[]{:S(2)}) async-start(bf16[8,2,2,4,16,512]{5,4,3,2,1,0:T(8,128)(2,1)} %get-tuple-element.98), calls=%async_computation.2 | async-start | bytes 4194304 | tf_op jit(solution)/shard_map/all_to_all | solution.py:766
  130.1 50.4 %middle.3 = (bf16[8,2,4,16,512]{4,3,2,1,0:T(8,128)(2,1)}, bf16[8,2,4,16,512]{4,3,2,1,0:T(8,128)(2,1)}, bf16[2,8,192,512]{3,2,1,0:T(8,128)(2,1)}, bf16[2,8,192,512]{3,2,1,0:T(8,128)(2,1)}, f32[4,512]{1,0:T(4,128)}) custom-call(s32[5]{0:T(128)} %stack.62.counts, bf16[8,2,2,4,16,512]{5,4,3,2,1,0:T(8,128)(2,1)} %copy-done.2, ...), custom_call_target="tpu_custom_call" | custom-call | flops 52899999744 | bytes 16777216 | tf_op jit(solution)/shard_map/middle/pallas_call | solution.py:523
  180.8 6.0 %all-to-all-start.4 = ((bf16[8,2,4,16,512]{4,3,2,1,0:T(8,128)(2,1)}), bf16[8,2,4,16,512]{4,3,2,1,0:T(8,128)(2,1)S(1)}, u32[]{:S(2)}, u32[]{:S(2)}) async-start(bf16[8,2,4,16,512]{4,3,2,1,0:T(8,128)(2,1)} %get-tuple-element.112), calls=%async_computation.4 | async-start | bytes 2097152 | tf_op jit(solution)/shard_map/all_to_all | solution.py:766
  186.8 3.9 %add_convert_fusion = bf16[2,8,192,512]{3,2,1,0:T(8,128)(2,1)S(1)} fusion(bf16[2,8,192,512]{3,2,1,0:T(8,128)(2,1)} %collective-permute-done, bf16[2,8,192,512]{3,2,1,0:T(8,128)(2,1)} %get-tuple-element.109), kind=kLoop, calls=%fused_computation | loop fusion | flops 6291456 | bytes 9437184 | tf_op jit(solution)/shard_map/convert_element_type | solution.py:794
  190.7 1.4 dynamic-slice_bitcast_fusion
  192.2 0.6 collective-permute-start.3
  192.8 2.9 collective-permute-start.2
  195.6 20.2 %sample_backward_early.1 = (bf16[4,256,512]{2,1,0:T(8,128)(2,1)}, f32[4,2,512,512]{3,2,1,0:T(8,128)}, f32[512,512]{1,0:T(8,128)}) custom-call(s32[5]{0:T(128)} %stack.62.counts, bf16[8,2,2,4,16,512]{5,4,3,2,1,0:T(8,128)(2,1)} %copy-done, bf16[4,3,512,512]{3,2,1,0:T(8,128)(2,1)} %get-tuple-element.115.heads.refs_7_, ...), custom_call_target="tpu_custom_call" | custom-call | flops 25300000768 | bytes 16777216 | tf_op jit(solution)/shard_map/sample_backward_early/pallas_call | solution.py:523
  215.9 3.6 all-to-all-start.5
  219.5 33.3 %sample_backward.1 = (bf16[4,512,512]{2,1,0:T(8,128)(2,1)}, bf16[2,8,64,512]{3,2,1,0:T(8,128)(2,1)}, bf16[2,8,64,512]{3,2,1,0:T(8,128)(2,1)}, f32[2,512]{1,0:T(2,128)}) custom-call(s32[5]{0:T(128)} %stack.62.counts, bf16[8,2,2,4,16,512]{5,4,3,2,1,0:T(8,128)(2,1)} %copy-done, bf16[4,256,512]{2,1,0:T(8,128)(2,1)} %get-tuple-element.122.refs_1_, ...), custom_call_target="tpu_custom_call" | custom-call | flops 34500001792 | bytes 16777216 | tf_op jit(solution)/shard_map/sample_backward/pallas_call | solution.py:523
  252.8 2.2 add_convert_fusion.2
  255.3 1.9 collective-permute-start.4
  257.2 0.6 collective-permute-done.7
  258.2 5.7 %collective-permute-start.10 = (bf16[4,64,512]{2,1,0:T(8,128)(2,1)S(1)}, bf16[4,64,512]{2,1,0:T(8,128)(2,1)S(1)}, u32[]{:S(2)}, u32[]{:S(2)}) collective-permute-start(bf16[4,64,512]{2,1,0:T(8,128)(2,1)S(1)} %get-tuple-element.180), channel_id=1, source_target_pairs={{0,17},{1,16},{2,19},{3,18},{4,21},{5,20},{6,23},{7,22},{8,25},{9,... | collective-permute-start | bytes 786440 | tf_op jit(solution)/shard_map/ppermute | solution.py:804
  264.0 0.6 collective-permute-start.8
  264.6 7.2 %collective-permute-done.5 = bf16[192,512]{1,0:T(8,128)(2,1)S(1)} collective-permute-done((bf16[192,512]{1,0:T(8,128)(2,1)S(1)}, bf16[192,512]{1,0:T(8,128)(2,1)S(1)}, u32[]{:S(2)}, u32[]{:S(2)}) %collective-permute-start.5) | collective-permute-done | bytes 196640 | tf_op jit(solution)/shard_map/ppermute | solution.py:771
  272.0 3.7 collective-permute-done.9
  276.2 3.0 collective-permute-start.13
  279.2 0.8 collective-permute-start.12
  280.4 0.7 multiply_reduce_fusion
  281.1 0.7 collective-permute-done.13
  281.7 4.6 %collective-permute-done.12 = bf16[64,512]{1,0:T(8,128)(2,1)S(1)} collective-permute-done((bf16[64,512]{1,0:T(8,128)(2,1)S(1)}, bf16[64,512]{1,0:T(8,128)(2,1)S(1)}, u32[]{:S(2)}, u32[]{:S(2)}) %collective-permute-start.12) | collective-permute-done | bytes 65568 | tf_op jit(solution)/shard_map/ppermute | solution.py:771
  286.4 0.6 multiply_reduce_fusion.1
  288.5 1.2 collective-permute-done.14
  289.7 2.2 collective-permute-start.16
  291.8 0.7 collective-permute-start.17
  292.5 0.9 collective-permute-start.15
  293.5 2.9 collective-permute-done.17
  296.5 3.8 %collective-permute-start.20 = (f32[8,512]{1,0:T(8,128)S(1)}, f32[8,512]{1,0:T(8,128)S(1)}, u32[]{:S(2)}, u32[]{:S(2)}) collective-permute-start(f32[8,512]{1,0:T(8,128)S(1)} %add_add_fusion.1), channel_id=1, source_target_pairs={{0,6},{1,7},{2,0},{3,1},{4,2},{5,3},{6,4},{7,5},{8,14},{9,15},{10,... | collective-permute-start | bytes 49160 | tf_op jit(solution)/shard_map/ppermute | solution.py:771
  300.4 1.8 collective-permute-start.21
  302.1 2.8 collective-permute-done.18
  305.5 0.5 slice.20
  306.0 0.6 multiply_reduce_fusion.2
  308.0 1.0 fusion.19
  309.0 0.6 collective-permute-start.24
  309.6 2.3 collective-permute-start.23
  311.9 2.0 collective-permute-start.22
  314.0 0.8 fusion.17
  314.8 0.8 convert_bitcast_fusion
  315.7 2.3 collective-permute-start.30
  318.0 1.5 collective-permute-start.31
  319.5 9.9 %collective-permute-done.23 = bf16[128,512]{1,0:T(8,128)(2,1)S(1)} collective-permute-done((bf16[128,512]{1,0:T(8,128)(2,1)S(1)}, bf16[128,512]{1,0:T(8,128)(2,1)S(1)}, u32[]{:S(2)}, u32[]{:S(2)}) %collective-permute-start.23) | collective-permute-done | bytes 131104 | tf_op jit(solution)/shard_map/ppermute | solution.py:771
  329.5 1.2 collective-permute-start.25
  330.9 0.9 collective-permute-done.31
  331.9 1.8 collective-permute-start.32
  333.8 5.6 %collective-permute-done.25 = bf16[4,128,512]{2,1,0:T(8,128)(2,1)S(1)} collective-permute-done((bf16[4,128,512]{2,1,0:T(8,128)(2,1)S(1)}, bf16[4,128,512]{2,1,0:T(8,128)(2,1)S(1)}, u32[]{:S(2)}, u32[]{:S(2)}) %collective-permute-start.25) | collective-permute-done | bytes 524320 | tf_op jit(solution)/shard_map/ppermute | solution.py:771
  339.4 1.8 collective-permute-start.26
  341.2 5.7 %collective-permute-done.32 = bf16[4,128,512]{2,1,0:T(8,128)(2,1)S(1)} collective-permute-done((bf16[4,128,512]{2,1,0:T(8,128)(2,1)S(1)}, bf16[4,128,512]{2,1,0:T(8,128)(2,1)S(1)}, u32[]{:S(2)}, u32[]{:S(2)}) %collective-permute-start.32) | collective-permute-done | bytes 524320 | tf_op jit(solution)/shard_map/ppermute | solution.py:771
  346.9 1.2 collective-permute-start.33
  348.6 14.7 %collective-permute-done.26.refs_1_ = bf16[2,4,128,512]{3,2,1,0:T(8,128)(2,1)S(1)} collective-permute-done((bf16[2,4,128,512]{3,2,1,0:T(8,128)(2,1)S(1)}, bf16[2,4,128,512]{3,2,1,0:T(8,128)(2,1)S(1)}, u32[]{:S(2)}, u32[]{:S(2)}) %collective-permute-start.26) | collective-permute-done | bytes 1048608 | tf_op jit(solution)/shard_map/ppermute | solution.py:771
  363.3 0.5 collective-permute-start.35
  363.9 0.6 multiply_subtract_fusion.3
  364.5 1.4 collective-permute-done.28.refs_3_
  365.9 1.5 collective-permute-done.35.refs_7_
  367.5 5.0 %place_copies.1 = (bf16[4096,512]{1,0:T(8,128)(2,1)}, bf16[512,2048]{1,0:T(8,128)(2,1)}, bf16[2048,512]{1,0:T(8,128)(2,1)}, bf16[4,4,8,16,512]{4,3,2,1,0:T(8,128)(2,1)}) custom-call(s32[6]{0:T(128)S(1)} %pad_add_fusion.table, bf16[2,4,128,512]{3,2,1,0:T(8,128)(2,1)S(1)} %pad_maximum_fusion.refs_0_, ...), custom_call_target="tpu_custom_call" | custom-call | tf_op jit(solution)/shard_map/place_copies/pallas_call | solution.py:946
  (109 shorter events, 4.0 us)
Async XLA Ops:
  0.7 1.2 slice-start
  2.9 34.3 %all-to-all-start = ((bf16[8,2,4,16,512]{4,3,2,1,0:T(8,128)(2,1)}), bf16[8,2,4,16,512]{4,3,2,1,0:T(8,128)(2,1)S(1)}, u32[]{:S(2)}, u32[]{:S(2)}) async-start(bf16[8,2,4,16,512]{4,3,2,1,0:T(8,128)(2,1)} %bitcast.77), calls=%async_computation | async-start | bytes 2097152 | tf_op jit(solution)/shard_map/all_to_all | solution.py:766
  37.3 31.4 %copy-start.4 = (bf16[8,2,4,16,512]{4,3,2,1,0:T(8,128)(2,1)}, bf16[8,2,4,16,512]{4,3,2,1,0:T(8,128)(2,1)S(1)}, u32[]{:S(2)}) copy-start(bf16[8,2,4,16,512]{4,3,2,1,0:T(8,128)(2,1)S(1)} %all-to-all-done.refs_1_) | copy-start | bytes 3145732
  68.6 54.3 %all-to-all-start.3 = ((bf16[8,2,2,4,16,512]{5,4,3,2,1,0:T(8,128)(2,1)}), bf16[8,2,2,4,16,512]{5,4,3,2,1,0:T(8,128)(2,1)S(1)}, u32[]{:S(2)}, u32[]{:S(2)}) async-start(bf16[8,2,2,4,16,512]{5,4,3,2,1,0:T(8,128)(2,1)} %get-tuple-element.99), calls=%async_computation.3 | async-start | bytes 4194304 | tf_op jit(solution)/shard_map/all_to_all | solution.py:766
  122.9 1.3 copy-start.2
  124.2 56.3 %all-to-all-start.2 = ((bf16[8,2,2,4,16,512]{5,4,3,2,1,0:T(8,128)(2,1)}), bf16[8,2,2,4,16,512]{5,4,3,2,1,0:T(8,128)(2,1)S(1)}, u32[]{:S(2)}, u32[]{:S(2)}) async-start(bf16[8,2,2,4,16,512]{5,4,3,2,1,0:T(8,128)(2,1)} %get-tuple-element.98), calls=%async_computation.2 | async-start | bytes 4194304 | tf_op jit(solution)/shard_map/all_to_all | solution.py:766
  180.5 10.2 %copy-start = (bf16[8,2,2,4,16,512]{5,4,3,2,1,0:T(8,128)(2,1)}, bf16[8,2,2,4,16,512]{5,4,3,2,1,0:T(8,128)(2,1)S(1)}, u32[]{:S(2)}) copy-start(bf16[8,2,2,4,16,512]{5,4,3,2,1,0:T(8,128)(2,1)S(1)} %all-to-all-done.2.d_early.refs_0_.refs_8_) | copy-start | bytes 6291460
  180.5 6.3 %collective-permute-start = (bf16[2,8,192,512]{3,2,1,0:T(8,128)(2,1)}, bf16[2,8,192,512]{3,2,1,0:T(8,128)(2,1)}, u32[]{:S(2)}, u32[]{:S(2)}) collective-permute-start(bf16[2,8,192,512]{3,2,1,0:T(8,128)(2,1)} %get-tuple-element.110), channel_id=1, source_target_pairs={{0,8},{8,0},{16,24},{24,16},{1,9},{9,1},{17,25},{25,17},{2,10},{10... | collective-permute-start | bytes 9437192 | tf_op jit(solution)/shard_map/ppermute | solution.py:771
  180.8 35.1 %all-to-all-start.4 = ((bf16[8,2,4,16,512]{4,3,2,1,0:T(8,128)(2,1)}), bf16[8,2,4,16,512]{4,3,2,1,0:T(8,128)(2,1)S(1)}, u32[]{:S(2)}, u32[]{:S(2)}) async-start(bf16[8,2,4,16,512]{4,3,2,1,0:T(8,128)(2,1)} %get-tuple-element.112), calls=%async_computation.4 | async-start | bytes 2097152 | tf_op jit(solution)/shard_map/all_to_all | solution.py:766
  192.2 60.6 %collective-permute-start.3 = (bf16[4,192,512]{2,1,0:T(8,128)(2,1)}, bf16[4,192,512]{2,1,0:T(8,128)(2,1)}, u32[]{:S(2)}, u32[]{:S(2)}) collective-permute-start(bf16[4,192,512]{2,1,0:T(8,128)(2,1)} %get-tuple-element.175), channel_id=1, source_target_pairs={{0,17},{1,16},{2,19},{3,18},{4,21},{5,20},{6,23},{7,22},{8,25},{9,... | collective-permute-start | bytes 2359304 | tf_op jit(solution)/shard_map/ppermute | solution.py:804
  192.8 60.0 %collective-permute-start.2 = (bf16[4,192,512]{2,1,0:T(8,128)(2,1)}, bf16[4,192,512]{2,1,0:T(8,128)(2,1)}, u32[]{:S(2)}, u32[]{:S(2)}) collective-permute-start(bf16[4,192,512]{2,1,0:T(8,128)(2,1)} %get-tuple-element.176), channel_id=1, source_target_pairs={{0,16},{1,17},{2,18},{3,19},{4,20},{5,21},{6,22},{7,23},{8,24},{9,... | collective-permute-start | bytes 2359304 | tf_op jit(solution)/shard_map/ppermute | solution.py:804
  195.6 57.2 %collective-permute-start.1 = (bf16[4,192,512]{2,1,0:T(8,128)(2,1)}, bf16[4,192,512]{2,1,0:T(8,128)(2,1)}, u32[]{:S(2)}, u32[]{:S(2)}) collective-permute-start(bf16[4,192,512]{2,1,0:T(8,128)(2,1)} %get-tuple-element.177), channel_id=1, source_target_pairs={{0,1},{1,0},{2,3},{3,2},{4,5},{5,4},{6,7},{7,6},{8,9},{9,8},{10,11... | collective-permute-start | bytes 2359304 | tf_op jit(solution)/shard_map/ppermute | solution.py:804
  215.9 3.6 copy-start.5
  215.9 36.9 %all-to-all-start.5 = ((bf16[8,2,4,16,512]{4,3,2,1,0:T(8,128)(2,1)}), bf16[8,2,4,16,512]{4,3,2,1,0:T(8,128)(2,1)S(1)}, u32[]{:S(2)}, u32[]{:S(2)}) async-start(bf16[8,2,4,16,512]{4,3,2,1,0:T(8,128)(2,1)} %get-tuple-element.121), calls=%async_computation.5 | async-start | bytes 2097152 | tf_op jit(solution)/shard_map/all_to_all | solution.py:766
  252.8 2.3 copy-start.20
  252.8 5.0 %copy-start.3 = (bf16[2,8,64,512]{3,2,1,0:T(8,128)(2,1)S(1)}, bf16[2,8,64,512]{3,2,1,0:T(8,128)(2,1)}, u32[]{:S(2)}) copy-start(bf16[2,8,64,512]{3,2,1,0:T(8,128)(2,1)} %get-tuple-element.140) | copy-start | bytes 3145732
  255.1 2.7 collective-permute-start.7
  255.1 8.8 %collective-permute-start.6 = (bf16[192,512]{1,0:T(8,128)(2,1)S(1)}, bf16[192,512]{1,0:T(8,128)(2,1)S(1)}, u32[]{:S(2)}, u32[]{:S(2)}) collective-permute-start(bf16[192,512]{1,0:T(8,128)(2,1)S(1)} %get-tuple-element.139), channel_id=1, source_target_pairs={{0,6},{1,7},{2,0},{3,1},{4,2},{5,3},{6,4},{7,5},{8,14},{9,15},{10,... | collective-permute-start | bytes 589832 | tf_op jit(solution)/shard_map/ppermute | solution.py:771
  255.2 16.6 %collective-permute-start.5 = (bf16[192,512]{1,0:T(8,128)(2,1)S(1)}, bf16[192,512]{1,0:T(8,128)(2,1)S(1)}, u32[]{:S(2)}, u32[]{:S(2)}) collective-permute-start(bf16[192,512]{1,0:T(8,128)(2,1)S(1)} %get-tuple-element.138), channel_id=1, source_target_pairs={{0,4},{1,5},{2,6},{3,7},{4,0},{5,1},{6,2},{7,3},{8,12},{9,13},{10,... | collective-permute-start | bytes 589832 | tf_op jit(solution)/shard_map/ppermute | solution.py:771
  255.3 16.5 %collective-permute-start.4 = (bf16[192,512]{1,0:T(8,128)(2,1)S(1)}, bf16[192,512]{1,0:T(8,128)(2,1)S(1)}, u32[]{:S(2)}, u32[]{:S(2)}) collective-permute-start(bf16[192,512]{1,0:T(8,128)(2,1)S(1)} %get-tuple-element.137), channel_id=1, source_target_pairs={{0,2},{1,3},{2,4},{3,5},{4,6},{5,7},{6,0},{7,1},{8,10},{9,11},{10,... | collective-permute-start | bytes 589832 | tf_op jit(solution)/shard_map/ppermute | solution.py:771
  258.2 30.2 %copy-start.18 = (f32[4,512]{1,0:T(4,128)S(1)}, f32[4,512]{1,0:T(4,128)}, u32[]{:S(2)}) copy-start(f32[4,512]{1,0:T(4,128)} %get-tuple-element.132) | copy-start | bytes 24580
  258.2 30.2 %copy-start.19 = (f32[2,512]{1,0:T(2,128)S(1)}, f32[2,512]{1,0:T(2,128)}, u32[]{:S(2)}) copy-start(f32[2,512]{1,0:T(2,128)} %get-tuple-element.131) | copy-start | bytes 12292
  258.2 13.7 %collective-permute-start.10 = (bf16[4,64,512]{2,1,0:T(8,128)(2,1)S(1)}, bf16[4,64,512]{2,1,0:T(8,128)(2,1)S(1)}, u32[]{:S(2)}, u32[]{:S(2)}) collective-permute-start(bf16[4,64,512]{2,1,0:T(8,128)(2,1)S(1)} %get-tuple-element.180), channel_id=1, source_target_pairs={{0,17},{1,16},{2,19},{3,18},{4,21},{5,20},{6,23},{7,22},{8,25},{9,... | collective-permute-start | bytes 786440 | tf_op jit(solution)/shard_map/ppermute | solution.py:804
  264.0 11.7 %collective-permute-start.9 = (bf16[4,64,512]{2,1,0:T(8,128)(2,1)S(1)}, bf16[4,64,512]{2,1,0:T(8,128)(2,1)S(1)}, u32[]{:S(2)}, u32[]{:S(2)}) collective-permute-start(bf16[4,64,512]{2,1,0:T(8,128)(2,1)S(1)} %get-tuple-element.181), channel_id=1, source_target_pairs={{0,16},{1,17},{2,18},{3,19},{4,20},{5,21},{6,22},{7,23},{8,24},{9,... | collective-permute-start | bytes 786440 | tf_op jit(solution)/shard_map/ppermute | solution.py:804
  264.0 12.0 %collective-permute-start.8 = (bf16[4,64,512]{2,1,0:T(8,128)(2,1)S(1)}, bf16[4,64,512]{2,1,0:T(8,128)(2,1)S(1)}, u32[]{:S(2)}, u32[]{:S(2)}) collective-permute-start(bf16[4,64,512]{2,1,0:T(8,128)(2,1)S(1)} %get-tuple-element.179), channel_id=1, source_target_pairs={{0,1},{1,0},{2,3},{3,2},{4,5},{5,4},{6,7},{7,6},{8,9},{9,8},{10,11... | collective-permute-start | bytes 786440 | tf_op jit(solution)/shard_map/ppermute | solution.py:804
  271.9 36.0 %copy-start.6 = (f32[128,512]{1,0:T(8,128)S(1)}, f32[128,512]{1,0:T(8,128)}, u32[]{:S(2)}) copy-start(f32[128,512]{1,0:T(8,128)} %param.25) | copy-start | bytes 786436
  271.9 36.0 %copy-start.7 = (f32[128,512]{1,0:T(8,128)S(1)}, f32[128,512]{1,0:T(8,128)}, u32[]{:S(2)}) copy-start(f32[128,512]{1,0:T(8,128)} %param.28) | copy-start | bytes 786436
  271.9 36.0 %copy-start.8 = (f32[128,512]{1,0:T(8,128)S(1)}, f32[128,512]{1,0:T(8,128)}, u32[]{:S(2)}) copy-start(f32[128,512]{1,0:T(8,128)} %param.32) | copy-start | bytes 786436
  276.2 5.6 %collective-permute-start.13 = (bf16[64,512]{1,0:T(8,128)(2,1)S(1)}, bf16[64,512]{1,0:T(8,128)(2,1)S(1)}, u32[]{:S(2)}, u32[]{:S(2)}) collective-permute-start(bf16[64,512]{1,0:T(8,128)(2,1)S(1)} %get-tuple-element.145), channel_id=1, source_target_pairs={{0,6},{1,7},{2,0},{3,1},{4,2},{5,3},{6,4},{7,5},{8,14},{9,15},{10,... | collective-permute-start | bytes 196616 | tf_op jit(solution)/shard_map/ppermute | solution.py:771
  279.2 7.1 %collective-permute-start.12 = (bf16[64,512]{1,0:T(8,128)(2,1)S(1)}, bf16[64,512]{1,0:T(8,128)(2,1)S(1)}, u32[]{:S(2)}, u32[]{:S(2)}) collective-permute-start(bf16[64,512]{1,0:T(8,128)(2,1)S(1)} %get-tuple-element.144), channel_id=1, source_target_pairs={{0,4},{1,5},{2,6},{3,7},{4,0},{5,1},{6,2},{7,3},{8,12},{9,13},{10,... | collective-permute-start | bytes 196616 | tf_op jit(solution)/shard_map/ppermute | solution.py:771
  280.1 6.3 %collective-permute-start.11 = (bf16[64,512]{1,0:T(8,128)(2,1)S(1)}, bf16[64,512]{1,0:T(8,128)(2,1)S(1)}, u32[]{:S(2)}, u32[]{:S(2)}) collective-permute-start(bf16[64,512]{1,0:T(8,128)(2,1)S(1)} %get-tuple-element.143), channel_id=1, source_target_pairs={{0,2},{1,3},{2,4},{3,5},{4,6},{5,7},{6,0},{7,1},{8,10},{9,11},{10,... | collective-permute-start | bytes 196616 | tf_op jit(solution)/shard_map/ppermute | solution.py:771
  281.1 32.9 %copy-start.9 = (f32[64,512]{1,0:T(8,128)S(1)}, f32[64,512]{1,0:T(8,128)}, u32[]{:S(2)}) copy-start(f32[64,512]{1,0:T(8,128)} %param.27) | copy-start | bytes 393220
  281.1 32.9 %copy-start.10 = (f32[64,512]{1,0:T(8,128)S(1)}, f32[64,512]{1,0:T(8,128)}, u32[]{:S(2)}) copy-start(f32[64,512]{1,0:T(8,128)} %param.30) | copy-start | bytes 393220
  281.1 32.9 %copy-start.11 = (f32[64,512]{1,0:T(8,128)S(1)}, f32[64,512]{1,0:T(8,128)}, u32[]{:S(2)}) copy-start(f32[64,512]{1,0:T(8,128)} %param.34) | copy-start | bytes 393220
  288.5 1.2 collective-permute-start.14
  289.7 3.9 %collective-permute-start.16 = (f32[8,512]{1,0:T(8,128)S(1)}, f32[8,512]{1,0:T(8,128)S(1)}, u32[]{:S(2)}, u32[]{:S(2)}) collective-permute-start(f32[8,512]{1,0:T(8,128)S(1)} %add.314), channel_id=1, source_target_pairs={{0,16},{1,17},{2,18},{3,19},{4,20},{5,21},{6,22},{7,23},{8,24},{9,... | collective-permute-start | bytes 49160 | tf_op jit(solution)/shard_map/ppermute | solution.py:804
  291.8 4.6 %collective-permute-start.17 = (f32[8,512]{1,0:T(8,128)S(1)}, f32[8,512]{1,0:T(8,128)S(1)}, u32[]{:S(2)}, u32[]{:S(2)}) collective-permute-start(f32[8,512]{1,0:T(8,128)S(1)} %add.314), channel_id=1, source_target_pairs={{0,17},{1,16},{2,19},{3,18},{4,21},{5,20},{6,23},{7,22},{8,25},{9,... | collective-permute-start | bytes 49160 | tf_op jit(solution)/shard_map/ppermute | solution.py:804
  292.5 4.0 %collective-permute-start.15 = (f32[8,512]{1,0:T(8,128)S(1)}, f32[8,512]{1,0:T(8,128)S(1)}, u32[]{:S(2)}, u32[]{:S(2)}) collective-permute-start(f32[8,512]{1,0:T(8,128)S(1)} %add.314), channel_id=1, source_target_pairs={{0,1},{1,0},{2,3},{3,2},{4,5},{5,4},{6,7},{7,6},{8,9},{9,8},{10,11... | collective-permute-start | bytes 49160 | tf_op jit(solution)/shard_map/ppermute | solution.py:804
  296.5 5.7 %collective-permute-start.19 = (f32[8,512]{1,0:T(8,128)S(1)}, f32[8,512]{1,0:T(8,128)S(1)}, u32[]{:S(2)}, u32[]{:S(2)}) collective-permute-start(f32[8,512]{1,0:T(8,128)S(1)} %add_add_fusion.1), channel_id=1, source_target_pairs={{0,2},{1,3},{2,4},{3,5},{4,6},{5,7},{6,0},{7,1},{8,10},{9,11},{10,... | collective-permute-start | bytes 49160 | tf_op jit(solution)/shard_map/ppermute | solution.py:771
  296.5 5.6 %collective-permute-start.20 = (f32[8,512]{1,0:T(8,128)S(1)}, f32[8,512]{1,0:T(8,128)S(1)}, u32[]{:S(2)}, u32[]{:S(2)}) collective-permute-start(f32[8,512]{1,0:T(8,128)S(1)} %add_add_fusion.1), channel_id=1, source_target_pairs={{0,6},{1,7},{2,0},{3,1},{4,2},{5,3},{6,4},{7,5},{8,14},{9,15},{10,... | collective-permute-start | bytes 49160 | tf_op jit(solution)/shard_map/ppermute | solution.py:771
  300.3 4.6 %collective-permute-start.18 = (f32[8,512]{1,0:T(8,128)S(1)}, f32[8,512]{1,0:T(8,128)S(1)}, u32[]{:S(2)}, u32[]{:S(2)}) collective-permute-start(f32[8,512]{1,0:T(8,128)S(1)} %add_add_fusion.1), channel_id=1, source_target_pairs={{0,4},{1,5},{2,6},{3,7},{4,0},{5,1},{6,2},{7,3},{8,12},{9,13},{10,... | collective-permute-start | bytes 49160 | tf_op jit(solution)/shard_map/ppermute | solution.py:771
  300.4 5.0 %collective-permute-start.21 = (f32[64,512]{1,0:T(8,128)S(1)}, f32[64,512]{1,0:T(8,128)S(1)}, u32[]{:S(2)}, u32[]{:S(2)}) collective-permute-start(f32[64,512]{1,0:T(8,128)S(1)} %broadcast_select_fusion), channel_id=1, source_target_pairs={{0,16},{8,24},{16,0},{24,8},{1,17},{9,25},{17,1},{25,9},{2,18},{10... | collective-permute-start | bytes 393224 | tf_op jit(solution)/shard_map/ppermute | solution.py:771
  305.0 9.8 %copy-start.12 = (f32[512,64]{0,1:T(8,128)S(1)}, f32[512,64]{0,1:T(8,128)}, u32[]{:S(2)}) copy-start(f32[512,64]{0,1:T(8,128)} %param.26) | copy-start | bytes 393220
  305.0 9.8 %copy-start.13 = (f32[512,64]{0,1:T(8,128)S(1)}, f32[512,64]{0,1:T(8,128)}, u32[]{:S(2)}) copy-start(f32[512,64]{0,1:T(8,128)} %param.29) | copy-start | bytes 393220
  305.0 9.8 %copy-start.14 = (f32[512,64]{0,1:T(8,128)S(1)}, f32[512,64]{0,1:T(8,128)}, u32[]{:S(2)}) copy-start(f32[512,64]{0,1:T(8,128)} %param.33) | copy-start | bytes 393220
  309.0 9.0 %collective-permute-start.24 = (bf16[128,512]{1,0:T(8,128)(2,1)S(1)}, bf16[128,512]{1,0:T(8,128)(2,1)S(1)}, u32[]{:S(2)}, u32[]{:S(2)}) collective-permute-start(bf16[128,512]{1,0:T(8,128)(2,1)S(1)} %get-tuple-element.169), channel_id=1, source_target_pairs={{0,6},{1,7},{2,0},{3,1},{4,2},{5,3},{6,4},{7,5},{8,14},{9,15},{10,... | collective-permute-start | bytes 393224 | tf_op jit(solution)/shard_map/ppermute | solution.py:771
  309.6 19.7 %collective-permute-start.23 = (bf16[128,512]{1,0:T(8,128)(2,1)S(1)}, bf16[128,512]{1,0:T(8,128)(2,1)S(1)}, u32[]{:S(2)}, u32[]{:S(2)}) collective-permute-start(bf16[128,512]{1,0:T(8,128)(2,1)S(1)} %get-tuple-element.169), channel_id=1, source_target_pairs={{0,4},{1,5},{2,6},{3,7},{4,0},{5,1},{6,2},{7,3},{8,12},{9,13},{10,... | collective-permute-start | bytes 393224 | tf_op jit(solution)/shard_map/ppermute | solution.py:771
  311.9 17.4 %collective-permute-start.22 = (bf16[128,512]{1,0:T(8,128)(2,1)S(1)}, bf16[128,512]{1,0:T(8,128)(2,1)S(1)}, u32[]{:S(2)}, u32[]{:S(2)}) collective-permute-start(bf16[128,512]{1,0:T(8,128)(2,1)S(1)} %get-tuple-element.169), channel_id=1, source_target_pairs={{0,2},{1,3},{2,4},{3,5},{4,6},{5,7},{6,0},{7,1},{8,10},{9,11},{10,... | collective-permute-start | bytes 393224 | tf_op jit(solution)/shard_map/ppermute | solution.py:771
  315.6 15.1 %collective-permute-start.29 = (bf16[128,512]{1,0:T(8,128)(2,1)S(1)}, bf16[128,512]{1,0:T(8,128)(2,1)S(1)}, u32[]{:S(2)}, u32[]{:S(2)}) collective-permute-start(bf16[128,512]{1,0:T(8,128)(2,1)S(1)} %get-tuple-element.195), channel_id=1, source_target_pairs={{0,2},{1,3},{2,4},{3,5},{4,6},{5,7},{6,0},{7,1},{8,10},{9,11},{10,... | collective-permute-start | bytes 393224 | tf_op jit(solution)/shard_map/ppermute | solution.py:771
  315.7 15.3 %collective-permute-start.30 = (bf16[128,512]{1,0:T(8,128)(2,1)S(1)}, bf16[128,512]{1,0:T(8,128)(2,1)S(1)}, u32[]{:S(2)}, u32[]{:S(2)}) collective-permute-start(bf16[128,512]{1,0:T(8,128)(2,1)S(1)} %get-tuple-element.195), channel_id=1, source_target_pairs={{0,4},{1,5},{2,6},{3,7},{4,0},{5,1},{6,2},{7,3},{8,12},{9,13},{10,... | collective-permute-start | bytes 393224 | tf_op jit(solution)/shard_map/ppermute | solution.py:771
  318.0 13.8 %collective-permute-start.31 = (bf16[128,512]{1,0:T(8,128)(2,1)S(1)}, bf16[128,512]{1,0:T(8,128)(2,1)S(1)}, u32[]{:S(2)}, u32[]{:S(2)}) collective-permute-start(bf16[128,512]{1,0:T(8,128)(2,1)S(1)} %get-tuple-element.195), channel_id=1, source_target_pairs={{0,6},{1,7},{2,0},{3,1},{4,2},{5,3},{6,4},{7,5},{8,14},{9,15},{10,... | collective-permute-start | bytes 393224 | tf_op jit(solution)/shard_map/ppermute | solution.py:771
  329.5 9.9 %collective-permute-start.25 = (bf16[4,128,512]{2,1,0:T(8,128)(2,1)S(1)}, bf16[4,128,512]{2,1,0:T(8,128)(2,1)S(1)}, u32[]{:S(2)}, u32[]{:S(2)}) collective-permute-start(bf16[4,128,512]{2,1,0:T(8,128)(2,1)S(1)} %get-tuple-element.187), channel_id=1, source_target_pairs={{0,1},{1,0},{2,3},{3,2},{4,5},{5,4},{6,7},{7,6},{8,9},{9,8},{10,11... | collective-permute-start | bytes 1572872 | tf_op jit(solution)/shard_map/ppermute | solution.py:771
  331.9 32.0 %copy-start.15 = (f32[6,512]{1,0:T(8,128)S(1)}, f32[6,512]{1,0:T(8,128)}, u32[]{:S(2)}) copy-start(f32[6,512]{1,0:T(8,128)} %refs_11_.1) | copy-start | bytes 36868
  331.9 32.0 %copy-start.16 = (f32[6,512]{1,0:T(8,128)S(1)}, f32[6,512]{1,0:T(8,128)}, u32[]{:S(2)}) copy-start(f32[6,512]{1,0:T(8,128)} %param.31) | copy-start | bytes 36868
  331.9 32.0 %copy-start.17 = (f32[6,512]{1,0:T(8,128)S(1)}, f32[6,512]{1,0:T(8,128)}, u32[]{:S(2)}) copy-start(f32[6,512]{1,0:T(8,128)} %param.35) | copy-start | bytes 36868
  331.9 35.5 %copy-start.1 = (bf16[8,2,2,4,16,512]{5,4,3,2,1,0:T(8,128)(2,1)S(1)}, bf16[8,2,2,4,16,512]{5,4,3,2,1,0:T(8,128)(2,1)}, u32[]{:S(2)}) copy-start(bf16[8,2,2,4,16,512]{5,4,3,2,1,0:T(8,128)(2,1)} %copy-done) | copy-start | bytes 6291460
  331.9 14.9 %collective-permute-start.32 = (bf16[4,128,512]{2,1,0:T(8,128)(2,1)S(1)}, bf16[4,128,512]{2,1,0:T(8,128)(2,1)S(1)}, u32[]{:S(2)}, u32[]{:S(2)}) collective-permute-start(bf16[4,128,512]{2,1,0:T(8,128)(2,1)S(1)} %pad_maximum_fusion.2), channel_id=1, source_target_pairs={{0,16},{8,24},{16,0},{24,8},{1,17},{9,25},{17,1},{25,9},{2,18},{10... | collective-permute-start | bytes 1572872 | tf_op jit(solution)/shard_map/ppermute | solution.py:771
  339.4 23.9 %collective-permute-start.26 = (bf16[2,4,128,512]{3,2,1,0:T(8,128)(2,1)S(1)}, bf16[2,4,128,512]{3,2,1,0:T(8,128)(2,1)S(1)}, u32[]{:S(2)}, u32[]{:S(2)}) collective-permute-start(bf16[2,4,128,512]{3,2,1,0:T(8,128)(2,1)S(1)} %pad_maximum_fusion.refs_0_), channel_id=1, source_target_pairs={{0,16},{8,24},{16,0},{24,8},{1,17},{9,25},{17,1},{25,9},{2,18},{10... | collective-permute-start | bytes 3145736 | tf_op jit(solution)/shard_map/ppermute | solution.py:771
  346.9 16.4 %collective-permute-start.33 = (bf16[8,128,512]{2,1,0:T(8,128)(2,1)S(1)}, bf16[8,128,512]{2,1,0:T(8,128)(2,1)S(1)}, u32[]{:S(2)}, u32[]{:S(2)}) collective-permute-start(bf16[8,128,512]{2,1,0:T(8,128)(2,1)S(1)} %constant_dynamic-update-slice_fusion.refs_4_), channel_id=1, source_target_pairs={{0,1},{1,0},{2,3},{3,2},{4,5},{5,4},{6,7},{7,6},{8,9},{9,8},{10,11... | collective-permute-start | bytes 3145736 | tf_op jit(solution)/shard_map/ppermute | solution.py:771
  348.1 16.4 %collective-permute-start.27 = (bf16[2,4,128,512]{3,2,1,0:T(8,128)(2,1)S(1)}, bf16[2,4,128,512]{3,2,1,0:T(8,128)(2,1)S(1)}, u32[]{:S(2)}, u32[]{:S(2)}) collective-permute-start(bf16[2,4,128,512]{3,2,1,0:T(8,128)(2,1)S(1)} %pad_maximum_fusion.refs_0_), channel_id=1, source_target_pairs={{0,8},{8,0},{16,24},{24,16},{1,9},{9,1},{17,25},{25,17},{2,10},{10... | collective-permute-start | bytes 3145736 | tf_op jit(solution)/shard_map/ppermute | solution.py:771
  348.1 16.4 %collective-permute-start.34 = (bf16[8,128,512]{2,1,0:T(8,128)(2,1)S(1)}, bf16[8,128,512]{2,1,0:T(8,128)(2,1)S(1)}, u32[]{:S(2)}, u32[]{:S(2)}) collective-permute-start(bf16[8,128,512]{2,1,0:T(8,128)(2,1)S(1)} %constant_dynamic-update-slice_fusion.refs_4_), channel_id=1, source_target_pairs={{0,8},{8,0},{16,24},{24,16},{1,9},{9,1},{17,25},{25,17},{2,10},{10... | collective-permute-start | bytes 3145736 | tf_op jit(solution)/shard_map/ppermute | solution.py:771
  363.3 2.7 collective-permute-start.28
  363.3 4.2 %collective-permute-start.35 = (bf16[8,128,512]{2,1,0:T(8,128)(2,1)S(1)}, bf16[8,128,512]{2,1,0:T(8,128)(2,1)S(1)}, u32[]{:S(2)}, u32[]{:S(2)}) collective-permute-start(bf16[8,128,512]{2,1,0:T(8,128)(2,1)S(1)} %collective-permute-done.33.refs_5_), channel_id=1, source_target_pairs={{0,8},{8,0},{16,24},{24,16},{1,9},{9,1},{17,25},{25,17},{2,10},{10... | collective-permute-start | bytes 3145736 | tf_op jit(solution)/shard_map/ppermute | solution.py:771

commit v9 on v8

--- a/solution.py
+++ b/solution.py
@@ -182,9 +182,9 @@
 def sample_backward(early, counts, *refs):
     if early:
         d_early, query_held, sums_held, weight_held, *refs = refs
-    d_late, tokens, first, heads, mixed, logs, weights, norms, *refs = refs
-    grad_out, keep_out, send_out, norm_out, d_rows, d_mix, d_query, d_turned, total, norm_total = refs
-    samples, width = tokens.shape[1:]
+    d_late, first, heads, mixed, logs, weights, *refs = refs
+    heads_out, keep_out, send_out, d_rows, d_mix, d_query, d_turned, total = refs
+    samples, width = first.shape[1:]
     group = d_late.shape[0] * BLOCK
     start = early * group
     rows = slice(start, samples)
@@ -195,13 +195,8 @@
         total[...] = jnp.zeros_like(total)
         if early:
             total[3 * width :] = weight_held[...]
-        norm_total[...] = jnp.zeros_like(norm_total)
 
     feature_live = counts[2] + step < counts[1]
-
-    @pl.when(jnp.logical_not(feature_live))
-    def _():
-        grad_out[...] = jnp.zeros_like(grad_out)
 
     @pl.when(feature_live)
     def _():
@@ -226,11 +221,43 @@
             d_turned[0, :start] = query_held[0]
         for which in range(3):
             total[which * width : (which + 1) * width] += dot(first[0], d_turned[which], TN)
+            heads_out[0, which] = d_turned[which]
+
+    @pl.when(step == pl.num_programs(0) - 1)
+    def _():
+        attention_parts(keep_out, total, counts[4], 0)
+        attention_parts(send_out, total, 1 - counts[4], 0)
+
+
+def input_backward(early, counts, *refs):
+    if early:
+        d_early, *refs = refs
+    d_late, d_heads, tokens, weights, norms, grad_out, norm_out, d_rows, norm_total = refs
+    samples, width = tokens.shape[1:]
+    group = d_late.shape[0] * BLOCK
+    step = pl.program_id(0)
+
+    @pl.when(step == 0)
+    def _():
+        norm_total[...] = jnp.zeros_like(norm_total)
+
+    feature_live = counts[2] + step < counts[1]
+
+    @pl.when(jnp.logical_not(feature_live))
+    def _():
+        grad_out[...] = jnp.zeros_like(grad_out)
+
+    @pl.when(feature_live)
+    def _():
+        for low in range(0, samples, group):
+            deal = low // group
+            part = d_early[:, deal, 0] if deal < early else d_late[:, deal - early, 0]
+            d_rows[low : low + group] = part.reshape(group, width)
         for low in range(0, samples, ROWS):
             part = slice(low, low + ROWS)
-            d_first = dot(d_turned[0, part], weights[0], NT)
-            d_first = d_first + dot(d_turned[1, part], weights[1], NT)
-            d_first = d_first + dot(d_turned[2, part], weights[2], NT)
+            d_first = dot(d_heads[0, 0, part], weights[0], NT)
+            d_first = d_first + dot(d_heads[0, 1, part], weights[1], NT)
+            d_first = d_first + dot(d_heads[0, 2, part], weights[2], NT)
             normal, scale = normalize(tokens[0, part].astype(F32))
             norm_total[0:1] += column_sum(d_first * normal)
             norm_total[1:2] += column_sum(d_first)
@@ -239,8 +266,6 @@
 
     @pl.when(step == pl.num_programs(0) - 1)
     def _():
-        attention_parts(keep_out, total, counts[4], 0)
-        attention_parts(send_out, total, 1 - counts[4], 0)
         norm_out[...] = norm_total[...]
 
 
@@ -708,10 +733,9 @@
     )
 
 
-def run_sample_backward(counts, both, held, d_late, saved, weights, norms, chips):
-    devices, late, local, _, width = d_late.shape
-    tokens = saved[0]
-    samples = tokens.shape[1]
+def run_sample_backward(counts, both, held, d_late, saved, weights, chips):
+    devices, _, local, _, width = d_late.shape
+    samples = saved[0].shape[1]
     early = 0 if both is None else both.shape[2]
     start = early * devices * BLOCK
     parts = (chips, devices, 4 * width // (2 * chips * devices), width)
@@ -720,23 +744,18 @@
         query, sums, weight = held
         ins = ins + [(early_spec(both), both), (lead(query.shape), query), (lead(sums.shape), sums)]
         ins.append((whole(weight.shape), weight))
-    ins.append(
-        (
-            pl.BlockSpec((devices, late, 1, BLOCK, width), lambda step: (0, 0, step, 0, 0)),
-            d_late,
-        )
-    )
-    ins = ins + [(lead(value.shape), value) for value in saved]
-    ins = ins + [(half(weights.shape, 0), weights), (whole(norms.shape), norms)]
+    ins.append((late_spec(d_late), d_late))
+    ins = ins + [(lead(value.shape), value) for value in saved[1:]]
+    ins.append((half(weights.shape, 0), weights))
+    heads = (local, 3, samples, width)
     return call(
         functools.partial(sample_backward, early),
         local,
         ins,
         [
-            (lead(tokens.shape), tokens.shape, BF),
+            (lead(heads), heads, BF),
             (once(parts), parts, BF),
             (once(parts), parts, BF),
-            (once((2, width)), (2, width), F32),
         ],
         [
             ((samples, width), BF),
@@ -744,10 +763,39 @@
             ((width, samples - start), BF),
             ((3, samples, width), BF),
             ((4 * width, width), F32),
-            ((2, width), F32),
         ],
-        30000,
+        25000,
         "sample_backward",
+    )
+
+
+def late_spec(d_late):
+    devices, late, _, _, width = d_late.shape
+    return pl.BlockSpec((devices, late, 1, BLOCK, width), lambda step: (0, 0, step, 0, 0))
+
+
+def run_input_backward(counts, both, d_late, d_heads, tokens, weights, norms):
+    early = 0 if both is None else both.shape[2]
+    local, samples, width = tokens.shape
+    ins = [(None, counts)] + ([(early_spec(both), both)] if early else [])
+    ins = ins + [
+        (late_spec(d_late), d_late),
+        (lead(d_heads.shape), d_heads),
+        (lead(tokens.shape), tokens),
+        (half(weights.shape, 0), weights),
+        (whole(norms.shape), norms),
+    ]
+    return call(
+        functools.partial(input_backward, early),
+        local,
+        ins,
+        [
+            (lead(tokens.shape), tokens.shape, BF),
+            (once((2, width)), (2, width), F32),
+        ],
+        [((samples, width), BF), ((2, width), F32)],
+        11000,
+        "input_backward",
     )
 
 
@@ -1070,15 +1118,23 @@
         held = run_sample_backward_early(counts, came_both, saved, weights)
     dealt_y, came_d, held = lax.optimization_barrier((dealt_y, came_d, held))
     came_y = exchange(dealt_y, "feat")
-    input_grad, keep_one, send_one, norms_one = run_sample_backward(
-        counts, came_both, held, came_d, saved, weights, norm_params, chips
-    )
-    parts_two[0], came_y, input_grad, keep_one, send_one, norms_one = lax.optimization_barrier(
-        (parts_two[0], came_y, input_grad, keep_one, send_one, norms_one)
+    d_heads, keep_one, send_one = run_sample_backward(
+        counts, came_both, held, came_d, saved, weights, chips
+    )
+    parts_two[0], came_y, d_heads, keep_one, send_one = lax.optimization_barrier(
+        (parts_two[0], came_y, d_heads, keep_one, send_one)
     )
     parts_two = layer_parts(reduce_plane(parts_two))
     parts_two, keep_one, send_one = lax.optimization_barrier((parts_two, keep_one, send_one))
-    parts_one = layer_parts(reduce_plane(plane_parts(reduce_core(keep_one, send_one))))
+    plane_one = plane_parts(reduce_core(keep_one, send_one))
+    plane_one, d_heads = lax.optimization_barrier((plane_one, d_heads))
+    input_grad, norms_one = run_input_backward(
+        counts, came_both, came_d, d_heads, tokens[0], weights, norm_params
+    )
+    plane_one[0], parts_two[0], input_grad, norms_one = lax.optimization_barrier(
+        (plane_one[0], parts_two[0], input_grad, norms_one)
+    )
+    parts_one = layer_parts(reduce_plane(plane_one))
     share_two, parts_one = lax.optimization_barrier((reduce_layers(parts_two), parts_one))
     share_one = reduce_layers(parts_one)
     share_in_turned = share_two[:own_ff]

time: 379 us -> 376 us (level)
  Pallas kernels: 185 us -> 154 us
  waiting for transfers between devices: 64.5 us -> 84 us
  starting transfers between devices: 67.7 us -> 74 us
    pallas_call x5 -> x6, Pallas kernels: 180 us -> 149 us  [call(): pl.pallas_call(body, grid=(grid,), in_specs=[pl.BlockSpec(memory_space=pl...]
    all_to_all x5, waiting for transfers between devices: 0.01 us -> 30.2 us  [exchange(): lax.all_to_all(values, axis, 0, 0, axis_index_groups=groups, tiled=True)]
    ppermute x27, starting transfers between devices: 27.8 us -> 36.4 us  [moved_by(): return lax.ppermute(values, axis, pairs)]
    ppermute x27, waiting for transfers between devices: 57.3 us -> 51.4 us  [moved_by(): return lax.ppermute(values, axis, pairs)]
    ppermute x9, waiting for transfers between devices: 7.14 us -> 2.29 us  [in_plane(): return lax.ppermute(values, ('task', 'feat'), pairs)]
  transfers between devices with their start and end apart: 41 -> 41, of which waited for: 19 -> 21; matrix products, arithmetic and copies ran while one was open for 3% -> 3% of each run, Pallas kernels for 48% -> 40%
where the time goes in v9:
time: 376 us; the launch traced here: 370 us
  Pallas kernels  154 us (41%)
  waiting for transfers between devices  84 us (22%)
  starting transfers between devices  74 us (20%)
  blocking collectives  31.4 us (8%)
  other arithmetic  13.4 us (4%)
  local copies, waits for them, and re-layouts  6.61 us (2%)
  between operations  6.5 us (2%)
    pallas_call x6, Pallas kernels, call(): pl.pallas_call(body, grid=(grid,), in_specs=[pl.BlockSpec(memory_space=pl...  149 us
    ppermute x27, waiting for transfers between devices, moved_by(): return lax.ppermute(values, axis, pairs)  51.4 us
    ppermute x27, starting transfers between devices, moved_by(): return lax.ppermute(values, axis, pairs)  36.4 us
    all_to_all x1, blocking collectives, exchange(): lax.all_to_all(values, axis, 0, 0, axis_index_groups=groups, tiled=True)  31.4 us
    all_to_all x5, waiting for transfers between devices, exchange(): lax.all_to_all(values, axis, 0, 0, axis_index_groups=groups, tiled=True)  30.2 us
    all_to_all x5, starting transfers between devices, exchange(): lax.all_to_all(values, axis, 0, 0, axis_index_groups=groups, tiled=True)  26.2 us
    ppermute x9, starting transfers between devices, in_plane(): return lax.ppermute(values, ('task', 'feat'), pairs)  11.4 us
  transfers between devices with their start and end apart: 41, of which 21 were waited for; matrix products, arithmetic and copies ran while one was open for 3% of the time, Pallas kernels for 40%

profile of v9, /device:TPU:0, one launch (start us, length us, event | category | flops | bytes accessed | tf_op | source)
XLA Modules:
  0.0 370.0 jit_solution(10199540878681109131)
XLA Ops:
  0.7 1.2 slice-done
  1.9 1.1 copy.39
  2.9 7.3 %all-to-all-start = ((bf16[8,2,4,16,512]{4,3,2,1,0:T(8,128)(2,1)}), bf16[8,2,4,16,512]{4,3,2,1,0:T(8,128)(2,1)S(1)}, u32[]{:S(2)}, u32[]{:S(2)}) async-start(bf16[8,2,4,16,512]{4,3,2,1,0:T(8,128)(2,1)} %bitcast.74), calls=%async_computation | async-start | bytes 2097152 | tf_op jit(solution)/shard_map/all_to_all | solution.py:814
  12.1 25.1 %sample_forward.1 = (bf16[8,2,4,16,512]{4,3,2,1,0:T(8,128)(2,1)}, bf16[8,2,2,4,16,512]{5,4,3,2,1,0:T(8,128)(2,1)}, bf16[4,512,512]{2,1,0:T(8,128)(2,1)}, bf16[4,...) custom-call(s32[5]{0:T(128)} %stack.62.counts, bf16[4,512,512]{2,1,0:T(8,128)(2,1)} %bitcast.93, ...), custom_call_target="tpu_custom_call" | custom-call | flops 28750000128 | bytes 16777216 | tf_op jit(solution)/shard_map/sample_forward/pallas_call | solution.py:548
  37.3 31.4 %all_to_all.30.refs_0_ = bf16[8,2,4,16,512]{4,3,2,1,0:T(8,128)(2,1)} all-to-all(bf16[8,2,4,16,512]{4,3,2,1,0:T(8,128)(2,1)} %get-tuple-element.104), channel_id=1, replica_groups=mesh['task'=4,'feat'=8] {'feat'}, dimensions={0} | all-to-all | bytes 2097152 | tf_op jit(solution)/shard_map/all_to_all | solution.py:814
  68.6 3.6 all-to-all-start.3
  72.2 40.4 %middle.2 = (bf16[8,2,2,4,16,512]{5,4,3,2,1,0:T(8,128)(2,1)}, f32[2048,512]{1,0:T(8,128)}, f32[2048,512]{1,0:T(8,128)}, f32[2048,512]{1,0:T(8,128)}, f32[4,512]{1,0:T(4,128)}) custom-call(s32[5]{0:T(128)} %stack.62.counts, bf16[8,2,4,16,512]{4,3,2,1,0:T(8,128)(2,1)} %all_to_all.30.refs_0_, bf16[8,2,4,16,512]{4,3,2,1,0:T(8,128)(2,1)} %copy-done.5, ...), custom_call_target="tpu_custom_call" | custom-call | flops 52899999744 | bytes 16777216 | tf_op jit(solution)/shard_map/middle/pallas_call | solution.py:548
  112.6 7.3 %all-to-all-done.3.refs_0_.refs_1_ = bf16[8,2,2,4,16,512]{5,4,3,2,1,0:T(8,128)(2,1)S(1)} async-done(((bf16[8,2,2,4,16,512]{5,4,3,2,1,0:T(8,128)(2,1)}), bf16[8,2,2,4,16,512]{5,4,3,2,1,0:T(8,128)(2,1)S(1)}, u32[]{:S(2)}, u32[]{:S(2)}) %all-to-all-start.3) | async-done | bytes 2097184 | tf_op jit(solution)/shard_map/all_to_all | solution.py:814
  119.9 1.3 copy-done.2
  121.3 3.6 all-to-all-start.2
  124.9 24.6 %middle.3 = (bf16[8,2,4,16,512]{4,3,2,1,0:T(8,128)(2,1)}, bf16[8,2,4,16,512]{4,3,2,1,0:T(8,128)(2,1)}, bf16[2,8,192,512]{3,2,1,0:T(8,128)(2,1)}, bf16[2,8,192,512]{3,2,1,0:T(8,128)(2,1)}, f32[4,512]{1,0:T(4,128)}) custom-call(s32[5]{0:T(128)} %stack.62.counts, bf16[8,2,2,4,16,512]{5,4,3,2,1,0:T(8,128)(2,1)} %copy-done.2, ...), custom_call_target="tpu_custom_call" | custom-call | flops 52899999744 | bytes 16777216 | tf_op jit(solution)/shard_map/middle/pallas_call | solution.py:548
  149.5 22.9 %all-to-all-done.2.d_early.refs_0_.refs_8_ = bf16[8,2,2,4,16,512]{5,4,3,2,1,0:T(8,128)(2,1)S(1)} async-done(((bf16[8,2,2,4,16,512]{5,4,3,2,1,0:T(8,128)(2,1)}), bf16[8,2,2,4,16,512]{5,4,3,2,1,0:T(8,128)(2,1)S(1)}, u32[]{:S(2)}, u32[]{:S(2)}) %all-to-all-start.2) | async-done | bytes 2097184 | tf_op jit(solution)/shard_map/all_to_all | solution.py:814
  172.5 6.6 %collective-permute-start = (bf16[2,8,192,512]{3,2,1,0:T(8,128)(2,1)}, bf16[2,8,192,512]{3,2,1,0:T(8,128)(2,1)}, u32[]{:S(2)}, u32[]{:S(2)}) collective-permute-start(bf16[2,8,192,512]{3,2,1,0:T(8,128)(2,1)} %get-tuple-element.119), channel_id=1, source_target_pairs={{0,8},{8,0},{16,24},{24,16},{1,9},{9,1},{17,25},{25,17},{2,10},{10... | collective-permute-start | bytes 9437192 | tf_op jit(solution)/shard_map/ppermute | solution.py:819
  179.1 5.7 %all-to-all-start.4 = ((bf16[8,2,4,16,512]{4,3,2,1,0:T(8,128)(2,1)}), bf16[8,2,4,16,512]{4,3,2,1,0:T(8,128)(2,1)S(1)}, u32[]{:S(2)}, u32[]{:S(2)}) async-start(bf16[8,2,4,16,512]{4,3,2,1,0:T(8,128)(2,1)} %get-tuple-element.121), calls=%async_computation.4 | async-start | bytes 2097152 | tf_op jit(solution)/shard_map/all_to_all | solution.py:814
  184.8 3.9 %add_convert_fusion = bf16[2,8,192,512]{3,2,1,0:T(8,128)(2,1)S(1)} fusion(bf16[2,8,192,512]{3,2,1,0:T(8,128)(2,1)} %collective-permute-done, bf16[2,8,192,512]{3,2,1,0:T(8,128)(2,1)} %get-tuple-element.118), kind=kLoop, calls=%fused_computation | loop fusion | flops 6291456 | bytes 9437184 | tf_op jit(solution)/shard_map/convert_element_type | solution.py:842
  188.7 1.5 dynamic-slice_bitcast_fusion.3
  190.2 3.5 collective-permute-start.2
  193.7 20.2 %sample_backward_early.1 = (bf16[4,256,512]{2,1,0:T(8,128)(2,1)}, f32[4,2,512,512]{3,2,1,0:T(8,128)}, f32[512,512]{1,0:T(8,128)}) custom-call(s32[5]{0:T(128)} %stack.62.counts, bf16[8,2,2,4,16,512]{5,4,3,2,1,0:T(8,128)(2,1)} %copy-done, bf16[4,3,512,512]{3,2,1,0:T(8,128)(2,1)} %get-tuple-element.124.heads.refs_6_, ...), custom_call_target="tpu_custom_call" | custom-call | flops 25300000768 | bytes 16777216 | tf_op jit(solution)/shard_map/sample_backward_early/pallas_call | solution.py:548
  213.9 6.0 %all-to-all-start.5 = ((bf16[8,2,4,16,512]{4,3,2,1,0:T(8,128)(2,1)}), bf16[8,2,4,16,512]{4,3,2,1,0:T(8,128)(2,1)S(1)}, u32[]{:S(2)}, u32[]{:S(2)}) async-start(bf16[8,2,4,16,512]{4,3,2,1,0:T(8,128)(2,1)} %get-tuple-element.130), calls=%async_computation.5 | async-start | bytes 2097152 | tf_op jit(solution)/shard_map/all_to_all | solution.py:814
  219.9 26.0 %sample_backward.1 = (bf16[4,3,512,512]{3,2,1,0:T(8,128)(2,1)}, bf16[2,8,64,512]{3,2,1,0:T(8,128)(2,1)}, bf16[2,8,64,512]{3,2,1,0:T(8,128)(2,1)}) custom-call(s32[5]{0:T(128)} %stack.62.counts, bf16[8,2,2,4,16,512]{5,4,3,2,1,0:T(8,128)(2,1)} %copy-done, bf16[4,256,512]{2,1,0:T(8,128)(2,1)} %get-tuple-element.131.refs_1_, ...), custom_call_target="tpu_custom_call" | custom-call | flops 28750000128 | bytes 16777216 | tf_op jit(solution)/shard_map/sample_backward/pallas_call | solution.py:548
  245.9 2.2 add_convert_fusion.2
  248.3 3.9 %collective-permute-start.7 = (bf16[192,512]{1,0:T(8,128)(2,1)S(1)}, bf16[192,512]{1,0:T(8,128)(2,1)S(1)}, u32[]{:S(2)}, u32[]{:S(2)}) collective-permute-start(bf16[192,512]{1,0:T(8,128)(2,1)S(1)} %get-tuple-element.155), channel_id=1, source_target_pairs={{0,6},{1,7},{2,0},{3,1},{4,2},{5,3},{6,4},{7,5},{8,14},{9,15},{10,... | collective-permute-start | bytes 589832 | tf_op jit(solution)/shard_map/ppermute | solution.py:819
  252.1 1.3 collective-permute-start.5
  254.0 2.9 collective-permute-start.9
  257.4 1.5 collective-permute-start.8
  258.9 12.8 %input_backward.1 = (bf16[4,512,512]{2,1,0:T(8,128)(2,1)}, f32[2,512]{1,0:T(2,128)}) custom-call(s32[5]{0:T(128)} %stack.62.counts, bf16[8,2,2,4,16,512]{5,4,3,2,1,0:T(8,128)(2,1)} %copy-done, bf16[8,2,4,16,512]{4,3,2,1,0:T(8,128)(2,1)} %copy-done.4, bf16[4,3,512,512]{3,2,1,0:T(8,128)(2,1)} %get-tuple-element.147.refs_2_, bf16[4,512,512]{2,1,0:T(8,128)(2,1)} %bitcast.94, ...), custom_call_target="tpu_custom_call" | custom-call | flops 12650000384 | bytes 16777216 | tf_op jit(solution)/shard_map/input_backward/pallas_call | solution.py:548
  271.9 1.1 add_convert_fusion.3
  273.1 4.4 %collective-permute-start.13 = (bf16[64,512]{1,0:T(8,128)(2,1)S(1)}, bf16[64,512]{1,0:T(8,128)(2,1)S(1)}, u32[]{:S(2)}, u32[]{:S(2)}) collective-permute-start(bf16[64,512]{1,0:T(8,128)(2,1)S(1)} %get-tuple-element.163), channel_id=1, source_target_pairs={{0,6},{1,7},{2,0},{3,1},{4,2},{5,3},{6,4},{7,5},{8,14},{9,15},{10,... | collective-permute-start | bytes 196616 | tf_op jit(solution)/shard_map/ppermute | solution.py:819
  277.5 0.6 collective-permute-start.11
  278.1 0.7 multiply_reduce_fusion
  279.4 3.3 collective-permute-done.12
  282.6 0.9 collective-permute-done.11
  283.5 0.6 multiply_reduce_fusion.1
  285.7 1.2 collective-permute-done.14
  286.9 2.0 collective-permute-start.17
  288.9 1.5 collective-permute-start.15
  290.6 1.0 collective-permute-done.17
  291.6 1.1 collective-permute-done.15
  292.7 3.8 %collective-permute-start.20 = (f32[8,512]{1,0:T(8,128)S(1)}, f32[8,512]{1,0:T(8,128)S(1)}, u32[]{:S(2)}, u32[]{:S(2)}) collective-permute-start(f32[8,512]{1,0:T(8,128)S(1)} %add_add_fusion.1), channel_id=1, source_target_pairs={{0,6},{1,7},{2,0},{3,1},{4,2},{5,3},{6,4},{7,5},{8,14},{9,15},{10,... | collective-permute-start | bytes 49160 | tf_op jit(solution)/shard_map/ppermute | solution.py:819
  296.5 1.0 collective-permute-start.21
  297.5 0.7 collective-permute-done.19
  298.2 2.9 collective-permute-done.18
  302.1 0.6 multiply_reduce_fusion.2
  304.1 1.0 fusion.16
  305.2 0.6 collective-permute-start.24
  305.8 2.3 collective-permute-start.23
  308.1 2.0 collective-permute-start.22
  310.1 0.8 fusion.14
  310.9 0.8 convert_bitcast_fusion
  311.8 2.3 collective-permute-start.30
  314.2 1.5 collective-permute-start.31
  315.7 9.9 %collective-permute-done.23 = bf16[128,512]{1,0:T(8,128)(2,1)S(1)} collective-permute-done((bf16[128,512]{1,0:T(8,128)(2,1)S(1)}, bf16[128,512]{1,0:T(8,128)(2,1)S(1)}, u32[]{:S(2)}, u32[]{:S(2)}) %collective-permute-start.23) | collective-permute-done | bytes 131104 | tf_op jit(solution)/shard_map/ppermute | solution.py:819
  325.6 1.4 collective-permute-start.25
  327.1 0.9 collective-permute-done.31
  328.1 1.0 collective-permute-start.32
  329.1 6.4 %collective-permute-done.25 = bf16[4,128,512]{2,1,0:T(8,128)(2,1)S(1)} collective-permute-done((bf16[4,128,512]{2,1,0:T(8,128)(2,1)S(1)}, bf16[4,128,512]{2,1,0:T(8,128)(2,1)S(1)}, u32[]{:S(2)}, u32[]{:S(2)}) %collective-permute-start.25) | collective-permute-done | bytes 524320 | tf_op jit(solution)/shard_map/ppermute | solution.py:819
  335.6 1.0 collective-permute-start.26
  336.6 6.5 %collective-permute-done.32 = bf16[4,128,512]{2,1,0:T(8,128)(2,1)S(1)} collective-permute-done((bf16[4,128,512]{2,1,0:T(8,128)(2,1)S(1)}, bf16[4,128,512]{2,1,0:T(8,128)(2,1)S(1)}, u32[]{:S(2)}, u32[]{:S(2)}) %collective-permute-start.32) | collective-permute-done | bytes 524320 | tf_op jit(solution)/shard_map/ppermute | solution.py:819
  343.1 1.4 collective-permute-start.33
  345.0 14.4 %collective-permute-done.26.refs_1_ = bf16[2,4,128,512]{3,2,1,0:T(8,128)(2,1)S(1)} collective-permute-done((bf16[2,4,128,512]{3,2,1,0:T(8,128)(2,1)S(1)}, bf16[2,4,128,512]{3,2,1,0:T(8,128)(2,1)S(1)}, u32[]{:S(2)}, u32[]{:S(2)}) %collective-permute-start.26) | collective-permute-done | bytes 1048608 | tf_op jit(solution)/shard_map/ppermute | solution.py:819
  360.1 0.6 multiply_subtract_fusion.3
  360.7 1.4 collective-permute-done.28.refs_3_
  362.1 1.5 collective-permute-done.35.refs_7_
  363.6 5.0 %place_copies.1 = (bf16[4096,512]{1,0:T(8,128)(2,1)}, bf16[512,2048]{1,0:T(8,128)(2,1)}, bf16[2048,512]{1,0:T(8,128)(2,1)}, bf16[4,4,8,16,512]{4,3,2,1,0:T(8,128)(2,1)}) custom-call(s32[6]{0:T(128)S(1)} %pad_add_fusion.table, bf16[2,4,128,512]{3,2,1,0:T(8,128)(2,1)S(1)} %pad_maximum_fusion.refs_0_, ...), custom_call_target="tpu_custom_call" | custom-call | tf_op jit(solution)/shard_map/place_copies/pallas_call | solution.py:994
  (110 shorter events, 5.7 us)
Async XLA Ops:
  0.7 1.2 slice-start
  2.9 34.3 %all-to-all-start = ((bf16[8,2,4,16,512]{4,3,2,1,0:T(8,128)(2,1)}), bf16[8,2,4,16,512]{4,3,2,1,0:T(8,128)(2,1)S(1)}, u32[]{:S(2)}, u32[]{:S(2)}) async-start(bf16[8,2,4,16,512]{4,3,2,1,0:T(8,128)(2,1)} %bitcast.74), calls=%async_computation | async-start | bytes 2097152 | tf_op jit(solution)/shard_map/all_to_all | solution.py:814
  37.3 31.4 %copy-start.5 = (bf16[8,2,4,16,512]{4,3,2,1,0:T(8,128)(2,1)}, bf16[8,2,4,16,512]{4,3,2,1,0:T(8,128)(2,1)S(1)}, u32[]{:S(2)}) copy-start(bf16[8,2,4,16,512]{4,3,2,1,0:T(8,128)(2,1)S(1)} %all-to-all-done.refs_1_) | copy-start | bytes 3145732
  68.6 51.3 %all-to-all-start.3 = ((bf16[8,2,2,4,16,512]{5,4,3,2,1,0:T(8,128)(2,1)}), bf16[8,2,2,4,16,512]{5,4,3,2,1,0:T(8,128)(2,1)S(1)}, u32[]{:S(2)}, u32[]{:S(2)}) async-start(bf16[8,2,2,4,16,512]{5,4,3,2,1,0:T(8,128)(2,1)} %get-tuple-element.108), calls=%async_computation.3 | async-start | bytes 4194304 | tf_op jit(solution)/shard_map/all_to_all | solution.py:814
  119.9 1.3 copy-start.2
  121.3 51.2 %all-to-all-start.2 = ((bf16[8,2,2,4,16,512]{5,4,3,2,1,0:T(8,128)(2,1)}), bf16[8,2,2,4,16,512]{5,4,3,2,1,0:T(8,128)(2,1)S(1)}, u32[]{:S(2)}, u32[]{:S(2)}) async-start(bf16[8,2,2,4,16,512]{5,4,3,2,1,0:T(8,128)(2,1)} %get-tuple-element.107), calls=%async_computation.2 | async-start | bytes 4194304 | tf_op jit(solution)/shard_map/all_to_all | solution.py:814
  172.5 16.2 %copy-start = (bf16[8,2,2,4,16,512]{5,4,3,2,1,0:T(8,128)(2,1)}, bf16[8,2,2,4,16,512]{5,4,3,2,1,0:T(8,128)(2,1)S(1)}, u32[]{:S(2)}) copy-start(bf16[8,2,2,4,16,512]{5,4,3,2,1,0:T(8,128)(2,1)S(1)} %all-to-all-done.2.d_early.refs_0_.refs_8_) | copy-start | bytes 6291460
  172.5 12.3 %collective-permute-start = (bf16[2,8,192,512]{3,2,1,0:T(8,128)(2,1)}, bf16[2,8,192,512]{3,2,1,0:T(8,128)(2,1)}, u32[]{:S(2)}, u32[]{:S(2)}) collective-permute-start(bf16[2,8,192,512]{3,2,1,0:T(8,128)(2,1)} %get-tuple-element.119), channel_id=1, source_target_pairs={{0,8},{8,0},{16,24},{24,16},{1,9},{9,1},{17,25},{25,17},{2,10},{10... | collective-permute-start | bytes 9437192 | tf_op jit(solution)/shard_map/ppermute | solution.py:819
  179.1 34.8 %all-to-all-start.4 = ((bf16[8,2,4,16,512]{4,3,2,1,0:T(8,128)(2,1)}), bf16[8,2,4,16,512]{4,3,2,1,0:T(8,128)(2,1)S(1)}, u32[]{:S(2)}, u32[]{:S(2)}) async-start(bf16[8,2,4,16,512]{4,3,2,1,0:T(8,128)(2,1)} %get-tuple-element.121), calls=%async_computation.4 | async-start | bytes 2097152 | tf_op jit(solution)/shard_map/all_to_all | solution.py:814
  190.2 55.7 %collective-permute-start.3 = (bf16[4,192,512]{2,1,0:T(8,128)(2,1)}, bf16[4,192,512]{2,1,0:T(8,128)(2,1)}, u32[]{:S(2)}, u32[]{:S(2)}) collective-permute-start(bf16[4,192,512]{2,1,0:T(8,128)(2,1)} %get-tuple-element.194), channel_id=1, source_target_pairs={{0,17},{1,16},{2,19},{3,18},{4,21},{5,20},{6,23},{7,22},{8,25},{9,... | collective-permute-start | bytes 2359304 | tf_op jit(solution)/shard_map/ppermute | solution.py:852
  190.2 55.7 %collective-permute-start.2 = (bf16[4,192,512]{2,1,0:T(8,128)(2,1)}, bf16[4,192,512]{2,1,0:T(8,128)(2,1)}, u32[]{:S(2)}, u32[]{:S(2)}) collective-permute-start(bf16[4,192,512]{2,1,0:T(8,128)(2,1)} %get-tuple-element.195), channel_id=1, source_target_pairs={{0,16},{1,17},{2,18},{3,19},{4,20},{5,21},{6,22},{7,23},{8,24},{9,... | collective-permute-start | bytes 2359304 | tf_op jit(solution)/shard_map/ppermute | solution.py:852
  193.7 52.3 %collective-permute-start.1 = (bf16[4,192,512]{2,1,0:T(8,128)(2,1)}, bf16[4,192,512]{2,1,0:T(8,128)(2,1)}, u32[]{:S(2)}, u32[]{:S(2)}) collective-permute-start(bf16[4,192,512]{2,1,0:T(8,128)(2,1)} %get-tuple-element.196), channel_id=1, source_target_pairs={{0,1},{1,0},{2,3},{3,2},{4,5},{5,4},{6,7},{7,6},{8,9},{9,8},{10,11... | collective-permute-start | bytes 2359304 | tf_op jit(solution)/shard_map/ppermute | solution.py:852
  213.9 6.0 %copy-start.4 = (bf16[8,2,4,16,512]{4,3,2,1,0:T(8,128)(2,1)}, bf16[8,2,4,16,512]{4,3,2,1,0:T(8,128)(2,1)S(1)}, u32[]{:S(2)}) copy-start(bf16[8,2,4,16,512]{4,3,2,1,0:T(8,128)(2,1)S(1)} %all-to-all-done.4.refs_4_.refs_1_) | copy-start | bytes 3145732
  213.9 32.0 %all-to-all-start.5 = ((bf16[8,2,4,16,512]{4,3,2,1,0:T(8,128)(2,1)}), bf16[8,2,4,16,512]{4,3,2,1,0:T(8,128)(2,1)S(1)}, u32[]{:S(2)}, u32[]{:S(2)}) async-start(bf16[8,2,4,16,512]{4,3,2,1,0:T(8,128)(2,1)} %get-tuple-element.130), calls=%async_computation.5 | async-start | bytes 2097152 | tf_op jit(solution)/shard_map/all_to_all | solution.py:814
  245.9 2.3 copy-start.20
  245.9 7.5 %copy-start.3 = (bf16[2,8,64,512]{3,2,1,0:T(8,128)(2,1)S(1)}, bf16[2,8,64,512]{3,2,1,0:T(8,128)(2,1)}, u32[]{:S(2)}) copy-start(bf16[2,8,64,512]{3,2,1,0:T(8,128)(2,1)} %get-tuple-element.142) | copy-start | bytes 3145732
  248.2 5.3 %collective-permute-start.4 = (bf16[2,8,64,512]{3,2,1,0:T(8,128)(2,1)S(1)}, bf16[2,8,64,512]{3,2,1,0:T(8,128)(2,1)S(1)}, u32[]{:S(2)}, u32[]{:S(2)}) collective-permute-start(bf16[2,8,64,512]{3,2,1,0:T(8,128)(2,1)S(1)} %copy-done.20), channel_id=1, source_target_pairs={{0,8},{8,0},{16,24},{24,16},{1,9},{9,1},{17,25},{25,17},{2,10},{10... | collective-permute-start | bytes 3145736 | tf_op jit(solution)/shard_map/ppermute | solution.py:819
  248.3 9.2 %collective-permute-start.7 = (bf16[192,512]{1,0:T(8,128)(2,1)S(1)}, bf16[192,512]{1,0:T(8,128)(2,1)S(1)}, u32[]{:S(2)}, u32[]{:S(2)}) collective-permute-start(bf16[192,512]{1,0:T(8,128)(2,1)S(1)} %get-tuple-element.155), channel_id=1, source_target_pairs={{0,6},{1,7},{2,0},{3,1},{4,2},{5,3},{6,4},{7,5},{8,14},{9,15},{10,... | collective-permute-start | bytes 589832 | tf_op jit(solution)/shard_map/ppermute | solution.py:819
  252.1 19.6 %collective-permute-start.6 = (bf16[192,512]{1,0:T(8,128)(2,1)S(1)}, bf16[192,512]{1,0:T(8,128)(2,1)S(1)}, u32[]{:S(2)}, u32[]{:S(2)}) collective-permute-start(bf16[192,512]{1,0:T(8,128)(2,1)S(1)} %get-tuple-element.154), channel_id=1, source_target_pairs={{0,4},{1,5},{2,6},{3,7},{4,0},{5,1},{6,2},{7,3},{8,12},{9,13},{10,... | collective-permute-start | bytes 589832 | tf_op jit(solution)/shard_map/ppermute | solution.py:819
  252.1 19.6 %collective-permute-start.5 = (bf16[192,512]{1,0:T(8,128)(2,1)S(1)}, bf16[192,512]{1,0:T(8,128)(2,1)S(1)}, u32[]{:S(2)}, u32[]{:S(2)}) collective-permute-start(bf16[192,512]{1,0:T(8,128)(2,1)S(1)} %get-tuple-element.153), channel_id=1, source_target_pairs={{0,2},{1,3},{2,4},{3,5},{4,6},{5,7},{6,0},{7,1},{8,10},{9,11},{10,... | collective-permute-start | bytes 589832 | tf_op jit(solution)/shard_map/ppermute | solution.py:819
  253.9 18.0 %collective-permute-start.10 = (bf16[4,64,512]{2,1,0:T(8,128)(2,1)S(1)}, bf16[4,64,512]{2,1,0:T(8,128)(2,1)S(1)}, u32[]{:S(2)}, u32[]{:S(2)}) collective-permute-start(bf16[4,64,512]{2,1,0:T(8,128)(2,1)S(1)} %get-tuple-element.159), channel_id=1, source_target_pairs={{0,17},{1,16},{2,19},{3,18},{4,21},{5,20},{6,23},{7,22},{8,25},{9,... | collective-permute-start | bytes 786440 | tf_op jit(solution)/shard_map/ppermute | solution.py:852
  254.0 17.9 %collective-permute-start.9 = (bf16[4,64,512]{2,1,0:T(8,128)(2,1)S(1)}, bf16[4,64,512]{2,1,0:T(8,128)(2,1)S(1)}, u32[]{:S(2)}, u32[]{:S(2)}) collective-permute-start(bf16[4,64,512]{2,1,0:T(8,128)(2,1)S(1)} %get-tuple-element.158), channel_id=1, source_target_pairs={{0,16},{1,17},{2,18},{3,19},{4,20},{5,21},{6,22},{7,23},{8,24},{9,... | collective-permute-start | bytes 786440 | tf_op jit(solution)/shard_map/ppermute | solution.py:852
  257.4 14.5 %collective-permute-start.8 = (bf16[4,64,512]{2,1,0:T(8,128)(2,1)S(1)}, bf16[4,64,512]{2,1,0:T(8,128)(2,1)}, u32[]{:S(2)}, u32[]{:S(2)}) collective-permute-start(bf16[4,64,512]{2,1,0:T(8,128)(2,1)S(1)} %get-tuple-element.157), channel_id=1, source_target_pairs={{0,1},{1,0},{2,3},{3,2},{4,5},{5,4},{6,7},{7,6},{8,9},{9,8},{10,11... | collective-permute-start | bytes 786440 | tf_op jit(solution)/shard_map/ppermute | solution.py:852
  271.7 13.9 %copy-start.18 = (f32[4,512]{1,0:T(4,128)S(1)}, f32[4,512]{1,0:T(4,128)}, u32[]{:S(2)}) copy-start(f32[4,512]{1,0:T(4,128)} %get-tuple-element.151) | copy-start | bytes 24580
  271.7 13.9 %copy-start.19 = (f32[2,512]{1,0:T(2,128)S(1)}, f32[2,512]{1,0:T(2,128)}, u32[]{:S(2)}) copy-start(f32[2,512]{1,0:T(2,128)} %get-tuple-element.150) | copy-start | bytes 12292
  271.8 32.3 %copy-start.6 = (f32[128,512]{1,0:T(8,128)S(1)}, f32[128,512]{1,0:T(8,128)}, u32[]{:S(2)}) copy-start(f32[128,512]{1,0:T(8,128)} %param.25) | copy-start | bytes 786436
  271.8 32.3 %copy-start.7 = (f32[128,512]{1,0:T(8,128)S(1)}, f32[128,512]{1,0:T(8,128)}, u32[]{:S(2)}) copy-start(f32[128,512]{1,0:T(8,128)} %param.28) | copy-start | bytes 786436
  271.9 32.3 %copy-start.8 = (f32[128,512]{1,0:T(8,128)S(1)}, f32[128,512]{1,0:T(8,128)}, u32[]{:S(2)}) copy-start(f32[128,512]{1,0:T(8,128)} %param.32) | copy-start | bytes 786436
  273.1 6.3 %collective-permute-start.13 = (bf16[64,512]{1,0:T(8,128)(2,1)S(1)}, bf16[64,512]{1,0:T(8,128)(2,1)S(1)}, u32[]{:S(2)}, u32[]{:S(2)}) collective-permute-start(bf16[64,512]{1,0:T(8,128)(2,1)S(1)} %get-tuple-element.163), channel_id=1, source_target_pairs={{0,6},{1,7},{2,0},{3,1},{4,2},{5,3},{6,4},{7,5},{8,14},{9,15},{10,... | collective-permute-start | bytes 196616 | tf_op jit(solution)/shard_map/ppermute | solution.py:819
  277.5 5.2 %collective-permute-start.12 = (bf16[64,512]{1,0:T(8,128)(2,1)S(1)}, bf16[64,512]{1,0:T(8,128)(2,1)S(1)}, u32[]{:S(2)}, u32[]{:S(2)}) collective-permute-start(bf16[64,512]{1,0:T(8,128)(2,1)S(1)} %get-tuple-element.162), channel_id=1, source_target_pairs={{0,4},{1,5},{2,6},{3,7},{4,0},{5,1},{6,2},{7,3},{8,12},{9,13},{10,... | collective-permute-start | bytes 196616 | tf_op jit(solution)/shard_map/ppermute | solution.py:819
  277.5 6.1 %collective-permute-start.11 = (bf16[64,512]{1,0:T(8,128)(2,1)S(1)}, bf16[64,512]{1,0:T(8,128)(2,1)S(1)}, u32[]{:S(2)}, u32[]{:S(2)}) collective-permute-start(bf16[64,512]{1,0:T(8,128)(2,1)S(1)} %get-tuple-element.161), channel_id=1, source_target_pairs={{0,2},{1,3},{2,4},{3,5},{4,6},{5,7},{6,0},{7,1},{8,10},{9,11},{10,... | collective-permute-start | bytes 196616 | tf_op jit(solution)/shard_map/ppermute | solution.py:819
  278.8 31.3 %copy-start.9 = (f32[64,512]{1,0:T(8,128)S(1)}, f32[64,512]{1,0:T(8,128)}, u32[]{:S(2)}) copy-start(f32[64,512]{1,0:T(8,128)} %param.27) | copy-start | bytes 393220
  278.8 31.3 %copy-start.10 = (f32[64,512]{1,0:T(8,128)S(1)}, f32[64,512]{1,0:T(8,128)}, u32[]{:S(2)}) copy-start(f32[64,512]{1,0:T(8,128)} %param.30) | copy-start | bytes 393220
  278.8 31.3 %copy-start.11 = (f32[64,512]{1,0:T(8,128)S(1)}, f32[64,512]{1,0:T(8,128)}, u32[]{:S(2)}) copy-start(f32[64,512]{1,0:T(8,128)} %param.34) | copy-start | bytes 393220
  285.6 1.2 collective-permute-start.14
  286.8 3.8 %collective-permute-start.16 = (f32[8,512]{1,0:T(8,128)S(1)}, f32[8,512]{1,0:T(8,128)S(1)}, u32[]{:S(2)}, u32[]{:S(2)}) collective-permute-start(f32[8,512]{1,0:T(8,128)S(1)} %add.314), channel_id=1, source_target_pairs={{0,16},{1,17},{2,18},{3,19},{4,20},{5,21},{6,22},{7,23},{8,24},{9,... | collective-permute-start | bytes 49160 | tf_op jit(solution)/shard_map/ppermute | solution.py:852
  286.9 4.7 %collective-permute-start.17 = (f32[8,512]{1,0:T(8,128)S(1)}, f32[8,512]{1,0:T(8,128)S(1)}, u32[]{:S(2)}, u32[]{:S(2)}) collective-permute-start(f32[8,512]{1,0:T(8,128)S(1)} %add.314), channel_id=1, source_target_pairs={{0,17},{1,16},{2,19},{3,18},{4,21},{5,20},{6,23},{7,22},{8,25},{9,... | collective-permute-start | bytes 49160 | tf_op jit(solution)/shard_map/ppermute | solution.py:852
  288.9 3.7 %collective-permute-start.15 = (f32[8,512]{1,0:T(8,128)S(1)}, f32[8,512]{1,0:T(8,128)S(1)}, u32[]{:S(2)}, u32[]{:S(2)}) collective-permute-start(f32[8,512]{1,0:T(8,128)S(1)} %add.314), channel_id=1, source_target_pairs={{0,1},{1,0},{2,3},{3,2},{4,5},{5,4},{6,7},{7,6},{8,9},{9,8},{10,11... | collective-permute-start | bytes 49160 | tf_op jit(solution)/shard_map/ppermute | solution.py:852
  292.6 5.6 %collective-permute-start.19 = (f32[8,512]{1,0:T(8,128)S(1)}, f32[8,512]{1,0:T(8,128)S(1)}, u32[]{:S(2)}, u32[]{:S(2)}) collective-permute-start(f32[8,512]{1,0:T(8,128)S(1)} %add_add_fusion.1), channel_id=1, source_target_pairs={{0,2},{1,3},{2,4},{3,5},{4,6},{5,7},{6,0},{7,1},{8,10},{9,11},{10,... | collective-permute-start | bytes 49160 | tf_op jit(solution)/shard_map/ppermute | solution.py:819
  292.7 5.5 %collective-permute-start.20 = (f32[8,512]{1,0:T(8,128)S(1)}, f32[8,512]{1,0:T(8,128)S(1)}, u32[]{:S(2)}, u32[]{:S(2)}) collective-permute-start(f32[8,512]{1,0:T(8,128)S(1)} %add_add_fusion.1), channel_id=1, source_target_pairs={{0,6},{1,7},{2,0},{3,1},{4,2},{5,3},{6,4},{7,5},{8,14},{9,15},{10,... | collective-permute-start | bytes 49160 | tf_op jit(solution)/shard_map/ppermute | solution.py:819
  296.5 4.6 %collective-permute-start.18 = (f32[8,512]{1,0:T(8,128)S(1)}, f32[8,512]{1,0:T(8,128)S(1)}, u32[]{:S(2)}, u32[]{:S(2)}) collective-permute-start(f32[8,512]{1,0:T(8,128)S(1)} %add_add_fusion.1), channel_id=1, source_target_pairs={{0,4},{1,5},{2,6},{3,7},{4,0},{5,1},{6,2},{7,3},{8,12},{9,13},{10,... | collective-permute-start | bytes 49160 | tf_op jit(solution)/shard_map/ppermute | solution.py:819
  296.5 5.0 %collective-permute-start.21 = (f32[64,512]{1,0:T(8,128)S(1)}, f32[64,512]{1,0:T(8,128)S(1)}, u32[]{:S(2)}, u32[]{:S(2)}) collective-permute-start(f32[64,512]{1,0:T(8,128)S(1)} %broadcast_select_fusion), channel_id=1, source_target_pairs={{0,16},{8,24},{16,0},{24,8},{1,17},{9,25},{17,1},{25,9},{2,18},{10... | collective-permute-start | bytes 393224 | tf_op jit(solution)/shard_map/ppermute | solution.py:819
  301.1 9.8 %copy-start.12 = (f32[512,64]{0,1:T(8,128)S(1)}, f32[512,64]{0,1:T(8,128)}, u32[]{:S(2)}) copy-start(f32[512,64]{0,1:T(8,128)} %param.26) | copy-start | bytes 393220
  301.1 9.8 %copy-start.13 = (f32[512,64]{0,1:T(8,128)S(1)}, f32[512,64]{0,1:T(8,128)}, u32[]{:S(2)}) copy-start(f32[512,64]{0,1:T(8,128)} %param.29) | copy-start | bytes 393220
  301.2 9.8 %copy-start.14 = (f32[512,64]{0,1:T(8,128)S(1)}, f32[512,64]{0,1:T(8,128)}, u32[]{:S(2)}) copy-start(f32[512,64]{0,1:T(8,128)} %param.33) | copy-start | bytes 393220
  305.2 9.0 %collective-permute-start.24 = (bf16[128,512]{1,0:T(8,128)(2,1)S(1)}, bf16[128,512]{1,0:T(8,128)(2,1)S(1)}, u32[]{:S(2)}, u32[]{:S(2)}) collective-permute-start(bf16[128,512]{1,0:T(8,128)(2,1)S(1)} %get-tuple-element.187), channel_id=1, source_target_pairs={{0,6},{1,7},{2,0},{3,1},{4,2},{5,3},{6,4},{7,5},{8,14},{9,15},{10,... | collective-permute-start | bytes 393224 | tf_op jit(solution)/shard_map/ppermute | solution.py:819
  305.8 19.7 %collective-permute-start.23 = (bf16[128,512]{1,0:T(8,128)(2,1)S(1)}, bf16[128,512]{1,0:T(8,128)(2,1)S(1)}, u32[]{:S(2)}, u32[]{:S(2)}) collective-permute-start(bf16[128,512]{1,0:T(8,128)(2,1)S(1)} %get-tuple-element.187), channel_id=1, source_target_pairs={{0,4},{1,5},{2,6},{3,7},{4,0},{5,1},{6,2},{7,3},{8,12},{9,13},{10,... | collective-permute-start | bytes 393224 | tf_op jit(solution)/shard_map/ppermute | solution.py:819
  308.1 17.4 %collective-permute-start.22 = (bf16[128,512]{1,0:T(8,128)(2,1)S(1)}, bf16[128,512]{1,0:T(8,128)(2,1)S(1)}, u32[]{:S(2)}, u32[]{:S(2)}) collective-permute-start(bf16[128,512]{1,0:T(8,128)(2,1)S(1)} %get-tuple-element.187), channel_id=1, source_target_pairs={{0,2},{1,3},{2,4},{3,5},{4,6},{5,7},{6,0},{7,1},{8,10},{9,11},{10,... | collective-permute-start | bytes 393224 | tf_op jit(solution)/shard_map/ppermute | solution.py:819
  311.8 15.3 %collective-permute-start.29 = (bf16[128,512]{1,0:T(8,128)(2,1)S(1)}, bf16[128,512]{1,0:T(8,128)(2,1)S(1)}, u32[]{:S(2)}, u32[]{:S(2)}) collective-permute-start(bf16[128,512]{1,0:T(8,128)(2,1)S(1)} %get-tuple-element.214), channel_id=1, source_target_pairs={{0,2},{1,3},{2,4},{3,5},{4,6},{5,7},{6,0},{7,1},{8,10},{9,11},{10,... | collective-permute-start | bytes 393224 | tf_op jit(solution)/shard_map/ppermute | solution.py:819
  311.8 15.3 %collective-permute-start.30 = (bf16[128,512]{1,0:T(8,128)(2,1)S(1)}, bf16[128,512]{1,0:T(8,128)(2,1)S(1)}, u32[]{:S(2)}, u32[]{:S(2)}) collective-permute-start(bf16[128,512]{1,0:T(8,128)(2,1)S(1)} %get-tuple-element.214), channel_id=1, source_target_pairs={{0,4},{1,5},{2,6},{3,7},{4,0},{5,1},{6,2},{7,3},{8,12},{9,13},{10,... | collective-permute-start | bytes 393224 | tf_op jit(solution)/shard_map/ppermute | solution.py:819
  314.2 13.8 %collective-permute-start.31 = (bf16[128,512]{1,0:T(8,128)(2,1)S(1)}, bf16[128,512]{1,0:T(8,128)(2,1)S(1)}, u32[]{:S(2)}, u32[]{:S(2)}) collective-permute-start(bf16[128,512]{1,0:T(8,128)(2,1)S(1)} %get-tuple-element.214), channel_id=1, source_target_pairs={{0,6},{1,7},{2,0},{3,1},{4,2},{5,3},{6,4},{7,5},{8,14},{9,15},{10,... | collective-permute-start | bytes 393224 | tf_op jit(solution)/shard_map/ppermute | solution.py:819
  325.6 9.9 %collective-permute-start.25 = (bf16[4,128,512]{2,1,0:T(8,128)(2,1)S(1)}, bf16[4,128,512]{2,1,0:T(8,128)(2,1)S(1)}, u32[]{:S(2)}, u32[]{:S(2)}) collective-permute-start(bf16[4,128,512]{2,1,0:T(8,128)(2,1)S(1)} %get-tuple-element.206), channel_id=1, source_target_pairs={{0,1},{1,0},{2,3},{3,2},{4,5},{5,4},{6,7},{7,6},{8,9},{9,8},{10,11... | collective-permute-start | bytes 1572872 | tf_op jit(solution)/shard_map/ppermute | solution.py:819
  328.0 32.0 %copy-start.15 = (f32[6,512]{1,0:T(8,128)S(1)}, f32[6,512]{1,0:T(8,128)}, u32[]{:S(2)}) copy-start(f32[6,512]{1,0:T(8,128)} %refs_5_.5) | copy-start | bytes 36868
  328.1 32.0 %copy-start.16 = (f32[6,512]{1,0:T(8,128)S(1)}, f32[6,512]{1,0:T(8,128)}, u32[]{:S(2)}) copy-start(f32[6,512]{1,0:T(8,128)} %param.31) | copy-start | bytes 36868
  328.1 32.0 %copy-start.17 = (f32[6,512]{1,0:T(8,128)S(1)}, f32[6,512]{1,0:T(8,128)}, u32[]{:S(2)}) copy-start(f32[6,512]{1,0:T(8,128)} %param.35) | copy-start | bytes 36868
  328.1 35.5 %copy-start.1 = (bf16[8,2,2,4,16,512]{5,4,3,2,1,0:T(8,128)(2,1)S(1)}, bf16[8,2,2,4,16,512]{5,4,3,2,1,0:T(8,128)(2,1)}, u32[]{:S(2)}) copy-start(bf16[8,2,2,4,16,512]{5,4,3,2,1,0:T(8,128)(2,1)} %copy-done) | copy-start | bytes 6291460
  328.1 14.9 %collective-permute-start.32 = (bf16[4,128,512]{2,1,0:T(8,128)(2,1)S(1)}, bf16[4,128,512]{2,1,0:T(8,128)(2,1)S(1)}, u32[]{:S(2)}, u32[]{:S(2)}) collective-permute-start(bf16[4,128,512]{2,1,0:T(8,128)(2,1)S(1)} %pad_maximum_fusion.2), channel_id=1, source_target_pairs={{0,16},{8,24},{16,0},{24,8},{1,17},{9,25},{17,1},{25,9},{2,18},{10... | collective-permute-start | bytes 1572872 | tf_op jit(solution)/shard_map/ppermute | solution.py:819
  335.6 23.9 %collective-permute-start.26 = (bf16[2,4,128,512]{3,2,1,0:T(8,128)(2,1)S(1)}, bf16[2,4,128,512]{3,2,1,0:T(8,128)(2,1)S(1)}, u32[]{:S(2)}, u32[]{:S(2)}) collective-permute-start(bf16[2,4,128,512]{3,2,1,0:T(8,128)(2,1)S(1)} %pad_maximum_fusion.refs_0_), channel_id=1, source_target_pairs={{0,16},{8,24},{16,0},{24,8},{1,17},{9,25},{17,1},{25,9},{2,18},{10... | collective-permute-start | bytes 3145736 | tf_op jit(solution)/shard_map/ppermute | solution.py:819
  343.1 16.4 %collective-permute-start.33 = (bf16[8,128,512]{2,1,0:T(8,128)(2,1)S(1)}, bf16[8,128,512]{2,1,0:T(8,128)(2,1)S(1)}, u32[]{:S(2)}, u32[]{:S(2)}) collective-permute-start(bf16[8,128,512]{2,1,0:T(8,128)(2,1)S(1)} %constant_dynamic-update-slice_fusion.refs_4_), channel_id=1, source_target_pairs={{0,1},{1,0},{2,3},{3,2},{4,5},{5,4},{6,7},{7,6},{8,9},{9,8},{10,11... | collective-permute-start | bytes 3145736 | tf_op jit(solution)/shard_map/ppermute | solution.py:819
  344.5 16.2 %collective-permute-start.27 = (bf16[2,4,128,512]{3,2,1,0:T(8,128)(2,1)S(1)}, bf16[2,4,128,512]{3,2,1,0:T(8,128)(2,1)S(1)}, u32[]{:S(2)}, u32[]{:S(2)}) collective-permute-start(bf16[2,4,128,512]{3,2,1,0:T(8,128)(2,1)S(1)} %pad_maximum_fusion.refs_0_), channel_id=1, source_target_pairs={{0,8},{8,0},{16,24},{24,16},{1,9},{9,1},{17,25},{25,17},{2,10},{10... | collective-permute-start | bytes 3145736 | tf_op jit(solution)/shard_map/ppermute | solution.py:819
  344.5 16.2 %collective-permute-start.34 = (bf16[8,128,512]{2,1,0:T(8,128)(2,1)S(1)}, bf16[8,128,512]{2,1,0:T(8,128)(2,1)S(1)}, u32[]{:S(2)}, u32[]{:S(2)}) collective-permute-start(bf16[8,128,512]{2,1,0:T(8,128)(2,1)S(1)} %constant_dynamic-update-slice_fusion.refs_4_), channel_id=1, source_target_pairs={{0,8},{8,0},{16,24},{24,16},{1,9},{9,1},{17,25},{25,17},{2,10},{10... | collective-permute-start | bytes 3145736 | tf_op jit(solution)/shard_map/ppermute | solution.py:819
  359.4 2.7 collective-permute-start.28
  359.4 4.2 %collective-permute-start.35 = (bf16[8,128,512]{2,1,0:T(8,128)(2,1)S(1)}, bf16[8,128,512]{2,1,0:T(8,128)(2,1)S(1)}, u32[]{:S(2)}, u32[]{:S(2)}) collective-permute-start(bf16[8,128,512]{2,1,0:T(8,128)(2,1)S(1)} %collective-permute-done.33.refs_5_), channel_id=1, source_target_pairs={{0,8},{8,0},{16,24},{24,16},{1,9},{9,1},{17,25},{25,17},{2,10},{10... | collective-permute-start | bytes 3145736 | tf_op jit(solution)/shard_map/ppermute | solution.py:819
